TPU v7x, 32 devices: a whole 2x2x4 slice. The times are simulated.
32 devices in a mesh: dp: 4 (over z), ctx: 4 (over y, x), tp: 2 (over core).
Axes of the slice: x: 2, y: 2, z: 4, core: 2. Of those that a mesh axis runs over, the one named last changes fastest.
Arguments:
- tokens: float32 [32, 580, 384], P('dp', 'ctx'), may hold values from -6 to 6
- valid_mask: int32 [32, 580], P('dp', 'ctx'), may hold values from 0 to 1, as said below
- cotangent: float32 [32, 580, 384], P('dp', 'ctx'), may hold values from -6 to 6
- w_query: bfloat16 [384, 384], P('dp', 'tp'), may hold values from -0.3125 to 0.3125
- w_key: bfloat16 [384, 384], P('dp', 'tp'), may hold values from -0.3125 to 0.3125
- w_value: bfloat16 [384, 384], P('dp', 'tp'), may hold values from -0.3125 to 0.3125
- query_bias: bfloat16 [384], P('tp'), may hold values from -3 to 3
- value_bias: bfloat16 [384], P('tp'), may hold values from -3 to 3
- w_out: bfloat16 [384, 384], P('tp', 'dp'), may hold values from -1.25 to 1.25
- w_up: bfloat16 [384, 1536], P('dp', 'tp'), may hold values from -0.3125 to 0.3125
- up_bias: bfloat16 [1536], P('tp'), may hold values from -3 to 3
- w_down: bfloat16 [1536, 384], P('tp', 'dp'), may hold values from -0.15625 to 0.15625
- norm1_gain: bfloat16 [384], P('dp'), may hold values from 0.25 to 1.75
- norm1_shift: bfloat16 [384], P('dp'), may hold values from -2 to 2
- norm2_gain: bfloat16 [384], P('dp'), may hold values from 0.25 to 1.75
- norm2_shift: bfloat16 [384], P('dp'), may hold values from -2 to 2
- out_bias: bfloat16 [384], P('dp'), may hold values from -2 to 2
- down_bias: bfloat16 [384], P('dp'), may hold values from -2 to 2
Outputs:
- block_out: float32 [32, 580, 384], P('dp', 'ctx')
- input_grad: float32 [32, 580, 384], P('dp', 'ctx')
- grad_query: float32 [384, 384], P('dp', 'tp')
- grad_key: float32 [384, 384], P('dp', 'tp')
- grad_value: float32 [384, 384], P('dp', 'tp')
- grad_query_bias: float32 [384], P('tp')
- grad_value_bias: float32 [384], P('tp')
- grad_out: float32 [384, 384], P('tp', 'dp')
- grad_up: float32 [384, 1536], P('dp', 'tp')
- grad_up_bias: float32 [1536], P('tp')
- grad_down: float32 [1536, 384], P('tp', 'dp')
- grad_norm1_gain: float32 [384], P('dp')
- grad_norm1_shift: float32 [384], P('dp')
- grad_norm2_gain: float32 [384], P('dp')
- grad_norm2_shift: float32 [384], P('dp')
- grad_out_bias: float32 [384], P('dp')
- grad_down_bias: float32 [384], P('dp')
Inputs may be any that keep to these rules, and one draw needn't show every extreme that they name: `valid_mask`: in every image each block of 145 slots (slots c * 145 to (c + 1) * 145 - 1) has its first 144 slots valid; in exactly one block of each image, the last slot is valid too; all other slots are 0.
All inputs are finite; a program needn't handle non-finite values.
Results may differ from a plain program's by a relative error of at most 0.018.
Values may be sent and summed in bfloat16 or wider, within the bound.
No kernel may reach another device: no remote copies, remote signals or barrier semaphores. Data moves between devices by JAX's collectives and lax.ppermute only.
A program may use at most 128 MiB of HBM per device.

v0:
```python
import jax
import jax.numpy as jnp
from jax import lax
from jax.sharding import PartitionSpec as P

HD = 64


EPS = 1e-06
SCALE = 0.125
FLOOR = -1e30


def layer_norm(values, gain_vec, shift_vec):
    row_mean = jnp.mean(values, axis=-1, keepdims=True)
    centered = values - row_mean
    spread = jnp.mean(centered * centered, axis=-1, keepdims=True)
    return centered * lax.rsqrt(spread + EPS) * gain_vec + shift_vec


def gelu_exact(values):
    return jax.nn.gelu(values, approximate=False)


def masked_scores(queries, keys_all, key_valid):
    scores = (
        jnp.einsum("iqhd,ikhd->ihqk", queries, keys_all, preferred_element_type=jnp.float32) * SCALE
    )
    return jnp.where(key_valid[:, None, None, :] > 0, scores, FLOOR)


def body(
    tokens,
    valid_mask,
    cotangent,
    w_query,
    w_key,
    w_value,
    query_bias,
    value_bias,
    w_out,
    w_up,
    up_bias,
    w_down,
    norm1_gain,
    norm1_shift,
    norm2_gain,
    norm2_shift,
    out_bias,
    down_bias,
):
    img_count, blk_rows, feat_width = tokens.shape
    tok_rows = img_count * blk_rows
    fetched = (
        lax.all_gather(w_query, "dp", axis=0, tiled=True),
        lax.all_gather(w_key, "dp", axis=0, tiled=True),
        lax.all_gather(w_value, "dp", axis=0, tiled=True),
        lax.all_gather(w_out, "dp", axis=1, tiled=True),
        lax.all_gather(w_up, "dp", axis=0, tiled=True),
        lax.all_gather(w_down, "dp", axis=1, tiled=True),
        lax.all_gather(norm1_gain, "dp", axis=0, tiled=True),
        lax.all_gather(norm1_shift, "dp", axis=0, tiled=True),
        lax.all_gather(norm2_gain, "dp", axis=0, tiled=True),
        lax.all_gather(norm2_shift, "dp", axis=0, tiled=True),
        lax.all_gather(out_bias, "dp", axis=0, tiled=True),
        lax.all_gather(down_bias, "dp", axis=0, tiled=True),
    )
    query_full, key_full, value_full, out_full, up_full, down_full = fetched[:6]
    gain_one = fetched[6].astype(jnp.float32)
    shift_one = fetched[7].astype(jnp.float32)
    gain_two = fetched[8].astype(jnp.float32)
    shift_two = fetched[9].astype(jnp.float32)
    bias_attn = fetched[10].astype(jnp.float32)
    bias_mlp = fetched[11].astype(jnp.float32)
    heads_local = query_full.shape[1] // HD
    resid_in = tokens.reshape(tok_rows, feat_width)
    valid_rows = valid_mask.reshape(tok_rows).astype(jnp.float32)[:, None]
    normed_one_f, norm_one_back = jax.vjp(layer_norm, resid_in, gain_one, shift_one)
    normed_one = normed_one_f.astype(jnp.bfloat16)
    queries = (
        jnp.dot(normed_one, query_full, preferred_element_type=jnp.float32)
        + query_bias.astype(jnp.float32)
    ).astype(jnp.bfloat16)
    keys_local = jnp.dot(normed_one, key_full, preferred_element_type=jnp.float32).astype(
        jnp.bfloat16
    )
    values_local = (
        jnp.dot(normed_one, value_full, preferred_element_type=jnp.float32)
        + value_bias.astype(jnp.float32)
    ).astype(jnp.bfloat16)
    query_heads = queries.reshape(img_count, blk_rows, heads_local, HD)
    key_heads = keys_local.reshape(img_count, blk_rows, heads_local, HD)
    value_heads = values_local.reshape(img_count, blk_rows, heads_local, HD)
    keys_seq, values_seq, valid_seq = (
        lax.all_gather(key_heads, "ctx", axis=1, tiled=True),
        lax.all_gather(value_heads, "ctx", axis=1, tiled=True),
        lax.all_gather(valid_mask.astype(jnp.bfloat16), "ctx", axis=1, tiled=True),
    )
    scores = masked_scores(query_heads, keys_seq, valid_seq)
    row_peak = jnp.max(scores, axis=-1, keepdims=True)
    log_total = row_peak + jnp.log(jnp.sum(jnp.exp(scores - row_peak), axis=-1, keepdims=True))
    weights = jnp.exp(scores - log_total).astype(jnp.bfloat16)
    context = jnp.einsum("ihqk,ikhd->iqhd", weights, values_seq, preferred_element_type=jnp.float32)
    context = context.astype(jnp.bfloat16).reshape(tok_rows, heads_local * HD)
    attended = (
        lax.psum(jnp.dot(context, out_full, preferred_element_type=jnp.float32), "tp") + bias_attn
    )
    middle = resid_in + valid_rows * attended
    normed_two_f, norm_two_back = jax.vjp(layer_norm, middle, gain_two, shift_two)
    normed_two = normed_two_f.astype(jnp.bfloat16)
    hidden_pre = jnp.dot(normed_two, up_full, preferred_element_type=jnp.float32) + up_bias.astype(
        jnp.float32
    )
    hidden_f, gelu_back = jax.vjp(gelu_exact, hidden_pre)
    hidden = hidden_f.astype(jnp.bfloat16)
    mlp_out = (
        lax.psum(
            jnp.dot(hidden, down_full, preferred_element_type=jnp.float32).astype(jnp.bfloat16),
            "tp",
        ).astype(jnp.float32)
        + bias_mlp
    )
    block_out = middle + valid_rows * mlp_out
    out_grad = cotangent.reshape(tok_rows, feat_width)
    down_cot = (valid_rows * out_grad).astype(jnp.bfloat16)
    grad_bias_mlp = jnp.sum(down_cot.astype(jnp.float32), axis=0)
    grad_down_local = jnp.einsum("tf,td->fd", hidden, down_cot, preferred_element_type=jnp.float32)
    hidden_cot = jnp.einsum("td,fd->tf", down_cot, down_full, preferred_element_type=jnp.float32)
    hidden_grad = gelu_back(hidden_cot)[0].astype(jnp.bfloat16)
    grad_up_bias_local = jnp.sum(hidden_grad.astype(jnp.float32), axis=0)
    grad_up_local = jnp.einsum(
        "td,tf->df", normed_two, hidden_grad, preferred_element_type=jnp.float32
    )
    normed_two_grad = lax.psum(
        jnp.einsum("tf,df->td", hidden_grad, up_full, preferred_element_type=jnp.float32), "tp"
    )
    middle_part, grad_gain_two, grad_shift_two = norm_two_back(normed_two_grad)
    middle_grad = out_grad + middle_part
    attended_grad = (valid_rows * middle_grad).astype(jnp.bfloat16)
    grad_bias_attn = jnp.sum(attended_grad.astype(jnp.float32), axis=0)
    grad_out_local = jnp.einsum(
        "tc,td->cd", context, attended_grad, preferred_element_type=jnp.float32
    )
    context_grad = jnp.einsum(
        "td,cd->tc", attended_grad, out_full, preferred_element_type=jnp.float32
    )
    context_grad = context_grad.astype(jnp.bfloat16).reshape(img_count, blk_rows, heads_local, HD)
    scores = masked_scores(query_heads, keys_seq, valid_seq)
    probabilities = jnp.exp(scores - log_total)
    weights_grad = jnp.einsum(
        "iqhd,ikhd->ihqk", context_grad, values_seq, preferred_element_type=jnp.float32
    )
    inner_sum = jnp.sum(probabilities * weights_grad, axis=-1, keepdims=True)
    scores_grad = (probabilities * (weights_grad - inner_sum)).astype(jnp.bfloat16)
    queries_grad = (
        jnp.einsum("ihqk,ikhd->iqhd", scores_grad, keys_seq, preferred_element_type=jnp.float32)
        * SCALE
    )
    queries_grad = queries_grad.astype(jnp.bfloat16).reshape(tok_rows, heads_local * HD)
    weights = probabilities.astype(jnp.bfloat16)
    values_grad_seq = jnp.einsum(
        "ihqk,iqhd->ikhd", weights, context_grad, preferred_element_type=jnp.float32
    )
    keys_grad_seq = (
        jnp.einsum("ihqk,iqhd->ikhd", scores_grad, query_heads, preferred_element_type=jnp.float32)
        * SCALE
    )
    keys_grad, values_grad = (
        lax.psum_scatter(
            keys_grad_seq.astype(jnp.bfloat16), "ctx", scatter_dimension=1, tiled=True
        ).astype(jnp.float32),
        lax.psum_scatter(
            values_grad_seq.astype(jnp.bfloat16), "ctx", scatter_dimension=1, tiled=True
        ).astype(jnp.float32),
    )
    keys_grad = keys_grad.astype(jnp.bfloat16).reshape(tok_rows, heads_local * HD)
    values_grad = values_grad.astype(jnp.bfloat16).reshape(tok_rows, heads_local * HD)
    grad_qbias_local = jnp.sum(queries_grad.astype(jnp.float32), axis=0)
    grad_vbias_local = jnp.sum(values_grad.astype(jnp.float32), axis=0)
    grad_query_local = jnp.einsum(
        "td,tc->dc", normed_one, queries_grad, preferred_element_type=jnp.float32
    )
    grad_key_local = jnp.einsum(
        "td,tc->dc", normed_one, keys_grad, preferred_element_type=jnp.float32
    )
    grad_value_local = jnp.einsum(
        "td,tc->dc", normed_one, values_grad, preferred_element_type=jnp.float32
    )
    normed_one_part = (
        jnp.einsum("tc,dc->td", queries_grad, query_full, preferred_element_type=jnp.float32)
        + jnp.einsum("tc,dc->td", keys_grad, key_full, preferred_element_type=jnp.float32)
        + jnp.einsum("tc,dc->td", values_grad, value_full, preferred_element_type=jnp.float32)
    )
    normed_one_grad = lax.psum(normed_one_part.astype(jnp.bfloat16), "tp").astype(jnp.float32)
    input_part, grad_gain_one, grad_shift_one = norm_one_back(normed_one_grad)
    input_grad = middle_grad + input_part
    shares = (
        lax.psum_scatter(
            grad_query_local.astype(jnp.bfloat16), "dp", scatter_dimension=0, tiled=True
        ).astype(jnp.float32),
        lax.psum_scatter(
            grad_key_local.astype(jnp.bfloat16), "dp", scatter_dimension=0, tiled=True
        ).astype(jnp.float32),
        lax.psum_scatter(
            grad_value_local.astype(jnp.bfloat16), "dp", scatter_dimension=0, tiled=True
        ).astype(jnp.float32),
        lax.psum_scatter(
            grad_out_local.astype(jnp.bfloat16), "dp", scatter_dimension=1, tiled=True
        ).astype(jnp.float32),
        lax.psum_scatter(
            grad_up_local.astype(jnp.bfloat16), "dp", scatter_dimension=0, tiled=True
        ).astype(jnp.float32),
        lax.psum_scatter(
            grad_down_local.astype(jnp.bfloat16), "dp", scatter_dimension=1, tiled=True
        ).astype(jnp.float32),
        lax.psum_scatter(
            grad_gain_one.astype(jnp.bfloat16), "dp", scatter_dimension=0, tiled=True
        ).astype(jnp.float32),
        lax.psum_scatter(
            grad_shift_one.astype(jnp.bfloat16), "dp", scatter_dimension=0, tiled=True
        ).astype(jnp.float32),
        lax.psum_scatter(
            grad_gain_two.astype(jnp.bfloat16), "dp", scatter_dimension=0, tiled=True
        ).astype(jnp.float32),
        lax.psum_scatter(
            grad_shift_two.astype(jnp.bfloat16), "dp", scatter_dimension=0, tiled=True
        ).astype(jnp.float32),
        lax.psum_scatter(
            grad_bias_attn.astype(jnp.bfloat16), "dp", scatter_dimension=0, tiled=True
        ).astype(jnp.float32),
        lax.psum_scatter(
            grad_bias_mlp.astype(jnp.bfloat16), "dp", scatter_dimension=0, tiled=True
        ).astype(jnp.float32),
    )
    owned = (
        lax.psum(shares[0].astype(jnp.bfloat16), "ctx").astype(jnp.float32),
        lax.psum(shares[1].astype(jnp.bfloat16), "ctx").astype(jnp.float32),
        lax.psum(shares[2].astype(jnp.bfloat16), "ctx").astype(jnp.float32),
        lax.psum(shares[3].astype(jnp.bfloat16), "ctx").astype(jnp.float32),
        lax.psum(shares[4].astype(jnp.bfloat16), "ctx").astype(jnp.float32),
        lax.psum(shares[5].astype(jnp.bfloat16), "ctx").astype(jnp.float32),
        lax.psum(shares[6].astype(jnp.bfloat16), "ctx").astype(jnp.float32),
        lax.psum(shares[7].astype(jnp.bfloat16), "ctx").astype(jnp.float32),
        lax.psum(shares[8].astype(jnp.bfloat16), "ctx").astype(jnp.float32),
        lax.psum(shares[9].astype(jnp.bfloat16), "ctx").astype(jnp.float32),
        lax.psum(shares[10].astype(jnp.bfloat16), "ctx").astype(jnp.float32),
        lax.psum(shares[11].astype(jnp.bfloat16), "ctx").astype(jnp.float32),
    )
    grad_qbias, grad_vbias, grad_ubias = lax.psum(
        (grad_qbias_local, grad_vbias_local, grad_up_bias_local), ("dp", "ctx")
    )
    return (
        block_out.reshape(img_count, blk_rows, feat_width),
        input_grad.reshape(img_count, blk_rows, feat_width),
        owned[0],
        owned[1],
        owned[2],
        grad_qbias,
        grad_vbias,
        owned[3],
        owned[4],
        grad_ubias,
        owned[5],
        owned[6],
        owned[7],
        owned[8],
        owned[9],
        owned[10],
        owned[11],
    )


def solution(mesh):
    placed = (
        P("dp", "ctx", None),
        P("dp", "ctx"),
        P("dp", "ctx", None),
        P("dp", "tp"),
        P("dp", "tp"),
        P("dp", "tp"),
        P("tp"),
        P("tp"),
        P("tp", "dp"),
        P("dp", "tp"),
        P("tp"),
        P("tp", "dp"),
        P("dp"),
        P("dp"),
        P("dp"),
        P("dp"),
        P("dp"),
        P("dp"),
    )
    return jax.shard_map(
        body,
        mesh=mesh,
        in_specs=placed,
        out_specs=(
            P("dp", "ctx", None),
            P("dp", "ctx", None),
            P("dp", "tp"),
            P("dp", "tp"),
            P("dp", "tp"),
            P("tp"),
            P("tp"),
            P("tp", "dp"),
            P("dp", "tp"),
            P("tp"),
            P("tp", "dp"),
            P("dp"),
            P("dp"),
            P("dp"),
            P("dp"),
            P("dp"),
            P("dp"),
        ),
        check_vma=False,
    )
```

profile of v0, /device:TPU:0, one launch (start us, length us, event | category | flops | bytes accessed | tf_op | source)
XLA Modules:
  0.0 574.1 jit_solution(2995554381992637526)
XLA Ops:
  13.6 13.7 %all-reduce.18 = (bf16[384]{0:T(512)(128)(2,1)S(1)}, bf16[384]{0:T(512)(128)(2,1)S(1)}, bf16[384]{0:T(512)(128)(2,1)S(1)}, bf16[384]{0:T(512)(128)(2,1)S(1)}, bf16[384]{0:T(512)(128)(2,1)S(1)}) all-reduce(bf16[384]{0:T(512)(128)(2,1)S(1)} %dynamic-update-slice.1, ...), channel_id=1, replica_groups=mesh['dp'=4,'ctx'=4,'tp'=2] {'dp'}, use_global_device_ids=true, to_apply=%add.1 | all-reduce | flops 1920 | bytes 7680
  28.5 13.6 %all_gather.51 = bf16[384,192]{1,0:T(8,128)(2,1)S(1)} all-gather(bf16[96,192]{1,0:T(8,128)(2,1)S(1)} %copy-done.53), channel_id=1, replica_groups=mesh['dp'=4,'ctx'=4,'tp'=2] {'dp'}, dimensions={0}, use_global_device_ids=true | all-gather | bytes 184320 | tf_op jit(solution)/shard_map/all_gather | solution.py:56
  50.5 13.6 %all_gather.47 = bf16[384,192]{1,0:T(8,128)(2,1)S(1)} all-gather(bf16[96,192]{1,0:T(8,128)(2,1)S(1)} %copy-done.54), channel_id=1, replica_groups=mesh['dp'=4,'ctx'=4,'tp'=2] {'dp'}, dimensions={0}, use_global_device_ids=true | all-gather | bytes 184320 | tf_op jit(solution)/shard_map/all_gather | solution.py:57
  70.8 8.3 %all-gather = bf16[4,145,8]{1,2,0:T(8,128)(2,1)S(1)} all-gather(bf16[1,145,8]{1,2,0:T(8,128)(2,1)S(1)} %get-tuple-element.134), channel_id=1, replica_groups=mesh['dp'=4,'ctx'=4,'tp'=2] {'ctx'}, dimensions={0}, use_global_device_ids=true | all-gather | bytes 11600 | tf_op jit(solution)/shard_map/all_gather | solution.py:97
  79.4 14.2 %all_gather.50 = bf16[384,192]{1,0:T(8,128)(2,1)S(1)} all-gather(bf16[96,192]{1,0:T(8,128)(2,1)} %param.21), channel_id=1, replica_groups=mesh['dp'=4,'ctx'=4,'tp'=2] {'dp'}, dimensions={0}, use_global_device_ids=true | all-gather | bytes 184320 | tf_op jit(solution)/shard_map/all_gather | solution.py:55
  97.9 13.9 %all_gather.53 = bf16[192,384]{0,1:T(8,128)(2,1)S(1)} all-gather(bf16[192,96]{0,1:T(8,128)(2,1)S(1)} %copy.100), channel_id=1, replica_groups=mesh['dp'=4,'ctx'=4,'tp'=2] {'dp'}, dimensions={1}, use_global_device_ids=true | all-gather | bytes 184320 | tf_op jit(solution)/shard_map/all_gather | solution.py:58
  111.7 5.6 copy.97
  124.6 21.7 %all-gather.4.cloned.1.call-done = bf16[8,580,3,64]{3,0,2,1:T(8,128)(2,1)} async-done(((bf16[8,145,3,64]{3,0,2,1:T(8,128)(2,1)}), bf16[8,580,3,64]{3,0,2,1:T(8,128)(2,1)}) %all-gather.4.cloned.1.call-update) | async-done | bytes 1781776 | tf_op jit(solution)/shard_map/all_gather | solution.py:96
  146.3 5.6 copy.98
  151.9 6.7 %fusion.16 = bf16[8,145,3,64]{1,3,2,0:T(8,128)(2,1)S(1)} fusion(bf16[8,580,3,64]{1,3,2,0:T(8,128)(2,1)} %copy.98, f32[8,3,145,580]{3,2,1,0:T(8,128)} %copy-done, f32[8,3,145]{2,1,0:T(4,128)S(1)} %log_add_fusion, pred[8,580]{1,0:T(8,128)(4,1)S(1)} %bitcast.95), kind=kOutput, calls=%fused_computation.67 | convolution fusion | flops 266651520 | bytes 10319360 | tf_op jit(solution)/shard_map/ihqk,ikhd->iqhd/dot_general | solution.py:103
  170.1 16.7 %all_gather.57 = bf16[384,768]{1,0:T(8,128)(2,1)} all-gather(bf16[96,768]{1,0:T(8,128)(2,1)S(1)} %copy-done.40), channel_id=1, replica_groups=mesh['dp'=4,'ctx'=4,'tp'=2] {'dp'}, dimensions={0}, use_global_device_ids=true | all-gather | bytes 737280 | tf_op jit(solution)/shard_map/all_gather | solution.py:59
  186.8 17.6 %all_gather.58 = bf16[768,384]{0,1:T(8,128)(2,1)} all-gather(bf16[768,96]{0,1:T(8,128)(2,1)S(1)} %copy-done.41), channel_id=1, replica_groups=mesh['dp'=4,'ctx'=4,'tp'=2] {'dp'}, dimensions={1}, use_global_device_ids=true | all-gather | bytes 737280 | tf_op jit(solution)/shard_map/all_gather | solution.py:60
  206.9 9.9 %multiply_convert_fusion.2 = (bf16[1160,768]{1,0:T(8,128)(2,1)}, f32[1160,768]{1,0:T(8,128)S(1)}, f32[1160,768]{1,0:T(8,128)S(1)}) fusion(f32[768]{0:T(1024)S(1)} %convert_element_type.249, bf16[384,768]{1,0:T(8,128)(2,1)S(1)} %copy-done.33, f32[1160,384]{1,0:T(8,128)S(1)} %get-tuple-element.130, f32[384]{0:T(512)S(1)} %convert_element_type.247, ...), kind=kOutput, calls=%fused_computation.13 | convolution fusion | flops 745221120 | bytes 11295808 | tf_op jit(solution)/shard_map/dot_general | solution.py:111
  223.6 4.0 convolution_convert_fusion.4
  227.6 4.6 convolution_convert_fusion.5
  232.8 11.1 %all-reduce.28.cloned.1.call-done = f32[1160,384]{1,0:T(8,128)} async-done(((f32[1160,384]{1,0:T(8,128)}), f32[1160,384]{1,0:T(8,128)}) %all-reduce.28.cloned.1.call-update) | async-done | bytes 1781776 | tf_op jit(solution)/shard_map/psum | solution.py:134
  255.0 8.2 %multiply_reduce_fusion = (f32[8,3,145]{2,1,0:T(4,128)S(1)}, f32[8,3,145,580]{3,2,1,0:T(8,128)S(1)}) fusion(f32[8,3,145,580]{3,2,1,0:T(8,128)} %copy-done, f32[8,3,145]{2,1,0:T(4,128)} %copy-done.34, pred[8,580]{1,0:T(8,128)(4,1)S(1)} %bitcast.96, bf16[8,580,3,64]{1,3,2,0:T(8,128)(2,1)} %copy.98, bf16[8,145,3,64]{1,0,3,2:T(8,128)(2,1)} %reshape.248), kind=kOutput, calls=%fused_computation.1 | convolution fusion | flops 268443712 | bytes 18406880 | tf_op jit(solution)/shard_map/iqhd,ikhd->ihqk/dot_general | solution.py:150
  274.5 17.3 %reduce-scatter.17.cloned.1.call-done = bf16[96,768]{1,0:T(8,128)(2,1)} async-done(((bf16[384,768]{1,0:T(8,128)(2,1)}), bf16[96,768]{1,0:T(8,128)(2,1)}) %reduce-scatter.17.cloned.1.call-update) | async-done | bytes 147472 | tf_op jit(solution)/shard_map/reduce_scatter | solution.py:210
  298.5 6.1 %convert_reduce_fusion.2 = (f32[3,64]{1,0:T(4,128)}, bf16[8,145,3,64]{1,3,2,0:T(8,128)(2,1)S(1)}) fusion(bf16[8,580,3,64]{1,3,2,0:T(8,128)(2,1)} %copy.97, bf16[8,3,145,580]{3,2,1,0:T(8,128)(2,1)} %copy-done.1), kind=kOutput, calls=%fused_computation.62 | convolution fusion | flops 259245888 | bytes 6264768 | tf_op jit(solution)/shard_map/ihqk,ikhd->iqhd/dot_general | solution.py:156
  307.6 91.7 %all-reduce.32.cloned.1.call-done = (bf16[8,580,3,64]{1,3,2,0:T(8,128)(2,1)}, bf16[8,580,3,64]{1,3,2,0:T(8,128)(2,1)}, bf16[96,768]{1,0:T(8,128)(2,1)}, bf16[768,96]{0,1:T(8,128)(2,1)}) async-done(((bf16[8,580,3,64]{1,3,2,0:T(8,128)(2,1)}, bf16[8,580,3,64]{1,3,2,0:T(8,128)(2,1)}, bf16[96,768]{1,0:T(8,128)(2,1)}, bf16[768,96]{0,1:T(8,128)(2,1)}), (bf16[8,580,3,64]{1,3,2,0:T(8,128)(2,1)}, ...) | async-done | bytes 3858448
  428.1 42.3 %all-reduce.14 = (f32[192]{0:T(256)}, f32[192]{0:T(256)}, f32[768]{0:T(1024)}) all-reduce(f32[192]{0:T(256)S(1)} %reduce_sum.227, f32[192]{0:T(256)S(1)} %reduce_sum.229, f32[768]{0:T(1024)} %get-tuple-element.144), channel_id=1, replica_groups=mesh['dp'=4,'ctx'=4,'tp'=2] {'dp','ctx'}, use_global_device_ids=true, to_apply=%region_24.25 | all-reduce | flops 1152 | bytes 9216 | tf_op jit(solution)/shard_map/psum | solution.py:249
  476.1 8.6 %all-reduce.17 = (bf16[384]{0:T(512)(128)(2,1)S(1)}, bf16[384]{0:T(512)(128)(2,1)S(1)}, bf16[384]{0:T(512)(128)(2,1)S(1)}, bf16[384]{0:T(512)(128)(2,1)S(1)}, bf...) all-reduce(bf16[384]{0:T(512)(128)(2,1)S(1)} %dynamic-update-slice., ...), channel_id=1, replica_groups=mesh['dp'=4,'ctx'=4,'tp'=2] {'dp'}, use_global_device_ids=true, to_apply=%add.5 | all-reduce | flops 2688 | bytes 10752
  488.2 17.8 %reduce-scatter.15.cloned.1.call-done = bf16[96,192]{1,0:T(8,128)(2,1)} async-done(((bf16[384,192]{1,0:T(8,128)(2,1)}), bf16[96,192]{1,0:T(8,128)(2,1)}) %reduce-scatter.15.cloned.1.call-update) | async-done | bytes 36880 | tf_op jit(solution)/shard_map/reduce_scatter | solution.py:204
  518.6 36.0 %all-reduce.30.cloned.1.call-done = (bf16[96,192]{1,0:T(8,128)(2,1)}, bf16[96,192]{1,0:T(8,128)(2,1)}, bf16[96,192]{1,0:T(8,128)(2,1)}, bf16[192,96]{1,0:T(8,128...) async-done(((bf16[96,192]{1,0:T(8,128)(2,1)}, ...) | async-done | bytes 148624 | tf_op jit(solution)/shard_map/psum | solution.py:236
  (319 shorter events, 148.1 us)
Async XLA Ops:
  7.2 104.5 %all-gather.6.cloned.1.call-start = ((), (), s32[]{:S(2)}) async-start(), calls=%async_computation.7 | async-start | bytes 4454400 | tf_op jit(solution)/shard_map/all_gather | solution.py:95
  9.3 34.7 %copy-start.36 = (f32[1160]{0:T(1024)}, f32[1160]{0:T(1024)S(1)}, u32[]{:S(2)}) copy-start(f32[1160]{0:T(1024)S(1)} %div.39) | copy-start | bytes 13924
  9.5 18.2 %copy-start.29 = (f32[8,145]{0,1:T(8,128)}, f32[8,145]{0,1:T(8,128)S(1)}, u32[]{:S(2)}) copy-start(f32[8,145]{0,1:T(8,128)S(1)} %copy.91) | copy-start | bytes 13924
  50.4 95.8 %all-gather.4.cloned.1.call-start = ((), (), s32[]{:S(2)}) async-start(), calls=%async_computation.6 | async-start | bytes 4454400 | tf_op jit(solution)/shard_map/all_gather | solution.py:96
  70.7 133.6 %all-reduce.26.cloned.1.call-start = ((), (), s32[]{:S(2)}) async-start(), calls=%async_computation.8 | async-start | bytes 3563520 | tf_op jit(solution)/shard_map/psum | solution.py:106
  70.8 93.0 %copy-start.48 = (f32[8,145]{1,0:T(8,128)}, f32[8,145]{1,0:T(8,128)S(1)}, u32[]{:S(2)}) copy-start(f32[8,145]{1,0:T(8,128)S(1)} %get-tuple-element.133) | copy-start | bytes 13924
  124.6 27.3 %copy-start.34 = (f32[8,3,145]{2,1,0:T(4,128)}, f32[8,3,145]{2,1,0:T(4,128)S(1)}, u32[]{:S(2)}) copy-start(f32[8,3,145]{2,1,0:T(4,128)S(1)} %log_add_fusion) | copy-start | bytes 41764
  163.7 80.2 %all-reduce.28.cloned.1.call-start = ((), (), s32[]{:S(2)}) async-start(), calls=%async_computation.9 | async-start | bytes 3563520 | tf_op jit(solution)/shard_map/psum | solution.py:134
  163.9 84.3 %copy-start.42 = (f32[1160]{0:T(1024)}, f32[1160]{0:T(1024)S(1)}, u32[]{:S(2)}) copy-start(f32[1160]{0:T(1024)S(1)} %convert_element_type.232) | copy-start | bytes 13924
  167.0 19.8 %copy-start.41 = (bf16[768,96]{0,1:T(8,128)(2,1)S(1)}, bf16[768,96]{0,1:T(8,128)(2,1)}, u32[]{:S(2)}) copy-start(bf16[768,96]{0,1:T(8,128)(2,1)} %param.29) | copy-start | bytes 442372
  223.5 50.9 %reduce-scatter.19.cloned.1.call-start = ((), (), s32[]{:S(2)}) async-start(), calls=%async_computation.14 | async-start | bytes 737280 | tf_op jit(solution)/shard_map/reduce_scatter | solution.py:213
  227.6 64.1 %reduce-scatter.17.cloned.1.call-start = ((), (), s32[]{:S(2)}) async-start(), calls=%async_computation.13 | async-start | bytes 737280 | tf_op jit(solution)/shard_map/reduce_scatter | solution.py:210
  232.3 167.1 %all-reduce.32.cloned.1.call-start = ((), (), s32[]{:S(2)}) async-start(), calls=%async_computation.17 | async-start | bytes 8454144
  291.7 132.0 %reduce-scatter.21.cloned.1.call-start = ((), (), s32[]{:S(2)}) async-start(), calls=%async_computation.15 | async-start | bytes 245760
  305.8 95.2 %copy-start.17 = (bf16[1160,192]{0,1:T(8,128)(2,1)}, bf16[1160,192]{0,1:T(8,128)(2,1)S(1)}, u32[]{:S(2)}) copy-start(bf16[1160,192]{0,1:T(8,128)(2,1)S(1)} %reshape.249) | copy-start | bytes 1336324
  307.6 162.8 %all-reduce.34.cloned.1.call-start = ((), (), s32[]{:S(2)}) async-start(), calls=%async_computation.18 | async-start | bytes 3563520 | tf_op jit(solution)/shard_map/psum | solution.py:117
  410.6 77.6 %reduce-scatter.11.cloned.1.call-start = ((), (), s32[]{:S(2)}) async-start(), calls=%async_computation.10 | async-start | bytes 245760 | tf_op jit(solution)/shard_map/reduce_scatter | solution.py:198
  416.4 71.8 %reduce-scatter.13.cloned.1.call-start = ((), (), s32[]{:S(2)}) async-start(), calls=%async_computation.11 | async-start | bytes 245760 | tf_op jit(solution)/shard_map/reduce_scatter | solution.py:201
  419.0 51.3 %copy-start.37 = (f32[1160]{0:T(1024)S(1)}, f32[1160]{0:T(1024)}, u32[]{:S(2)}) copy-start(f32[1160]{0:T(1024)} %copy-done.36) | copy-start | bytes 13924
  419.0 87.0 %reduce-scatter.15.cloned.1.call-start = ((), (), s32[]{:S(2)}) async-start(), calls=%async_computation.12 | async-start | bytes 245760 | tf_op jit(solution)/shard_map/reduce_scatter | solution.py:204
  426.9 45.4 %copy-start.47 = (f32[1160]{0:T(1024)S(1)}, f32[1160]{0:T(1024)}, u32[]{:S(2)}) copy-start(f32[1160]{0:T(1024)} %copy-done.46) | copy-start | bytes 13924
  426.9 45.4 %copy-start.45 = (f32[1160]{0:T(1024)S(1)}, f32[1160]{0:T(1024)}, u32[]{:S(2)}) copy-start(f32[1160]{0:T(1024)} %copy-done.44) | copy-start | bytes 13924
  428.0 126.6 %all-reduce.30.cloned.1.call-start = ((), (), s32[]{:S(2)}) async-start(), calls=%async_computation.16 | async-start | bytes 399360 | tf_op jit(solution)/shard_map/psum | solution.py:236
  473.8 32.2 %copy-start.43 = (f32[1160]{0:T(1024)S(1)}, f32[1160]{0:T(1024)}, u32[]{:S(2)}) copy-start(f32[1160]{0:T(1024)} %copy-done.42) | copy-start | bytes 13924
  (67 other events, 310.6 us)
Sparse Core Ops, SparseCore 0:
  50.6 45.8 all-gather.5
  98.9 47.3 all-gather.3
  163.8 20.7 all-reduce.25
  223.7 20.1 all-reduce.27
  246.0 23.1 reduce-scatter.18
  271.4 20.2 reduce-scatter.16
  295.5 103.8 all-reduce.31
  401.6 19.6 reduce-scatter.20
  424.5 18.9 all-reduce.33
  445.7 20.5 reduce-scatter.10
  468.6 17.6 reduce-scatter.12
  488.5 17.4 reduce-scatter.14
  511.7 42.8 all-reduce.29
where the time goes:
time: 583 us; the launch traced here: 574 us
  waiting for transfers between devices  196 us (34%)
  blocking collectives  162 us (28%)
  matrix products  77 us (13%)
  local copies, waits for them, and re-layouts  75.8 us (13%)
  other arithmetic  44.6 us (8%)
  between operations  17.3 us (3%)
    unnamed x15, waiting for transfers between devices  91.9 us
    psum x1, blocking collectives, body(): lax.psum((grad_qbias_local, grad_vbias_local, grad_up_bias_local), ('dp',...  42.3 us
    psum x1, waiting for transfers between devices, body(): lax.psum(shares[0].astype(jnp.bfloat16), 'ctx').astype(jnp.float32)  36 us
    unnamed x184, local copies, waits for them, and re-layouts  30.1 us
    unnamed x2, blocking collectives  22.3 us
    all_gather x1, waiting for transfers between devices, body(): lax.all_gather(value_heads, 'ctx', axis=1, tiled=True)  21.7 us
    reduce_scatter x1, waiting for transfers between devices, body(): lax.psum_scatter(grad_value_local.astype(jnp.bfloat16), 'dp', scatter_dim...  17.8 us
    all_gather x1, blocking collectives, body(): lax.all_gather(w_down, 'dp', axis=1, tiled=True)  17.6 us
  transfers between devices with their start and end apart: 13, of which 6 were waited for; matrix products, arithmetic and copies ran while one was open for 22% of the time, Pallas kernels for 0%

commit v1 on v0

v1 whole, which is shorter than its diff:
```python
import functools

import jax
import jax.numpy as jnp
from jax import lax
from jax.experimental import pallas as pl
from jax.experimental.pallas import tpu as pltpu
from jax.sharding import PartitionSpec as P

HD = 64
EPS = 1e-06
SCALE = 0.125
FLOOR = -1e30
BF = jnp.bfloat16
F32 = jnp.float32
TILE = 128
EXTRA = 16
VMEM_LIMIT = 56 * 1024 * 1024


def call(kernel, out_shape, scratch=(), flops=0, smem=()):
    def run(*args):
        specs = [
            pl.BlockSpec(memory_space=pltpu.SMEM if i in smem else pltpu.VMEM)
            for i in range(len(args))
        ]
        return pl.pallas_call(
            kernel,
            out_shape=out_shape,
            in_specs=specs,
            out_specs=jax.tree.map(lambda _: pl.BlockSpec(memory_space=pltpu.VMEM), out_shape),
            scratch_shapes=list(scratch),
            compiler_params=pltpu.CompilerParams(vmem_limit_bytes=VMEM_LIMIT),
            cost_estimate=pl.CostEstimate(flops=flops, bytes_accessed=1 << 20, transcendentals=0),
        )(*args)

    return run


def sds(shape, dtype):
    return jax.ShapeDtypeStruct(shape, dtype)


def nn(a, b):
    return lax.dot_general(a, b, (((1,), (0,)), ((), ())), preferred_element_type=F32)


def nt(a, b):
    return lax.dot_general(a, b, (((1,), (1,)), ((), ())), preferred_element_type=F32)


def tn(a, b):
    return lax.dot_general(a, b, (((0,), (0,)), ((), ())), preferred_element_type=F32)


def swap(v):
    return pltpu.roll(v, HD, axis=1)


def low_lanes(shape):
    return lax.broadcasted_iota(jnp.int32, shape, 1) < HD


def row_is(shape, row):
    return lax.broadcasted_iota(jnp.int32, shape, 0) == row


def tile(v, i):
    return v[:, i * TILE : (i + 1) * TILE]


def assemble(own, oth):
    low = low_lanes((own.shape[0], TILE))
    own_qk, own_vo, oth_qk, oth_vo = tile(own, 4), tile(own, 5), tile(oth, 4), tile(oth, 5)
    qkv = [
        tile(own, 0), tile(oth, 0), jnp.where(low, own_qk, swap(oth_qk)),
        tile(own, 1), tile(oth, 1), jnp.where(low, swap(own_qk), oth_qk),
        tile(own, 2), tile(oth, 2), jnp.where(low, own_vo, swap(oth_vo)),
    ]
    out = [tile(own, 3), tile(oth, 3), jnp.where(low, swap(own_vo), oth_vo)]
    return qkv, out


def disassemble(qkv, out):
    low = low_lanes(qkv[0].shape)
    own = [qkv[0], qkv[3], qkv[6], out[0], jnp.where(low, qkv[2], swap(qkv[5])), jnp.where(low, qkv[8], swap(out[2]))]
    oth = [qkv[1], qkv[4], qkv[7], out[1], jnp.where(low, swap(qkv[2]), qkv[5]), jnp.where(low, swap(qkv[8]), out[2])]
    return own, oth


def norm_stats(v):
    mean = jnp.mean(v, axis=-1, keepdims=True)
    centered = v - mean
    r = lax.rsqrt(jnp.mean(centered * centered, axis=-1, keepdims=True) + EPS)
    return centered * r, r


def norm_back(e, xhat, r):
    return r * (
        e
        - jnp.mean(e, axis=-1, keepdims=True)
        - xhat * jnp.mean(e * xhat, axis=-1, keepdims=True)
    )


def gelu_pair(v):
    a = jnp.abs(v)
    t = 1.0 / (1.0 + (0.3275911 * 0.7071067811865476) * a)
    g = jnp.exp(-0.5 * v * v)
    poly = t * (
        0.254829592 + t * (-0.284496736 + t * (1.421413741 + t * (-1.453152027 + t * 1.061405429)))
    )
    tail = 0.5 * poly * g
    phi = jnp.where(v < 0, tail, 1.0 - tail)
    return v * phi, phi + v * (0.3989422804014327 * g)


def pack_kernel(sizes, tok, cot, mask, wq, wk, wv, wo, wu, wd, qb, vb, ub, *rest):
    nctx, ntp, ndp, main, width, rows, padded = sizes
    vecs, outs = rest[:6], rest[6:]
    t_out, c_out, (p1, p2, tex, cex) = outs[:nctx], outs[nctx : 2 * nctx], outs[2 * nctx :]
    me_c, me_t, me_d = lax.axis_index("ctx"), lax.axis_index("tp"), lax.axis_index("dp")
    for k in range(nctx):
        img = (me_c ^ k) * ntp + me_t
        t_out[k][0:main, :] = tok[img, 0:main, :].astype(BF)
        c_out[k][...] = cot[img, 0:main, :].astype(BF)
        gate = mask[img, main].astype(F32)
        te = tok[img, main : main + 1, :] * gate
        ce = cot[img, main : main + 1, :] * gate
        shape = (EXTRA, width)
        t_out[k][main : main + EXTRA, :] = jnp.where(
            row_is(shape, 0), te, jnp.where(row_is(shape, 1), ce, 0.0)
        ).astype(BF)
    for i in range(nctx * ntp):
        tex[i : i + 1, :] = tok[i, main : main + 1, :]
        cex[i : i + 1, :] = cot[i, main : main + 1, :]

    def put(ref, lo, value):
        ref[0:rows, lo : lo + value.shape[1]] = value.astype(BF)

    if padded > rows:
        p1[0:padded, :] = jnp.zeros((padded, p1.shape[1]), BF)
        for j in range(4):
            p2[j] = jnp.zeros(p2.shape[1:], BF)
    fq, fk, fv = wq[...].astype(F32), wk[...].astype(F32), wv[...].astype(F32)
    fo = jnp.transpose(wo[...].astype(F32))
    for i, w in enumerate((fq, fk, fv, fo)):
        put(p1, i * TILE, tile(w, 0))
    put(p1, 4 * TILE, jnp.concatenate([fq[:, TILE:], fk[:, TILE:]], axis=1))
    put(p1, 5 * TILE, jnp.concatenate([fv[:, TILE:], fo[:, TILE:]], axis=1))
    fd = jnp.transpose(wd[...].astype(F32))
    half = fd.shape[1] // 2
    for j in range(2):
        p2[j, 0:rows, :] = wu[:, j * half : (j + 1) * half]
        p2[2 + j, 0:rows, :] = fd[:, j * half : (j + 1) * half].astype(BF)
    cols = p1.shape[1]
    fqb, fvb = qb[...].astype(F32)[None, :], vb[...].astype(F32)[None, :]
    none = jnp.zeros((1, TILE), F32)
    short = jnp.zeros((1, HD), F32)
    bias = jnp.concatenate(
        [fqb[:, :TILE], none, fvb[:, :TILE], none, fqb[:, TILE:], short, fvb[:, TILE:], short], axis=1
    )
    spread = lax.broadcasted_iota(jnp.int32, (rows, width), 1) == (
        lax.broadcasted_iota(jnp.int32, (rows, width), 0) + rows * me_d
    )
    spread = spread.astype(F32).astype(BF)
    block = jnp.where(row_is((EXTRA, cols), 0), bias, 0.0)
    block = jnp.where(row_is((EXTRA, cols), 7), ub[...].astype(F32)[None, :], block)
    lanes = jnp.zeros((EXTRA, width), F32)
    for i in range(6):
        one = nn(jnp.broadcast_to(vecs[i][...].astype(F32)[None, :], (8, rows)).astype(BF), spread)
        lanes = jnp.where(row_is((EXTRA, width), 1 + i), one[0:1, :], lanes)
    p1[padded : padded + EXTRA, :] = block.astype(BF)
    mixed = jnp.where(
        (lax.broadcasted_iota(jnp.int32, (EXTRA, width), 0) - 1).astype(jnp.uint32) < 6,
        lanes,
        block[:, :width],
    )
    p1[padded : padded + EXTRA, 0:width] = mixed.astype(BF)


def attention_kernel(sizes, *refs):
    nctx, ntp, ndp, main, width, rows, padded = sizes
    t_in, refs = refs[:nctx], refs[nctx:]
    own_in, refs = refs[:ndp], refs[ndp:]
    oth_in, refs = refs[:ndp], refs[ndp:]
    x_out, mid_out, n1_out, n2_out, qkv, ctx, lse, wqkv, wot, vec, ub, cex = refs[:12]
    wf = refs[12]
    me_d = lax.axis_index("dp")
    body = nctx * main
    total = body + EXTRA
    vec_sum = jnp.zeros((EXTRA, width), F32)
    for k in range(ndp):
        own, oth = own_in[k][...].astype(F32), oth_in[k][...].astype(F32)
        tiles, outs = assemble(own[:rows], oth[:rows])
        at = pl.ds(pl.multiple_of((me_d ^ k) * rows, 8), rows)
        for i, v in enumerate(tiles + outs):
            wf[at, i * TILE : (i + 1) * TILE] = v
        vec_sum += own[padded:, :width]
        if k == 0:
            tiles, _ = assemble(own[padded:], oth[padded:])
            bias = jnp.concatenate(tiles, axis=1)[0:1, :]
            ub[...] = jnp.broadcast_to(
                jnp.concatenate([own[padded + 7 : padded + 8], oth[padded + 7 : padded + 8]], axis=1),
                ub.shape,
            )
    vec[...] = vec_sum
    wqkv[...] = wf[:, 0 : 9 * TILE].astype(BF)
    wot[...] = wf[:, 9 * TILE :].astype(BF)
    extra = jnp.zeros((EXTRA, width), F32)
    for k in range(nctx):
        x_out[k * main : (k + 1) * main, :] = t_in[k][0:main, :].astype(F32)
        extra += t_in[k][main:, :].astype(F32)
    x_out[body:, :] = jnp.where(row_is((EXTRA, width), 0), extra, 0.0)
    cex[...] = jnp.where(row_is((EXTRA, width), 0), extra[1:2, :], 0.0).astype(BF)
    x = x_out[...]
    xhat, _ = norm_stats(x)
    n1 = (xhat * vec_sum[1:2, :] + vec_sum[2:3, :]).astype(BF)
    n1_out[...] = n1
    proj = nn(n1, wqkv[...]) + bias
    qkv[0:total, 0:width] = (proj[:, 0:width].astype(BF).astype(F32) * SCALE).astype(BF)
    qkv[0:total, width:] = proj[:, width:].astype(BF)
    keys = qkv.shape[0]
    qkv[total:, :] = jnp.zeros((keys - total, qkv.shape[1]), BF)
    off = jnp.where(lax.broadcasted_iota(jnp.int32, (1, keys), 1) > body, FLOOR, 0.0)
    low = low_lanes((total, TILE))
    lane = lax.broadcasted_iota(jnp.int32, (total, TILE), 1)
    all_lse = jnp.zeros((total, TILE), F32)
    for p in range(3):
        qp = qkv[0:total, p * TILE : (p + 1) * TILE]
        kp = qkv[:, width + p * TILE : width + (p + 1) * TILE]
        vp = qkv[:, 2 * width + p * TILE : 2 * width + (p + 1) * TILE]
        parts = []
        for a in range(2):
            qa = jnp.where(low if a == 0 else ~low, qp, jnp.zeros_like(qp))
            s = nt(qa, kp) + off
            m = jnp.max(s, axis=-1, keepdims=True)
            e = jnp.exp(s - m)
            l = jnp.sum(e, axis=-1, keepdims=True)
            w = (e * (1.0 / l)).astype(BF)
            parts.append(nn(w, vp))
            all_lse = jnp.where(lane == 2 * p + a, m + jnp.log(l), all_lse)
        ctx[:, p * TILE : (p + 1) * TILE] = jnp.where(low, parts[0], parts[1]).astype(BF)
    lse[...] = all_lse
    attended = nt(ctx[...], wot[...]) + vec_sum[5:6, :]
    valid = lax.broadcasted_iota(jnp.int32, (total, 1), 0) <= body
    middle = x_out[...] + jnp.where(valid, attended, 0.0)
    mid_out[...] = middle
    xhat2, _ = norm_stats(middle)
    n2_out[...] = (xhat2 * vec_sum[3:4, :] + vec_sum[4:5, :]).astype(BF)


def mlp_kernel(sizes, *refs):
    nctx, ntp, ndp, main, width, rows, padded = sizes
    c_in, refs = refs[:nctx], refs[nctx:]
    own_in, refs = refs[:ndp], refs[ndp:]
    oth_in, refs = refs[:ndp], refs[ndp:]
    mid, n2, ctx, wot, vec, ub, cex = refs[:7]
    refs = refs[7:]
    bo, refs = refs[:nctx], refs[nctx:]
    dmid, dctx, g_own, g_oth, g_out, vgrad, ubgrad = refs[:7]
    wf, cot, hid, hgr = refs[7:]
    me_d = lax.axis_index("dp")
    body = nctx * main
    total = body + EXTRA
    ff = wf.shape[2]
    quarter = ff // 4
    for k in range(ndp):
        at = pl.ds(pl.multiple_of((me_d ^ k) * rows, 8), rows)
        for j in range(4):
            part, lo = j // 2, (j % 2) * quarter
            wf[part, at, lo : lo + quarter] = own_in[k][j].astype(F32)[:rows]
            wf[part, at, 2 * quarter + lo : 3 * quarter + lo] = oth_in[k][j].astype(F32)[:rows]
    wu, wd = wf[0].astype(BF), wf[1].astype(BF)
    for k in range(nctx):
        cot[k * main : (k + 1) * main, :] = c_in[k][...]
    cot[body:, :] = cex[...]
    dcot = cot[...]
    n2v = n2[...]
    for j in range(ff // 256):
        sl = slice(j * 256, (j + 1) * 256)
        pre = nn(n2v, wu[:, sl]) + ub[0:1, sl]
        hc = nn(dcot, wd[:, sl])
        act, slope = gelu_pair(pre)
        h = act.astype(BF)
        hg = (hc * slope).astype(BF)
        hid[:, sl] = h
        hgr[:, sl] = hg
        ubgrad[:, sl] = jnp.broadcast_to(jnp.sum(hg.astype(F32), axis=0, keepdims=True), (8, 256))
        gu, gd = tn(n2v, hg).astype(BF), tn(dcot, h).astype(BF)
        to = g_own if j * 256 < ff // 2 else g_oth
        lo = (j * 256) % (ff // 2)
        for part, g in ((0, gu), (1, gd)):
            for d in range(ndp):
                for c in range(2):
                    col = lo + c * 128
                    to[2 * part + col // quarter, d, 0:rows, col % quarter : col % quarter + 128] = (
                        g[d * rows : (d + 1) * rows, c * 128 : (c + 1) * 128]
                    )
    middle = mid[...]
    valid = lax.broadcasted_iota(jnp.int32, (total, 1), 0) <= body
    mlp_out = nt(hid[...], wd) + vec[6:7, :]
    out = (middle + jnp.where(valid, mlp_out, 0.0)).astype(BF)
    for k in range(nctx):
        bo[k][0:main, :] = out[k * main : (k + 1) * main]
        bo[k][main:, :] = out[body:]
    n2g = nt(hgr[...], wu)
    xhat, r = norm_stats(middle)
    back = norm_back(n2g * vec[3:4, :], xhat, r)
    middle_grad = dcot.astype(F32) + back
    dmid[...] = middle_grad
    agrad = jnp.where(valid, middle_grad, 0.0).astype(BF)
    dctx[...] = nn(agrad, wot[...]).astype(BF)
    g_out[...] = tn(agrad, ctx[...])
    shape = vgrad.shape
    v = jnp.where(row_is(shape, 2), jnp.sum(n2g * xhat, axis=0, keepdims=True), 0.0)
    v = jnp.where(row_is(shape, 3), jnp.sum(n2g, axis=0, keepdims=True), v)
    v = jnp.where(row_is(shape, 4), jnp.sum(agrad.astype(F32), axis=0, keepdims=True), v)
    v = jnp.where(row_is(shape, 5), jnp.sum(dcot.astype(F32), axis=0, keepdims=True), v)
    vgrad[...] = v


def attention_back_kernel(sizes, *refs):
    nctx, ntp, ndp, main, width, rows, padded = sizes
    qkv, dctx, lse, n1, x_in, dmid, wqkv, vec, g_out, vgrad, ubgrad = refs[:11]
    refs = refs[11:]
    ig, refs = refs[:nctx], refs[nctx:]
    g_own, g_oth = refs[:2]
    dqkv = refs[2]
    body = nctx * main
    total = body + EXTRA
    keys = qkv.shape[0]
    off = jnp.where(lax.broadcasted_iota(jnp.int32, (1, keys), 1) > body, FLOOR, 0.0)
    low = low_lanes((total, TILE))
    for p in range(3):
        qp = qkv[0:total, p * TILE : (p + 1) * TILE]
        kp = qkv[:, width + p * TILE : width + (p + 1) * TILE]
        vp = qkv[:, 2 * width + p * TILE : 2 * width + (p + 1) * TILE]
        dp = dctx[:, p * TILE : (p + 1) * TILE]
        dq, dk, dv = [], 0.0, 0.0
        for a in range(2):
            sel = low if a == 0 else ~low
            qa = jnp.where(sel, qp, jnp.zeros_like(qp))
            da = jnp.where(sel, dp, jnp.zeros_like(dp))
            prob = jnp.exp(nt(qa, kp) + off - lse[:, 2 * p + a : 2 * p + a + 1])
            wg = nt(da, vp)
            inner = jnp.sum(prob * wg, axis=-1, keepdims=True)
            ds = (prob * (wg - inner)).astype(BF)
            w = prob.astype(BF)
            dq.append(nn(ds, kp))
            dk = dk + tn(ds, qa)
            dv = dv + tn(w, da)
        dqkv[:, p * TILE : (p + 1) * TILE] = (jnp.where(low, dq[0], dq[1]) * SCALE).astype(BF)
        dqkv[:, width + p * TILE : width + (p + 1) * TILE] = dk[0:total].astype(BF)
        dqkv[:, 2 * width + p * TILE : 2 * width + (p + 1) * TILE] = dv[0:total].astype(BF)
    d = dqkv[...]
    bias = jnp.sum(d.astype(F32), axis=0, keepdims=True)
    g = tn(n1[...], d)
    go = g_out[...]
    own, oth = disassemble([tile(g, i) for i in range(9)], [tile(go, i) for i in range(3)])
    for to, tiles in ((g_own, own), (g_oth, oth)):
        for j in range(6):
            for e in range(ndp):
                to[j // 2, e, 0:rows, (j % 2) * TILE : (j % 2 + 1) * TILE] = (
                    tiles[j][e * rows : (e + 1) * rows].astype(BF)
                )
    dn1 = nt(d, wqkv[...])
    xhat, r = norm_stats(x_in[...])
    grad = dmid[...] + norm_back(dn1 * vec[1:2, :], xhat, r)
    out = grad.astype(BF)
    for k in range(nctx):
        ig[k][0:main, :] = out[k * main : (k + 1) * main]
        ig[k][main:, :] = out[body:]
    gains = jnp.sum(dn1 * xhat, axis=0, keepdims=True)
    shifts = jnp.sum(dn1, axis=0, keepdims=True)
    vecs = [gains, shifts] + [vgrad[i : i + 1, :] for i in range(2, 6)]
    zero = [jnp.zeros((1, TILE), F32)] * 3
    bias_own, bias_oth = disassemble([tile(bias, i) for i in range(9)], zero)
    half = ubgrad.shape[1] // 2
    for to, tiles, lo in ((g_own, bias_own, 0), (g_oth, bias_oth, half)):
        rows_ = [tile(v, i) for v in vecs for i in range(3)] + tiles
        rows_ += [ubgrad[0:1, lo + i * TILE : lo + (i + 1) * TILE] for i in range(6)]
        for side in range(2):
            block = jnp.zeros((EXTRA, TILE), F32)
            for i, v in enumerate(rows_[side * EXTRA : (side + 1) * EXTRA]):
                block = jnp.where(row_is(block.shape, i), v, block)
            for e in range(ndp):
                to[3, e, 0:EXTRA, side * TILE : (side + 1) * TILE] = block.astype(BF)
                if padded > EXTRA:
                    to[3, e, EXTRA:padded, side * TILE : (side + 1) * TILE] = jnp.zeros(
                        (padded - EXTRA, TILE), BF
                    )


def sum_core_kernel(n, own, oth, *outs):
    me = lax.axis_index("ctx")
    for k in range(n):
        outs[k][...] = (own[me ^ k].astype(F32) + oth[me ^ k].astype(F32)).astype(BF)


def sum_ctx_kernel(n, ndp, *refs):
    me = lax.axis_index("dp")
    for part in range(len(refs) // (n + ndp)):
        base = part * n
        outs = refs[(len(refs) // (n + ndp)) * n + part * ndp :]
        for k in range(ndp):
            v = refs[base][me ^ k].astype(F32)
            for i in range(1, n):
                v = v + refs[base + i][me ^ k].astype(F32)
            outs[k][...] = v.astype(BF)


def sum_dp_kernel(ndp, *refs):
    parts = len(refs) // (ndp + 1)
    for part in range(parts):
        v = refs[part * ndp][...].astype(F32)
        for i in range(1, ndp):
            v = v + refs[part * ndp + i][...].astype(F32)
        refs[parts * ndp + part][...] = v.astype(BF)


def grads_kernel(sizes, *refs):
    nctx, ntp, ndp, main, width, rows, padded = sizes
    in1, in2, refs = refs[:nctx], refs[nctx : 2 * nctx], refs[2 * nctx :]
    gq, gk, gv, gqb, gvb, go, gu, gub, gd = refs[:9]
    gvec = refs[9:15]
    f1, f2 = refs[15:]
    me, me_d = lax.axis_index("ctx"), lax.axis_index("dp")
    for k in range(nctx):
        f1[me ^ k] = in1[k][...].astype(F32)
        f2[me ^ k] = in2[k][...].astype(F32)
    q01, k01 = f1[0, 0:rows, 0:TILE], f1[0, 0:rows, TILE:]
    v01, o01 = f1[1, 0:rows, 0:TILE], f1[1, 0:rows, TILE:]
    qk2, vo2 = f1[2, 0:rows, 0:TILE], f1[2, 0:rows, TILE:]
    gq[:, 0:TILE] = q01
    gq[:, TILE:] = qk2[:, 0:HD]
    gk[:, 0:TILE] = k01
    gk[:, TILE:] = swap(qk2)[:, 0:HD]
    gv[:, 0:TILE] = v01
    gv[:, TILE:] = vo2[:, 0:HD]
    go[0:TILE, :] = jnp.transpose(o01)
    go[TILE:, :] = jnp.transpose(vo2)[HD:, :]
    half = f2.shape[2]
    for j in range(2):
        gu[:, j * half : (j + 1) * half] = f2[j, 0:rows, :]
        gd[j * half : (j + 1) * half, :] = jnp.transpose(f2[2 + j, 0:rows, :])
    ex = [f1[3, 0:EXTRA, 0:TILE], f1[3, 0:EXTRA, TILE:]]

    def line(i):
        return ex[i // EXTRA][i % EXTRA : i % EXTRA + 1, :]

    for i in range(6):
        v = jnp.concatenate([line(3 * i), line(3 * i + 1), line(3 * i + 2)], axis=1)
        v = jnp.broadcast_to(v, (8, width))
        v = pltpu.roll(v, lax.rem(width - me_d * rows, width), axis=1)
        gvec[i][...] = v[0, 0:rows]
    b = [line(18 + i) for i in range(6)]
    gqb[...] = jnp.concatenate([b[0], b[4][:, 0:HD]], axis=1)[0]
    gvb[...] = jnp.concatenate([b[2], b[5][:, 0:HD]], axis=1)[0]
    gub[...] = jnp.concatenate([line(24 + i) for i in range(6)], axis=1)[0]


def unpack_kernel(sizes, *refs):
    nctx, ntp, ndp, main, width, rows, padded = sizes
    own, oth, (extra, mask, out) = refs[:nctx], refs[nctx : 2 * nctx], refs[2 * nctx :]
    me_c, me_t = lax.axis_index("ctx"), lax.axis_index("tp")
    for k in range(nctx):
        for src, t in ((own[k], me_t), (oth[k], 1 - me_t)):
            img = (me_c ^ k) * ntp + t
            out[img, 0:main, :] = src[0:main, :].astype(F32)
            got = src[main:, :].astype(F32)[0:1, :]
            out[img, main : main + 1, :] = jnp.where(
                mask[img, main] > 0, got, extra[pl.ds(img, 1), :]
            )


def xor(n, k):
    return [(i, i ^ k) for i in range(n)]


def over(axis, n, items):
    return [items[0]] + [lax.ppermute(items[k], axis, xor(n, k)) for k in range(1, n)]


def body(nctx, ntp, ndp, *args):
    (tokens, valid_mask, cotangent, w_query, w_key, w_value, query_bias, value_bias, w_out, w_up, up_bias, w_down) = args[:12]
    vecs = args[12:]
    images, slots, width = tokens.shape
    main = slots - 1
    rows = w_query.shape[0]
    padded = -(-rows // EXTRA) * EXTRA
    ff = w_up.shape[1]
    heads_cols = w_query.shape[1]
    p1_cols = 4 * heads_cols
    quarter = ff // 2
    sizes = (nctx, ntp, ndp, main, width, rows, padded)
    total = nctx * main + EXTRA
    keys = -(-total // TILE) * TILE
    one = lambda f: functools.partial(f, sizes)
    packed = call(
        one(pack_kernel),
        [sds((main + EXTRA, width), BF)] * nctx
        + [sds((main, width), BF)] * nctx
        + [sds((padded + EXTRA, p1_cols), BF), sds((4, padded, quarter), BF)]
        + [sds((images, width), F32)] * 2,
        smem=(2,),
    )(tokens, cotangent, valid_mask, w_query, w_key, w_value, w_out, w_up, w_down, query_bias, value_bias, up_bias, *vecs)
    t_send, c_send = packed[:nctx], packed[nctx : 2 * nctx]
    p1, p2, tex, cex = packed[2 * nctx :]
    flip = xor(ntp, 1)
    t_in = over("ctx", nctx, t_send)
    w1_own = over("dp", ndp, [p1] * ndp)
    c_in = over("ctx", nctx, c_send)
    w2_own = over("dp", ndp, [p2] * ndp)
    w1_oth = [lax.ppermute(v, "tp", flip) for v in w1_own]
    w2_oth = [lax.ppermute(v, "tp", flip) for v in w2_own]
    x, mid, n1, n2, qkv, ctx, lse, wqkv, wot, vec, ub, cex_in = call(
        one(attention_kernel),
        [
            sds((total, width), F32), sds((total, width), F32), sds((total, width), BF), sds((total, width), BF),
            sds((keys, 3 * width), BF), sds((total, width), BF), sds((total, TILE), F32),
            sds((width, 3 * width), BF), sds((width, width), BF), sds((EXTRA, width), F32), sds((8, 2 * ff), F32),
            sds((EXTRA, width), BF),
        ],
        scratch=[pltpu.VMEM((width, 4 * width), F32)],
        flops=2 * 10**9,
    )(*t_in, *w1_own, *w1_oth)
    out = call(
        one(mlp_kernel),
        [sds((main + EXTRA, width), BF)] * nctx
        + [sds((total, width), F32), sds((total, width), BF)]
        + [sds((4, ndp, padded, quarter), BF)] * 2
        + [sds((width, width), F32), sds((EXTRA, width), F32), sds((8, 2 * ff), F32)],
        scratch=[
            pltpu.VMEM((2, width, 2 * ff), F32),
            pltpu.VMEM((total, width), BF),
            pltpu.VMEM((total, 2 * ff), BF),
            pltpu.VMEM((total, 2 * ff), BF),
        ],
        flops=4 * 10**9,
    )(*c_in, *w2_own, *w2_oth, mid, n2, ctx, wot, vec, ub, cex_in)
    bo, (dmid, dctx, g2_own, g2_oth, g_out, vgrad, ubgrad) = out[:nctx], out[nctx:]
    quarter_sums = lambda own, oth: call(
        functools.partial(sum_core_kernel, nctx), [sds(own.shape[1:], BF)] * nctx
    )(own, oth)
    s2 = quarter_sums(g2_own, lax.ppermute(g2_oth, "tp", flip))
    s2 = over("ctx", nctx, s2)
    bo_own = over("ctx", nctx, bo)
    out = call(
        one(attention_back_kernel),
        [sds((main + EXTRA, width), BF)] * nctx + [sds((4, ndp, padded, 2 * TILE), BF)] * 2,
        scratch=[pltpu.VMEM((total, 3 * width), BF)],
        flops=4 * 10**9,
    )(qkv, dctx, lse, n1, x, dmid, wqkv, vec, g_out, vgrad, ubgrad)
    ig, (g1_own, g1_oth) = out[:nctx], out[nctx:]
    s1 = quarter_sums(g1_own, lax.ppermute(g1_oth, "tp", flip))
    s1 = over("ctx", nctx, s1)
    ig_own = over("ctx", nctx, ig)
    parts = call(
        functools.partial(sum_ctx_kernel, nctx, ndp),
        [sds(s1[0].shape[1:], BF)] * ndp + [sds(s2[0].shape[1:], BF)] * ndp,
    )(*s1, *s2)
    u1, u2 = over("dp", ndp, parts[:ndp]), over("dp", ndp, parts[ndp:])
    v1, v2 = call(
        functools.partial(sum_dp_kernel, ndp), [sds(u1[0].shape, BF), sds(u2[0].shape, BF)]
    )(*u1, *u2)
    f1, f2 = over("ctx", nctx, [v1] * nctx), over("ctx", nctx, [v2] * nctx)
    gq, gk, gv, gqb, gvb, go, gu, gub, gd, *gvec = call(
        one(grads_kernel),
        [
            sds(w_query.shape, F32), sds(w_key.shape, F32), sds(w_value.shape, F32),
            sds(query_bias.shape, F32), sds(value_bias.shape, F32), sds(w_out.shape, F32),
            sds(w_up.shape, F32), sds(up_bias.shape, F32), sds(w_down.shape, F32),
        ]
        + [sds((rows,), F32)] * 6,
        scratch=[pltpu.VMEM((4,) + v1.shape, F32), pltpu.VMEM((4,) + v2.shape, F32)],
    )(*f1, *f2)
    results = []
    for own, extra in ((bo_own, tex), (ig_own, cex)):
        oth = [lax.ppermute(v, "tp", flip) for v in own]
        results.append(
            call(one(unpack_kernel), sds(tokens.shape, F32), smem=(2 * nctx + 1,))(
                *own, *oth, extra, valid_mask
            )
        )
    return (*results, gq, gk, gv, gqb, gvb, go, gu, gub, gd, *gvec)


def solution(mesh):
    rows, cols, tp, dp = P("dp", "tp"), P("tp", "dp"), P("tp"), P("dp")
    act = P("dp", "ctx", None)
    return jax.shard_map(
        functools.partial(body, mesh.shape["ctx"], mesh.shape["tp"], mesh.shape["dp"]),
        mesh=mesh,
        in_specs=(act, P("dp", "ctx"), act, rows, rows, rows, tp, tp, cols, rows, tp, cols) + (dp,) * 6,
        out_specs=(act, act, rows, rows, rows, tp, tp, cols, rows, tp, cols) + (dp,) * 6,
        check_vma=False,
    )
```

time: 583 us -> 187 us (0.32); the launches traced: 574 us -> 187 us
  blocking collectives: 162 us -> 0 us
  waiting for transfers between devices: 196 us -> 47.1 us
  matrix products: 77 us -> 0 us
  starting transfers between devices: 1.18 us -> 61 us
  Pallas kernels: 0 us -> 58.6 us
  local copies, waits for them, and re-layouts: 75.8 us -> 19 us
  other arithmetic: 44.6 us -> 0 us
  between operations: 17.3 us -> 1.26 us
    all_gather x7 -> x0, blocking collectives: 97.9 us -> none  [the longest x1 17.6 us: body(): lax.all_gather(w_down, 'dp', axis=1, tiled=True)]
    unnamed x15 -> x0, waiting for transfers between devices: 91.9 us -> none
    dot_general x24 -> x0, matrix products: 77 us -> none  [the longest x1 9.94 us: body(): jnp.dot(normed_two, up_full, preferred_element_type=jnp.float32)]
    ppermute x0 -> x54, starting transfers between devices: none -> 61 us  [the longest x36 57.7 us: over(): lax.ppermute(items[k], axis, xor(n, k))]
    pallas_call x0 -> x11, Pallas kernels: none -> 58.6 us  [run(): pl.pallas_call(kernel, out_shape=out_shape, in_specs=specs, out_specs=jax...]
    psum x4 -> x0, waiting for transfers between devices: 47.1 us -> none  [the longest x1 36 us: body(): lax.psum(shares[0].astype(jnp.bfloat16), 'ctx').astype(jnp.float32)]
    ppermute x0 -> x54, waiting for transfers between devices: none -> 47.1 us  [the longest x36 47 us: over(): lax.ppermute(items[k], axis, xor(n, k))]
    psum x1 -> x0, blocking collectives: 42.3 us -> none  [body(): lax.psum((grad_qbias_local, grad_vbias_local, grad_up_bias_local), ('dp',...]
  transfers between devices with their start and end apart: 13 -> 54, of which waited for: 6 -> 9; matrix products, arithmetic and copies ran while one was open for 22% -> 3% of each run, Pallas kernels for 0% -> 21%
where the time goes in v1:
time: 187 us
  starting transfers between devices  61 us (33%)
  Pallas kernels  58.6 us (31%)
  waiting for transfers between devices  47.1 us (25%)
  local copies, waits for them, and re-layouts  19 us (10%)
    pallas_call x11, Pallas kernels, run(): pl.pallas_call(kernel, out_shape=out_shape, in_specs=specs, out_specs=jax...  58.6 us
    ppermute x36, starting transfers between devices, over(): lax.ppermute(items[k], axis, xor(n, k))  57.7 us
    ppermute x36, waiting for transfers between devices, over(): lax.ppermute(items[k], axis, xor(n, k))  47 us
    unnamed x134, local copies, waits for them, and re-layouts  19 us
  transfers between devices with their start and end apart: 54, of which 9 were waited for; matrix products, arithmetic and copies ran while one was open for 3% of the time, Pallas kernels for 21%

profile of v1, /device:TPU:0, one launch (start us, length us, event | category | flops | bytes accessed | tf_op | source)
XLA Modules:
  0.0 186.9 jit_solution(9240528883341966550)
XLA Ops:
  2.4 3.2 %copy.35.tok = f32[8,145,384]{2,1,0:T(8,128)} copy(f32[8,145,384]{2,0,1:T(8,128)} %param.18) | data formatting | bytes 3563520 | tf_op args[0]
  7.2 3.5 %shard_map.305 = (bf16[160,384]{1,0:T(8,128)(2,1)}, bf16[160,384]{1,0:T(8,128)(2,1)}, bf16[160,384]{1,0:T(8,128)(2,1)}, bf16[160,384]{1,0:T(8,128)(2,1)}, bf16[1...) custom-call(f32[8,145,384]{2,1,0:T(8,128)} %copy.35.tok, ...), custom_call_target="tpu_custom_call" | custom-call | bytes 1048576 | tf_op jit(solution)/shard_map/pallas_call | solution.py:27
  10.7 3.0 %collective-permute-start = (bf16[144,384]{1,0:T(8,128)(2,1)}, bf16[144,384]{1,0:T(8,128)(2,1)S(1)}, u32[]{:S(2)}, u32[]{:S(2)}) collective-permute-start(bf16[144,384]{1,0:T(8,128)(2,1)} %get-tuple-element.92), channel_id=1, source_target_pairs={{0,2},{2,0},{4,6},{6,4},{1,3},{3,1},{5,7},{7,5},{8,10},{10,8},{12,... | collective-permute-start | bytes 331784 | tf_op jit(solution)/shard_map/ppermute | solution.py:482
  15.8 3.6 %collective-permute-start.15 = (bf16[112,768]{1,0:T(8,128)(2,1)}, bf16[112,768]{1,0:T(8,128)(2,1)S(1)}, u32[]{:S(2)}, u32[]{:S(2)}) collective-permute-start(bf16[112,768]{1,0:T(8,128)(2,1)} %get-tuple-element.100.refs_4_), channel_id=1, source_target_pairs={{0,24},{8,16},{16,8},{24,0},{1,25},{9,17},{17,9},{25,1},{2,26},{10... | collective-permute-start | bytes 516104 | tf_op jit(solution)/shard_map/ppermute | solution.py:482
  19.9 2.4 %collective-permute-start.12 = (bf16[160,384]{1,0:T(8,128)(2,1)}, bf16[160,384]{1,0:T(8,128)(2,1)S(1)}, u32[]{:S(2)}, u32[]{:S(2)}) collective-permute-start(bf16[160,384]{1,0:T(8,128)(2,1)} %get-tuple-element.99), channel_id=1, source_target_pairs={{0,6},{2,4},{4,2},{6,0},{1,7},{3,5},{5,3},{7,1},{8,14},{10,12},{12... | collective-permute-start | bytes 368648 | tf_op jit(solution)/shard_map/ppermute | solution.py:482
  24.7 3.0 %collective-permute-done.11.refs_2_ = bf16[160,384]{1,0:T(8,128)(2,1)S(1)} collective-permute-done((bf16[160,384]{1,0:T(8,128)(2,1)}, bf16[160,384]{1,0:T(8,128)(2,1)S(1)}, u32[]{:S(2)}, u32[]{:S(2)}) %collective-permute-start.11) | collective-permute-done | bytes 122912 | tf_op jit(solution)/shard_map/ppermute | solution.py:482
  30.7 7.6 %collective-permute-start.3 = (bf16[4,96,384]{2,1,0:T(8,128)(2,1)}, bf16[4,96,384]{2,1,0:T(8,128)(2,1)S(1)}, u32[]{:S(2)}, u32[]{:S(2)}) collective-permute-start(bf16[4,96,384]{2,1,0:T(8,128)(2,1)} %get-tuple-element.95.refs_4_), channel_id=1, source_target_pairs={{0,8},{8,0},{16,24},{24,16},{1,9},{9,1},{17,25},{25,17},{2,10},{10... | collective-permute-start | bytes 884744 | tf_op jit(solution)/shard_map/ppermute | solution.py:482
  38.3 15.9 %collective-permute-done.14.refs_6_ = bf16[112,768]{1,0:T(8,128)(2,1)S(1)} collective-permute-done((bf16[112,768]{1,0:T(8,128)(2,1)}, bf16[112,768]{1,0:T(8,128)(2,1)S(1)}, u32[]{:S(2)}, u32[]{:S(2)}) %collective-permute-start.14) | collective-permute-done | bytes 172064 | tf_op jit(solution)/shard_map/ppermute | solution.py:482
  54.8 5.3 %collective-permute-done.4.refs_6_ = bf16[4,96,384]{2,1,0:T(8,128)(2,1)S(1)} collective-permute-done((bf16[4,96,384]{2,1,0:T(8,128)(2,1)}, bf16[4,96,384]{2,1,0:T(8,128)(2,1)S(1)}, u32[]{:S(2)}, u32[]{:S(2)}) %collective-permute-start.4) | collective-permute-done | bytes 294944 | tf_op jit(solution)/shard_map/ppermute | solution.py:482
  62.7 9.6 %shard_map.306 = (f32[592,384]{1,0:T(8,128)}, f32[592,384]{1,0:T(8,128)}, bf16[592,384]{1,0:T(8,128)(2,1)}, bf16[592,384]{1,0:T(8,128)(2,1)}, bf16[640,1152]{1,0...) custom-call(bf16[160,384]{1,0:T(8,128)(2,1)} %get-tuple-element.96.r, ...), custom_call_target="tpu_custom_call" | custom-call | flops 2000000000 | bytes 1048576 | tf_op jit(solution)/shard_map/pallas_call | solution.py:27
  73.4 13.8 %shard_map.307 = (bf16[160,384]{1,0:T(8,128)(2,1)}, bf16[160,384]{1,0:T(8,128)(2,1)}, bf16[160,384]{1,0:T(8,128)(2,1)}, bf16[160,384]{1,0:T(8,128)(2,1)}, f32[59...) custom-call(bf16[144,384]{1,0:T(8,128)(2,1)} %get-tuple-element.91.r, ...), custom_call_target="tpu_custom_call" | custom-call | flops 4000000000 | bytes 1048576 | tf_op jit(solution)/shard_map/pallas_call | solution.py:27
  87.3 14.6 %shard_map.309 = (bf16[160,384]{1,0:T(8,128)(2,1)}, bf16[160,384]{1,0:T(8,128)(2,1)}, bf16[160,384]{1,0:T(8,128)(2,1)}, bf16[160,384]{1,0:T(8,128)(2,1)}, bf16[4...) custom-call(bf16[640,1152]{1,0:T(8,128)(2,1)} %get-tuple-element.113.refs_0_, ...), custom_call_target="tpu_custom_call" | custom-call | flops 4000000000 | bytes 1048576 | tf_op jit(solution)/shard_map/pallas_call | solution.py:27
  111.2 2.7 %shard_map.312 = (bf16[4,96,384]{2,1,0:T(8,128)(2,1)}, bf16[4,96,384]{2,1,0:T(8,128)(2,1)}, bf16[4,96,384]{2,1,0:T(8,128)(2,1)}, bf16[4,96,384]{2,1,0:T(8,128)(2,1)}) custom-call(bf16[4,4,96,384]{3,2,1,0:T(8,128)(2,1)} %get-tuple-element.134.own, bf16[4,4,96,384]{3,2,1,0:T(8,128)(2,1)} %copy-done.1), custom_call_target="tpu_custom_call" | custom-call | bytes 1048576 | tf_op jit(solution)/shard_map/pallas_call | solution.py:27
  122.1 15.5 %collective-permute-done.36.refs_2_ = bf16[4,96,256]{2,1,0:T(8,128)(2,1)S(1)} collective-permute-done((bf16[4,96,256]{2,1,0:T(8,128)(2,1)S(1)}, bf16[4,96,256]{2,1,0:T(8,128)(2,1)S(1)}, u32[]{:S(2)}, u32[]{:S(2)}) %collective-permute-start.36) | collective-permute-done | bytes 196640 | tf_op jit(solution)/shard_map/ppermute | solution.py:482
  139.1 3.4 %collective-permute-start.29 = (bf16[160,384]{1,0:T(8,128)(2,1)S(1)}, bf16[160,384]{1,0:T(8,128)(2,1)S(1)}, u32[]{:S(2)}, u32[]{:S(2)}) collective-permute-start(bf16[160,384]{1,0:T(8,128)(2,1)S(1)} %copy-done.53), channel_id=1, source_target_pairs={{0,6},{2,4},{4,2},{6,0},{1,7},{3,5},{5,3},{7,1},{8,14},{10,12},{12... | collective-permute-start | bytes 368648 | tf_op jit(solution)/shard_map/ppermute | solution.py:482
  143.8 2.5 %shard_map.313 = (bf16[96,256]{1,0:T(8,128)(2,1)}, bf16[96,256]{1,0:T(8,128)(2,1)}, bf16[96,256]{1,0:T(8,128)(2,1)}, bf16[96,256]{1,0:T(8,128)(2,1)}, bf16[96,38...) custom-call(bf16[4,96,256]{2,1,0:T(8,128)(2,1)} %get-tuple-element.130.refs_0_, ...), custom_call_target="tpu_custom_call" | custom-call | bytes 1048576 | tf_op jit(solution)/shard_map/pallas_call | solution.py:27
  146.4 3.0 %collective-permute-start.43 = (bf16[96,256]{1,0:T(8,128)(2,1)}, bf16[96,256]{1,0:T(8,128)(2,1)S(1)}, u32[]{:S(2)}, u32[]{:S(2)}) collective-permute-start(bf16[96,256]{1,0:T(8,128)(2,1)} %get-tuple-element.142), channel_id=1, source_target_pairs={{0,16},{8,24},{16,0},{24,8},{1,17},{9,25},{17,1},{25,9},{2,18},{10... | collective-permute-start | bytes 147464 | tf_op jit(solution)/shard_map/ppermute | solution.py:482
  151.3 2.5 %collective-permute-start.44 = (bf16[96,256]{1,0:T(8,128)(2,1)}, bf16[96,256]{1,0:T(8,128)(2,1)S(1)}, u32[]{:S(2)}, u32[]{:S(2)}) collective-permute-start(bf16[96,256]{1,0:T(8,128)(2,1)} %get-tuple-element.143), channel_id=1, source_target_pairs={{0,24},{8,16},{16,8},{24,0},{1,25},{9,17},{17,9},{25,1},{2,26},{10... | collective-permute-start | bytes 147464 | tf_op jit(solution)/shard_map/ppermute | solution.py:482
  155.2 2.7 %collective-permute-done.44.refs_3_ = bf16[96,256]{1,0:T(8,128)(2,1)S(1)} collective-permute-done((bf16[96,256]{1,0:T(8,128)(2,1)}, bf16[96,256]{1,0:T(8,128)(2,1)S(1)}, u32[]{:S(2)}, u32[]{:S(2)}) %collective-permute-start.44) | collective-permute-done | bytes 49184 | tf_op jit(solution)/shard_map/ppermute | solution.py:482
  163.2 2.5 %collective-permute-start.53 = (bf16[96,384]{1,0:T(8,128)(2,1)}, bf16[96,384]{1,0:T(8,128)(2,1)S(1)}, u32[]{:S(2)}, u32[]{:S(2)}) collective-permute-start(bf16[96,384]{1,0:T(8,128)(2,1)} %get-tuple-element.149.refs_4_), channel_id=1, source_target_pairs={{0,6},{2,4},{4,2},{6,0},{1,7},{3,5},{5,3},{7,1},{8,14},{10,12},{12... | collective-permute-start | bytes 221192 | tf_op jit(solution)/shard_map/ppermute | solution.py:482
  169.8 2.7 %shard_map.308 = f32[8,145,384]{2,1,0:T(8,128)} custom-call(bf16[160,384]{1,0:T(8,128)(2,1)} %get-tuple-element.108.refs_0_, bf16[160,384]{1,0:T(8,128)(2,1)} %copy-done.11, bf16[160,384]{1,0:T(8,128)(2,1)} %copy-done.12, bf16[160,384]{1,0:T(8,128)(2,1)} %copy-done.13, bf16[160,384]{1,0:T(8,128)(2,1)} %copy-done.18, bf16[160,384]{1,0:T(8,128)(2,1)} %copy-done.19, ...), custom_call_target="tpu_custom_call" | custom-call | bytes 1048576 | tf_op jit(solution)/shard_map/pallas_call | solution.py:27
  172.5 3.1 %copy.38 = f32[8,145,384]{2,0,1:T(8,128)} copy(f32[8,145,384]{2,1,0:T(8,128)} %shard_map.308) | data formatting | bytes 3563520
  175.6 2.7 %shard_map.310 = f32[8,145,384]{2,1,0:T(8,128)} custom-call(bf16[160,384]{1,0:T(8,128)(2,1)} %get-tuple-element.123.refs_0_, bf16[160,384]{1,0:T(8,128)(2,1)} %copy-done.14, bf16[160,384]{1,0:T(8,128)(2,1)} %copy-done.15, bf16[160,384]{1,0:T(8,128)(2,1)} %copy-done.16, bf16[160,384]{1,0:T(8,128)(2,1)} %copy-done.17, bf16[160,384]{1,0:T(8,128)(2,1)} %copy-done.21, ...), custom_call_target="tpu_custom_call" | custom-call | bytes 1048576 | tf_op jit(solution)/shard_map/pallas_call | solution.py:27
  178.3 3.1 %copy.39 = f32[8,145,384]{2,0,1:T(8,128)} copy(f32[8,145,384]{2,1,0:T(8,128)} %shard_map.310) | data formatting | bytes 3563520
  (229 shorter events, 53.7 us)
Async XLA Ops:
  15.8 12.6 %collective-permute-start.16 = (bf16[112,768]{1,0:T(8,128)(2,1)}, bf16[112,768]{1,0:T(8,128)(2,1)S(1)}, u32[]{:S(2)}, u32[]{:S(2)}) collective-permute-start(bf16[112,768]{1,0:T(8,128)(2,1)} %get-tuple-element.100.refs_4_), channel_id=1, source_target_pairs={{0,1},{1,0},{2,3},{3,2},{4,5},{5,4},{6,7},{7,6},{8,9},{9,8},{10,11... | collective-permute-start | bytes 516104 | tf_op jit(solution)/shard_map/ppermute | solution.py:515
  15.8 14.9 %collective-permute-start.15 = (bf16[112,768]{1,0:T(8,128)(2,1)}, bf16[112,768]{1,0:T(8,128)(2,1)S(1)}, u32[]{:S(2)}, u32[]{:S(2)}) collective-permute-start(bf16[112,768]{1,0:T(8,128)(2,1)} %get-tuple-element.100.refs_4_), channel_id=1, source_target_pairs={{0,24},{8,16},{16,8},{24,0},{1,25},{9,17},{17,9},{25,1},{2,26},{10... | collective-permute-start | bytes 516104 | tf_op jit(solution)/shard_map/ppermute | solution.py:482
  22.3 32.4 %collective-permute-start.5 = (bf16[4,96,384]{2,1,0:T(8,128)(2,1)}, bf16[4,96,384]{2,1,0:T(8,128)(2,1)S(1)}, u32[]{:S(2)}, u32[]{:S(2)}) collective-permute-start(bf16[4,96,384]{2,1,0:T(8,128)(2,1)} %get-tuple-element.95.refs_4_), channel_id=1, source_target_pairs={{0,24},{8,16},{16,8},{24,0},{1,25},{9,17},{17,9},{25,1},{2,26},{10... | collective-permute-start | bytes 884744 | tf_op jit(solution)/shard_map/ppermute | solution.py:482
  27.7 26.5 %collective-permute-start.14 = (bf16[112,768]{1,0:T(8,128)(2,1)}, bf16[112,768]{1,0:T(8,128)(2,1)S(1)}, u32[]{:S(2)}, u32[]{:S(2)}) collective-permute-start(bf16[112,768]{1,0:T(8,128)(2,1)} %get-tuple-element.100.refs_4_), channel_id=1, source_target_pairs={{0,16},{8,24},{16,0},{24,8},{1,17},{9,25},{17,1},{25,9},{2,18},{10... | collective-permute-start | bytes 516104 | tf_op jit(solution)/shard_map/ppermute | solution.py:482
  27.7 26.5 %collective-permute-start.13 = (bf16[112,768]{1,0:T(8,128)(2,1)}, bf16[112,768]{1,0:T(8,128)(2,1)S(1)}, u32[]{:S(2)}, u32[]{:S(2)}) collective-permute-start(bf16[112,768]{1,0:T(8,128)(2,1)} %get-tuple-element.100.refs_4_), channel_id=1, source_target_pairs={{0,8},{8,0},{16,24},{24,16},{1,9},{9,1},{17,25},{25,17},{2,10},{10... | collective-permute-start | bytes 516104 | tf_op jit(solution)/shard_map/ppermute | solution.py:482
  28.4 31.7 %collective-permute-start.4 = (bf16[4,96,384]{2,1,0:T(8,128)(2,1)}, bf16[4,96,384]{2,1,0:T(8,128)(2,1)S(1)}, u32[]{:S(2)}, u32[]{:S(2)}) collective-permute-start(bf16[4,96,384]{2,1,0:T(8,128)(2,1)} %get-tuple-element.95.refs_4_), channel_id=1, source_target_pairs={{0,16},{8,24},{16,0},{24,8},{1,17},{9,25},{17,1},{25,9},{2,18},{10... | collective-permute-start | bytes 884744 | tf_op jit(solution)/shard_map/ppermute | solution.py:482
  30.7 29.4 %collective-permute-start.3 = (bf16[4,96,384]{2,1,0:T(8,128)(2,1)}, bf16[4,96,384]{2,1,0:T(8,128)(2,1)S(1)}, u32[]{:S(2)}, u32[]{:S(2)}) collective-permute-start(bf16[4,96,384]{2,1,0:T(8,128)(2,1)} %get-tuple-element.95.refs_4_), channel_id=1, source_target_pairs={{0,8},{8,0},{16,24},{24,16},{1,9},{9,1},{17,25},{25,17},{2,10},{10... | collective-permute-start | bytes 884744 | tf_op jit(solution)/shard_map/ppermute | solution.py:482
  60.1 12.3 %collective-permute-start.6 = (bf16[4,96,384]{2,1,0:T(8,128)(2,1)}, bf16[4,96,384]{2,1,0:T(8,128)(2,1)S(1)}, u32[]{:S(2)}, u32[]{:S(2)}) collective-permute-start(bf16[4,96,384]{2,1,0:T(8,128)(2,1)} %get-tuple-element.95.refs_4_), channel_id=1, source_target_pairs={{0,1},{1,0},{2,3},{3,2},{4,5},{5,4},{6,7},{7,6},{8,9},{9,8},{10,11... | collective-permute-start | bytes 884744 | tf_op jit(solution)/shard_map/ppermute | solution.py:516
  60.1 12.3 %collective-permute-start.9 = (bf16[4,96,384]{2,1,0:T(8,128)(2,1)S(1)}, bf16[4,96,384]{2,1,0:T(8,128)(2,1)S(1)}, u32[]{:S(2)}, u32[]{:S(2)}) collective-permute-start(bf16[4,96,384]{2,1,0:T(8,128)(2,1)S(1)} %collective-permute-done.5.refs_7_), channel_id=1, source_target_pairs={{0,1},{1,0},{2,3},{3,2},{4,5},{5,4},{6,7},{7,6},{8,9},{9,8},{10,11... | collective-permute-start | bytes 884744 | tf_op jit(solution)/shard_map/ppermute | solution.py:516
  60.6 11.8 %collective-permute-start.8 = (bf16[4,96,384]{2,1,0:T(8,128)(2,1)S(1)}, bf16[4,96,384]{2,1,0:T(8,128)(2,1)S(1)}, u32[]{:S(2)}, u32[]{:S(2)}) collective-permute-start(bf16[4,96,384]{2,1,0:T(8,128)(2,1)S(1)} %collective-permute-done.4.refs_6_), channel_id=1, source_target_pairs={{0,1},{1,0},{2,3},{3,2},{4,5},{5,4},{6,7},{7,6},{8,9},{9,8},{10,11... | collective-permute-start | bytes 884744 | tf_op jit(solution)/shard_map/ppermute | solution.py:516
  87.2 22.7 %collective-permute-start.38 = (bf16[4,4,96,384]{3,2,1,0:T(8,128)(2,1)}, bf16[4,4,96,384]{3,2,1,0:T(8,128)(2,1)S(1)}, u32[]{:S(2)}, u32[]{:S(2)}) collective-permute-start(bf16[4,4,96,384]{3,2,1,0:T(8,128)(2,1)} %get-tuple-element.135), channel_id=1, source_target_pairs={{0,1},{1,0},{2,3},{3,2},{4,5},{5,4},{6,7},{7,6},{8,9},{9,8},{10,11... | collective-permute-start | bytes 3538952 | tf_op jit(solution)/shard_map/ppermute | solution.py:546
  103.0 12.0 %collective-permute-start.21 = (bf16[160,384]{1,0:T(8,128)(2,1)S(1)}, bf16[160,384]{1,0:T(8,128)(2,1)S(1)}, u32[]{:S(2)}, u32[]{:S(2)}) collective-permute-start(bf16[160,384]{1,0:T(8,128)(2,1)S(1)} %copy-done.59), channel_id=1, source_target_pairs={{0,4},{2,6},{4,0},{6,2},{1,5},{3,7},{5,1},{7,3},{8,12},{10,14},{12... | collective-permute-start | bytes 368648 | tf_op jit(solution)/shard_map/ppermute | solution.py:482
  104.5 12.1 %collective-permute-start.22 = (bf16[160,384]{1,0:T(8,128)(2,1)S(1)}, bf16[160,384]{1,0:T(8,128)(2,1)S(1)}, u32[]{:S(2)}, u32[]{:S(2)}) collective-permute-start(bf16[160,384]{1,0:T(8,128)(2,1)S(1)} %copy-done.58), channel_id=1, source_target_pairs={{0,6},{2,4},{4,2},{6,0},{1,7},{3,5},{5,3},{7,1},{8,14},{10,12},{12... | collective-permute-start | bytes 368648 | tf_op jit(solution)/shard_map/ppermute | solution.py:482
  109.2 12.2 %collective-permute-start.35 = (bf16[4,96,256]{2,1,0:T(8,128)(2,1)}, bf16[4,96,256]{2,1,0:T(8,128)(2,1)S(1)}, u32[]{:S(2)}, u32[]{:S(2)}) collective-permute-start(bf16[4,96,256]{2,1,0:T(8,128)(2,1)} %get-tuple-element.131), channel_id=1, source_target_pairs={{0,2},{2,0},{4,6},{6,4},{1,3},{3,1},{5,7},{7,5},{8,10},{10,8},{12,... | collective-permute-start | bytes 589832 | tf_op jit(solution)/shard_map/ppermute | solution.py:482
  113.9 28.5 %collective-permute-start.39 = (bf16[4,96,384]{2,1,0:T(8,128)(2,1)}, bf16[4,96,384]{2,1,0:T(8,128)(2,1)S(1)}, u32[]{:S(2)}, u32[]{:S(2)}) collective-permute-start(bf16[4,96,384]{2,1,0:T(8,128)(2,1)} %get-tuple-element.137), channel_id=1, source_target_pairs={{0,2},{2,0},{4,6},{6,4},{1,3},{3,1},{5,7},{7,5},{8,10},{10,8},{12,... | collective-permute-start | bytes 884744 | tf_op jit(solution)/shard_map/ppermute | solution.py:482
  115.0 27.5 %collective-permute-start.40 = (bf16[4,96,384]{2,1,0:T(8,128)(2,1)}, bf16[4,96,384]{2,1,0:T(8,128)(2,1)S(1)}, u32[]{:S(2)}, u32[]{:S(2)}) collective-permute-start(bf16[4,96,384]{2,1,0:T(8,128)(2,1)} %get-tuple-element.138), channel_id=1, source_target_pairs={{0,4},{2,6},{4,0},{6,2},{1,5},{3,7},{5,1},{7,3},{8,12},{10,14},{12... | collective-permute-start | bytes 884744 | tf_op jit(solution)/shard_map/ppermute | solution.py:482
  116.5 26.6 %collective-permute-start.41 = (bf16[4,96,384]{2,1,0:T(8,128)(2,1)}, bf16[4,96,384]{2,1,0:T(8,128)(2,1)S(1)}, u32[]{:S(2)}, u32[]{:S(2)}) collective-permute-start(bf16[4,96,384]{2,1,0:T(8,128)(2,1)} %get-tuple-element.139), channel_id=1, source_target_pairs={{0,6},{2,4},{4,2},{6,0},{1,7},{3,5},{5,3},{7,1},{8,14},{10,12},{12... | collective-permute-start | bytes 884744 | tf_op jit(solution)/shard_map/ppermute | solution.py:482
  119.9 17.7 %collective-permute-start.36 = (bf16[4,96,256]{2,1,0:T(8,128)(2,1)S(1)}, bf16[4,96,256]{2,1,0:T(8,128)(2,1)S(1)}, u32[]{:S(2)}, u32[]{:S(2)}) collective-permute-start(bf16[4,96,256]{2,1,0:T(8,128)(2,1)S(1)} %copy-done.45), channel_id=1, source_target_pairs={{0,4},{2,6},{4,0},{6,2},{1,5},{3,7},{5,1},{7,3},{8,12},{10,14},{12... | collective-permute-start | bytes 589832 | tf_op jit(solution)/shard_map/ppermute | solution.py:482
  121.4 17.7 %collective-permute-start.37 = (bf16[4,96,256]{2,1,0:T(8,128)(2,1)S(1)}, bf16[4,96,256]{2,1,0:T(8,128)(2,1)S(1)}, u32[]{:S(2)}, u32[]{:S(2)}) collective-permute-start(bf16[4,96,256]{2,1,0:T(8,128)(2,1)S(1)} %copy-done.44), channel_id=1, source_target_pairs={{0,6},{2,4},{4,2},{6,0},{1,7},{3,5},{5,3},{7,1},{8,14},{10,12},{12... | collective-permute-start | bytes 589832 | tf_op jit(solution)/shard_map/ppermute | solution.py:482
  163.2 18.2 %collective-permute-start.53 = (bf16[96,384]{1,0:T(8,128)(2,1)}, bf16[96,384]{1,0:T(8,128)(2,1)S(1)}, u32[]{:S(2)}, u32[]{:S(2)}) collective-permute-start(bf16[96,384]{1,0:T(8,128)(2,1)} %get-tuple-element.149.refs_4_), channel_id=1, source_target_pairs={{0,6},{2,4},{4,2},{6,0},{1,7},{3,5},{5,3},{7,1},{8,14},{10,12},{12... | collective-permute-start | bytes 221192 | tf_op jit(solution)/shard_map/ppermute | solution.py:482
  165.7 15.8 %collective-permute-start.52 = (bf16[96,384]{1,0:T(8,128)(2,1)}, bf16[96,384]{1,0:T(8,128)(2,1)S(1)}, u32[]{:S(2)}, u32[]{:S(2)}) collective-permute-start(bf16[96,384]{1,0:T(8,128)(2,1)} %get-tuple-element.149.refs_4_), channel_id=1, source_target_pairs={{0,4},{2,6},{4,0},{6,2},{1,5},{3,7},{5,1},{7,3},{8,12},{10,14},{12... | collective-permute-start | bytes 221192 | tf_op jit(solution)/shard_map/ppermute | solution.py:482
  167.2 14.2 %collective-permute-start.51 = (bf16[96,384]{1,0:T(8,128)(2,1)}, bf16[96,384]{1,0:T(8,128)(2,1)S(1)}, u32[]{:S(2)}, u32[]{:S(2)}) collective-permute-start(bf16[96,384]{1,0:T(8,128)(2,1)} %get-tuple-element.149.refs_4_), channel_id=1, source_target_pairs={{0,2},{2,0},{4,6},{6,4},{1,3},{3,1},{5,7},{7,5},{8,10},{10,8},{12,... | collective-permute-start | bytes 221192 | tf_op jit(solution)/shard_map/ppermute | solution.py:482
  167.2 14.2 %collective-permute-start.49 = (bf16[96,256]{1,0:T(8,128)(2,1)}, bf16[96,256]{1,0:T(8,128)(2,1)S(1)}, u32[]{:S(2)}, u32[]{:S(2)}) collective-permute-start(bf16[96,256]{1,0:T(8,128)(2,1)} %get-tuple-element.148.refs_0_), channel_id=1, source_target_pairs={{0,4},{2,6},{4,0},{6,2},{1,5},{3,7},{5,1},{7,3},{8,12},{10,14},{12... | collective-permute-start | bytes 147464 | tf_op jit(solution)/shard_map/ppermute | solution.py:482
  168.3 13.1 %collective-permute-start.48 = (bf16[96,256]{1,0:T(8,128)(2,1)}, bf16[96,256]{1,0:T(8,128)(2,1)S(1)}, u32[]{:S(2)}, u32[]{:S(2)}) collective-permute-start(bf16[96,256]{1,0:T(8,128)(2,1)} %get-tuple-element.148.refs_0_), channel_id=1, source_target_pairs={{0,2},{2,0},{4,6},{6,4},{1,3},{3,1},{5,7},{7,5},{8,10},{10,8},{12,... | collective-permute-start | bytes 147464 | tf_op jit(solution)/shard_map/ppermute | solution.py:482
  (94 other events, 1240.0 us)

commit v2 on v1

v2 whole, which is shorter than its diff:
```python
import functools

import jax
import jax.numpy as jnp
from jax import lax
from jax.experimental import pallas as pl
from jax.experimental.pallas import tpu as pltpu
from jax.sharding import PartitionSpec as P

HD = 64
EPS = 1e-06
SCALE = 0.125
FLOOR = -1e30
BF = jnp.bfloat16
F32 = jnp.float32
TILE = 128
TIMES = {
    "pack_weights": 2.0, "pack_slots": 3.0, "pack_cotangent": 2.0, "attention": 6.0, "mlp_own": 4.0, "mlp_oth": 4.0, "mlp_sums": 2.0, "attention_back": 11.0,
    "place_grads": 1.0, "place_slots": 2.3,
}
EXTRA = 16


def call(name, kernel, out_shape, scratch=(), mib=8, after=(), raw=(), raw_out=False):
    after = list(after)

    def ordered(*refs):
        kernel(*refs[len(after) :])

    def run(*args):
        specs = [pl.BlockSpec(memory_space=pl.ANY)] * len(after) + [
            pl.BlockSpec(memory_space=pltpu.HBM if i in raw else pltpu.VMEM)
            for i in range(len(args))
        ]
        return pl.pallas_call(
            ordered,
            name=name,
            out_shape=out_shape,
            in_specs=specs,
            out_specs=jax.tree.map(
                lambda _: pl.BlockSpec(memory_space=pltpu.HBM if raw_out else pltpu.VMEM), out_shape
            ),
            scratch_shapes=list(scratch),
            compiler_params=pltpu.CompilerParams(vmem_limit_bytes=mib << 20),
            cost_estimate=pl.CostEstimate(
                flops=int(TIMES.get(name, 0.2) * 1.15e9), bytes_accessed=1, transcendentals=0
            ),
        )(*after, *args)

    return run


def sds(shape, dtype):
    return jax.ShapeDtypeStruct(shape, dtype)


def nn(a, b):
    return lax.dot_general(a, b, (((1,), (0,)), ((), ())), preferred_element_type=F32)


def nt(a, b):
    return lax.dot_general(a, b, (((1,), (1,)), ((), ())), preferred_element_type=F32)


def tn(a, b):
    return lax.dot_general(a, b, (((0,), (0,)), ((), ())), preferred_element_type=F32)


def swap(v):
    return pltpu.roll(v, HD, axis=1)


def low_lanes(shape):
    return lax.broadcasted_iota(jnp.int32, shape, 1) < HD


def row_is(shape, row):
    return lax.broadcasted_iota(jnp.int32, shape, 0) == row


def tile(v, i):
    return v[:, i * TILE : (i + 1) * TILE]


def assemble(own, oth):
    low = low_lanes((own.shape[0], TILE))
    own_qk, own_vo, oth_qk, oth_vo = tile(own, 4), tile(own, 5), tile(oth, 4), tile(oth, 5)
    qkv = [
        tile(own, 0), tile(oth, 0), jnp.where(low, own_qk, swap(oth_qk)),
        tile(own, 1), tile(oth, 1), jnp.where(low, swap(own_qk), oth_qk),
        tile(own, 2), tile(oth, 2), jnp.where(low, own_vo, swap(oth_vo)),
    ]
    out = [tile(own, 3), tile(oth, 3), jnp.where(low, swap(own_vo), oth_vo)]
    return qkv, out


def disassemble(qkv, out):
    low = low_lanes(qkv[0].shape)
    own = [qkv[0], qkv[3], qkv[6], out[0], jnp.where(low, qkv[2], swap(qkv[5])), jnp.where(low, qkv[8], swap(out[2]))]
    oth = [qkv[1], qkv[4], qkv[7], out[1], jnp.where(low, swap(qkv[2]), qkv[5]), jnp.where(low, swap(qkv[8]), out[2])]
    return own, oth


def norm_stats(v):
    mean = jnp.mean(v, axis=-1, keepdims=True)
    centered = v - mean
    r = lax.rsqrt(jnp.mean(centered * centered, axis=-1, keepdims=True) + EPS)
    return centered * r, r


def norm_back(e, xhat, r):
    return r * (
        e
        - jnp.mean(e, axis=-1, keepdims=True)
        - xhat * jnp.mean(e * xhat, axis=-1, keepdims=True)
    )


def gelu_pair(v):
    a = jnp.abs(v)
    t = 1.0 / (1.0 + (0.3275911 * 0.7071067811865476) * a)
    g = jnp.exp(-0.5 * v * v)
    poly = t * (
        0.254829592 + t * (-0.284496736 + t * (1.421413741 + t * (-1.453152027 + t * 1.061405429)))
    )
    tail = 0.5 * poly * g
    phi = jnp.where(v < 0, tail, 1.0 - tail)
    return v * phi, phi + v * (0.3989422804014327 * g)


BLOCK = 16


def one_hot(shape, hit):
    r, c = (lax.broadcasted_iota(jnp.int32, shape, i) for i in range(2))
    return hit(r, c).astype(F32).astype(BF)


def picker(wanted, images):
    def hit(r, c):
        img = wanted[-1]
        for k in range(len(wanted) - 1):
            img = jnp.where(r // BLOCK == k, wanted[k], img)
        return c == (r % BLOCK) * images + img

    return one_hot((len(wanted) * BLOCK, images * BLOCK), hit)


def take_images(ref, outs, at, pick, images, count):
    for b in range(count // BLOCK):
        got = nn(pick, ref[b * BLOCK * images : (b + 1) * BLOCK * images, :].astype(BF)).astype(BF)
        for k in range(len(outs)):
            outs[k][at + b * BLOCK : at + (b + 1) * BLOCK, :] = got[k * BLOCK : (k + 1) * BLOCK]


def fetch(sources, held, sem):
    copies = [pltpu.make_async_copy(sources[i], held[i], sem.at[i]) for i in range(len(sources))]
    for c in copies:
        c.start()
    return copies


def pack_weights_kernel(sizes, count, *refs):
    nctx, ntp, ndp, main, width, rows, padded = sizes
    sources, (p1, p2q), refs = refs[:count], refs[count : count + 2], refs[count + 2 :]
    held, sem = refs[:count], refs[count]
    copies = fetch(sources, held, sem)
    wq, wk, wv, wo, wu, wd, qb, vb, ub = held[:9]
    vecs = held[9:]
    me_c, me_d = lax.axis_index("ctx"), lax.axis_index("dp")
    for c in copies:
        c.wait()
    if padded > rows:
        p1[0:padded, :] = jnp.zeros((padded, p1.shape[1]), BF)
        p2q[...] = jnp.zeros(p2q.shape, BF)
    quarter = p2q.shape[1]
    for j in range(nctx):
        src = (wu, wd)[j // 2][:, (j % 2) * quarter : (j % 2 + 1) * quarter]

        @pl.when(me_c == j)
        def _(src=src):
            p2q[0:rows, :] = src

    def put(lo, value):
        p1[0:rows, lo : lo + value.shape[1]] = value.astype(BF)

    fq, fk, fv = wq[...].astype(F32), wk[...].astype(F32), wv[...].astype(F32)
    fo = jnp.transpose(wo[...].astype(F32))
    for i, w in enumerate((fq, fk, fv, fo)):
        put(i * TILE, tile(w, 0))
    put(4 * TILE, jnp.concatenate([fq[:, TILE:], fk[:, TILE:]], axis=1))
    put(5 * TILE, jnp.concatenate([fv[:, TILE:], fo[:, TILE:]], axis=1))
    cols = p1.shape[1]
    fqb, fvb = qb[...].astype(F32)[None, :], vb[...].astype(F32)[None, :]
    none = jnp.zeros((1, TILE), F32)
    short = jnp.zeros((1, HD), F32)
    bias = jnp.concatenate(
        [fqb[:, :TILE], none, fvb[:, :TILE], none, fqb[:, TILE:], short, fvb[:, TILE:], short], axis=1
    )
    spread = one_hot((rows, width), lambda r, c: c == r + rows * me_d)
    block = jnp.where(row_is((EXTRA, cols), 0), bias, 0.0)
    block = jnp.where(row_is((EXTRA, cols), 7), ub[...].astype(F32)[None, :], block)
    lanes = jnp.zeros((EXTRA, rows), F32)
    for i in range(6):
        lanes = jnp.where(row_is((EXTRA, rows), 1 + i), vecs[i][...].astype(F32)[None, :], lanes)
    lanes = nn(lanes.astype(BF), spread)
    p1[padded : padded + EXTRA, :] = block.astype(BF)
    mixed = jnp.where(
        (lax.broadcasted_iota(jnp.int32, (EXTRA, width), 0) - 1).astype(jnp.uint32) < 6,
        lanes,
        block[:, :width],
    )
    p1[padded : padded + EXTRA, 0:width] = mixed.astype(BF)


def pack_slots_kernel(sizes, *refs):
    nctx, ntp, ndp, main, width, rows, padded = sizes
    count = len(refs) - nctx
    count = count // 2
    sources, sent, refs = refs[:count], refs[count : count + nctx], refs[count + nctx :]
    held, sem = refs[:count], refs[count]
    images = nctx * ntp
    last = pl.ds(main * images, images)
    copies = [pltpu.make_async_copy(sources[0], held[0], sem.at[0])]
    if count > 1:
        copies.append(pltpu.make_async_copy(sources[1].at[last, :], held[1], sem.at[1]))
        copies.append(pltpu.make_async_copy(sources[2], held[2], sem.at[2]))
    for c in copies:
        c.start()
    me_c, me_t = lax.axis_index("ctx"), lax.axis_index("tp")
    wanted = [(me_c ^ k) * ntp + me_t for k in range(nctx)]
    pick = picker(wanted, images)
    for c in copies:
        c.wait()
    take_images(held[0], sent, 0, pick, images, main)
    if count > 1:
        tok, cot, mask = held
        for k in range(nctx):
            gate = mask[wanted[k], main].astype(F32)
            te = tok[pl.ds(main * images + wanted[k], 1), :] * gate
            ce = cot[pl.ds(wanted[k], 1), :] * gate
            shape = (EXTRA, width)
            sent[k][main : main + EXTRA, :] = jnp.where(
                row_is(shape, 0), te, jnp.where(row_is(shape, 1), ce, 0.0)
            ).astype(BF)


def join_kernel(axis, stride, own, got, out):
    bit = lax.rem(lax.div(lax.axis_index(axis), stride), 2)
    for i in range(own.shape[0]):
        out[2 * i + bit] = own[i]
        out[2 * i + 1 - bit] = got[i]


def place_rows(out, own, got, rows, stage):
    bit = lax.rem(lax.axis_index("dp"), 2)
    for i in range(own.shape[0]):
        for piece, last in ((own[i], bit), (got[i], 1 - bit)):
            at = pl.ds(pl.multiple_of((2 * i + last) * rows, 16 if rows % 16 == 0 else 8), rows)
            stage[at, :] = piece.astype(stage.dtype)[:rows]
    out[0 : stage.shape[0], :] = stage[...].astype(BF)


def merge_quarter_kernel(sizes, own, got, out, stage):
    place_rows(out, own, got, sizes[5], stage)


def merge_attn_kernel(sizes, own, got, out, stage):
    nctx, ntp, ndp, main, width, rows, padded = sizes
    place_rows(out, own, got, rows, stage)
    extra = own[0, padded:, :].astype(F32)
    for more in [own[i] for i in range(1, own.shape[0])] + [got[i] for i in range(own.shape[0])]:
        more = more[padded:, :].astype(F32)
        row = lax.broadcasted_iota(jnp.int32, more.shape, 0)
        extra += jnp.where((row > 0) & (row < 7), more, 0.0)
    out[width:, :] = extra.astype(BF)


def merge_ff_kernel(nctx, *refs):
    out = refs[nctx]
    me_c = lax.axis_index("ctx")
    for k in range(nctx):
        quarter = refs[k].shape[1]
        out[:, pl.ds(pl.multiple_of((me_c ^ k) * quarter, quarter), quarter)] = refs[k][...]


def attention_kernel(sizes, *refs):
    nctx, ntp, ndp, main, width, rows, padded = sizes
    t_in, c_in, refs = refs[:nctx], refs[nctx : 2 * nctx], refs[2 * nctx :]
    (own_in, oth_in), refs = refs[:2], refs[2:]
    x_out, mid_out, n1_out, n2_out, qkv, ctx, lse, wqkv, wot, vec, ub, cot = refs
    body = nctx * main
    total = body + EXTRA
    own, oth = own_in[...].astype(F32), oth_in[...].astype(F32)
    tiles, outs = assemble(own, oth)
    for i, v in enumerate(tiles):
        wqkv[:, i * TILE : (i + 1) * TILE] = v[:width].astype(BF)
    for i, v in enumerate(outs):
        wot[:, i * TILE : (i + 1) * TILE] = v[:width].astype(BF)
    bias = jnp.concatenate([v[width : width + 1] for v in tiles], axis=1)
    vec_sum = own[width:, :width]
    vec[...] = vec_sum
    ub[...] = jnp.broadcast_to(
        jnp.concatenate([own[width + 7 : width + 8], oth[width + 7 : width + 8]], axis=1), ub.shape
    )
    extra = jnp.zeros((EXTRA, width), F32)
    for k in range(nctx):
        x_out[k * main : (k + 1) * main, :] = t_in[k][0:main, :].astype(F32)
        cot[k * main : (k + 1) * main, :] = c_in[k][...]
        extra += t_in[k][main : main + EXTRA, :].astype(F32)
    x_out[body:, :] = jnp.where(row_is((EXTRA, width), 0), extra, 0.0)
    cot[body:, :] = jnp.where(row_is((EXTRA, width), 0), extra[1:2, :], 0.0).astype(BF)
    x = x_out[...]
    xhat, _ = norm_stats(x)
    n1 = (xhat * vec_sum[1:2, :] + vec_sum[2:3, :]).astype(BF)
    n1_out[...] = n1
    proj = nn(n1, wqkv[...]) + bias
    qkv[0:total, 0:width] = (proj[:, 0:width].astype(BF).astype(F32) * SCALE).astype(BF)
    qkv[0:total, width:] = proj[:, width:].astype(BF)
    keys = qkv.shape[0]
    qkv[total:, :] = jnp.zeros((keys - total, qkv.shape[1]), BF)
    off = jnp.where(lax.broadcasted_iota(jnp.int32, (1, keys), 1) > body, FLOOR, 0.0)
    low = low_lanes((total, TILE))
    lane = lax.broadcasted_iota(jnp.int32, (total, TILE), 1)
    all_lse = jnp.zeros((total, TILE), F32)
    for p in range(3):
        qp = qkv[0:total, p * TILE : (p + 1) * TILE]
        kp = qkv[:, width + p * TILE : width + (p + 1) * TILE]
        vp = qkv[:, 2 * width + p * TILE : 2 * width + (p + 1) * TILE]
        parts = []
        for a in range(2):
            qa = jnp.where(low if a == 0 else ~low, qp, jnp.zeros_like(qp))
            s = nt(qa, kp) + off
            m = jnp.max(s, axis=-1, keepdims=True)
            e = jnp.exp(s - m)
            l = jnp.sum(e, axis=-1, keepdims=True)
            w = (e * (1.0 / l)).astype(BF)
            parts.append(nn(w, vp))
            all_lse = jnp.where(lane == 2 * p + a, m + jnp.log(l), all_lse)
        ctx[:, p * TILE : (p + 1) * TILE] = jnp.where(low, parts[0], parts[1]).astype(BF)
    lse[...] = all_lse
    attended = nt(ctx[...], wot[...]) + vec_sum[5:6, :]
    valid = lax.broadcasted_iota(jnp.int32, (total, 1), 0) <= body
    middle = x_out[...] + jnp.where(valid, attended, 0.0)
    mid_out[...] = middle
    xhat2, _ = norm_stats(middle)
    n2_out[...] = (xhat2 * vec_sum[3:4, :] + vec_sum[4:5, :]).astype(BF)


def ff_half(n2v, dcot, w, ub, hid, hgr, ubgrad, grads, ndp, rows):
    half = w.shape[1] // 2
    quarter = half // 2
    for lo in range(0, half, 256):
        sl = slice(lo, lo + 256)
        pre = nn(n2v, w[:, sl]) + ub[0:1, sl]
        hc = nn(dcot, w[:, half + lo : half + lo + 256])
        act, slope = gelu_pair(pre)
        h = act.astype(BF)
        hg = (hc * slope).astype(BF)
        hid[:, sl] = h
        hgr[:, sl] = hg
        ubgrad[:, sl] = jnp.broadcast_to(jnp.sum(hg.astype(F32), axis=0, keepdims=True), (8, 256))
        for part, g in ((0, tn(n2v, hg).astype(BF)), (1, tn(dcot, h).astype(BF))):
            for d in range(ndp):
                for c in range(2):
                    col = lo + c * TILE
                    at = slice(col % quarter, col % quarter + TILE)
                    grads[2 * part + col // quarter, d, 0:rows, at] = (
                        g[d * rows : (d + 1) * rows, c * TILE : (c + 1) * TILE]
                    )


def mlp_half_kernel(sizes, side, n2, cot, w, ub, hid, hgr, ubgrad, grads):
    half = w.shape[1] // 2
    ff_half(
        n2[...], cot[...], w[...], ub[:, side * half : (side + 1) * half], hid, hgr, ubgrad, grads, sizes[2], sizes[5]
    )


def mlp_sums_kernel(sizes, mid, ctx, wot, vec, cot, w_own, w_oth, hid_own, hid_oth, hgr_own, hgr_oth, bo, dmid, dctx, g_out, vgrad):
    nctx, ntp, ndp, main, width, rows, padded = sizes
    body = nctx * main
    total = body + EXTRA
    half = w_own.shape[1] // 2
    dcot = cot[...]
    middle = mid[...]
    valid = lax.broadcasted_iota(jnp.int32, (total, 1), 0) <= body
    n2g = nt(hgr_own[...], w_own[:, :half]) + nt(hgr_oth[...], w_oth[:, :half])
    xhat, r = norm_stats(middle)
    back = norm_back(n2g * vec[3:4, :], xhat, r)
    middle_grad = dcot.astype(F32) + back
    dmid[...] = middle_grad
    agrad = jnp.where(valid, middle_grad, 0.0).astype(BF)
    dctx[...] = nn(agrad, wot[...]).astype(BF)
    g_out[...] = tn(agrad, ctx[...])
    mlp_out = nt(hid_own[...], w_own[:, half:]) + nt(hid_oth[...], w_oth[:, half:]) + vec[6:7, :]
    bo[...] = (middle + jnp.where(valid, mlp_out, 0.0)).astype(BF)
    shape = vgrad.shape
    v = jnp.where(row_is(shape, 2), jnp.sum(n2g * xhat, axis=0, keepdims=True), 0.0)
    v = jnp.where(row_is(shape, 3), jnp.sum(n2g, axis=0, keepdims=True), v)
    v = jnp.where(row_is(shape, 4), jnp.sum(agrad.astype(F32), axis=0, keepdims=True), v)
    v = jnp.where(row_is(shape, 5), jnp.sum(dcot.astype(F32), axis=0, keepdims=True), v)
    vgrad[...] = v


def pair_back(p, width, total, body, qkv, dctx, lse):
    keys = qkv.shape[0]
    off = jnp.where(lax.broadcasted_iota(jnp.int32, (1, keys), 1) > body, FLOOR, 0.0)
    low = low_lanes((total, TILE))
    qp = qkv[0:total, p * TILE : (p + 1) * TILE]
    kp = qkv[:, width + p * TILE : width + (p + 1) * TILE]
    vp = qkv[:, 2 * width + p * TILE : 2 * width + (p + 1) * TILE]
    dp = dctx[:, p * TILE : (p + 1) * TILE]
    dq, dk, dv = [], 0.0, 0.0
    for a in range(2):
        sel = low if a == 0 else ~low
        qa = jnp.where(sel, qp, jnp.zeros_like(qp))
        da = jnp.where(sel, dp, jnp.zeros_like(dp))
        prob = jnp.exp(nt(qa, kp) + off - lse[:, 2 * p + a : 2 * p + a + 1])
        wg = nt(da, vp)
        inner = jnp.sum(prob * wg, axis=-1, keepdims=True)
        ds = (prob * (wg - inner)).astype(BF)
        w = prob.astype(BF)
        dq.append(nn(ds, kp))
        dk = dk + tn(ds, qa)
        dv = dv + tn(w, da)
    dq = jnp.where(low, dq[0], dq[1]) * SCALE
    return dq.astype(BF), dk[0:total].astype(BF), dv[0:total].astype(BF)


def attention_back_kernel(sizes, *refs):
    nctx, ntp, ndp, main, width, rows, padded = sizes
    qkv, dctx, lse, n1, x_in, dmid, wqkv, vec, g_out, vgrad, ub_own, ub_oth = refs[:12]
    ig, g_own, g_oth, dqkv = refs[12:]
    body = nctx * main
    total = body + EXTRA
    for p in range(3):
        for i, v in enumerate(pair_back(p, width, total, body, qkv, dctx, lse)):
            dqkv[:, i * width + p * TILE : i * width + (p + 1) * TILE] = v
    d = dqkv[...]
    bias = jnp.sum(d.astype(F32), axis=0, keepdims=True)
    g = tn(n1[...], d)
    go = g_out[...]
    own, oth = disassemble([tile(g, i) for i in range(9)], [tile(go, i) for i in range(3)])
    for to, tiles in ((g_own, own), (g_oth, oth)):
        for j in range(6):
            for e in range(ndp):
                to[j // 2, e, 0:rows, (j % 2) * TILE : (j % 2 + 1) * TILE] = (
                    tiles[j][e * rows : (e + 1) * rows].astype(BF)
                )
    dn1 = nt(d, wqkv[...])
    xhat, r = norm_stats(x_in[...])
    grad = dmid[...] + norm_back(dn1 * vec[1:2, :], xhat, r)
    ig[...] = grad.astype(BF)
    gains = jnp.sum(dn1 * xhat, axis=0, keepdims=True)
    shifts = jnp.sum(dn1, axis=0, keepdims=True)
    vecs = [gains, shifts] + [vgrad[i : i + 1, :] for i in range(2, 6)]
    zero = [jnp.zeros((1, TILE), F32)] * 3
    bias_own, bias_oth = disassemble([tile(bias, i) for i in range(9)], zero)
    for to, tiles, ub in ((g_own, bias_own, ub_own), (g_oth, bias_oth, ub_oth)):
        rows_ = [tile(v, i) for v in vecs for i in range(3)] + tiles
        rows_ += [ub[0:1, i * TILE : (i + 1) * TILE] for i in range(6)]
        for side in range(2):
            block = jnp.zeros((EXTRA, TILE), F32)
            for i, v in enumerate(rows_[side * EXTRA : (side + 1) * EXTRA]):
                block = jnp.where(row_is(block.shape, i), v, block)
            for e in range(ndp):
                to[3, e, 0:EXTRA, side * TILE : (side + 1) * TILE] = block.astype(BF)
                if padded > EXTRA:
                    to[3, e, EXTRA:padded, side * TILE : (side + 1) * TILE] = jnp.zeros(
                        (padded - EXTRA, TILE), BF
                    )


def sum_core_kernel(n, own, oth, *outs):
    me = lax.axis_index("ctx")
    for k in range(n):
        outs[k][...] = (own[me ^ k].astype(F32) + oth[me ^ k].astype(F32)).astype(BF)


def sum_ctx_kernel(n, ndp, *refs):
    me = lax.axis_index("dp")
    if len(refs) > n + ndp:
        refs[-1][...] = refs[n][...]
        refs = refs[:n] + refs[n + 1 : -1]
    for k in range(ndp):
        v = refs[0][me ^ k].astype(F32)
        for i in range(1, n):
            v = v + refs[i][me ^ k].astype(F32)
        refs[n + k][...] = v.astype(BF)


def sum_dp(refs):
    v = refs[0][...].astype(F32)
    for r in refs[1:]:
        v = v + r[...].astype(F32)
    return v.astype(BF)


def sum_dp_kernel(n, *refs):
    out = refs[2 * n]
    cols = refs[0].shape[1]
    out[:, :cols] = sum_dp(refs[:n])
    out[:, cols:] = sum_dp(refs[n : 2 * n])


def returns_kernel(sizes, bo, ig, *outs):
    nctx, ntp, ndp, main, width, rows, padded = sizes
    span = main + EXTRA
    for k in range(nctx):
        at = slice(k * main, (k + 1) * main)
        for i, src in enumerate((bo, ig)):
            outs[k][i * span : i * span + main, :] = src[at, :]
            outs[k][i * span + main : (i + 1) * span, :] = src[nctx * main :, :]


def stack_kernel(*refs):
    out = refs[-1]
    for i, r in enumerate(refs[:-1]):
        out[i] = r[...]


def grads_kernel(sizes, *refs):
    nctx, ntp, ndp, main, width, rows, padded = sizes
    parts, refs = refs[:nctx], refs[nctx:]
    gq, gk, gv, gqb, gvb, go, gu, gub, gd = refs[:9]
    gvec, f, f2 = refs[9:15], refs[15], refs[16]
    me, me_d = lax.axis_index("ctx"), lax.axis_index("dp")
    half = f2.shape[2]
    for k in range(nctx):
        f2[me ^ k] = parts[k][:, :half].astype(F32)
        f[me ^ k] = parts[k][:, half:].astype(F32)
    for j in range(2):
        gu[:, j * half : (j + 1) * half] = f2[j, 0:rows, :]
        gd[:, j * half : (j + 1) * half] = f2[2 + j, 0:rows, :]
    q01, k01 = f[0, 0:rows, 0:TILE], f[0, 0:rows, TILE:]
    v01, o01 = f[1, 0:rows, 0:TILE], f[1, 0:rows, TILE:]
    qk2, vo2 = f[2, 0:rows, 0:TILE], f[2, 0:rows, TILE:]
    gq[:, 0:TILE] = q01
    gq[:, TILE:] = qk2[:, 0:HD]
    gk[:, 0:TILE] = k01
    gk[:, TILE:] = swap(qk2)[:, 0:HD]
    gv[:, 0:TILE] = v01
    gv[:, TILE:] = vo2[:, 0:HD]
    go[0:TILE, :] = jnp.transpose(o01)
    go[TILE:, :] = jnp.transpose(vo2)[HD:, :]
    ex = [f[3, 0:EXTRA, 0:TILE], f[3, 0:EXTRA, TILE:]]

    def line(i):
        return ex[i // EXTRA][i % EXTRA : i % EXTRA + 1, :]

    for i in range(6):
        v = jnp.concatenate([line(3 * i), line(3 * i + 1), line(3 * i + 2)], axis=1)
        v = jnp.broadcast_to(v, (8, width))
        v = pltpu.roll(v, lax.rem(width - me_d * rows, width), axis=1)
        gvec[i][...] = v[0, 0:rows]
    b = [line(18 + i) for i in range(6)]
    gqb[...] = jnp.concatenate([b[0], b[4][:, 0:HD]], axis=1)[0]
    gvb[...] = jnp.concatenate([b[2], b[5][:, 0:HD]], axis=1)[0]
    gub[...] = jnp.concatenate([line(24 + i) for i in range(6)], axis=1)[0]


def unpack_kernel(sizes, *refs):
    nctx, ntp, ndp, main, width, rows, padded = sizes
    own, oth, refs = refs[:nctx], refs[nctx], refs[nctx + 1 :]
    kept, mask, outs, refs = refs[:2], refs[2], refs[3:5], refs[5:]
    stage, tail, valid, sem = refs
    images = nctx * ntp
    me_c, me_t = lax.axis_index("ctx"), lax.axis_index("tp")
    where = [(me_c ^ k) * ntp + t for t in (me_t, 1 - me_t) for k in range(nctx)]
    sources = [own[k] for k in range(nctx)] + [oth.at[k] for k in range(nctx)]
    blocks = main // BLOCK
    span = main + EXTRA
    last = pl.ds(main * images, images)
    gets = [pltpu.make_async_copy(kept[i].at[last, :], tail.at[i], sem.at[2, i]) for i in range(2)]
    gets.append(pltpu.make_async_copy(mask, valid, sem.at[2, 2]))
    for c in gets:
        c.start()

    def hit(r, c):
        img = where[-1]
        for j in range(images - 1):
            img = jnp.where(c // BLOCK == j, where[j], img)
        return r == (c % BLOCK) * images + img

    put = one_hot((images * BLOCK, images * BLOCK), hit)
    copies = []
    for i in range(2):
        for b in range(blocks):
            lo = i * span + b * BLOCK
            got = jnp.concatenate([src[lo : lo + BLOCK, :] for src in sources], axis=0)
            at = pl.ds(b * BLOCK * images, BLOCK * images)
            stage[i, at, :] = nn(put, got)
            copies.append(pltpu.make_async_copy(stage.at[i, at, :], outs[i].at[at, :], sem.at[i, b]))
            copies[-1].start()
    for c in gets:
        c.wait()
    for i in range(2):
        for src, img in zip(sources, where):
            got = src[i * span + main : (i + 1) * span, :].astype(F32)[0:1, :]
            stage[i, pl.ds(main * images + img, 1), :] = jnp.where(
                valid[img, main] > 0, got, tail[i, pl.ds(img, 1), :]
            )
        copies.append(pltpu.make_async_copy(stage.at[i, last, :], outs[i].at[last, :], sem.at[i, blocks]))
        copies[-1].start()
    for c in copies:
        c.wait()


def xor(n, k):
    return [(i, i ^ k) for i in range(n)]


def over(axis, n, items):
    return [items[0]] + [lax.ppermute(items[k], axis, xor(n, k)) for k in range(1, n)]


def body(nctx, ntp, ndp, *args):
    (tokens, valid_mask, cotangent, w_query, w_key, w_value, query_bias, value_bias, w_out, w_up, up_bias, w_down) = args[:12]
    vecs = args[12:]
    images, slots, width = tokens.shape
    main = slots - 1
    rows = w_query.shape[0]
    padded = -(-rows // EXTRA) * EXTRA
    ff = w_up.shape[1]
    p1_cols = 4 * w_query.shape[1]
    sizes = (nctx, ntp, ndp, main, width, rows, padded)
    total = nctx * main + EXTRA
    keys = -(-total // TILE) * TILE
    stage = BF if rows % 16 == 0 else F32
    flip = xor(ntp, 1)
    tok = jnp.transpose(tokens, (1, 0, 2)).reshape(slots * images, width)
    cot = jnp.transpose(cotangent, (1, 0, 2)).reshape(slots * images, width)

    def one(f):
        return functools.partial(f, sizes)

    def other(v):
        return lax.ppermute(v, "tp", flip)

    def held(arrays):
        return [
            (pltpu.SMEM if v.dtype == jnp.int32 else pltpu.VMEM)(v.shape, v.dtype) for v in arrays
        ] + [pltpu.SemaphoreType.DMA((len(arrays),))]

    def gather_dp(name, piece, after):
        v = piece[None]
        stride = ndp // 2
        while stride > 1:
            v = call(
                name,
                functools.partial(join_kernel, "dp", stride),
                sds((2 * v.shape[0],) + v.shape[1:], v.dtype),
                after=after,
            )(v, lax.ppermute(v, "dp", xor(ndp, stride)))
            stride //= 2
        return v, lax.ppermute(v, "dp", xor(ndp, 1))

    sources = [w_query, w_key, w_value, w_out, w_up, jnp.transpose(w_down), query_bias, value_bias, up_bias, *vecs]
    p1, p2q = call(
        "pack_weights",
        functools.partial(pack_weights_kernel, sizes, len(sources)),
        [sds((padded + EXTRA, p1_cols), BF), sds((padded, ff // 2), BF)],
        scratch=held(sources),
        mib=60,
        raw=range(len(sources)),
    )(*sources)
    sources = [tok, cot, valid_mask]
    scratch = held(sources)
    scratch[1] = pltpu.VMEM((images, width), F32)
    sent = call(
        "pack_slots",
        one(pack_slots_kernel),
        [sds((main + EXTRA, width), BF)] * nctx,
        scratch=scratch,
        mib=60,
        raw=range(3),
        after=[p1],
    )(*sources)
    t_in = over("ctx", nctx, sent)
    w2q = gather_dp("join_quarter", p2q, [sent[0]])
    sent = call(
        "pack_cotangent",
        one(pack_slots_kernel),
        [sds((main, width), BF)] * nctx,
        scratch=held([cot]),
        mib=60,
        raw=range(1),
        after=[w2q[0]],
    )(cot)
    w1 = gather_dp("join_attn", p1, [w2q[0], sent[0], *t_in[1:]])
    c_in = over("ctx", nctx, sent)
    w2q = call(
        "merge_quarter",
        one(merge_quarter_kernel),
        sds((width, ff // 2), BF),
        scratch=[pltpu.VMEM((width, ff // 2), stage)],
        after=[w1[0], *c_in[1:]],
    )(*w2q)
    w1_own = call(
        "merge_attn",
        one(merge_attn_kernel),
        sds((width + EXTRA, p1_cols), BF),
        scratch=[pltpu.VMEM((width, p1_cols), stage)],
        after=[w2q],
    )(*w1)
    w2q = over("ctx", nctx, [w2q] * nctx)
    x, mid, n1, n2, qkv, ctx, lse, wqkv, wot, vec, ub, cot_in = call(
        "attention",
        one(attention_kernel),
        [
            sds((total, width), F32), sds((total, width), F32), sds((total, width), BF), sds((total, width), BF),
            sds((keys, 3 * width), BF), sds((total, width), BF), sds((total, TILE), F32),
            sds((width, 3 * width), BF), sds((width, width), BF), sds((EXTRA, width), F32), sds((8, 2 * ff), F32),
            sds((total, width), BF),
        ],
        mib=32,
    )(*t_in, *c_in, w1_own, other(w1_own))
    w2_own = call(
        "merge_ff", functools.partial(merge_ff_kernel, nctx), sds((width, 2 * ff), BF), after=[vec]
    )(*w2q)
    w2_oth = other(w2_own)
    ff_grads = sds((4, ndp, padded, ff // 2), BF)

    def mlp_half(name, side, w, after=()):
        return call(
            name,
            functools.partial(mlp_half_kernel, sizes, side),
            [sds((total, ff), BF), sds((total, ff), BF), sds((8, ff), F32), ff_grads],
            mib=32,
            after=after,
        )(n2, cot_in, w, ub)

    hid_own, hgr_own, ub_own, g2_own = mlp_half("mlp_own", 0, w2_own)
    hid_oth, hgr_oth, ub_oth, g2_oth = mlp_half("mlp_oth", 1, w2_oth, [ub_own])
    bo, dmid, dctx, g_out, vgrad = call(
        "mlp_sums",
        one(mlp_sums_kernel),
        [
            sds((total, width), BF), sds((total, width), F32), sds((total, width), BF), sds((width, width), F32),
            sds((EXTRA, width), F32),
        ],
        mib=32,
    )(mid, ctx, wot, vec, cot_in, w2_own, w2_oth, hid_own, hid_oth, hgr_own, hgr_oth)

    def core_sums(name, own, oth, after=()):
        outs = [sds(own.shape[1:], BF)] * nctx
        return call(name, functools.partial(sum_core_kernel, nctx), outs, after=after)(own, other(oth))

    def ctx_sums(name, s, through=(), after=()):
        outs = [sds(s[0].shape[1:], BF)] * ndp + [sds(v.shape, v.dtype) for v in through]
        return call(name, functools.partial(sum_ctx_kernel, nctx, ndp), outs, after=after)(*s, *through)

    def by_image(v):
        return jnp.transpose(v.reshape(slots, images, width), (1, 0, 2))

    s2_send = core_sums("sum_core_ff", g2_own, g2_oth, after=[vgrad])
    s2 = over("ctx", nctx, s2_send)
    ig, g1_own, g1_oth = call(
        "attention_back",
        one(attention_back_kernel),
        [sds((total, width), BF)] + [sds((4, ndp, padded, 2 * TILE), BF)] * 2,
        scratch=[pltpu.VMEM((total, 3 * width), BF)],
        mib=32,
        after=[s2_send[0]],
    )(qkv, dctx, lse, n1, x, dmid, wqkv, vec, g_out, vgrad, ub_own, ub_oth)
    *u2_send, g1_oth = ctx_sums("sum_ctx_ff", s2, through=[g1_oth], after=[g1_own])
    s1_send = core_sums("sum_core_attn", g1_own, g1_oth)
    s1 = over("ctx", nctx, s1_send)
    u2 = over("dp", ndp, u2_send)
    back = call(
        "returns",
        one(returns_kernel),
        [sds((2 * (main + EXTRA), width), BF)] * nctx,
        after=[s1_send[0]],
    )(bo, ig)
    back = over("ctx", nctx, back)
    u1_send = ctx_sums("sum_ctx_attn", s1, after=[back[0]])
    u1 = over("dp", ndp, u1_send)
    summed = call(
        "sum_dp",
        functools.partial(sum_dp_kernel, ndp),
        sds((padded, ff // 2 + 2 * TILE), BF),
    )(*u2, *u1)
    shares = over("ctx", nctx, [summed] * nctx)
    stacked = call("stack", stack_kernel, sds((nctx,) + back[0].shape, BF), after=[summed])(*back)
    block_out, input_grad = call(
        "place_slots",
        one(unpack_kernel),
        [sds(tok.shape, F32)] * 2,
        scratch=[
            pltpu.VMEM((2,) + tok.shape, F32),
            pltpu.VMEM((2, images, width), F32),
            pltpu.SMEM(valid_mask.shape, valid_mask.dtype),
            pltpu.SemaphoreType.DMA((3, max(main // BLOCK + 1, 3))),
        ],
        raw=range(nctx + 1, nctx + 4),
        raw_out=True,
    )(*back, other(stacked), tok, cot, valid_mask)
    gq, gk, gv, gqb, gvb, go, gu, gub, gd, *gvec = call(
        "place_grads",
        one(grads_kernel),
        [
            sds(w_query.shape, F32), sds(w_key.shape, F32), sds(w_value.shape, F32),
            sds(query_bias.shape, F32), sds(value_bias.shape, F32), sds(w_out.shape, F32),
            sds(w_up.shape, F32), sds(up_bias.shape, F32), sds((rows, ff), F32),
        ]
        + [sds((rows,), F32)] * 6,
        scratch=[
            pltpu.VMEM((nctx, padded, 2 * TILE), F32),
            pltpu.VMEM((nctx, padded, ff // 2), F32),
        ],
    )(*shares)
    return (by_image(block_out), by_image(input_grad), gq, gk, gv, gqb, gvb, go, gu, gub, jnp.transpose(gd), *gvec)


def solution(mesh):
    rows, cols, tp, dp = P("dp", "tp"), P("tp", "dp"), P("tp"), P("dp")
    act = P("dp", "ctx", None)
    return jax.shard_map(
        functools.partial(body, mesh.shape["ctx"], mesh.shape["tp"], mesh.shape["dp"]),
        mesh=mesh,
        in_specs=(act, P("dp", "ctx"), act, rows, rows, rows, tp, tp, cols, rows, tp, cols) + (dp,) * 6,
        out_specs=(act, act, rows, rows, rows, tp, tp, cols, rows, tp, cols) + (dp,) * 6,
        check_vma=False,
    )
```

time: 187 us -> 123 us (0.66)
  Pallas kernels: 58.6 us -> 39.1 us
  local copies, waits for them, and re-layouts: 19 us -> 3.4 us
  starting transfers between devices: 61 us -> 45.7 us
  waiting for transfers between devices: 47.1 us -> 33.5 us
    pallas_call x11 -> x22, Pallas kernels: 58.6 us -> 39.1 us  [run(): pl.pallas_call(ordered, name=name, out_shape=out_shape, in_specs=specs, o...]
    ppermute x36 -> x27, starting transfers between devices: 57.7 us -> 38.5 us  [over(): lax.ppermute(items[k], axis, xor(n, k))]
    ppermute x36 -> x27, waiting for transfers between devices: 47 us -> 28.6 us  [over(): lax.ppermute(items[k], axis, xor(n, k))]
    unnamed x134 -> x22, local copies, waits for them, and re-layouts: 19 us -> 3.4 us
    ppermute x18 -> x9, waiting for transfers between devices: 0.05 us -> 4.96 us  [the longest x5 2.28 us: other(): return lax.ppermute(v, 'tp', flip)]
    ppermute x18 -> x9, starting transfers between devices: 3.32 us -> 7.12 us  [the longest x2 4.18 us: gather_dp(): lax.ppermute(v, 'dp', xor(ndp, stride))]
  transfers between devices with their start and end apart: 54 -> 36, of which waited for: 9 -> 16; matrix products, arithmetic and copies ran while one was open for 3% -> 0% of each run, Pallas kernels for 21% -> 24%
where the time goes in v2:
time: 123 us
  starting transfers between devices  45.7 us (37%)
  Pallas kernels  39.1 us (32%)
  waiting for transfers between devices  33.5 us (27%)
  local copies, waits for them, and re-layouts  3.4 us (3%)
    pallas_call x22, Pallas kernels, run(): pl.pallas_call(ordered, name=name, out_shape=out_shape, in_specs=specs, o...  39.1 us
    ppermute x27, starting transfers between devices, over(): lax.ppermute(items[k], axis, xor(n, k))  38.5 us
    ppermute x27, waiting for transfers between devices, over(): lax.ppermute(items[k], axis, xor(n, k))  28.6 us
    ppermute x2, starting transfers between devices, gather_dp(): lax.ppermute(v, 'dp', xor(ndp, stride))  4.18 us
    unnamed x22, local copies, waits for them, and re-layouts  3.4 us
  transfers between devices with their start and end apart: 36, of which 16 were waited for; matrix products, arithmetic and copies ran while one was open for 0% of the time, Pallas kernels for 24%

profile of v2, /device:TPU:0, one launch (start us, length us, event | category | flops | bytes accessed | tf_op | source)
XLA Modules:
  0.0 122.9 jit_solution(16548719793014624929)
XLA Ops:
  0.7 2.1 %pack_weights.1 = (bf16[112,768]{1,0:T(8,128)(2,1)}, bf16[96,384]{1,0:T(8,128)(2,1)}) custom-call(bf16[96,192]{1,0:T(8,128)(2,1)} %refs_0_.1, bf16[96,192]{1,0:T(8,128)(2,1)} %refs_1_.1, bf16[96,192]{1,0:T(8,128)(2,1)} %refs_2_.1, bf16[192,96]{1,0:T(8,128)(2,1)} %refs_3_.2, bf16[96,768]{1,0:T(8,128)(2,1)} %refs_4_.1, bf16[96,768]{1,0:T(8,128)(2,1)} %bitcast.25, ...), custom_call_target="tpu_custom_call" | custom-call | flops 2300000000 | bytes 1 | tf_op jit(solution)/shard_map/pack_weights/pallas_call | solution.py:35
  2.8 4.1 %collective-permute-start.3 = (bf16[1,96,384]{2,1,0:T(8,128)(2,1)}, bf16[1,96,384]{2,1,0:T(8,128)(2,1)S(1)}, u32[]{:S(2)}, u32[]{:S(2)}) collective-permute-start(bf16[1,96,384]{2,1,0:T(8,128)(2,1)} %bitcast.23), channel_id=1, source_target_pairs={{0,16},{8,24},{16,0},{24,8},{1,17},{9,25},{17,1},{25,9},{2,18},{10... | collective-permute-start | bytes 221192 | tf_op jit(solution)/shard_map/ppermute | solution.py:655
  7.0 2.6 %pack_slots.1 = (bf16[160,384]{1,0:T(8,128)(2,1)}, bf16[160,384]{1,0:T(8,128)(2,1)}, bf16[160,384]{1,0:T(8,128)(2,1)}, bf16[160,384]{1,0:T(8,128)(2,1)}) custom-call(bf16[112,768]{1,0:T(8,128)(2,1)} %get-tuple-element.93.refs_0_, f32[1160,384]{1,0:T(8,128)} %bitcast.18, f32[1160,384]{1,0:T(8,128)} %bitcast.20, s32[8,145]{1,0:T(8,128)} %refs_7_.3), custom_call_target="tpu_custom_call" | custom-call | flops 3449999872 | bytes 1 | tf_op jit(solution)/shard_map/pack_slots/pallas_call | solution.py:35
  16.5 2.6 %pack_cotangent.1 = (bf16[144,384]{1,0:T(8,128)(2,1)}, bf16[144,384]{1,0:T(8,128)(2,1)}, bf16[144,384]{1,0:T(8,128)(2,1)}, bf16[144,384]{1,0:T(8,128)(2,1)}) custom-call(bf16[2,96,384]{2,1,0:T(8,128)(2,1)} %copy-done, f32[1160,384]{1,0:T(8,128)} %bitcast.21), custom_call_target="tpu_custom_call" | custom-call | flops 2300000000 | bytes 1 | tf_op jit(solution)/shard_map/pack_cotangent/pallas_call | solution.py:35
  26.6 2.6 %collective-permute-done.4.refs_1_.refs_5_ = bf16[144,384]{1,0:T(8,128)(2,1)S(1)} collective-permute-done((bf16[144,384]{1,0:T(8,128)(2,1)}, bf16[144,384]{1,0:T(8,128)(2,1)S(1)}, u32[]{:S(2)}, u32[]{:S(2)}) %collective-permute-start.4) | collective-permute-done | bytes 110624 | tf_op jit(solution)/shard_map/ppermute | solution.py:615
  33.6 2.4 %collective-permute-start.13 = (bf16[384,384]{1,0:T(8,128)(2,1)S(1)}, bf16[384,384]{1,0:T(8,128)(2,1)S(1)}, u32[]{:S(2)}, u32[]{:S(2)}) collective-permute-start(bf16[384,384]{1,0:T(8,128)(2,1)S(1)} %merge_quarter.1.refs_0_.refs_1_), channel_id=1, source_target_pairs={{0,6},{2,4},{4,2},{6,0},{1,7},{3,5},{5,3},{7,1},{8,14},{10,12},{12... | collective-permute-start | bytes 884744 | tf_op jit(solution)/shard_map/ppermute | solution.py:615
  37.2 6.1 %attention.1 = (f32[592,384]{1,0:T(8,128)S(1)}, f32[592,384]{1,0:T(8,128)S(1)}, bf16[592,384]{1,0:T(8,128)(2,1)S(1)}, bf16[592,384]{1,0:T(8,128)(2,1)S(1)}, bf16...) custom-call(bf16[160,384]{1,0:T(8,128)(2,1)S(1)} %copy-done.10, ...), custom_call_target="tpu_custom_call" | custom-call | flops 6899999744 | bytes 1 | tf_op jit(solution)/shard_map/attention/pallas_call | solution.py:35
  44.5 5.8 %collective-permute-done.12.refs_3_ = bf16[384,384]{1,0:T(8,128)(2,1)S(1)} collective-permute-done((bf16[384,384]{1,0:T(8,128)(2,1)S(1)}, bf16[384,384]{1,0:T(8,128)(2,1)S(1)}, u32[]{:S(2)}, u32[]{:S(2)}) %collective-permute-start.12) | collective-permute-done | bytes 294944 | tf_op jit(solution)/shard_map/ppermute | solution.py:615
  50.5 3.5 %mlp_own.1 = (bf16[592,768]{1,0:T(8,128)(2,1)S(1)}, bf16[592,768]{1,0:T(8,128)(2,1)S(1)}, f32[8,768]{1,0:T(8,128)S(1)}, bf16[4,4,96,384]{3,2,1,0:T(8,128)(2,1)S(1)}) custom-call(bf16[592,384]{1,0:T(8,128)(2,1)S(1)} %get-tuple-element.108.refs_0_.refs_1_, bf16[592,384]{1,0:T(8,128)(2,1)S(1)} %get-tuple-element.107.refs_1_.refs_2_.refs_4_, ...), custom_call_target="tpu_custom_call" | custom-call | flops 4600000000 | bytes 1 | tf_op jit(solution)/shard_map/mlp_own/pallas_call | solution.py:35
  54.0 3.7 %mlp_oth.1 = (bf16[592,768]{1,0:T(8,128)(2,1)S(1)}, bf16[592,768]{1,0:T(8,128)(2,1)S(1)}, f32[8,768]{1,0:T(8,128)S(1)}, bf16[4,4,96,384]{3,2,1,0:T(8,128)(2,1)S(1)}) custom-call(f32[8,768]{1,0:T(8,128)S(1)} %get-tuple-element.111.refs_0_.refs_11_, bf16[592,384]{1,0:T(8,128)(2,1)S(1)} %get-tuple-element.108.refs_0_.refs_1_, ...), custom_call_target="tpu_custom_call" | custom-call | flops 4600000000 | bytes 1 | tf_op jit(solution)/shard_map/mlp_oth/pallas_call | solution.py:35
  58.3 3.1 %mlp_sums.1 = (bf16[592,384]{1,0:T(8,128)(2,1)S(1)}, f32[592,384]{1,0:T(8,128)S(1)}, bf16[592,384]{1,0:T(8,128)(2,1)S(1)}, f32[384,384]{1,0:T(8,128)S(1)}, f32[16,384]{1,0:T(8,128)S(1)}) custom-call(f32[592,384]{1,0:T(8,128)S(1)} %get-tuple-element.103.refs_0_, bf16[592,384]{1,0:T(8,128)(2,1)S(1)} %get-tuple-element.104.refs_1_, ...), custom_call_target="tpu_custom_call" | custom-call | flops 2300000000 | bytes 1 | tf_op jit(solution)/shard_map/mlp_sums/pallas_call | solution.py:35
  65.2 10.7 %attention_back.1 = (bf16[592,384]{1,0:T(8,128)(2,1)S(1)}, bf16[4,4,96,256]{3,2,1,0:T(8,128)(2,1)S(1)}, bf16[4,4,96,256]{3,2,1,0:T(8,128)(2,1)S(1)}) custom-call(bf16[4,96,384]{2,1,0:T(8,128)(2,1)S(1)} %get-tuple-element.118.refs_0_.refs_1_, bf16[640,1152]{1,0:T(8,128)(2,1)S(1)} %get-tuple-element.119.refs_1_, ...), custom_call_target="tpu_custom_call" | custom-call | flops 12650000384 | bytes 1 | tf_op jit(solution)/shard_map/attention_back/pallas_call | solution.py:35
  75.9 2.3 %collective-permute-done.17.refs_3_ = bf16[4,96,384]{2,1,0:T(8,128)(2,1)S(1)} collective-permute-done((bf16[4,96,384]{2,1,0:T(8,128)(2,1)S(1)}, bf16[4,96,384]{2,1,0:T(8,128)(2,1)S(1)}, u32[]{:S(2)}, u32[]{:S(2)}) %collective-permute-start.17) | collective-permute-done | bytes 294944 | tf_op jit(solution)/shard_map/ppermute | solution.py:615
  78.5 2.3 %collective-permute-done.19.refs_1_ = bf16[4,4,96,256]{3,2,1,0:T(8,128)(2,1)S(1)} collective-permute-done((bf16[4,4,96,256]{3,2,1,0:T(8,128)(2,1)S(1)}, bf16[4,4,96,256]{3,2,1,0:T(8,128)(2,1)S(1)}, u32[]{:S(2)}, u32[]{:S(2)}) %collective-permute-start.19) | collective-permute-done | bytes 786464 | tf_op jit(solution)/shard_map/ppermute | solution.py:639
  86.7 2.2 %collective-permute-done.23.refs_1_ = bf16[96,384]{1,0:T(8,128)(2,1)S(1)} collective-permute-done((bf16[96,384]{1,0:T(8,128)(2,1)S(1)}, bf16[96,384]{1,0:T(8,128)(2,1)S(1)}, u32[]{:S(2)}, u32[]{:S(2)}) %collective-permute-start.23) | collective-permute-done | bytes 73760 | tf_op jit(solution)/shard_map/ppermute | solution.py:615
  90.9 3.0 %collective-permute-start.24 = (bf16[96,384]{1,0:T(8,128)(2,1)S(1)}, bf16[96,384]{1,0:T(8,128)(2,1)S(1)}, u32[]{:S(2)}, u32[]{:S(2)}) collective-permute-start(bf16[96,384]{1,0:T(8,128)(2,1)S(1)} %get-tuple-element.143), channel_id=1, source_target_pairs={{0,16},{8,24},{16,0},{24,8},{1,17},{9,25},{17,1},{25,9},{2,18},{10... | collective-permute-start | bytes 221192 | tf_op jit(solution)/shard_map/ppermute | solution.py:615
  93.9 3.5 %collective-permute-start.25 = (bf16[96,384]{1,0:T(8,128)(2,1)S(1)}, bf16[96,384]{1,0:T(8,128)(2,1)S(1)}, u32[]{:S(2)}, u32[]{:S(2)}) collective-permute-start(bf16[96,384]{1,0:T(8,128)(2,1)S(1)} %get-tuple-element.144), channel_id=1, source_target_pairs={{0,24},{8,16},{16,8},{24,0},{1,25},{9,17},{17,9},{25,1},{2,26},{10... | collective-permute-start | bytes 221192 | tf_op jit(solution)/shard_map/ppermute | solution.py:615
  100.2 2.1 %collective-permute-start.30 = (bf16[96,256]{1,0:T(8,128)(2,1)S(1)}, bf16[96,256]{1,0:T(8,128)(2,1)S(1)}, u32[]{:S(2)}, u32[]{:S(2)}) collective-permute-start(bf16[96,256]{1,0:T(8,128)(2,1)S(1)} %get-tuple-element.150), channel_id=1, source_target_pairs={{0,16},{8,24},{16,0},{24,8},{1,17},{9,25},{17,1},{25,9},{2,18},{10... | collective-permute-start | bytes 147464 | tf_op jit(solution)/shard_map/ppermute | solution.py:615
  102.7 3.2 %collective-permute-start.31 = (bf16[96,256]{1,0:T(8,128)(2,1)S(1)}, bf16[96,256]{1,0:T(8,128)(2,1)S(1)}, u32[]{:S(2)}, u32[]{:S(2)}) collective-permute-start(bf16[96,256]{1,0:T(8,128)(2,1)S(1)} %get-tuple-element.151), channel_id=1, source_target_pairs={{0,24},{8,16},{16,8},{24,0},{1,25},{9,17},{17,9},{25,1},{2,26},{10... | collective-permute-start | bytes 147464 | tf_op jit(solution)/shard_map/ppermute | solution.py:615
  105.8 2.8 %collective-permute-done.31.refs_7_ = bf16[96,256]{1,0:T(8,128)(2,1)S(1)} collective-permute-done((bf16[96,256]{1,0:T(8,128)(2,1)S(1)}, bf16[96,256]{1,0:T(8,128)(2,1)S(1)}, u32[]{:S(2)}, u32[]{:S(2)}) %collective-permute-start.31) | collective-permute-done | bytes 49184 | tf_op jit(solution)/shard_map/ppermute | solution.py:615
  109.0 3.7 %collective-permute-start.35 = (bf16[96,640]{1,0:T(8,128)(2,1)S(1)}, bf16[96,640]{1,0:T(8,128)(2,1)S(1)}, u32[]{:S(2)}, u32[]{:S(2)}) collective-permute-start(bf16[96,640]{1,0:T(8,128)(2,1)S(1)} %sum_dp.1.refs_0_), channel_id=1, source_target_pairs={{0,6},{2,4},{4,2},{6,0},{1,7},{3,5},{5,3},{7,1},{8,14},{10,12},{12... | collective-permute-start | bytes 368648 | tf_op jit(solution)/shard_map/ppermute | solution.py:615
  113.5 3.2 %collective-permute-done.35.refs_3_ = bf16[96,640]{1,0:T(8,128)(2,1)S(1)} collective-permute-done((bf16[96,640]{1,0:T(8,128)(2,1)S(1)}, bf16[96,640]{1,0:T(8,128)(2,1)S(1)}, u32[]{:S(2)}, u32[]{:S(2)}) %collective-permute-start.35) | collective-permute-done | bytes 122912 | tf_op jit(solution)/shard_map/ppermute | solution.py:615
  116.7 2.5 %collective-permute-done.34.refs_2_ = bf16[96,640]{1,0:T(8,128)(2,1)S(1)} collective-permute-done((bf16[96,640]{1,0:T(8,128)(2,1)S(1)}, bf16[96,640]{1,0:T(8,128)(2,1)S(1)}, u32[]{:S(2)}, u32[]{:S(2)}) %collective-permute-start.34) | collective-permute-done | bytes 122912 | tf_op jit(solution)/shard_map/ppermute | solution.py:615
  120.4 2.3 %place_slots.1 = (f32[1160,384]{1,0:T(8,128)}, f32[1160,384]{1,0:T(8,128)}) custom-call(bf16[320,384]{1,0:T(8,128)(2,1)S(1)} %get-tuple-element.137.refs_0_.refs_1_, bf16[320,384]{1,0:T(8,128)(2,1)S(1)} %collective-permute-done.20.refs_2_.refs_1_, bf16[320,384]{1,0:T(8,128)(2,1)S(1)} %collective-permute-done.21.refs_3_.refs_2_, ...), custom_call_target="tpu_custom_call" | custom-call | flops 2644999936 | bytes 1 | tf_op jit(solution)/shard_map/place_slots/pallas_call | solution.py:35
  (92 shorter events, 39.2 us)
Async XLA Ops:
  2.8 12.1 %collective-permute-start.3 = (bf16[1,96,384]{2,1,0:T(8,128)(2,1)}, bf16[1,96,384]{2,1,0:T(8,128)(2,1)S(1)}, u32[]{:S(2)}, u32[]{:S(2)}) collective-permute-start(bf16[1,96,384]{2,1,0:T(8,128)(2,1)} %bitcast.23), channel_id=1, source_target_pairs={{0,16},{8,24},{16,0},{24,8},{1,17},{9,25},{17,1},{25,9},{2,18},{10... | collective-permute-start | bytes 221192 | tf_op jit(solution)/shard_map/ppermute | solution.py:655
  6.9 12.2 %collective-permute-start.7 = (bf16[1,112,768]{2,1,0:T(8,128)(2,1)}, bf16[1,112,768]{2,1,0:T(8,128)(2,1)S(1)}, u32[]{:S(2)}, u32[]{:S(2)}) collective-permute-start(bf16[1,112,768]{2,1,0:T(8,128)(2,1)} %bitcast.16), channel_id=1, source_target_pairs={{0,16},{8,24},{16,0},{24,8},{1,17},{9,25},{17,1},{25,9},{2,18},{10... | collective-permute-start | bytes 516104 | tf_op jit(solution)/shard_map/ppermute | solution.py:655
  9.6 9.5 %collective-permute-start = (bf16[160,384]{1,0:T(8,128)(2,1)}, bf16[160,384]{1,0:T(8,128)(2,1)S(1)}, u32[]{:S(2)}, u32[]{:S(2)}) collective-permute-start(bf16[160,384]{1,0:T(8,128)(2,1)} %get-tuple-element.95), channel_id=1, source_target_pairs={{0,2},{2,0},{4,6},{6,4},{1,3},{3,1},{5,7},{7,5},{8,10},{10,8},{12,... | collective-permute-start | bytes 368648 | tf_op jit(solution)/shard_map/ppermute | solution.py:615
  11.4 7.7 %collective-permute-start.1 = (bf16[160,384]{1,0:T(8,128)(2,1)}, bf16[160,384]{1,0:T(8,128)(2,1)S(1)}, u32[]{:S(2)}, u32[]{:S(2)}) collective-permute-start(bf16[160,384]{1,0:T(8,128)(2,1)} %get-tuple-element.96), channel_id=1, source_target_pairs={{0,4},{2,6},{4,0},{6,2},{1,5},{3,7},{5,1},{7,3},{8,12},{10,14},{12... | collective-permute-start | bytes 368648 | tf_op jit(solution)/shard_map/ppermute | solution.py:615
  12.9 6.2 %collective-permute-start.2 = (bf16[160,384]{1,0:T(8,128)(2,1)}, bf16[160,384]{1,0:T(8,128)(2,1)S(1)}, u32[]{:S(2)}, u32[]{:S(2)}) collective-permute-start(bf16[160,384]{1,0:T(8,128)(2,1)} %get-tuple-element.97), channel_id=1, source_target_pairs={{0,6},{2,4},{4,2},{6,0},{1,7},{3,5},{5,3},{7,1},{8,14},{10,12},{12... | collective-permute-start | bytes 368648 | tf_op jit(solution)/shard_map/ppermute | solution.py:615
  21.0 12.5 %collective-permute-start.9 = (bf16[2,112,768]{2,1,0:T(8,128)(2,1)S(1)}, bf16[2,112,768]{2,1,0:T(8,128)(2,1)S(1)}, u32[]{:S(2)}, u32[]{:S(2)}) collective-permute-start(bf16[2,112,768]{2,1,0:T(8,128)(2,1)S(1)} %join_attn.1.refs_0_.refs_1_), channel_id=1, source_target_pairs={{0,8},{8,0},{16,24},{24,16},{1,9},{9,1},{17,25},{25,17},{2,10},{10... | collective-permute-start | bytes 1032200 | tf_op jit(solution)/shard_map/ppermute | solution.py:657
  22.6 10.7 %collective-permute-start.8 = (bf16[2,96,384]{2,1,0:T(8,128)(2,1)S(1)}, bf16[2,96,384]{2,1,0:T(8,128)(2,1)S(1)}, u32[]{:S(2)}, u32[]{:S(2)}) collective-permute-start(bf16[2,96,384]{2,1,0:T(8,128)(2,1)S(1)} %copy-done.1), channel_id=1, source_target_pairs={{0,8},{8,0},{16,24},{24,16},{1,9},{9,1},{17,25},{25,17},{2,10},{10... | collective-permute-start | bytes 442376 | tf_op jit(solution)/shard_map/ppermute | solution.py:657
  33.6 10.8 %collective-permute-start.13 = (bf16[384,384]{1,0:T(8,128)(2,1)S(1)}, bf16[384,384]{1,0:T(8,128)(2,1)S(1)}, u32[]{:S(2)}, u32[]{:S(2)}) collective-permute-start(bf16[384,384]{1,0:T(8,128)(2,1)S(1)} %merge_quarter.1.refs_0_.refs_1_), channel_id=1, source_target_pairs={{0,6},{2,4},{4,2},{6,0},{1,7},{3,5},{5,3},{7,1},{8,14},{10,12},{12... | collective-permute-start | bytes 884744 | tf_op jit(solution)/shard_map/ppermute | solution.py:615
  36.1 14.2 %collective-permute-start.12 = (bf16[384,384]{1,0:T(8,128)(2,1)S(1)}, bf16[384,384]{1,0:T(8,128)(2,1)S(1)}, u32[]{:S(2)}, u32[]{:S(2)}) collective-permute-start(bf16[384,384]{1,0:T(8,128)(2,1)S(1)} %merge_quarter.1.refs_0_.refs_1_), channel_id=1, source_target_pairs={{0,4},{2,6},{4,0},{6,2},{1,5},{3,7},{5,1},{7,3},{8,12},{10,14},{12... | collective-permute-start | bytes 884744 | tf_op jit(solution)/shard_map/ppermute | solution.py:615
  36.6 13.7 %collective-permute-start.11 = (bf16[384,384]{1,0:T(8,128)(2,1)S(1)}, bf16[384,384]{1,0:T(8,128)(2,1)S(1)}, u32[]{:S(2)}, u32[]{:S(2)}) collective-permute-start(bf16[384,384]{1,0:T(8,128)(2,1)S(1)} %merge_quarter.1.refs_0_.refs_1_), channel_id=1, source_target_pairs={{0,2},{2,0},{4,6},{6,4},{1,3},{3,1},{5,7},{7,5},{8,10},{10,8},{12,... | collective-permute-start | bytes 884744 | tf_op jit(solution)/shard_map/ppermute | solution.py:615
  61.7 14.2 %collective-permute-start.16 = (bf16[4,96,384]{2,1,0:T(8,128)(2,1)S(1)}, bf16[4,96,384]{2,1,0:T(8,128)(2,1)S(1)}, u32[]{:S(2)}, u32[]{:S(2)}) collective-permute-start(bf16[4,96,384]{2,1,0:T(8,128)(2,1)S(1)} %get-tuple-element.129), channel_id=1, source_target_pairs={{0,2},{2,0},{4,6},{6,4},{1,3},{3,1},{5,7},{7,5},{8,10},{10,8},{12,... | collective-permute-start | bytes 884744 | tf_op jit(solution)/shard_map/ppermute | solution.py:615
  63.2 15.0 %collective-permute-start.17 = (bf16[4,96,384]{2,1,0:T(8,128)(2,1)S(1)}, bf16[4,96,384]{2,1,0:T(8,128)(2,1)S(1)}, u32[]{:S(2)}, u32[]{:S(2)}) collective-permute-start(bf16[4,96,384]{2,1,0:T(8,128)(2,1)S(1)} %get-tuple-element.130), channel_id=1, source_target_pairs={{0,4},{2,6},{4,0},{6,2},{1,5},{3,7},{5,1},{7,3},{8,12},{10,14},{12... | collective-permute-start | bytes 884744 | tf_op jit(solution)/shard_map/ppermute | solution.py:615
  64.0 14.2 %collective-permute-start.18 = (bf16[4,96,384]{2,1,0:T(8,128)(2,1)S(1)}, bf16[4,96,384]{2,1,0:T(8,128)(2,1)S(1)}, u32[]{:S(2)}, u32[]{:S(2)}) collective-permute-start(bf16[4,96,384]{2,1,0:T(8,128)(2,1)S(1)} %get-tuple-element.131), channel_id=1, source_target_pairs={{0,6},{2,4},{4,2},{6,0},{1,7},{3,5},{5,3},{7,1},{8,14},{10,12},{12... | collective-permute-start | bytes 884744 | tf_op jit(solution)/shard_map/ppermute | solution.py:615
  81.0 8.7 %collective-permute-start.26 = (bf16[4,96,256]{2,1,0:T(8,128)(2,1)S(1)}, bf16[4,96,256]{2,1,0:T(8,128)(2,1)S(1)}, u32[]{:S(2)}, u32[]{:S(2)}) collective-permute-start(bf16[4,96,256]{2,1,0:T(8,128)(2,1)S(1)} %get-tuple-element.145), channel_id=1, source_target_pairs={{0,2},{2,0},{4,6},{6,4},{1,3},{3,1},{5,7},{7,5},{8,10},{10,8},{12,... | collective-permute-start | bytes 589832 | tf_op jit(solution)/shard_map/ppermute | solution.py:615
  81.6 9.3 %collective-permute-start.27 = (bf16[4,96,256]{2,1,0:T(8,128)(2,1)S(1)}, bf16[4,96,256]{2,1,0:T(8,128)(2,1)S(1)}, u32[]{:S(2)}, u32[]{:S(2)}) collective-permute-start(bf16[4,96,256]{2,1,0:T(8,128)(2,1)S(1)} %get-tuple-element.146), channel_id=1, source_target_pairs={{0,4},{2,6},{4,0},{6,2},{1,5},{3,7},{5,1},{7,3},{8,12},{10,14},{12... | collective-permute-start | bytes 589832 | tf_op jit(solution)/shard_map/ppermute | solution.py:615
  83.0 10.9 %collective-permute-start.28 = (bf16[4,96,256]{2,1,0:T(8,128)(2,1)S(1)}, bf16[4,96,256]{2,1,0:T(8,128)(2,1)S(1)}, u32[]{:S(2)}, u32[]{:S(2)}) collective-permute-start(bf16[4,96,256]{2,1,0:T(8,128)(2,1)S(1)} %get-tuple-element.147), channel_id=1, source_target_pairs={{0,6},{2,4},{4,2},{6,0},{1,7},{3,5},{5,3},{7,1},{8,14},{10,12},{12... | collective-permute-start | bytes 589832 | tf_op jit(solution)/shard_map/ppermute | solution.py:615
  86.1 22.6 %collective-permute-start.20 = (bf16[320,384]{1,0:T(8,128)(2,1)S(1)}, bf16[320,384]{1,0:T(8,128)(2,1)S(1)}, u32[]{:S(2)}, u32[]{:S(2)}) collective-permute-start(bf16[320,384]{1,0:T(8,128)(2,1)S(1)} %get-tuple-element.138), channel_id=1, source_target_pairs={{0,2},{2,0},{4,6},{6,4},{1,3},{3,1},{5,7},{7,5},{8,10},{10,8},{12,... | collective-permute-start | bytes 737288 | tf_op jit(solution)/shard_map/ppermute | solution.py:615
  88.9 19.9 %collective-permute-start.21 = (bf16[320,384]{1,0:T(8,128)(2,1)S(1)}, bf16[320,384]{1,0:T(8,128)(2,1)S(1)}, u32[]{:S(2)}, u32[]{:S(2)}) collective-permute-start(bf16[320,384]{1,0:T(8,128)(2,1)S(1)} %get-tuple-element.139), channel_id=1, source_target_pairs={{0,4},{2,6},{4,0},{6,2},{1,5},{3,7},{5,1},{7,3},{8,12},{10,14},{12... | collective-permute-start | bytes 737288 | tf_op jit(solution)/shard_map/ppermute | solution.py:615
  89.7 19.1 %collective-permute-start.22 = (bf16[320,384]{1,0:T(8,128)(2,1)S(1)}, bf16[320,384]{1,0:T(8,128)(2,1)S(1)}, u32[]{:S(2)}, u32[]{:S(2)}) collective-permute-start(bf16[320,384]{1,0:T(8,128)(2,1)S(1)} %get-tuple-element.140), channel_id=1, source_target_pairs={{0,6},{2,4},{4,2},{6,0},{1,7},{3,5},{5,3},{7,1},{8,14},{10,12},{12... | collective-permute-start | bytes 737288 | tf_op jit(solution)/shard_map/ppermute | solution.py:615
  90.9 7.6 %collective-permute-start.24 = (bf16[96,384]{1,0:T(8,128)(2,1)S(1)}, bf16[96,384]{1,0:T(8,128)(2,1)S(1)}, u32[]{:S(2)}, u32[]{:S(2)}) collective-permute-start(bf16[96,384]{1,0:T(8,128)(2,1)S(1)} %get-tuple-element.143), channel_id=1, source_target_pairs={{0,16},{8,24},{16,0},{24,8},{1,17},{9,25},{17,1},{25,9},{2,18},{10... | collective-permute-start | bytes 221192 | tf_op jit(solution)/shard_map/ppermute | solution.py:615
  93.9 6.3 %collective-permute-start.25 = (bf16[96,384]{1,0:T(8,128)(2,1)S(1)}, bf16[96,384]{1,0:T(8,128)(2,1)S(1)}, u32[]{:S(2)}, u32[]{:S(2)}) collective-permute-start(bf16[96,384]{1,0:T(8,128)(2,1)S(1)} %get-tuple-element.144), channel_id=1, source_target_pairs={{0,24},{8,16},{16,8},{24,0},{1,25},{9,17},{17,9},{25,1},{2,26},{10... | collective-permute-start | bytes 221192 | tf_op jit(solution)/shard_map/ppermute | solution.py:615
  108.9 11.5 %collective-permute-start.32 = (bf16[4,320,384]{2,1,0:T(8,128)(2,1)S(1)}, bf16[4,320,384]{2,1,0:T(8,128)(2,1)S(1)}, u32[]{:S(2)}, u32[]{:S(2)}) collective-permute-start(bf16[4,320,384]{2,1,0:T(8,128)(2,1)S(1)} %stack.1), channel_id=1, source_target_pairs={{0,1},{1,0},{2,3},{3,2},{4,5},{5,4},{6,7},{7,6},{8,9},{9,8},{10,11... | collective-permute-start | bytes 2949128 | tf_op jit(solution)/shard_map/ppermute | solution.py:639
  109.0 7.8 %collective-permute-start.35 = (bf16[96,640]{1,0:T(8,128)(2,1)S(1)}, bf16[96,640]{1,0:T(8,128)(2,1)S(1)}, u32[]{:S(2)}, u32[]{:S(2)}) collective-permute-start(bf16[96,640]{1,0:T(8,128)(2,1)S(1)} %sum_dp.1.refs_0_), channel_id=1, source_target_pairs={{0,6},{2,4},{4,2},{6,0},{1,7},{3,5},{5,3},{7,1},{8,14},{10,12},{12... | collective-permute-start | bytes 368648 | tf_op jit(solution)/shard_map/ppermute | solution.py:615
  112.7 6.5 %collective-permute-start.34 = (bf16[96,640]{1,0:T(8,128)(2,1)S(1)}, bf16[96,640]{1,0:T(8,128)(2,1)S(1)}, u32[]{:S(2)}, u32[]{:S(2)}) collective-permute-start(bf16[96,640]{1,0:T(8,128)(2,1)S(1)} %sum_dp.1.refs_0_), channel_id=1, source_target_pairs={{0,4},{2,6},{4,0},{6,2},{1,5},{3,7},{5,1},{7,3},{8,12},{10,14},{12... | collective-permute-start | bytes 368648 | tf_op jit(solution)/shard_map/ppermute | solution.py:615
  (23 other events, 137.5 us)

commit v3 on v2

--- a/solution.py
+++ b/solution.py
@@ -15,13 +15,13 @@
 F32 = jnp.float32
 TILE = 128
 TIMES = {
-    "pack_weights": 2.0, "pack_slots": 3.0, "pack_cotangent": 2.0, "attention": 6.0, "mlp_own": 4.0, "mlp_oth": 4.0, "mlp_sums": 2.0, "attention_back": 11.0,
-    "place_grads": 1.0, "place_slots": 2.3,
+    "pack_weights": 2.0, "pack_slots": 3.0, "pack_cotangent": 2.0, "attention": 0.0, "mlp_own": 4.0, "mlp_oth": 4.0, "mlp_sums": 2.0, "attention_back": 11.0,
+    "place_grads": 1.0, "place_slots": 2.3, "join_quarter": 20.0, "sum_ctx_attn": 50.0, "sum_ctx_ff": 50.0,
 }
 EXTRA = 16
 
 
-def call(name, kernel, out_shape, scratch=(), mib=8, after=(), raw=(), raw_out=False):
+def call(name, kernel, out_shape, scratch=(), mib=8, after=(), raw=()):
     after = list(after)
 
     def ordered(*refs):
@@ -37,9 +37,7 @@
             name=name,
             out_shape=out_shape,
             in_specs=specs,
-            out_specs=jax.tree.map(
-                lambda _: pl.BlockSpec(memory_space=pltpu.HBM if raw_out else pltpu.VMEM), out_shape
-            ),
+            out_specs=jax.tree.map(lambda _: pl.BlockSpec(memory_space=pltpu.VMEM), out_shape),
             scratch_shapes=list(scratch),
             compiler_params=pltpu.CompilerParams(vmem_limit_bytes=mib << 20),
             cost_estimate=pl.CostEstimate(
@@ -215,34 +213,27 @@
 
 def pack_slots_kernel(sizes, *refs):
     nctx, ntp, ndp, main, width, rows, padded = sizes
-    count = len(refs) - nctx
-    count = count // 2
-    sources, sent, refs = refs[:count], refs[count : count + nctx], refs[count + nctx :]
-    held, sem = refs[:count], refs[count]
+    sources, sent, tails, refs = refs[:3], refs[3 : 3 + nctx], refs[3 + nctx], refs[4 + nctx :]
+    held, sem = refs[:3], refs[3]
+    copies = fetch(sources, held, sem)
+    tok, cot, mask = held
     images = nctx * ntp
-    last = pl.ds(main * images, images)
-    copies = [pltpu.make_async_copy(sources[0], held[0], sem.at[0])]
-    if count > 1:
-        copies.append(pltpu.make_async_copy(sources[1].at[last, :], held[1], sem.at[1]))
-        copies.append(pltpu.make_async_copy(sources[2], held[2], sem.at[2]))
-    for c in copies:
-        c.start()
     me_c, me_t = lax.axis_index("ctx"), lax.axis_index("tp")
     wanted = [(me_c ^ k) * ntp + me_t for k in range(nctx)]
     pick = picker(wanted, images)
-    for c in copies:
-        c.wait()
-    take_images(held[0], sent, 0, pick, images, main)
-    if count > 1:
-        tok, cot, mask = held
-        for k in range(nctx):
-            gate = mask[wanted[k], main].astype(F32)
-            te = tok[pl.ds(main * images + wanted[k], 1), :] * gate
-            ce = cot[pl.ds(wanted[k], 1), :] * gate
-            shape = (EXTRA, width)
-            sent[k][main : main + EXTRA, :] = jnp.where(
-                row_is(shape, 0), te, jnp.where(row_is(shape, 1), ce, 0.0)
-            ).astype(BF)
+    for i in range(2):
+        copies[i].wait()
+        take_images(held[i], sent, i * (main + EXTRA), pick, images, main)
+        tails[i] = held[i][main * images :, :]
+    copies[2].wait()
+    for k in range(nctx):
+        gate = mask[wanted[k], main].astype(F32)
+        te = tok[pl.ds(main * images + wanted[k], 1), :] * gate
+        ce = cot[pl.ds(main * images + wanted[k], 1), :] * gate
+        shape = (EXTRA, width)
+        sent[k][main : main + EXTRA, :] = jnp.where(
+            row_is(shape, 0), te, jnp.where(row_is(shape, 1), ce, 0.0)
+        ).astype(BF)
 
 
 def join_kernel(axis, stride, own, got, out):
@@ -252,28 +243,32 @@
         out[2 * i + 1 - bit] = got[i]
 
 
-def place_rows(out, own, got, rows, stage):
+def place_rows(outs, own, got, rows, stage):
     bit = lax.rem(lax.axis_index("dp"), 2)
     for i in range(own.shape[0]):
         for piece, last in ((own[i], bit), (got[i], 1 - bit)):
             at = pl.ds(pl.multiple_of((2 * i + last) * rows, 16 if rows % 16 == 0 else 8), rows)
             stage[at, :] = piece.astype(stage.dtype)[:rows]
-    out[0 : stage.shape[0], :] = stage[...].astype(BF)
+    cols = outs[0].shape[1]
+    for i, out in enumerate(outs):
+        out[0 : stage.shape[0], :] = stage[:, i * cols : (i + 1) * cols].astype(BF)
 
 
 def merge_quarter_kernel(sizes, own, got, out, stage):
-    place_rows(out, own, got, sizes[5], stage)
-
-
-def merge_attn_kernel(sizes, own, got, out, stage):
+    place_rows([out], own, got, sizes[5], stage)
+
+
+def merge_attn_kernel(sizes, own, got, *refs):
     nctx, ntp, ndp, main, width, rows, padded = sizes
-    place_rows(out, own, got, rows, stage)
+    outs, stage = refs[:-1], refs[-1]
+    place_rows(outs, own, got, rows, stage)
     extra = own[0, padded:, :].astype(F32)
     for more in [own[i] for i in range(1, own.shape[0])] + [got[i] for i in range(own.shape[0])]:
         more = more[padded:, :].astype(F32)
         row = lax.broadcasted_iota(jnp.int32, more.shape, 0)
         extra += jnp.where((row > 0) & (row < 7), more, 0.0)
-    out[width:, :] = extra.astype(BF)
+    for i, out in enumerate(outs):
+        out[width:, :] = extra[:, 2 * i * TILE : 2 * (i + 1) * TILE].astype(BF)
 
 
 def merge_ff_kernel(nctx, *refs):
@@ -286,12 +281,11 @@
 
 def attention_kernel(sizes, *refs):
     nctx, ntp, ndp, main, width, rows, padded = sizes
-    t_in, c_in, refs = refs[:nctx], refs[nctx : 2 * nctx], refs[2 * nctx :]
-    (own_in, oth_in), refs = refs[:2], refs[2:]
+    t_in, own_in, oth_in, refs = refs[:nctx], refs[nctx : nctx + 3], refs[nctx + 3 : nctx + 6], refs[nctx + 6 :]
     x_out, mid_out, n1_out, n2_out, qkv, ctx, lse, wqkv, wot, vec, ub, cot = refs
     body = nctx * main
     total = body + EXTRA
-    own, oth = own_in[...].astype(F32), oth_in[...].astype(F32)
+    own, oth = (jnp.concatenate([v[...] for v in part], axis=1).astype(F32) for part in (own_in, oth_in))
     tiles, outs = assemble(own, oth)
     for i, v in enumerate(tiles):
         wqkv[:, i * TILE : (i + 1) * TILE] = v[:width].astype(BF)
@@ -306,7 +300,7 @@
     extra = jnp.zeros((EXTRA, width), F32)
     for k in range(nctx):
         x_out[k * main : (k + 1) * main, :] = t_in[k][0:main, :].astype(F32)
-        cot[k * main : (k + 1) * main, :] = c_in[k][...]
+        cot[k * main : (k + 1) * main, :] = t_in[k][main + EXTRA :, :]
         extra += t_in[k][main : main + EXTRA, :].astype(F32)
     x_out[body:, :] = jnp.where(row_is((EXTRA, width), 0), extra, 0.0)
     cot[body:, :] = jnp.where(row_is((EXTRA, width), 0), extra[1:2, :], 0.0).astype(BF)
@@ -480,9 +474,6 @@
 
 def sum_ctx_kernel(n, ndp, *refs):
     me = lax.axis_index("dp")
-    if len(refs) > n + ndp:
-        refs[-1][...] = refs[n][...]
-        refs = refs[:n] + refs[n + 1 : -1]
     for k in range(ndp):
         v = refs[0][me ^ k].astype(F32)
         for i in range(1, n):
@@ -490,34 +481,52 @@
         refs[n + k][...] = v.astype(BF)
 
 
-def sum_dp(refs):
+def halve(axis, stride, item, keep, send):
+    bit = lax.rem(lax.div(lax.axis_index(axis), stride), 2)
+    for j in range(keep.shape[0]):
+        keep[j] = item(2 * j + bit).astype(BF)
+        send[j] = item(2 * j + 1 - bit).astype(BF)
+
+
+def sum_ctx_halves_kernel(n, *refs):
+    terms, (keep, send) = refs[:n], refs[n:]
+
+    def item(i):
+        v = terms[0][i].astype(F32)
+        for t in terms[1:]:
+            v = v + t[i].astype(F32)
+        return v
+
+    halve("dp", 1, item, keep, send)
+
+
+def add_halves_kernel(stride, own, got, keep, send):
+    halve("dp", stride, lambda i: own[i].astype(F32) + got[i].astype(F32), keep, send)
+
+
+def sum_dp_kernel(n, own, got, *refs):
+    out = refs[n]
+    cols = own.shape[2]
+    out[:, :cols] = (own[0].astype(F32) + got[0].astype(F32)).astype(BF)
     v = refs[0][...].astype(F32)
-    for r in refs[1:]:
+    for r in refs[1:n]:
         v = v + r[...].astype(F32)
-    return v.astype(BF)
-
-
-def sum_dp_kernel(n, *refs):
-    out = refs[2 * n]
-    cols = refs[0].shape[1]
-    out[:, :cols] = sum_dp(refs[:n])
-    out[:, cols:] = sum_dp(refs[n : 2 * n])
-
-
-def returns_kernel(sizes, bo, ig, *outs):
+    out[:, cols:] = v.astype(BF)
+
+
+def returns_kernel(sizes, bo, ig, out):
     nctx, ntp, ndp, main, width, rows, padded = sizes
+    me = lax.axis_index("ctx")
     span = main + EXTRA
     for k in range(nctx):
         at = slice(k * main, (k + 1) * main)
         for i, src in enumerate((bo, ig)):
-            outs[k][i * span : i * span + main, :] = src[at, :]
-            outs[k][i * span + main : (i + 1) * span, :] = src[nctx * main :, :]
-
-
-def stack_kernel(*refs):
-    out = refs[-1]
-    for i, r in enumerate(refs[:-1]):
-        out[i] = r[...]
+            out[me ^ k, i * span : i * span + main, :] = src[at, :]
+            out[me ^ k, i * span + main : (i + 1) * span, :] = src[nctx * main :, :]
+
+
+def hand_on_kernel(held, out):
+    out[...] = held[...]
 
 
 def grads_kernel(sizes, *refs):
@@ -560,22 +569,16 @@
     gub[...] = jnp.concatenate([line(24 + i) for i in range(6)], axis=1)[0]
 
 
-def unpack_kernel(sizes, *refs):
+def unpack_kernel(sizes, own, oth, tails, mask, *refs):
     nctx, ntp, ndp, main, width, rows, padded = sizes
-    own, oth, refs = refs[:nctx], refs[nctx], refs[nctx + 1 :]
-    kept, mask, outs, refs = refs[:2], refs[2], refs[3:5], refs[5:]
-    stage, tail, valid, sem = refs
+    outs, done, valid, sem = refs[:2], refs[2], refs[3], refs[4]
     images = nctx * ntp
-    me_c, me_t = lax.axis_index("ctx"), lax.axis_index("tp")
-    where = [(me_c ^ k) * ntp + t for t in (me_t, 1 - me_t) for k in range(nctx)]
-    sources = [own[k] for k in range(nctx)] + [oth.at[k] for k in range(nctx)]
-    blocks = main // BLOCK
+    me_t = lax.axis_index("tp")
+    where = [j * ntp + t for t in (me_t, 1 - me_t) for j in range(nctx)]
+    sources = [v.at[j] for v in (own, oth) for j in range(nctx)]
     span = main + EXTRA
-    last = pl.ds(main * images, images)
-    gets = [pltpu.make_async_copy(kept[i].at[last, :], tail.at[i], sem.at[2, i]) for i in range(2)]
-    gets.append(pltpu.make_async_copy(mask, valid, sem.at[2, 2]))
-    for c in gets:
-        c.start()
+    get_valid = pltpu.make_async_copy(mask, valid, sem.at[0])
+    get_valid.start()
 
     def hit(r, c):
         img = where[-1]
@@ -584,27 +587,19 @@
         return r == (c % BLOCK) * images + img
 
     put = one_hot((images * BLOCK, images * BLOCK), hit)
-    copies = []
     for i in range(2):
-        for b in range(blocks):
+        for b in range(main // BLOCK):
             lo = i * span + b * BLOCK
             got = jnp.concatenate([src[lo : lo + BLOCK, :] for src in sources], axis=0)
-            at = pl.ds(b * BLOCK * images, BLOCK * images)
-            stage[i, at, :] = nn(put, got)
-            copies.append(pltpu.make_async_copy(stage.at[i, at, :], outs[i].at[at, :], sem.at[i, b]))
-            copies[-1].start()
-    for c in gets:
-        c.wait()
+            outs[i][b * BLOCK * images : (b + 1) * BLOCK * images, :] = nn(put, got)
+    get_valid.wait()
     for i in range(2):
         for src, img in zip(sources, where):
             got = src[i * span + main : (i + 1) * span, :].astype(F32)[0:1, :]
-            stage[i, pl.ds(main * images + img, 1), :] = jnp.where(
-                valid[img, main] > 0, got, tail[i, pl.ds(img, 1), :]
+            outs[i][pl.ds(main * images + img, 1), :] = jnp.where(
+                valid[img, main] > 0, got, tails[i, pl.ds(img, 1), :]
             )
-        copies.append(pltpu.make_async_copy(stage.at[i, last, :], outs[i].at[last, :], sem.at[i, blocks]))
-        copies[-1].start()
-    for c in copies:
-        c.wait()
+    done[...] = jnp.zeros_like(done)
 
 
 def xor(n, k):
@@ -666,45 +661,32 @@
         raw=range(len(sources)),
     )(*sources)
     sources = [tok, cot, valid_mask]
-    scratch = held(sources)
-    scratch[1] = pltpu.VMEM((images, width), F32)
-    sent = call(
+    *sent, tails = call(
         "pack_slots",
         one(pack_slots_kernel),
-        [sds((main + EXTRA, width), BF)] * nctx,
-        scratch=scratch,
+        [sds((2 * main + EXTRA, width), BF)] * nctx + [sds((2, images, width), F32)],
+        scratch=held(sources),
         mib=60,
         raw=range(3),
         after=[p1],
     )(*sources)
     t_in = over("ctx", nctx, sent)
-    w2q = gather_dp("join_quarter", p2q, [sent[0]])
-    sent = call(
-        "pack_cotangent",
-        one(pack_slots_kernel),
-        [sds((main, width), BF)] * nctx,
-        scratch=held([cot]),
-        mib=60,
-        raw=range(1),
-        after=[w2q[0]],
-    )(cot)
-    w1 = gather_dp("join_attn", p1, [w2q[0], sent[0], *t_in[1:]])
-    c_in = over("ctx", nctx, sent)
     w2q = call(
         "merge_quarter",
         one(merge_quarter_kernel),
         sds((width, ff // 2), BF),
         scratch=[pltpu.VMEM((width, ff // 2), stage)],
-        after=[w1[0], *c_in[1:]],
-    )(*w2q)
+        after=t_in[1:],
+    )(*gather_dp("join_quarter", p2q, [sent[0]]))
+    w1 = gather_dp("join_attn", p1, [sent[0]])
+    w2q = over("ctx", nctx, [w2q] * nctx)
     w1_own = call(
         "merge_attn",
         one(merge_attn_kernel),
-        sds((width + EXTRA, p1_cols), BF),
+        [sds((width + EXTRA, 2 * TILE), BF)] * (p1_cols // (2 * TILE)),
         scratch=[pltpu.VMEM((width, p1_cols), stage)],
-        after=[w2q],
+        after=w2q[1:-1],
     )(*w1)
-    w2q = over("ctx", nctx, [w2q] * nctx)
     x, mid, n1, n2, qkv, ctx, lse, wqkv, wot, vec, ub, cot_in = call(
         "attention",
         one(attention_kernel),
@@ -715,7 +697,7 @@
             sds((total, width), BF),
         ],
         mib=32,
-    )(*t_in, *c_in, w1_own, other(w1_own))
+    )(*t_in, *w1_own, *[other(v) for v in w1_own])
     w2_own = call(
         "merge_ff", functools.partial(merge_ff_kernel, nctx), sds((width, 2 * ff), BF), after=[vec]
     )(*w2q)
@@ -747,10 +729,6 @@
         outs = [sds(own.shape[1:], BF)] * nctx
         return call(name, functools.partial(sum_core_kernel, nctx), outs, after=after)(own, other(oth))
 
-    def ctx_sums(name, s, through=(), after=()):
-        outs = [sds(s[0].shape[1:], BF)] * ndp + [sds(v.shape, v.dtype) for v in through]
-        return call(name, functools.partial(sum_ctx_kernel, nctx, ndp), outs, after=after)(*s, *through)
-
     def by_image(v):
         return jnp.transpose(v.reshape(slots, images, width), (1, 0, 2))
 
@@ -764,39 +742,46 @@
         mib=32,
         after=[s2_send[0]],
     )(qkv, dctx, lse, n1, x, dmid, wqkv, vec, g_out, vgrad, ub_own, ub_oth)
-    *u2_send, g1_oth = ctx_sums("sum_ctx_ff", s2, through=[g1_oth], after=[g1_own])
-    s1_send = core_sums("sum_core_attn", g1_own, g1_oth)
+    half = sds((ndp // 2,) + s2[0].shape[1:], BF)
+    keep, send = call(
+        "sum_ctx_ff", functools.partial(sum_ctx_halves_kernel, nctx), [half, half], after=[g1_own]
+    )(*s2)
+    s1_send = core_sums("sum_core_attn", g1_own, g1_oth, after=[keep])
     s1 = over("ctx", nctx, s1_send)
-    u2 = over("dp", ndp, u2_send)
     back = call(
         "returns",
         one(returns_kernel),
-        [sds((2 * (main + EXTRA), width), BF)] * nctx,
-        after=[s1_send[0]],
+        sds((nctx, 2 * (main + EXTRA), width), BF),
+        after=[s1[1]],
     )(bo, ig)
-    back = over("ctx", nctx, back)
-    u1_send = ctx_sums("sum_ctx_attn", s1, after=[back[0]])
+    returned = lax.all_to_all(back, "ctx", 0, 0)
+    u1_send = call(
+        "sum_ctx_attn",
+        functools.partial(sum_ctx_kernel, nctx, ndp),
+        [sds(s1[0].shape[1:], BF)] * ndp,
+        after=[back],
+    )(*s1)
     u1 = over("dp", ndp, u1_send)
+    stride = 2
+    while stride < ndp:
+        half = sds((keep.shape[0] // 2,) + keep.shape[1:], BF)
+        keep, send = call(
+            "add_dp_ff", functools.partial(add_halves_kernel, stride), [half, half], after=[u1_send[0]]
+        )(keep, lax.ppermute(send, "dp", xor(ndp, stride // 2)))
+        stride *= 2
     summed = call(
-        "sum_dp",
-        functools.partial(sum_dp_kernel, ndp),
-        sds((padded, ff // 2 + 2 * TILE), BF),
-    )(*u2, *u1)
+        "sum_dp", functools.partial(sum_dp_kernel, ndp), sds((padded, ff // 2 + 2 * TILE), BF)
+    )(keep, lax.ppermute(send, "dp", xor(ndp, ndp // 2)), *u1)
     shares = over("ctx", nctx, [summed] * nctx)
-    stacked = call("stack", stack_kernel, sds((nctx,) + back[0].shape, BF), after=[summed])(*back)
-    block_out, input_grad = call(
+    back = call("hand_on", hand_on_kernel, sds(returned.shape, BF), after=[summed])(returned)
+    block_out, input_grad, placed = call(
         "place_slots",
         one(unpack_kernel),
-        [sds(tok.shape, F32)] * 2,
-        scratch=[
-            pltpu.VMEM((2,) + tok.shape, F32),
-            pltpu.VMEM((2, images, width), F32),
-            pltpu.SMEM(valid_mask.shape, valid_mask.dtype),
-            pltpu.SemaphoreType.DMA((3, max(main // BLOCK + 1, 3))),
-        ],
-        raw=range(nctx + 1, nctx + 4),
-        raw_out=True,
-    )(*back, other(stacked), tok, cot, valid_mask)
+        [sds(tok.shape, F32)] * 2 + [sds((8, TILE), F32)],
+        scratch=[pltpu.SMEM(valid_mask.shape, valid_mask.dtype), pltpu.SemaphoreType.DMA((1,))],
+        raw=(3,),
+        mib=16,
+    )(back, other(back), tails, valid_mask)
     gq, gk, gv, gqb, gvb, go, gu, gub, gd, *gvec = call(
         "place_grads",
         one(grads_kernel),
@@ -810,6 +795,7 @@
             pltpu.VMEM((nctx, padded, 2 * TILE), F32),
             pltpu.VMEM((nctx, padded, ff // 2), F32),
         ],
+        after=[placed],
     )(*shares)
     return (by_image(block_out), by_image(input_grad), gq, gk, gv, gqb, gvb, go, gu, gub, jnp.transpose(gd), *gvec)
 

time: 123 us -> 107 us (0.87)
  starting transfers between devices: 45.7 us -> 37.2 us
  waiting for transfers between devices: 33.5 us -> 28.4 us
  local copies, waits for them, and re-layouts: 3.4 us -> 0.96 us
    ppermute x27 -> x18, starting transfers between devices: 38.5 us -> 22.2 us  [over(): lax.ppermute(items[k], axis, xor(n, k))]
    ppermute x27 -> x18, waiting for transfers between devices: 28.6 us -> 19.3 us  [over(): lax.ppermute(items[k], axis, xor(n, k))]
    ppermute x0 -> x2, starting transfers between devices: none -> 4.23 us  [the longest x1 2.64 us: body(): lax.ppermute(send, 'dp', xor(ndp, ndp // 2))]
    all_to_all x0 -> x1, starting transfers between devices: none -> 3.51 us  [body(): returned = lax.all_to_all(back, 'ctx', 0, 0)]
    ppermute x2, waiting for transfers between devices: 0.95 us -> 4.02 us  [gather_dp(): return (v, lax.ppermute(v, 'dp', xor(ndp, 1)))]
    unnamed x22 -> x12, local copies, waits for them, and re-layouts: 3.4 us -> 0.96 us
  transfers between devices with their start and end apart: 36 -> 32, of which waited for: 16 -> 17; matrix products, arithmetic and copies ran while one was open for 0% -> 0% of each run, Pallas kernels for 24% -> 29%
where the time goes in v3:
time: 107 us; the launch traced here: 106 us
  Pallas kernels  38.8 us (36%)
  starting transfers between devices  37.2 us (35%)
  waiting for transfers between devices  28.4 us (27%)
  between operations  1.11 us (1%)
    pallas_call x22, Pallas kernels, run(): pl.pallas_call(ordered, name=name, out_shape=out_shape, in_specs=specs, o...  38.8 us
    ppermute x18, starting transfers between devices, over(): lax.ppermute(items[k], axis, xor(n, k))  22.2 us
    ppermute x18, waiting for transfers between devices, over(): lax.ppermute(items[k], axis, xor(n, k))  19.3 us
    ppermute x2, starting transfers between devices, gather_dp(): lax.ppermute(v, 'dp', xor(ndp, stride))  4.18 us
    ppermute x2, waiting for transfers between devices, gather_dp(): return (v, lax.ppermute(v, 'dp', xor(ndp, 1)))  4.02 us
    all_to_all x1, starting transfers between devices, body(): returned = lax.all_to_all(back, 'ctx', 0, 0)  3.51 us
    ppermute x2, waiting for transfers between devices, gather_dp(): lax.ppermute(v, 'dp', xor(ndp, stride))  2.66 us
    ppermute x1, starting transfers between devices, body(): lax.ppermute(send, 'dp', xor(ndp, ndp // 2))  2.64 us
  transfers between devices with their start and end apart: 32, of which 17 were waited for; matrix products, arithmetic and copies ran while one was open for 0% of the time, Pallas kernels for 29%

profile of v3, /device:TPU:0, one launch (start us, length us, event | category | flops | bytes accessed | tf_op | source)
XLA Modules:
  0.0 106.4 jit_solution(4324139541188744109)
XLA Ops:
  0.7 2.1 %pack_weights.1 = (bf16[112,768]{1,0:T(8,128)(2,1)}, bf16[96,384]{1,0:T(8,128)(2,1)}) custom-call(bf16[96,192]{1,0:T(8,128)(2,1)} %refs_0_.1, bf16[96,192]{1,0:T(8,128)(2,1)} %refs_1_.1, bf16[96,192]{1,0:T(8,128)(2,1)} %refs_2_.1, bf16[192,96]{1,0:T(8,128)(2,1)} %refs_3_.3, bf16[96,768]{1,0:T(8,128)(2,1)} %refs_4_.1, bf16[96,768]{1,0:T(8,128)(2,1)} %bitcast.22, ...), custom_call_target="tpu_custom_call" | custom-call | flops 2300000000 | bytes 1 | tf_op jit(solution)/shard_map/pack_weights/pallas_call | solution.py:35
  2.8 4.1 %collective-permute-start.3 = (bf16[1,96,384]{2,1,0:T(8,128)(2,1)}, bf16[1,96,384]{2,1,0:T(8,128)(2,1)S(1)}, u32[]{:S(2)}, u32[]{:S(2)}) collective-permute-start(bf16[1,96,384]{2,1,0:T(8,128)(2,1)} %bitcast.18), channel_id=1, source_target_pairs={{0,16},{8,24},{16,0},{24,8},{1,17},{9,25},{17,1},{25,9},{2,18},{10... | collective-permute-start | bytes 221192 | tf_op jit(solution)/shard_map/ppermute | solution.py:650
  7.0 3.4 %pack_slots.1 = (bf16[304,384]{1,0:T(8,128)(2,1)}, bf16[304,384]{1,0:T(8,128)(2,1)}, bf16[304,384]{1,0:T(8,128)(2,1)}, bf16[304,384]{1,0:T(8,128)(2,1)}, f32[2,8,384]{2,1,0:T(8,128)}) custom-call(bf16[112,768]{1,0:T(8,128)(2,1)} %get-tuple-element.89.refs_0_, f32[1160,384]{1,0:T(8,128)} %bitcast.20, f32[1160,384]{1,0:T(8,128)} %bitcast.21, s32[8,145]{1,0:T(8,128)} %refs_3_.5), custom_call_target="tpu_custom_call" | custom-call | flops 3449999872 | bytes 1 | tf_op jit(solution)/shard_map/pack_slots/pallas_call | solution.py:35
  10.3 1.8 %collective-permute-start = (bf16[304,384]{1,0:T(8,128)(2,1)}, bf16[304,384]{1,0:T(8,128)(2,1)S(1)}, u32[]{:S(2)}, u32[]{:S(2)}) collective-permute-start(bf16[304,384]{1,0:T(8,128)(2,1)} %get-tuple-element.91), channel_id=1, source_target_pairs={{0,2},{2,0},{4,6},{6,4},{1,3},{3,1},{5,7},{7,5},{8,10},{10,8},{12,... | collective-permute-start | bytes 700424 | tf_op jit(solution)/shard_map/ppermute | solution.py:610
  16.8 1.7 %collective-permute-done.7.refs_2_ = bf16[1,112,768]{2,1,0:T(8,128)(2,1)S(1)} collective-permute-done((bf16[1,112,768]{2,1,0:T(8,128)(2,1)}, bf16[1,112,768]{2,1,0:T(8,128)(2,1)S(1)}, u32[]{:S(2)}, u32[]{:S(2)}) %collective-permute-start.7) | collective-permute-done | bytes 172064 | tf_op jit(solution)/shard_map/ppermute | solution.py:650
  19.2 2.7 %collective-permute-done.4.refs_4_ = bf16[2,96,384]{2,1,0:T(8,128)(2,1)S(1)} collective-permute-done((bf16[2,96,384]{2,1,0:T(8,128)(2,1)S(1)}, bf16[2,96,384]{2,1,0:T(8,128)(2,1)S(1)}, u32[]{:S(2)}, u32[]{:S(2)}) %collective-permute-start.4) | collective-permute-done | bytes 147488 | tf_op jit(solution)/shard_map/ppermute | solution.py:652
  22.0 2.0 %collective-permute-done.1.refs_1_.refs_2_ = bf16[304,384]{1,0:T(8,128)(2,1)S(1)} collective-permute-done((bf16[304,384]{1,0:T(8,128)(2,1)}, bf16[304,384]{1,0:T(8,128)(2,1)S(1)}, u32[]{:S(2)}, u32[]{:S(2)}) %collective-permute-start.1) | collective-permute-done | bytes 233504 | tf_op jit(solution)/shard_map/ppermute | solution.py:610
  28.9 4.3 %collective-permute-done.6.refs_1_.refs_3_ = bf16[384,384]{1,0:T(8,128)(2,1)S(1)} collective-permute-done((bf16[384,384]{1,0:T(8,128)(2,1)S(1)}, bf16[384,384]{1,0:T(8,128)(2,1)S(1)}, u32[]{:S(2)}, u32[]{:S(2)}) %collective-permute-start.6) | collective-permute-done | bytes 294944 | tf_op jit(solution)/shard_map/ppermute | solution.py:610
  33.2 1.7 %collective-permute-done.5.refs_0_.refs_2_ = bf16[384,384]{1,0:T(8,128)(2,1)S(1)} collective-permute-done((bf16[384,384]{1,0:T(8,128)(2,1)S(1)}, bf16[384,384]{1,0:T(8,128)(2,1)S(1)}, u32[]{:S(2)}, u32[]{:S(2)}) %collective-permute-start.5) | collective-permute-done | bytes 294944 | tf_op jit(solution)/shard_map/ppermute | solution.py:610
  37.1 6.2 %attention.1 = (f32[592,384]{1,0:T(8,128)S(1)}, f32[592,384]{1,0:T(8,128)S(1)}, bf16[592,384]{1,0:T(8,128)(2,1)S(1)}, bf16[592,384]{1,0:T(8,128)(2,1)S(1)}, bf16...) custom-call(bf16[304,384]{1,0:T(8,128)(2,1)S(1)} %copy-done.1, ...), custom_call_target="tpu_custom_call" | custom-call | bytes 1 | tf_op jit(solution)/shard_map/attention/pallas_call | solution.py:35
  43.7 3.5 %mlp_own.1 = (bf16[592,768]{1,0:T(8,128)(2,1)S(1)}, bf16[592,768]{1,0:T(8,128)(2,1)S(1)}, f32[8,768]{1,0:T(8,128)S(1)}, bf16[4,4,96,384]{3,2,1,0:T(8,128)(2,1)S(1)}) custom-call(bf16[592,384]{1,0:T(8,128)(2,1)S(1)} %get-tuple-element.103.refs_0_.refs_1_, bf16[592,384]{1,0:T(8,128)(2,1)S(1)} %get-tuple-element.102.refs_1_.refs_2_.refs_4_, ...), custom_call_target="tpu_custom_call" | custom-call | flops 4600000000 | bytes 1 | tf_op jit(solution)/shard_map/mlp_own/pallas_call | solution.py:35
  47.2 3.7 %mlp_oth.1 = (bf16[592,768]{1,0:T(8,128)(2,1)S(1)}, bf16[592,768]{1,0:T(8,128)(2,1)S(1)}, f32[8,768]{1,0:T(8,128)S(1)}, bf16[4,4,96,384]{3,2,1,0:T(8,128)(2,1)S(1)}) custom-call(f32[8,768]{1,0:T(8,128)S(1)} %get-tuple-element.106.refs_0_.refs_11_, bf16[592,384]{1,0:T(8,128)(2,1)S(1)} %get-tuple-element.103.refs_0_.refs_1_, ...), custom_call_target="tpu_custom_call" | custom-call | flops 4600000000 | bytes 1 | tf_op jit(solution)/shard_map/mlp_oth/pallas_call | solution.py:35
  51.3 3.1 %mlp_sums.1 = (bf16[592,384]{1,0:T(8,128)(2,1)S(1)}, f32[592,384]{1,0:T(8,128)S(1)}, bf16[592,384]{1,0:T(8,128)(2,1)S(1)}, f32[384,384]{1,0:T(8,128)S(1)}, f32[16,384]{1,0:T(8,128)S(1)}) custom-call(f32[592,384]{1,0:T(8,128)S(1)} %get-tuple-element.98.refs_0_, bf16[592,384]{1,0:T(8,128)(2,1)S(1)} %get-tuple-element.99.refs_1_, ...), custom_call_target="tpu_custom_call" | custom-call | flops 2300000000 | bytes 1 | tf_op jit(solution)/shard_map/mlp_sums/pallas_call | solution.py:35
  58.2 10.7 %attention_back.1 = (bf16[592,384]{1,0:T(8,128)(2,1)S(1)}, bf16[4,4,96,256]{3,2,1,0:T(8,128)(2,1)S(1)}, bf16[4,4,96,256]{3,2,1,0:T(8,128)(2,1)S(1)}) custom-call(bf16[4,96,384]{2,1,0:T(8,128)(2,1)S(1)} %get-tuple-element.113.refs_0_.refs_1_, bf16[640,1152]{1,0:T(8,128)(2,1)S(1)} %get-tuple-element.114.refs_1_, ...), custom_call_target="tpu_custom_call" | custom-call | flops 12650000384 | bytes 1 | tf_op jit(solution)/shard_map/attention_back/pallas_call | solution.py:35
  69.0 2.1 %collective-permute-done.16.refs_3_ = bf16[4,96,384]{2,1,0:T(8,128)(2,1)S(1)} collective-permute-done((bf16[4,96,384]{2,1,0:T(8,128)(2,1)S(1)}, bf16[4,96,384]{2,1,0:T(8,128)(2,1)S(1)}, u32[]{:S(2)}, u32[]{:S(2)}) %collective-permute-start.16) | collective-permute-done | bytes 294944 | tf_op jit(solution)/shard_map/ppermute | solution.py:610
  75.0 1.6 %collective-permute-start.22 = (bf16[2,96,384]{2,1,0:T(8,128)(2,1)S(1)}, bf16[2,96,384]{2,1,0:T(8,128)(2,1)S(1)}, u32[]{:S(2)}, u32[]{:S(2)}) collective-permute-start(bf16[2,96,384]{2,1,0:T(8,128)(2,1)S(1)} %get-tuple-element.136), channel_id=1, source_target_pairs={{0,8},{8,0},{16,24},{24,16},{1,9},{9,1},{17,25},{25,17},{2,10},{10... | collective-permute-start | bytes 442376 | tf_op jit(solution)/shard_map/ppermute | solution.py:770
  76.6 2.7 %collective-permute-done.19.refs_0_.refs_2_ = bf16[4,96,256]{2,1,0:T(8,128)(2,1)S(1)} collective-permute-done((bf16[4,96,256]{2,1,0:T(8,128)(2,1)S(1)}, bf16[4,96,256]{2,1,0:T(8,128)(2,1)S(1)}, u32[]{:S(2)}, u32[]{:S(2)}) %collective-permute-start.19) | collective-permute-done | bytes 196640 | tf_op jit(solution)/shard_map/ppermute | solution.py:610
  80.3 3.5 %all-to-all-start = ((bf16[4,320,384]{2,1,0:T(8,128)(2,1)}), bf16[4,320,384]{2,1,0:T(8,128)(2,1)S(1)}, u32[]{:S(2)}, u32[]{:S(2)}) async-start(bf16[4,320,384]{2,1,0:T(8,128)(2,1)} %returns.1.refs_0_), calls=%async_computation | async-start | bytes 1966080 | tf_op jit(solution)/shard_map/all_to_all | solution.py:757
  84.1 2.6 %collective-permute-start.23 = (bf16[1,96,384]{2,1,0:T(8,128)(2,1)S(1)}, bf16[1,96,384]{2,1,0:T(8,128)(2,1)S(1)}, u32[]{:S(2)}, u32[]{:S(2)}) collective-permute-start(bf16[1,96,384]{2,1,0:T(8,128)(2,1)S(1)} %get-tuple-element.138), channel_id=1, source_target_pairs={{0,16},{8,24},{16,0},{24,8},{1,17},{9,25},{17,1},{25,9},{2,18},{10... | collective-permute-start | bytes 221192 | tf_op jit(solution)/shard_map/ppermute | solution.py:774
  88.7 2.4 %collective-permute-start.26 = (bf16[96,256]{1,0:T(8,128)(2,1)S(1)}, bf16[96,256]{1,0:T(8,128)(2,1)S(1)}, u32[]{:S(2)}, u32[]{:S(2)}) collective-permute-start(bf16[96,256]{1,0:T(8,128)(2,1)S(1)} %get-tuple-element.141), channel_id=1, source_target_pairs={{0,24},{8,16},{16,8},{24,0},{1,25},{9,17},{17,9},{25,1},{2,26},{10... | collective-permute-start | bytes 147464 | tf_op jit(solution)/shard_map/ppermute | solution.py:610
  91.1 2.6 %collective-permute-done.25.refs_4_ = bf16[96,256]{1,0:T(8,128)(2,1)S(1)} collective-permute-done((bf16[96,256]{1,0:T(8,128)(2,1)S(1)}, bf16[96,256]{1,0:T(8,128)(2,1)S(1)}, u32[]{:S(2)}, u32[]{:S(2)}) %collective-permute-start.25) | collective-permute-done | bytes 49184 | tf_op jit(solution)/shard_map/ppermute | solution.py:610
  95.9 2.0 %collective-permute-start.30 = (bf16[96,640]{1,0:T(8,128)(2,1)S(1)}, bf16[96,640]{1,0:T(8,128)(2,1)S(1)}, u32[]{:S(2)}, u32[]{:S(2)}) collective-permute-start(bf16[96,640]{1,0:T(8,128)(2,1)S(1)} %sum_dp.1.refs_0_.refs_1_), channel_id=1, source_target_pairs={{0,6},{2,4},{4,2},{6,0},{1,7},{3,5},{5,3},{7,1},{8,14},{10,12},{12... | collective-permute-start | bytes 368648 | tf_op jit(solution)/shard_map/ppermute | solution.py:610
  99.4 2.7 %place_slots.1 = (f32[1160,384]{1,0:T(8,128)}, f32[1160,384]{1,0:T(8,128)}, f32[8,128]{1,0:T(8,128)S(1)}) custom-call(bf16[4,320,384]{2,1,0:T(8,128)(2,1)S(1)} %hand_on.1.refs_0_, bf16[4,320,384]{2,1,0:T(8,128)(2,1)S(1)} %collective-permute-done.27.refs_1_, f32[2,8,384]{2,1,0:T(8,128)S(1)} %copy-done.5, s32[8,145]{1,0:T(8,128)S(1)} %copy-done.4), custom_call_target="tpu_custom_call" | custom-call | flops 2644999936 | bytes 1 | tf_op jit(solution)/shard_map/place_slots/pallas_call | solution.py:35
  102.9 2.2 %collective-permute-done.29.refs_3_ = bf16[96,640]{1,0:T(8,128)(2,1)S(1)} collective-permute-done((bf16[96,640]{1,0:T(8,128)(2,1)S(1)}, bf16[96,640]{1,0:T(8,128)(2,1)S(1)}, u32[]{:S(2)}, u32[]{:S(2)}) %collective-permute-start.29) | collective-permute-done | bytes 122912 | tf_op jit(solution)/shard_map/ppermute | solution.py:610
  (74 shorter events, 30.0 us)
Async XLA Ops:
  2.8 12.1 %collective-permute-start.3 = (bf16[1,96,384]{2,1,0:T(8,128)(2,1)}, bf16[1,96,384]{2,1,0:T(8,128)(2,1)S(1)}, u32[]{:S(2)}, u32[]{:S(2)}) collective-permute-start(bf16[1,96,384]{2,1,0:T(8,128)(2,1)} %bitcast.18), channel_id=1, source_target_pairs={{0,16},{8,24},{16,0},{24,8},{1,17},{9,25},{17,1},{25,9},{2,18},{10... | collective-permute-start | bytes 221192 | tf_op jit(solution)/shard_map/ppermute | solution.py:650
  6.9 11.6 %collective-permute-start.7 = (bf16[1,112,768]{2,1,0:T(8,128)(2,1)}, bf16[1,112,768]{2,1,0:T(8,128)(2,1)S(1)}, u32[]{:S(2)}, u32[]{:S(2)}) collective-permute-start(bf16[1,112,768]{2,1,0:T(8,128)(2,1)} %bitcast.16), channel_id=1, source_target_pairs={{0,16},{8,24},{16,0},{24,8},{1,17},{9,25},{17,1},{25,9},{2,18},{10... | collective-permute-start | bytes 516104 | tf_op jit(solution)/shard_map/ppermute | solution.py:650
  10.3 11.6 %collective-permute-start = (bf16[304,384]{1,0:T(8,128)(2,1)}, bf16[304,384]{1,0:T(8,128)(2,1)S(1)}, u32[]{:S(2)}, u32[]{:S(2)}) collective-permute-start(bf16[304,384]{1,0:T(8,128)(2,1)} %get-tuple-element.91), channel_id=1, source_target_pairs={{0,2},{2,0},{4,6},{6,4},{1,3},{3,1},{5,7},{7,5},{8,10},{10,8},{12,... | collective-permute-start | bytes 700424 | tf_op jit(solution)/shard_map/ppermute | solution.py:610
  12.1 11.8 %collective-permute-start.1 = (bf16[304,384]{1,0:T(8,128)(2,1)}, bf16[304,384]{1,0:T(8,128)(2,1)S(1)}, u32[]{:S(2)}, u32[]{:S(2)}) collective-permute-start(bf16[304,384]{1,0:T(8,128)(2,1)} %get-tuple-element.92), channel_id=1, source_target_pairs={{0,4},{2,6},{4,0},{6,2},{1,5},{3,7},{5,1},{7,3},{8,12},{10,14},{12... | collective-permute-start | bytes 700424 | tf_op jit(solution)/shard_map/ppermute | solution.py:610
  13.7 10.3 %collective-permute-start.2 = (bf16[304,384]{1,0:T(8,128)(2,1)}, bf16[304,384]{1,0:T(8,128)(2,1)S(1)}, u32[]{:S(2)}, u32[]{:S(2)}) collective-permute-start(bf16[304,384]{1,0:T(8,128)(2,1)} %get-tuple-element.93), channel_id=1, source_target_pairs={{0,6},{2,4},{4,2},{6,0},{1,7},{3,5},{5,3},{7,1},{8,14},{10,12},{12... | collective-permute-start | bytes 700424 | tf_op jit(solution)/shard_map/ppermute | solution.py:610
  15.8 6.1 %collective-permute-start.4 = (bf16[2,96,384]{2,1,0:T(8,128)(2,1)S(1)}, bf16[2,96,384]{2,1,0:T(8,128)(2,1)S(1)}, u32[]{:S(2)}, u32[]{:S(2)}) collective-permute-start(bf16[2,96,384]{2,1,0:T(8,128)(2,1)S(1)} %join_quarter.1.refs_3_), channel_id=1, source_target_pairs={{0,8},{8,0},{16,24},{24,16},{1,9},{9,1},{17,25},{25,17},{2,10},{10... | collective-permute-start | bytes 442376 | tf_op jit(solution)/shard_map/ppermute | solution.py:652
  18.5 10.4 %collective-permute-start.8 = (bf16[2,112,768]{2,1,0:T(8,128)(2,1)S(1)}, bf16[2,112,768]{2,1,0:T(8,128)(2,1)S(1)}, u32[]{:S(2)}, u32[]{:S(2)}) collective-permute-start(bf16[2,112,768]{2,1,0:T(8,128)(2,1)S(1)} %join_attn.1.refs_2_), channel_id=1, source_target_pairs={{0,8},{8,0},{16,24},{24,16},{1,9},{9,1},{17,25},{25,17},{2,10},{10... | collective-permute-start | bytes 1032200 | tf_op jit(solution)/shard_map/ppermute | solution.py:652
  24.1 9.1 %collective-permute-start.6 = (bf16[384,384]{1,0:T(8,128)(2,1)S(1)}, bf16[384,384]{1,0:T(8,128)(2,1)S(1)}, u32[]{:S(2)}, u32[]{:S(2)}) collective-permute-start(bf16[384,384]{1,0:T(8,128)(2,1)S(1)} %merge_quarter.1.refs_1_), channel_id=1, source_target_pairs={{0,4},{2,6},{4,0},{6,2},{1,5},{3,7},{5,1},{7,3},{8,12},{10,14},{12... | collective-permute-start | bytes 884744 | tf_op jit(solution)/shard_map/ppermute | solution.py:610
  25.6 9.2 %collective-permute-start.5 = (bf16[384,384]{1,0:T(8,128)(2,1)S(1)}, bf16[384,384]{1,0:T(8,128)(2,1)S(1)}, u32[]{:S(2)}, u32[]{:S(2)}) collective-permute-start(bf16[384,384]{1,0:T(8,128)(2,1)S(1)} %merge_quarter.1.refs_1_), channel_id=1, source_target_pairs={{0,2},{2,0},{4,6},{6,4},{1,3},{3,1},{5,7},{7,5},{8,10},{10,8},{12,... | collective-permute-start | bytes 884744 | tf_op jit(solution)/shard_map/ppermute | solution.py:610
  26.2 17.1 %collective-permute-start.12 = (bf16[384,384]{1,0:T(8,128)(2,1)S(1)}, bf16[384,384]{1,0:T(8,128)(2,1)S(1)}, u32[]{:S(2)}, u32[]{:S(2)}) collective-permute-start(bf16[384,384]{1,0:T(8,128)(2,1)S(1)} %merge_quarter.1.refs_1_), channel_id=1, source_target_pairs={{0,6},{2,4},{4,2},{6,0},{1,7},{3,5},{5,3},{7,1},{8,14},{10,12},{12... | collective-permute-start | bytes 884744 | tf_op jit(solution)/shard_map/ppermute | solution.py:610
  54.6 14.4 %collective-permute-start.15 = (bf16[4,96,384]{2,1,0:T(8,128)(2,1)S(1)}, bf16[4,96,384]{2,1,0:T(8,128)(2,1)S(1)}, u32[]{:S(2)}, u32[]{:S(2)}) collective-permute-start(bf16[4,96,384]{2,1,0:T(8,128)(2,1)S(1)} %get-tuple-element.124), channel_id=1, source_target_pairs={{0,2},{2,0},{4,6},{6,4},{1,3},{3,1},{5,7},{7,5},{8,10},{10,8},{12,... | collective-permute-start | bytes 884744 | tf_op jit(solution)/shard_map/ppermute | solution.py:610
  55.9 15.2 %collective-permute-start.16 = (bf16[4,96,384]{2,1,0:T(8,128)(2,1)S(1)}, bf16[4,96,384]{2,1,0:T(8,128)(2,1)S(1)}, u32[]{:S(2)}, u32[]{:S(2)}) collective-permute-start(bf16[4,96,384]{2,1,0:T(8,128)(2,1)S(1)} %get-tuple-element.125), channel_id=1, source_target_pairs={{0,4},{2,6},{4,0},{6,2},{1,5},{3,7},{5,1},{7,3},{8,12},{10,14},{12... | collective-permute-start | bytes 884744 | tf_op jit(solution)/shard_map/ppermute | solution.py:610
  57.2 13.9 %collective-permute-start.17 = (bf16[4,96,384]{2,1,0:T(8,128)(2,1)S(1)}, bf16[4,96,384]{2,1,0:T(8,128)(2,1)S(1)}, u32[]{:S(2)}, u32[]{:S(2)}) collective-permute-start(bf16[4,96,384]{2,1,0:T(8,128)(2,1)S(1)} %get-tuple-element.126), channel_id=1, source_target_pairs={{0,6},{2,4},{4,2},{6,0},{1,7},{3,5},{5,3},{7,1},{8,14},{10,12},{12... | collective-permute-start | bytes 884744 | tf_op jit(solution)/shard_map/ppermute | solution.py:610
  71.5 7.8 %collective-permute-start.19 = (bf16[4,96,256]{2,1,0:T(8,128)(2,1)S(1)}, bf16[4,96,256]{2,1,0:T(8,128)(2,1)S(1)}, u32[]{:S(2)}, u32[]{:S(2)}) collective-permute-start(bf16[4,96,256]{2,1,0:T(8,128)(2,1)S(1)} %get-tuple-element.129), channel_id=1, source_target_pairs={{0,2},{2,0},{4,6},{6,4},{1,3},{3,1},{5,7},{7,5},{8,10},{10,8},{12,... | collective-permute-start | bytes 589832 | tf_op jit(solution)/shard_map/ppermute | solution.py:610
  72.8 11.1 %collective-permute-start.20 = (bf16[4,96,256]{2,1,0:T(8,128)(2,1)S(1)}, bf16[4,96,256]{2,1,0:T(8,128)(2,1)S(1)}, u32[]{:S(2)}, u32[]{:S(2)}) collective-permute-start(bf16[4,96,256]{2,1,0:T(8,128)(2,1)S(1)} %get-tuple-element.133), channel_id=1, source_target_pairs={{0,4},{2,6},{4,0},{6,2},{1,5},{3,7},{5,1},{7,3},{8,12},{10,14},{12... | collective-permute-start | bytes 589832 | tf_op jit(solution)/shard_map/ppermute | solution.py:610
  74.0 9.8 %collective-permute-start.21 = (bf16[4,96,256]{2,1,0:T(8,128)(2,1)S(1)}, bf16[4,96,256]{2,1,0:T(8,128)(2,1)S(1)}, u32[]{:S(2)}, u32[]{:S(2)}) collective-permute-start(bf16[4,96,256]{2,1,0:T(8,128)(2,1)S(1)} %get-tuple-element.134), channel_id=1, source_target_pairs={{0,6},{2,4},{4,2},{6,0},{1,7},{3,5},{5,3},{7,1},{8,14},{10,12},{12... | collective-permute-start | bytes 589832 | tf_op jit(solution)/shard_map/ppermute | solution.py:610
  75.0 9.0 %collective-permute-start.22 = (bf16[2,96,384]{2,1,0:T(8,128)(2,1)S(1)}, bf16[2,96,384]{2,1,0:T(8,128)(2,1)S(1)}, u32[]{:S(2)}, u32[]{:S(2)}) collective-permute-start(bf16[2,96,384]{2,1,0:T(8,128)(2,1)S(1)} %get-tuple-element.136), channel_id=1, source_target_pairs={{0,8},{8,0},{16,24},{24,16},{1,9},{9,1},{17,25},{25,17},{2,10},{10... | collective-permute-start | bytes 442376 | tf_op jit(solution)/shard_map/ppermute | solution.py:770
  80.3 15.3 %all-to-all-start = ((bf16[4,320,384]{2,1,0:T(8,128)(2,1)}), bf16[4,320,384]{2,1,0:T(8,128)(2,1)S(1)}, u32[]{:S(2)}, u32[]{:S(2)}) async-start(bf16[4,320,384]{2,1,0:T(8,128)(2,1)} %returns.1.refs_0_), calls=%async_computation | async-start | bytes 1966080 | tf_op jit(solution)/shard_map/all_to_all | solution.py:757
  84.1 10.6 %collective-permute-start.23 = (bf16[1,96,384]{2,1,0:T(8,128)(2,1)S(1)}, bf16[1,96,384]{2,1,0:T(8,128)(2,1)S(1)}, u32[]{:S(2)}, u32[]{:S(2)}) collective-permute-start(bf16[1,96,384]{2,1,0:T(8,128)(2,1)S(1)} %get-tuple-element.138), channel_id=1, source_target_pairs={{0,16},{8,24},{16,0},{24,8},{1,17},{9,25},{17,1},{25,9},{2,18},{10... | collective-permute-start | bytes 221192 | tf_op jit(solution)/shard_map/ppermute | solution.py:774
  88.3 5.4 %collective-permute-start.25 = (bf16[96,256]{1,0:T(8,128)(2,1)S(1)}, bf16[96,256]{1,0:T(8,128)(2,1)S(1)}, u32[]{:S(2)}, u32[]{:S(2)}) collective-permute-start(bf16[96,256]{1,0:T(8,128)(2,1)S(1)} %get-tuple-element.140), channel_id=1, source_target_pairs={{0,16},{8,24},{16,0},{24,8},{1,17},{9,25},{17,1},{25,9},{2,18},{10... | collective-permute-start | bytes 147464 | tf_op jit(solution)/shard_map/ppermute | solution.py:610
  88.7 6.0 %collective-permute-start.26 = (bf16[96,256]{1,0:T(8,128)(2,1)S(1)}, bf16[96,256]{1,0:T(8,128)(2,1)S(1)}, u32[]{:S(2)}, u32[]{:S(2)}) collective-permute-start(bf16[96,256]{1,0:T(8,128)(2,1)S(1)} %get-tuple-element.141), channel_id=1, source_target_pairs={{0,24},{8,16},{16,8},{24,0},{1,25},{9,17},{17,9},{25,1},{2,26},{10... | collective-permute-start | bytes 147464 | tf_op jit(solution)/shard_map/ppermute | solution.py:610
  95.9 7.1 %collective-permute-start.30 = (bf16[96,640]{1,0:T(8,128)(2,1)S(1)}, bf16[96,640]{1,0:T(8,128)(2,1)S(1)}, u32[]{:S(2)}, u32[]{:S(2)}) collective-permute-start(bf16[96,640]{1,0:T(8,128)(2,1)S(1)} %sum_dp.1.refs_0_.refs_1_), channel_id=1, source_target_pairs={{0,6},{2,4},{4,2},{6,0},{1,7},{3,5},{5,3},{7,1},{8,14},{10,12},{12... | collective-permute-start | bytes 368648 | tf_op jit(solution)/shard_map/ppermute | solution.py:610
  97.9 7.3 %collective-permute-start.29 = (bf16[96,640]{1,0:T(8,128)(2,1)S(1)}, bf16[96,640]{1,0:T(8,128)(2,1)S(1)}, u32[]{:S(2)}, u32[]{:S(2)}) collective-permute-start(bf16[96,640]{1,0:T(8,128)(2,1)S(1)} %sum_dp.1.refs_0_.refs_1_), channel_id=1, source_target_pairs={{0,4},{2,6},{4,0},{6,2},{1,5},{3,7},{5,1},{7,3},{8,12},{10,14},{12... | collective-permute-start | bytes 368648 | tf_op jit(solution)/shard_map/ppermute | solution.py:610
  98.8 6.4 %collective-permute-start.28 = (bf16[96,640]{1,0:T(8,128)(2,1)S(1)}, bf16[96,640]{1,0:T(8,128)(2,1)S(1)}, u32[]{:S(2)}, u32[]{:S(2)}) collective-permute-start(bf16[96,640]{1,0:T(8,128)(2,1)S(1)} %sum_dp.1.refs_0_.refs_1_), channel_id=1, source_target_pairs={{0,2},{2,0},{4,6},{6,4},{1,3},{3,1},{5,7},{7,5},{8,10},{10,8},{12,... | collective-permute-start | bytes 368648 | tf_op jit(solution)/shard_map/ppermute | solution.py:610
  (14 other events, 67.2 us)

commit v4 on v3

--- a/solution.py
+++ b/solution.py
@@ -115,15 +115,8 @@
 
 
 def gelu_pair(v):
-    a = jnp.abs(v)
-    t = 1.0 / (1.0 + (0.3275911 * 0.7071067811865476) * a)
-    g = jnp.exp(-0.5 * v * v)
-    poly = t * (
-        0.254829592 + t * (-0.284496736 + t * (1.421413741 + t * (-1.453152027 + t * 1.061405429)))
-    )
-    tail = 0.5 * poly * g
-    phi = jnp.where(v < 0, tail, 1.0 - tail)
-    return v * phi, phi + v * (0.3989422804014327 * g)
+    phi = 0.5 + 0.5 * lax.erf(v * 0.7071067811865476)
+    return v * phi, phi + (0.3989422804014327 * v) * jnp.exp(-0.5 * v * v)
 
 
 BLOCK = 16
@@ -243,32 +236,24 @@
         out[2 * i + 1 - bit] = got[i]
 
 
-def place_rows(outs, own, got, rows, stage):
+def place_rows(stage, own, got, rows):
     bit = lax.rem(lax.axis_index("dp"), 2)
     for i in range(own.shape[0]):
-        for piece, last in ((own[i], bit), (got[i], 1 - bit)):
+        for piece, last in ((own, bit), (got, 1 - bit)):
             at = pl.ds(pl.multiple_of((2 * i + last) * rows, 16 if rows % 16 == 0 else 8), rows)
-            stage[at, :] = piece.astype(stage.dtype)[:rows]
-    cols = outs[0].shape[1]
+            stage[at, :] = piece[i].astype(stage.dtype)[:rows]
+
+
+def merge_quarter_kernel(sizes, attn, own, got, out, attn_out, stage):
+    place_rows(stage, own, got, sizes[5])
+    out[...] = stage[...].astype(BF)
+    attn_out[...] = attn[...]
+
+
+def split_kernel(got, *outs):
     for i, out in enumerate(outs):
-        out[0 : stage.shape[0], :] = stage[:, i * cols : (i + 1) * cols].astype(BF)
-
-
-def merge_quarter_kernel(sizes, own, got, out, stage):
-    place_rows([out], own, got, sizes[5], stage)
-
-
-def merge_attn_kernel(sizes, own, got, *refs):
-    nctx, ntp, ndp, main, width, rows, padded = sizes
-    outs, stage = refs[:-1], refs[-1]
-    place_rows(outs, own, got, rows, stage)
-    extra = own[0, padded:, :].astype(F32)
-    for more in [own[i] for i in range(1, own.shape[0])] + [got[i] for i in range(own.shape[0])]:
-        more = more[padded:, :].astype(F32)
-        row = lax.broadcasted_iota(jnp.int32, more.shape, 0)
-        extra += jnp.where((row > 0) & (row < 7), more, 0.0)
-    for i, out in enumerate(outs):
-        out[width:, :] = extra[:, 2 * i * TILE : 2 * (i + 1) * TILE].astype(BF)
+        cols = out.shape[2]
+        out[...] = got[:, :, i * cols : (i + 1) * cols]
 
 
 def merge_ff_kernel(nctx, *refs):
@@ -281,22 +266,28 @@
 
 def attention_kernel(sizes, *refs):
     nctx, ntp, ndp, main, width, rows, padded = sizes
-    t_in, own_in, oth_in, refs = refs[:nctx], refs[nctx : nctx + 3], refs[nctx + 3 : nctx + 6], refs[nctx + 6 :]
-    x_out, mid_out, n1_out, n2_out, qkv, ctx, lse, wqkv, wot, vec, ub, cot = refs
+    t_in, (own, got, own_oth, got_oth_a, got_oth_b), refs = refs[:nctx], refs[nctx : nctx + 5], refs[nctx + 5 :]
+    x_out, mid_out, n1_out, n2_out, qkv, ctx, lse, wqkv, wot, vec, ub, cot, stage, stage_oth = refs
     body = nctx * main
     total = body + EXTRA
-    own, oth = (jnp.concatenate([v[...] for v in part], axis=1).astype(F32) for part in (own_in, oth_in))
-    tiles, outs = assemble(own, oth)
+    half = got_oth_a.shape[2]
+    place_rows(stage, own, got, rows)
+    place_rows(stage_oth.at[:, :half], own_oth.at[:, :, :half], got_oth_a, rows)
+    place_rows(stage_oth.at[:, half:], own_oth.at[:, :, half:], got_oth_b, rows)
+    tiles, outs = assemble(stage[...].astype(F32), stage_oth[...].astype(F32))
     for i, v in enumerate(tiles):
-        wqkv[:, i * TILE : (i + 1) * TILE] = v[:width].astype(BF)
+        wqkv[:, i * TILE : (i + 1) * TILE] = v.astype(BF)
     for i, v in enumerate(outs):
-        wot[:, i * TILE : (i + 1) * TILE] = v[:width].astype(BF)
-    bias = jnp.concatenate([v[width : width + 1] for v in tiles], axis=1)
-    vec_sum = own[width:, :width]
+        wot[:, i * TILE : (i + 1) * TILE] = v.astype(BF)
+    extra = own[0, padded:, :].astype(F32)
+    extra_oth = own_oth[0, padded:, :].astype(F32)
+    tiles, _ = assemble(extra, extra_oth)
+    bias = jnp.concatenate([v[0:1] for v in tiles], axis=1)
+    vec_sum = jnp.zeros((EXTRA, width), F32)
+    for i in range(own.shape[0]):
+        vec_sum += own[i, padded:, :width].astype(F32) + got[i, padded:, :width].astype(F32)
     vec[...] = vec_sum
-    ub[...] = jnp.broadcast_to(
-        jnp.concatenate([own[width + 7 : width + 8], oth[width + 7 : width + 8]], axis=1), ub.shape
-    )
+    ub[...] = jnp.broadcast_to(jnp.concatenate([extra[7:8], extra_oth[7:8]], axis=1), ub.shape)
     extra = jnp.zeros((EXTRA, width), F32)
     for k in range(nctx):
         x_out[k * main : (k + 1) * main, :] = t_in[k][0:main, :].astype(F32)
@@ -328,8 +319,7 @@
             m = jnp.max(s, axis=-1, keepdims=True)
             e = jnp.exp(s - m)
             l = jnp.sum(e, axis=-1, keepdims=True)
-            w = (e * (1.0 / l)).astype(BF)
-            parts.append(nn(w, vp))
+            parts.append(nn(e.astype(BF), vp) * (1.0 / l))
             all_lse = jnp.where(lane == 2 * p + a, m + jnp.log(l), all_lse)
         ctx[:, p * TILE : (p + 1) * TILE] = jnp.where(low, parts[0], parts[1]).astype(BF)
     lse[...] = all_lse
@@ -397,39 +387,42 @@
     vgrad[...] = v
 
 
-def pair_back(p, width, total, body, qkv, dctx, lse):
+def pair_back(p, width, total, body, qkv, dctx, lse, ctx):
     keys = qkv.shape[0]
     off = jnp.where(lax.broadcasted_iota(jnp.int32, (1, keys), 1) > body, FLOOR, 0.0)
     low = low_lanes((total, TILE))
-    qp = qkv[0:total, p * TILE : (p + 1) * TILE]
+    at = slice(p * TILE, (p + 1) * TILE)
+    qp = qkv[0:total, at]
     kp = qkv[:, width + p * TILE : width + (p + 1) * TILE]
     vp = qkv[:, 2 * width + p * TILE : 2 * width + (p + 1) * TILE]
-    dp = dctx[:, p * TILE : (p + 1) * TILE]
-    dq, dk, dv = [], 0.0, 0.0
+    dp = dctx[:, at]
+    both = dp.astype(F32) * ctx[:, at].astype(F32)
+    qt = jnp.transpose(qp.astype(F32)).astype(BF)
+    dt = jnp.transpose(dp.astype(F32)).astype(BF)
+    dq, dk, dv = [], [], []
     for a in range(2):
         sel = low if a == 0 else ~low
         qa = jnp.where(sel, qp, jnp.zeros_like(qp))
         da = jnp.where(sel, dp, jnp.zeros_like(dp))
+        inner = jnp.sum(jnp.where(sel, both, 0.0), axis=-1, keepdims=True)
         prob = jnp.exp(nt(qa, kp) + off - lse[:, 2 * p + a : 2 * p + a + 1])
-        wg = nt(da, vp)
-        inner = jnp.sum(prob * wg, axis=-1, keepdims=True)
-        ds = (prob * (wg - inner)).astype(BF)
-        w = prob.astype(BF)
+        ds = (prob * (nt(da, vp) - inner)).astype(BF)
         dq.append(nn(ds, kp))
-        dk = dk + tn(ds, qa)
-        dv = dv + tn(w, da)
+        dk.append(nn(qt[a * HD : (a + 1) * HD], ds))
+        dv.append(nn(dt[a * HD : (a + 1) * HD], prob.astype(BF)))
     dq = jnp.where(low, dq[0], dq[1]) * SCALE
-    return dq.astype(BF), dk[0:total].astype(BF), dv[0:total].astype(BF)
+    dk, dv = (jnp.transpose(jnp.concatenate(v, axis=0))[0:total] for v in (dk, dv))
+    return dq.astype(BF), dk.astype(BF), dv.astype(BF)
 
 
 def attention_back_kernel(sizes, *refs):
     nctx, ntp, ndp, main, width, rows, padded = sizes
-    qkv, dctx, lse, n1, x_in, dmid, wqkv, vec, g_out, vgrad, ub_own, ub_oth = refs[:12]
-    ig, g_own, g_oth, dqkv = refs[12:]
+    qkv, dctx, lse, ctx, n1, x_in, dmid, wqkv, vec, g_out, vgrad, ub_own, ub_oth = refs[:13]
+    ig, g_own, g_oth, dqkv = refs[13:]
     body = nctx * main
     total = body + EXTRA
     for p in range(3):
-        for i, v in enumerate(pair_back(p, width, total, body, qkv, dctx, lse)):
+        for i, v in enumerate(pair_back(p, width, total, body, qkv, dctx, lse, ctx)):
             dqkv[:, i * width + p * TILE : i * width + (p + 1) * TILE] = v
     d = dqkv[...]
     bias = jnp.sum(d.astype(F32), axis=0, keepdims=True)
@@ -671,22 +664,24 @@
         after=[p1],
     )(*sources)
     t_in = over("ctx", nctx, sent)
-    w2q = call(
+    w2q = gather_dp("join_quarter", p2q, [sent[0]])
+    w1, w1_got = gather_dp("join_attn", p1, [sent[0]])
+    w2q, w1_early = call(
         "merge_quarter",
         one(merge_quarter_kernel),
-        sds((width, ff // 2), BF),
+        [sds((width, ff // 2), BF), sds(w1.shape, BF)],
         scratch=[pltpu.VMEM((width, ff // 2), stage)],
         after=t_in[1:],
-    )(*gather_dp("join_quarter", p2q, [sent[0]]))
-    w1 = gather_dp("join_attn", p1, [sent[0]])
+    )(w1, *w2q)
+    w1_oth = other(w1_early)
     w2q = over("ctx", nctx, [w2q] * nctx)
-    w1_own = call(
-        "merge_attn",
-        one(merge_attn_kernel),
-        [sds((width + EXTRA, 2 * TILE), BF)] * (p1_cols // (2 * TILE)),
-        scratch=[pltpu.VMEM((width, p1_cols), stage)],
-        after=w2q[1:-1],
-    )(*w1)
+    late = call(
+        "split_attn",
+        split_kernel,
+        [sds(w1.shape[:2] + (p1_cols // 2,), BF)] * 2,
+        after=[w1_oth, w2q[0]],
+    )(w1_got)
+    w1 = [w1, w1_got, w1_oth, *[other(v) for v in late]]
     x, mid, n1, n2, qkv, ctx, lse, wqkv, wot, vec, ub, cot_in = call(
         "attention",
         one(attention_kernel),
@@ -696,8 +691,9 @@
             sds((width, 3 * width), BF), sds((width, width), BF), sds((EXTRA, width), F32), sds((8, 2 * ff), F32),
             sds((total, width), BF),
         ],
+        scratch=[pltpu.VMEM((width, p1_cols), stage)] * 2,
         mib=32,
-    )(*t_in, *w1_own, *[other(v) for v in w1_own])
+    )(*t_in, *w1)
     w2_own = call(
         "merge_ff", functools.partial(merge_ff_kernel, nctx), sds((width, 2 * ff), BF), after=[vec]
     )(*w2q)
@@ -741,7 +737,7 @@
         scratch=[pltpu.VMEM((total, 3 * width), BF)],
         mib=32,
         after=[s2_send[0]],
-    )(qkv, dctx, lse, n1, x, dmid, wqkv, vec, g_out, vgrad, ub_own, ub_oth)
+    )(qkv, dctx, lse, ctx, n1, x, dmid, wqkv, vec, g_out, vgrad, ub_own, ub_oth)
     half = sds((ndp // 2,) + s2[0].shape[1:], BF)
     keep, send = call(
         "sum_ctx_ff", functools.partial(sum_ctx_halves_kernel, nctx), [half, half], after=[g1_own]

time: 107 us -> 102 us (0.953)
  Pallas kernels: 38.8 us -> 35 us
    pallas_call x22, Pallas kernels: 38.8 us -> 35 us  [run(): pl.pallas_call(ordered, name=name, out_shape=out_shape, in_specs=specs, o...]
  transfers between devices with their start and end apart: 32 -> 32, of which waited for: 17 -> 17; matrix products, arithmetic and copies ran while one was open for 0% -> 0% of each run, Pallas kernels for 29% -> 28%
where the time goes in v4:
time: 102 us
  starting transfers between devices  37.1 us (36%)
  Pallas kernels  35 us (34%)
  waiting for transfers between devices  27.8 us (27%)
  between operations  1.11 us (1%)
    pallas_call x22, Pallas kernels, run(): pl.pallas_call(ordered, name=name, out_shape=out_shape, in_specs=specs, o...  35 us
    ppermute x18, starting transfers between devices, over(): lax.ppermute(items[k], axis, xor(n, k))  22.2 us
    ppermute x18, waiting for transfers between devices, over(): lax.ppermute(items[k], axis, xor(n, k))  20 us
    ppermute x2, starting transfers between devices, gather_dp(): lax.ppermute(v, 'dp', xor(ndp, stride))  4.18 us
    ppermute x2, waiting for transfers between devices, gather_dp(): return (v, lax.ppermute(v, 'dp', xor(ndp, 1)))  3.92 us
    all_to_all x1, starting transfers between devices, body(): returned = lax.all_to_all(back, 'ctx', 0, 0)  3.51 us
    ppermute x2, waiting for transfers between devices, gather_dp(): lax.ppermute(v, 'dp', xor(ndp, stride))  2.67 us
    ppermute x1, starting transfers between devices, body(): lax.ppermute(send, 'dp', xor(ndp, ndp // 2))  2.63 us
  transfers between devices with their start and end apart: 32, of which 17 were waited for; matrix products, arithmetic and copies ran while one was open for 0% of the time, Pallas kernels for 28%

profile of v4, /device:TPU:0, one launch (start us, length us, event | category | flops | bytes accessed | tf_op | source)
XLA Modules:
  0.0 101.9 jit_solution(9547551217145484833)
XLA Ops:
  0.7 2.1 %pack_weights.1 = (bf16[112,768]{1,0:T(8,128)(2,1)}, bf16[96,384]{1,0:T(8,128)(2,1)}) custom-call(bf16[96,192]{1,0:T(8,128)(2,1)} %refs_0_.1, bf16[96,192]{1,0:T(8,128)(2,1)} %refs_1_.1, bf16[96,192]{1,0:T(8,128)(2,1)} %refs_2_.1, bf16[192,96]{1,0:T(8,128)(2,1)} %refs_3_.3, bf16[96,768]{1,0:T(8,128)(2,1)} %refs_4_.1, bf16[96,768]{1,0:T(8,128)(2,1)} %bitcast.22, ...), custom_call_target="tpu_custom_call" | custom-call | flops 2300000000 | bytes 1 | tf_op jit(solution)/shard_map/pack_weights/pallas_call | solution.py:35
  2.8 4.1 %collective-permute-start.5 = (bf16[1,96,384]{2,1,0:T(8,128)(2,1)}, bf16[1,96,384]{2,1,0:T(8,128)(2,1)S(1)}, u32[]{:S(2)}, u32[]{:S(2)}) collective-permute-start(bf16[1,96,384]{2,1,0:T(8,128)(2,1)} %bitcast.18), channel_id=1, source_target_pairs={{0,16},{8,24},{16,0},{24,8},{1,17},{9,25},{17,1},{25,9},{2,18},{10... | collective-permute-start | bytes 221192 | tf_op jit(solution)/shard_map/ppermute | solution.py:643
  6.9 3.4 %pack_slots.1 = (bf16[304,384]{1,0:T(8,128)(2,1)}, bf16[304,384]{1,0:T(8,128)(2,1)}, bf16[304,384]{1,0:T(8,128)(2,1)}, bf16[304,384]{1,0:T(8,128)(2,1)}, f32[2,8,384]{2,1,0:T(8,128)}) custom-call(bf16[112,768]{1,0:T(8,128)(2,1)} %get-tuple-element.90.refs_0_, f32[1160,384]{1,0:T(8,128)} %bitcast.20, f32[1160,384]{1,0:T(8,128)} %bitcast.21, s32[8,145]{1,0:T(8,128)} %refs_3_.5), custom_call_target="tpu_custom_call" | custom-call | flops 3449999872 | bytes 1 | tf_op jit(solution)/shard_map/pack_slots/pallas_call | solution.py:35
  10.3 1.8 %collective-permute-start = (bf16[304,384]{1,0:T(8,128)(2,1)}, bf16[304,384]{1,0:T(8,128)(2,1)S(1)}, u32[]{:S(2)}, u32[]{:S(2)}) collective-permute-start(bf16[304,384]{1,0:T(8,128)(2,1)} %get-tuple-element.92), channel_id=1, source_target_pairs={{0,2},{2,0},{4,6},{6,4},{1,3},{3,1},{5,7},{7,5},{8,10},{10,8},{12,... | collective-permute-start | bytes 700424 | tf_op jit(solution)/shard_map/ppermute | solution.py:603
  16.8 1.7 %collective-permute-done.3.refs_2_ = bf16[1,112,768]{2,1,0:T(8,128)(2,1)S(1)} collective-permute-done((bf16[1,112,768]{2,1,0:T(8,128)(2,1)}, bf16[1,112,768]{2,1,0:T(8,128)(2,1)S(1)}, u32[]{:S(2)}, u32[]{:S(2)}) %collective-permute-start.3) | collective-permute-done | bytes 172064 | tf_op jit(solution)/shard_map/ppermute | solution.py:643
  19.2 2.7 %collective-permute-done.6.refs_5_ = bf16[2,96,384]{2,1,0:T(8,128)(2,1)S(1)} collective-permute-done((bf16[2,96,384]{2,1,0:T(8,128)(2,1)S(1)}, bf16[2,96,384]{2,1,0:T(8,128)(2,1)S(1)}, u32[]{:S(2)}, u32[]{:S(2)}) %collective-permute-start.6) | collective-permute-done | bytes 147488 | tf_op jit(solution)/shard_map/ppermute | solution.py:645
  22.0 2.0 %collective-permute-done.1.refs_1_.refs_2_ = bf16[304,384]{1,0:T(8,128)(2,1)S(1)} collective-permute-done((bf16[304,384]{1,0:T(8,128)(2,1)}, bf16[304,384]{1,0:T(8,128)(2,1)S(1)}, u32[]{:S(2)}, u32[]{:S(2)}) %collective-permute-start.1) | collective-permute-done | bytes 233504 | tf_op jit(solution)/shard_map/ppermute | solution.py:603
  30.7 5.9 %attention.1 = (f32[592,384]{1,0:T(8,128)S(1)}, f32[592,384]{1,0:T(8,128)S(1)}, bf16[592,384]{1,0:T(8,128)(2,1)S(1)}, bf16[592,384]{1,0:T(8,128)(2,1)S(1)}, bf16...) custom-call(bf16[304,384]{1,0:T(8,128)(2,1)S(1)} %copy-done.1, ...), custom_call_target="tpu_custom_call" | custom-call | bytes 1 | tf_op jit(solution)/shard_map/attention/pallas_call | solution.py:35
  36.5 4.3 %collective-permute-done.11.refs_3_ = bf16[384,384]{1,0:T(8,128)(2,1)S(1)} collective-permute-done((bf16[384,384]{1,0:T(8,128)(2,1)S(1)}, bf16[384,384]{1,0:T(8,128)(2,1)S(1)}, u32[]{:S(2)}, u32[]{:S(2)}) %collective-permute-start.11) | collective-permute-done | bytes 294944 | tf_op jit(solution)/shard_map/ppermute | solution.py:603
  41.1 2.8 %mlp_own.1 = (bf16[592,768]{1,0:T(8,128)(2,1)S(1)}, bf16[592,768]{1,0:T(8,128)(2,1)S(1)}, f32[8,768]{1,0:T(8,128)S(1)}, bf16[4,4,96,384]{3,2,1,0:T(8,128)(2,1)S(1)}) custom-call(bf16[592,384]{1,0:T(8,128)(2,1)S(1)} %get-tuple-element.105.refs_0_.refs_1_, bf16[592,384]{1,0:T(8,128)(2,1)S(1)} %get-tuple-element.104.refs_1_.refs_2_.refs_4_, ...), custom_call_target="tpu_custom_call" | custom-call | flops 4600000000 | bytes 1 | tf_op jit(solution)/shard_map/mlp_own/pallas_call | solution.py:35
  43.9 2.9 %mlp_oth.1 = (bf16[592,768]{1,0:T(8,128)(2,1)S(1)}, bf16[592,768]{1,0:T(8,128)(2,1)S(1)}, f32[8,768]{1,0:T(8,128)S(1)}, bf16[4,4,96,384]{3,2,1,0:T(8,128)(2,1)S(1)}) custom-call(f32[8,768]{1,0:T(8,128)S(1)} %get-tuple-element.108.refs_0_.refs_12_, bf16[592,384]{1,0:T(8,128)(2,1)S(1)} %get-tuple-element.105.refs_0_.refs_1_, ...), custom_call_target="tpu_custom_call" | custom-call | flops 4600000000 | bytes 1 | tf_op jit(solution)/shard_map/mlp_oth/pallas_call | solution.py:35
  47.4 3.1 %mlp_sums.1 = (bf16[592,384]{1,0:T(8,128)(2,1)S(1)}, f32[592,384]{1,0:T(8,128)S(1)}, bf16[592,384]{1,0:T(8,128)(2,1)S(1)}, f32[384,384]{1,0:T(8,128)S(1)}, f32[16,384]{1,0:T(8,128)S(1)}) custom-call(f32[592,384]{1,0:T(8,128)S(1)} %get-tuple-element.100.refs_0_, bf16[592,384]{1,0:T(8,128)(2,1)S(1)} %get-tuple-element.101.refs_1_.refs_4_, ...), custom_call_target="tpu_custom_call" | custom-call | flops 2300000000 | bytes 1 | tf_op jit(solution)/shard_map/mlp_sums/pallas_call | solution.py:35
  54.3 8.8 %attention_back.1 = (bf16[592,384]{1,0:T(8,128)(2,1)S(1)}, bf16[4,4,96,256]{3,2,1,0:T(8,128)(2,1)S(1)}, bf16[4,4,96,256]{3,2,1,0:T(8,128)(2,1)S(1)}) custom-call(bf16[4,96,384]{2,1,0:T(8,128)(2,1)S(1)} %get-tuple-element.115.refs_0_.refs_1_, bf16[640,1152]{1,0:T(8,128)(2,1)S(1)} %get-tuple-element.116.refs_1_, ...), custom_call_target="tpu_custom_call" | custom-call | flops 12650000384 | bytes 1 | tf_op jit(solution)/shard_map/attention_back/pallas_call | solution.py:35
  63.2 3.8 %collective-permute-done.17.refs_4_ = bf16[4,96,384]{2,1,0:T(8,128)(2,1)S(1)} collective-permute-done((bf16[4,96,384]{2,1,0:T(8,128)(2,1)S(1)}, bf16[4,96,384]{2,1,0:T(8,128)(2,1)S(1)}, u32[]{:S(2)}, u32[]{:S(2)}) %collective-permute-start.17) | collective-permute-done | bytes 294944 | tf_op jit(solution)/shard_map/ppermute | solution.py:603
  70.9 1.6 %collective-permute-start.22 = (bf16[2,96,384]{2,1,0:T(8,128)(2,1)S(1)}, bf16[2,96,384]{2,1,0:T(8,128)(2,1)S(1)}, u32[]{:S(2)}, u32[]{:S(2)}) collective-permute-start(bf16[2,96,384]{2,1,0:T(8,128)(2,1)S(1)} %get-tuple-element.138), channel_id=1, source_target_pairs={{0,8},{8,0},{16,24},{24,16},{1,9},{9,1},{17,25},{25,17},{2,10},{10... | collective-permute-start | bytes 442376 | tf_op jit(solution)/shard_map/ppermute | solution.py:766
  72.5 2.8 %collective-permute-done.19.refs_0_.refs_2_ = bf16[4,96,256]{2,1,0:T(8,128)(2,1)S(1)} collective-permute-done((bf16[4,96,256]{2,1,0:T(8,128)(2,1)S(1)}, bf16[4,96,256]{2,1,0:T(8,128)(2,1)S(1)}, u32[]{:S(2)}, u32[]{:S(2)}) %collective-permute-start.19) | collective-permute-done | bytes 196640 | tf_op jit(solution)/shard_map/ppermute | solution.py:603
  76.3 3.5 %all-to-all-start = ((bf16[4,320,384]{2,1,0:T(8,128)(2,1)}), bf16[4,320,384]{2,1,0:T(8,128)(2,1)S(1)}, u32[]{:S(2)}, u32[]{:S(2)}) async-start(bf16[4,320,384]{2,1,0:T(8,128)(2,1)} %returns.1.refs_0_), calls=%async_computation | async-start | bytes 1966080 | tf_op jit(solution)/shard_map/all_to_all | solution.py:753
  80.1 2.6 %collective-permute-start.23 = (bf16[1,96,384]{2,1,0:T(8,128)(2,1)S(1)}, bf16[1,96,384]{2,1,0:T(8,128)(2,1)S(1)}, u32[]{:S(2)}, u32[]{:S(2)}) collective-permute-start(bf16[1,96,384]{2,1,0:T(8,128)(2,1)S(1)} %get-tuple-element.140), channel_id=1, source_target_pairs={{0,16},{8,24},{16,0},{24,8},{1,17},{9,25},{17,1},{25,9},{2,18},{10... | collective-permute-start | bytes 221192 | tf_op jit(solution)/shard_map/ppermute | solution.py:770
  82.7 1.6 %collective-permute-start.24 = (bf16[96,256]{1,0:T(8,128)(2,1)S(1)}, bf16[96,256]{1,0:T(8,128)(2,1)S(1)}, u32[]{:S(2)}, u32[]{:S(2)}) collective-permute-start(bf16[96,256]{1,0:T(8,128)(2,1)S(1)} %get-tuple-element.141), channel_id=1, source_target_pairs={{0,8},{8,0},{16,24},{24,16},{1,9},{9,1},{17,25},{25,17},{2,10},{10... | collective-permute-start | bytes 147464 | tf_op jit(solution)/shard_map/ppermute | solution.py:603
  84.7 2.5 %collective-permute-start.26 = (bf16[96,256]{1,0:T(8,128)(2,1)S(1)}, bf16[96,256]{1,0:T(8,128)(2,1)S(1)}, u32[]{:S(2)}, u32[]{:S(2)}) collective-permute-start(bf16[96,256]{1,0:T(8,128)(2,1)S(1)} %get-tuple-element.143), channel_id=1, source_target_pairs={{0,24},{8,16},{16,8},{24,0},{1,25},{9,17},{17,9},{25,1},{2,26},{10... | collective-permute-start | bytes 147464 | tf_op jit(solution)/shard_map/ppermute | solution.py:603
  87.1 2.6 %collective-permute-done.25.refs_4_ = bf16[96,256]{1,0:T(8,128)(2,1)S(1)} collective-permute-done((bf16[96,256]{1,0:T(8,128)(2,1)S(1)}, bf16[96,256]{1,0:T(8,128)(2,1)S(1)}, u32[]{:S(2)}, u32[]{:S(2)}) %collective-permute-start.25) | collective-permute-done | bytes 49184 | tf_op jit(solution)/shard_map/ppermute | solution.py:603
  90.9 2.9 %collective-permute-start.30 = (bf16[96,640]{1,0:T(8,128)(2,1)S(1)}, bf16[96,640]{1,0:T(8,128)(2,1)S(1)}, u32[]{:S(2)}, u32[]{:S(2)}) collective-permute-start(bf16[96,640]{1,0:T(8,128)(2,1)S(1)} %sum_dp.1.refs_0_.refs_1_), channel_id=1, source_target_pairs={{0,6},{2,4},{4,2},{6,0},{1,7},{3,5},{5,3},{7,1},{8,14},{10,12},{12... | collective-permute-start | bytes 368648 | tf_op jit(solution)/shard_map/ppermute | solution.py:603
  94.5 2.7 %place_slots.1 = (f32[1160,384]{1,0:T(8,128)}, f32[1160,384]{1,0:T(8,128)}, f32[8,128]{1,0:T(8,128)S(1)}) custom-call(bf16[4,320,384]{2,1,0:T(8,128)(2,1)S(1)} %hand_on.1.refs_0_, bf16[4,320,384]{2,1,0:T(8,128)(2,1)S(1)} %collective-permute-done.27.refs_1_, f32[2,8,384]{2,1,0:T(8,128)S(1)} %copy-done.5, s32[8,145]{1,0:T(8,128)S(1)} %copy-done.4), custom_call_target="tpu_custom_call" | custom-call | flops 2644999936 | bytes 1 | tf_op jit(solution)/shard_map/place_slots/pallas_call | solution.py:35
  97.8 2.5 %collective-permute-done.29.refs_3_ = bf16[96,640]{1,0:T(8,128)(2,1)S(1)} collective-permute-done((bf16[96,640]{1,0:T(8,128)(2,1)S(1)}, bf16[96,640]{1,0:T(8,128)(2,1)S(1)}, u32[]{:S(2)}, u32[]{:S(2)}) %collective-permute-start.29) | collective-permute-done | bytes 122912 | tf_op jit(solution)/shard_map/ppermute | solution.py:603
  (74 shorter events, 26.3 us)
Async XLA Ops:
  2.8 12.1 %collective-permute-start.5 = (bf16[1,96,384]{2,1,0:T(8,128)(2,1)}, bf16[1,96,384]{2,1,0:T(8,128)(2,1)S(1)}, u32[]{:S(2)}, u32[]{:S(2)}) collective-permute-start(bf16[1,96,384]{2,1,0:T(8,128)(2,1)} %bitcast.18), channel_id=1, source_target_pairs={{0,16},{8,24},{16,0},{24,8},{1,17},{9,25},{17,1},{25,9},{2,18},{10... | collective-permute-start | bytes 221192 | tf_op jit(solution)/shard_map/ppermute | solution.py:643
  6.9 11.6 %collective-permute-start.3 = (bf16[1,112,768]{2,1,0:T(8,128)(2,1)}, bf16[1,112,768]{2,1,0:T(8,128)(2,1)S(1)}, u32[]{:S(2)}, u32[]{:S(2)}) collective-permute-start(bf16[1,112,768]{2,1,0:T(8,128)(2,1)} %bitcast.16), channel_id=1, source_target_pairs={{0,16},{8,24},{16,0},{24,8},{1,17},{9,25},{17,1},{25,9},{2,18},{10... | collective-permute-start | bytes 516104 | tf_op jit(solution)/shard_map/ppermute | solution.py:643
  10.3 11.6 %collective-permute-start = (bf16[304,384]{1,0:T(8,128)(2,1)}, bf16[304,384]{1,0:T(8,128)(2,1)S(1)}, u32[]{:S(2)}, u32[]{:S(2)}) collective-permute-start(bf16[304,384]{1,0:T(8,128)(2,1)} %get-tuple-element.92), channel_id=1, source_target_pairs={{0,2},{2,0},{4,6},{6,4},{1,3},{3,1},{5,7},{7,5},{8,10},{10,8},{12,... | collective-permute-start | bytes 700424 | tf_op jit(solution)/shard_map/ppermute | solution.py:603
  12.1 11.8 %collective-permute-start.1 = (bf16[304,384]{1,0:T(8,128)(2,1)}, bf16[304,384]{1,0:T(8,128)(2,1)S(1)}, u32[]{:S(2)}, u32[]{:S(2)}) collective-permute-start(bf16[304,384]{1,0:T(8,128)(2,1)} %get-tuple-element.93), channel_id=1, source_target_pairs={{0,4},{2,6},{4,0},{6,2},{1,5},{3,7},{5,1},{7,3},{8,12},{10,14},{12... | collective-permute-start | bytes 700424 | tf_op jit(solution)/shard_map/ppermute | solution.py:603
  13.7 10.3 %collective-permute-start.2 = (bf16[304,384]{1,0:T(8,128)(2,1)}, bf16[304,384]{1,0:T(8,128)(2,1)S(1)}, u32[]{:S(2)}, u32[]{:S(2)}) collective-permute-start(bf16[304,384]{1,0:T(8,128)(2,1)} %get-tuple-element.94), channel_id=1, source_target_pairs={{0,6},{2,4},{4,2},{6,0},{1,7},{3,5},{5,3},{7,1},{8,14},{10,12},{12... | collective-permute-start | bytes 700424 | tf_op jit(solution)/shard_map/ppermute | solution.py:603
  15.8 6.1 %collective-permute-start.6 = (bf16[2,96,384]{2,1,0:T(8,128)(2,1)S(1)}, bf16[2,96,384]{2,1,0:T(8,128)(2,1)S(1)}, u32[]{:S(2)}, u32[]{:S(2)}) collective-permute-start(bf16[2,96,384]{2,1,0:T(8,128)(2,1)S(1)} %join_quarter.1.refs_4_), channel_id=1, source_target_pairs={{0,8},{8,0},{16,24},{24,16},{1,9},{9,1},{17,25},{25,17},{2,10},{10... | collective-permute-start | bytes 442376 | tf_op jit(solution)/shard_map/ppermute | solution.py:645
  18.5 10.4 %collective-permute-start.4 = (bf16[2,112,768]{2,1,0:T(8,128)(2,1)S(1)}, bf16[2,112,768]{2,1,0:T(8,128)(2,1)S(1)}, u32[]{:S(2)}, u32[]{:S(2)}) collective-permute-start(bf16[2,112,768]{2,1,0:T(8,128)(2,1)S(1)} %join_attn.1.refs_3_.refs_4_), channel_id=1, source_target_pairs={{0,8},{8,0},{16,24},{24,16},{1,9},{9,1},{17,25},{25,17},{2,10},{10... | collective-permute-start | bytes 1032200 | tf_op jit(solution)/shard_map/ppermute | solution.py:645
  24.1 12.4 %collective-permute-start.12 = (bf16[384,384]{1,0:T(8,128)(2,1)S(1)}, bf16[384,384]{1,0:T(8,128)(2,1)S(1)}, u32[]{:S(2)}, u32[]{:S(2)}) collective-permute-start(bf16[384,384]{1,0:T(8,128)(2,1)S(1)} %get-tuple-element.97.refs_1_), channel_id=1, source_target_pairs={{0,6},{2,4},{4,2},{6,0},{1,7},{3,5},{5,3},{7,1},{8,14},{10,12},{12... | collective-permute-start | bytes 884744 | tf_op jit(solution)/shard_map/ppermute | solution.py:603
  25.7 15.1 %collective-permute-start.11 = (bf16[384,384]{1,0:T(8,128)(2,1)S(1)}, bf16[384,384]{1,0:T(8,128)(2,1)S(1)}, u32[]{:S(2)}, u32[]{:S(2)}) collective-permute-start(bf16[384,384]{1,0:T(8,128)(2,1)S(1)} %get-tuple-element.97.refs_1_), channel_id=1, source_target_pairs={{0,4},{2,6},{4,0},{6,2},{1,5},{3,7},{5,1},{7,3},{8,12},{10,14},{12... | collective-permute-start | bytes 884744 | tf_op jit(solution)/shard_map/ppermute | solution.py:603
  26.9 14.0 %collective-permute-start.10 = (bf16[384,384]{1,0:T(8,128)(2,1)S(1)}, bf16[384,384]{1,0:T(8,128)(2,1)S(1)}, u32[]{:S(2)}, u32[]{:S(2)}) collective-permute-start(bf16[384,384]{1,0:T(8,128)(2,1)S(1)} %get-tuple-element.97.refs_1_), channel_id=1, source_target_pairs={{0,2},{2,0},{4,6},{6,4},{1,3},{3,1},{5,7},{7,5},{8,10},{10,8},{12,... | collective-permute-start | bytes 884744 | tf_op jit(solution)/shard_map/ppermute | solution.py:603
  50.8 12.4 %collective-permute-start.15 = (bf16[4,96,384]{2,1,0:T(8,128)(2,1)S(1)}, bf16[4,96,384]{2,1,0:T(8,128)(2,1)S(1)}, u32[]{:S(2)}, u32[]{:S(2)}) collective-permute-start(bf16[4,96,384]{2,1,0:T(8,128)(2,1)S(1)} %get-tuple-element.126), channel_id=1, source_target_pairs={{0,2},{2,0},{4,6},{6,4},{1,3},{3,1},{5,7},{7,5},{8,10},{10,8},{12,... | collective-permute-start | bytes 884744 | tf_op jit(solution)/shard_map/ppermute | solution.py:603
  52.0 11.2 %collective-permute-start.16 = (bf16[4,96,384]{2,1,0:T(8,128)(2,1)S(1)}, bf16[4,96,384]{2,1,0:T(8,128)(2,1)S(1)}, u32[]{:S(2)}, u32[]{:S(2)}) collective-permute-start(bf16[4,96,384]{2,1,0:T(8,128)(2,1)S(1)} %get-tuple-element.127), channel_id=1, source_target_pairs={{0,4},{2,6},{4,0},{6,2},{1,5},{3,7},{5,1},{7,3},{8,12},{10,14},{12... | collective-permute-start | bytes 884744 | tf_op jit(solution)/shard_map/ppermute | solution.py:603
  52.8 14.2 %collective-permute-start.17 = (bf16[4,96,384]{2,1,0:T(8,128)(2,1)S(1)}, bf16[4,96,384]{2,1,0:T(8,128)(2,1)S(1)}, u32[]{:S(2)}, u32[]{:S(2)}) collective-permute-start(bf16[4,96,384]{2,1,0:T(8,128)(2,1)S(1)} %get-tuple-element.128), channel_id=1, source_target_pairs={{0,6},{2,4},{4,2},{6,0},{1,7},{3,5},{5,3},{7,1},{8,14},{10,12},{12... | collective-permute-start | bytes 884744 | tf_op jit(solution)/shard_map/ppermute | solution.py:603
  67.4 7.9 %collective-permute-start.19 = (bf16[4,96,256]{2,1,0:T(8,128)(2,1)S(1)}, bf16[4,96,256]{2,1,0:T(8,128)(2,1)S(1)}, u32[]{:S(2)}, u32[]{:S(2)}) collective-permute-start(bf16[4,96,256]{2,1,0:T(8,128)(2,1)S(1)} %get-tuple-element.131), channel_id=1, source_target_pairs={{0,2},{2,0},{4,6},{6,4},{1,3},{3,1},{5,7},{7,5},{8,10},{10,8},{12,... | collective-permute-start | bytes 589832 | tf_op jit(solution)/shard_map/ppermute | solution.py:603
  68.3 11.5 %collective-permute-start.20 = (bf16[4,96,256]{2,1,0:T(8,128)(2,1)S(1)}, bf16[4,96,256]{2,1,0:T(8,128)(2,1)S(1)}, u32[]{:S(2)}, u32[]{:S(2)}) collective-permute-start(bf16[4,96,256]{2,1,0:T(8,128)(2,1)S(1)} %get-tuple-element.135), channel_id=1, source_target_pairs={{0,4},{2,6},{4,0},{6,2},{1,5},{3,7},{5,1},{7,3},{8,12},{10,14},{12... | collective-permute-start | bytes 589832 | tf_op jit(solution)/shard_map/ppermute | solution.py:603
  69.8 10.1 %collective-permute-start.21 = (bf16[4,96,256]{2,1,0:T(8,128)(2,1)S(1)}, bf16[4,96,256]{2,1,0:T(8,128)(2,1)S(1)}, u32[]{:S(2)}, u32[]{:S(2)}) collective-permute-start(bf16[4,96,256]{2,1,0:T(8,128)(2,1)S(1)} %get-tuple-element.136), channel_id=1, source_target_pairs={{0,6},{2,4},{4,2},{6,0},{1,7},{3,5},{5,3},{7,1},{8,14},{10,12},{12... | collective-permute-start | bytes 589832 | tf_op jit(solution)/shard_map/ppermute | solution.py:603
  70.9 9.1 %collective-permute-start.22 = (bf16[2,96,384]{2,1,0:T(8,128)(2,1)S(1)}, bf16[2,96,384]{2,1,0:T(8,128)(2,1)S(1)}, u32[]{:S(2)}, u32[]{:S(2)}) collective-permute-start(bf16[2,96,384]{2,1,0:T(8,128)(2,1)S(1)} %get-tuple-element.138), channel_id=1, source_target_pairs={{0,8},{8,0},{16,24},{24,16},{1,9},{9,1},{17,25},{25,17},{2,10},{10... | collective-permute-start | bytes 442376 | tf_op jit(solution)/shard_map/ppermute | solution.py:766
  76.3 14.4 %all-to-all-start = ((bf16[4,320,384]{2,1,0:T(8,128)(2,1)}), bf16[4,320,384]{2,1,0:T(8,128)(2,1)S(1)}, u32[]{:S(2)}, u32[]{:S(2)}) async-start(bf16[4,320,384]{2,1,0:T(8,128)(2,1)} %returns.1.refs_0_), calls=%async_computation | async-start | bytes 1966080 | tf_op jit(solution)/shard_map/all_to_all | solution.py:753
  80.1 10.6 %collective-permute-start.23 = (bf16[1,96,384]{2,1,0:T(8,128)(2,1)S(1)}, bf16[1,96,384]{2,1,0:T(8,128)(2,1)S(1)}, u32[]{:S(2)}, u32[]{:S(2)}) collective-permute-start(bf16[1,96,384]{2,1,0:T(8,128)(2,1)S(1)} %get-tuple-element.140), channel_id=1, source_target_pairs={{0,16},{8,24},{16,0},{24,8},{1,17},{9,25},{17,1},{25,9},{2,18},{10... | collective-permute-start | bytes 221192 | tf_op jit(solution)/shard_map/ppermute | solution.py:770
  84.3 5.4 %collective-permute-start.25 = (bf16[96,256]{1,0:T(8,128)(2,1)S(1)}, bf16[96,256]{1,0:T(8,128)(2,1)S(1)}, u32[]{:S(2)}, u32[]{:S(2)}) collective-permute-start(bf16[96,256]{1,0:T(8,128)(2,1)S(1)} %get-tuple-element.142), channel_id=1, source_target_pairs={{0,16},{8,24},{16,0},{24,8},{1,17},{9,25},{17,1},{25,9},{2,18},{10... | collective-permute-start | bytes 147464 | tf_op jit(solution)/shard_map/ppermute | solution.py:603
  84.7 6.0 %collective-permute-start.26 = (bf16[96,256]{1,0:T(8,128)(2,1)S(1)}, bf16[96,256]{1,0:T(8,128)(2,1)S(1)}, u32[]{:S(2)}, u32[]{:S(2)}) collective-permute-start(bf16[96,256]{1,0:T(8,128)(2,1)S(1)} %get-tuple-element.143), channel_id=1, source_target_pairs={{0,24},{8,16},{16,8},{24,0},{1,25},{9,17},{17,9},{25,1},{2,26},{10... | collective-permute-start | bytes 147464 | tf_op jit(solution)/shard_map/ppermute | solution.py:603
  90.9 6.9 %collective-permute-start.30 = (bf16[96,640]{1,0:T(8,128)(2,1)S(1)}, bf16[96,640]{1,0:T(8,128)(2,1)S(1)}, u32[]{:S(2)}, u32[]{:S(2)}) collective-permute-start(bf16[96,640]{1,0:T(8,128)(2,1)S(1)} %sum_dp.1.refs_0_.refs_1_), channel_id=1, source_target_pairs={{0,6},{2,4},{4,2},{6,0},{1,7},{3,5},{5,3},{7,1},{8,14},{10,12},{12... | collective-permute-start | bytes 368648 | tf_op jit(solution)/shard_map/ppermute | solution.py:603
  93.8 6.5 %collective-permute-start.29 = (bf16[96,640]{1,0:T(8,128)(2,1)S(1)}, bf16[96,640]{1,0:T(8,128)(2,1)S(1)}, u32[]{:S(2)}, u32[]{:S(2)}) collective-permute-start(bf16[96,640]{1,0:T(8,128)(2,1)S(1)} %sum_dp.1.refs_0_.refs_1_), channel_id=1, source_target_pairs={{0,4},{2,6},{4,0},{6,2},{1,5},{3,7},{5,1},{7,3},{8,12},{10,14},{12... | collective-permute-start | bytes 368648 | tf_op jit(solution)/shard_map/ppermute | solution.py:603
  94.4 6.3 %collective-permute-start.28 = (bf16[96,640]{1,0:T(8,128)(2,1)S(1)}, bf16[96,640]{1,0:T(8,128)(2,1)S(1)}, u32[]{:S(2)}, u32[]{:S(2)}) collective-permute-start(bf16[96,640]{1,0:T(8,128)(2,1)S(1)} %sum_dp.1.refs_0_.refs_1_), channel_id=1, source_target_pairs={{0,2},{2,0},{4,6},{6,4},{1,3},{3,1},{5,7},{7,5},{8,10},{10,8},{12,... | collective-permute-start | bytes 368648 | tf_op jit(solution)/shard_map/ppermute | solution.py:603
  (14 other events, 69.5 us)

commit v5 on v4

--- a/solution.py
+++ b/solution.py
@@ -153,7 +153,7 @@
 
 def pack_weights_kernel(sizes, count, *refs):
     nctx, ntp, ndp, main, width, rows, padded = sizes
-    sources, (p1, p2q), refs = refs[:count], refs[count : count + 2], refs[count + 2 :]
+    sources, (p1, p2q, done), refs = refs[:count], refs[count : count + 3], refs[count + 3 :]
     held, sem = refs[:count], refs[count]
     copies = fetch(sources, held, sem)
     wq, wk, wv, wo, wu, wd, qb, vb, ub = held[:9]
@@ -202,6 +202,7 @@
         block[:, :width],
     )
     p1[padded : padded + EXTRA, 0:width] = mixed.astype(BF)
+    done[...] = jnp.zeros_like(done)
 
 
 def pack_slots_kernel(sizes, *refs):
@@ -267,7 +268,7 @@
 def attention_kernel(sizes, *refs):
     nctx, ntp, ndp, main, width, rows, padded = sizes
     t_in, (own, got, own_oth, got_oth_a, got_oth_b), refs = refs[:nctx], refs[nctx : nctx + 5], refs[nctx + 5 :]
-    x_out, mid_out, n1_out, n2_out, qkv, ctx, lse, wqkv, wot, vec, ub, cot, stage, stage_oth = refs
+    x_out, mid_out, n1_out, n2_out, qkv, ctx, ctx_full, lse, wqkv, wot, vec, ub, cot, stage, stage_oth = refs
     body = nctx * main
     total = body + EXTRA
     half = got_oth_a.shape[2]
@@ -321,7 +322,8 @@
             l = jnp.sum(e, axis=-1, keepdims=True)
             parts.append(nn(e.astype(BF), vp) * (1.0 / l))
             all_lse = jnp.where(lane == 2 * p + a, m + jnp.log(l), all_lse)
-        ctx[:, p * TILE : (p + 1) * TILE] = jnp.where(low, parts[0], parts[1]).astype(BF)
+        ctx_full[:, p * TILE : (p + 1) * TILE] = jnp.where(low, parts[0], parts[1])
+    ctx[...] = ctx_full[...].astype(BF)
     lse[...] = all_lse
     attended = nt(ctx[...], wot[...]) + vec_sum[5:6, :]
     valid = lax.broadcasted_iota(jnp.int32, (total, 1), 0) <= body
@@ -396,7 +398,7 @@
     kp = qkv[:, width + p * TILE : width + (p + 1) * TILE]
     vp = qkv[:, 2 * width + p * TILE : 2 * width + (p + 1) * TILE]
     dp = dctx[:, at]
-    both = dp.astype(F32) * ctx[:, at].astype(F32)
+    both = dp.astype(F32) * ctx[:, at]
     qt = jnp.transpose(qp.astype(F32)).astype(BF)
     dt = jnp.transpose(dp.astype(F32)).astype(BF)
     dq, dk, dv = [], [], []
@@ -429,12 +431,14 @@
     g = tn(n1[...], d)
     go = g_out[...]
     own, oth = disassemble([tile(g, i) for i in range(9)], [tile(go, i) for i in range(3)])
+    half = padded // 2
     for to, tiles in ((g_own, own), (g_oth, oth)):
-        for j in range(6):
+        for j in range(4):
+            lo = j % 2 * half
             for e in range(ndp):
-                to[j // 2, e, 0:rows, (j % 2) * TILE : (j % 2 + 1) * TILE] = (
-                    tiles[j][e * rows : (e + 1) * rows].astype(BF)
-                )
+                to[j, e, 0:rows, :] = tiles[j][e * rows : (e + 1) * rows].astype(BF)
+                shared = tiles[4 + j // 2][e * rows + lo : e * rows + min(rows, lo + half)]
+                to[j, e, padded : padded + shared.shape[0], :] = shared.astype(BF)
     dn1 = nt(d, wqkv[...])
     xhat, r = norm_stats(x_in[...])
     grad = dmid[...] + norm_back(dn1 * vec[1:2, :], xhat, r)
@@ -447,16 +451,12 @@
     for to, tiles, ub in ((g_own, bias_own, ub_own), (g_oth, bias_oth, ub_oth)):
         rows_ = [tile(v, i) for v in vecs for i in range(3)] + tiles
         rows_ += [ub[0:1, i * TILE : (i + 1) * TILE] for i in range(6)]
-        for side in range(2):
+        for j in range(4):
             block = jnp.zeros((EXTRA, TILE), F32)
-            for i, v in enumerate(rows_[side * EXTRA : (side + 1) * EXTRA]):
+            for i, v in enumerate(rows_[8 * j : 8 * (j + 1)]):
                 block = jnp.where(row_is(block.shape, i), v, block)
             for e in range(ndp):
-                to[3, e, 0:EXTRA, side * TILE : (side + 1) * TILE] = block.astype(BF)
-                if padded > EXTRA:
-                    to[3, e, EXTRA:padded, side * TILE : (side + 1) * TILE] = jnp.zeros(
-                        (padded - EXTRA, TILE), BF
-                    )
+                to[j, e, padded + half :, :] = block.astype(BF)
 
 
 def sum_core_kernel(n, own, oth, *outs):
@@ -499,23 +499,34 @@
 
 def sum_dp_kernel(n, own, got, *refs):
     out = refs[n]
-    cols = own.shape[2]
-    out[:, :cols] = (own[0].astype(F32) + got[0].astype(F32)).astype(BF)
+    rows = own.shape[1]
+    out[:rows, :] = (own[0].astype(F32) + got[0, 0:rows, :].astype(F32)).astype(BF)
     v = refs[0][...].astype(F32)
     for r in refs[1:n]:
         v = v + r[...].astype(F32)
-    out[:, cols:] = v.astype(BF)
+    span = out.shape[0] - rows
+    out[rows:, :] = jnp.zeros((span, out.shape[1]), BF)
+    for i in range(out.shape[1] // TILE):
+        part = v[i * span : (i + 1) * span].astype(BF)
+        if part.shape[0]:
+            out[rows : rows + part.shape[0], i * TILE : (i + 1) * TILE] = part
 
 
 def returns_kernel(sizes, bo, ig, out):
     nctx, ntp, ndp, main, width, rows, padded = sizes
     me = lax.axis_index("ctx")
-    span = main + EXTRA
+    body = nctx * main
+    shape = (EXTRA, width)
+    extra = jnp.where(
+        row_is(shape, 0),
+        bo[body:, :].astype(F32),
+        jnp.where(row_is(shape, 1), ig[body:, :].astype(F32)[0:1, :], 0.0),
+    ).astype(BF)
     for k in range(nctx):
         at = slice(k * main, (k + 1) * main)
-        for i, src in enumerate((bo, ig)):
-            out[me ^ k, i * span : i * span + main, :] = src[at, :]
-            out[me ^ k, i * span + main : (i + 1) * span, :] = src[nctx * main :, :]
+        out[me ^ k, 0:main, :] = bo[at, :]
+        out[me ^ k, main : main + EXTRA, :] = extra
+        out[me ^ k, main + EXTRA :, :] = ig[at, :]
 
 
 def hand_on_kernel(held, out):
@@ -528,16 +539,23 @@
     gq, gk, gv, gqb, gvb, go, gu, gub, gd = refs[:9]
     gvec, f, f2 = refs[9:15], refs[15], refs[16]
     me, me_d = lax.axis_index("ctx"), lax.axis_index("dp")
+    span = parts[0].shape[0] - padded
+    for k in range(nctx):
+        f2[me ^ k] = parts[k][0:padded, :].astype(F32)
+        for i in range(f2.shape[2] // TILE):
+            n = min(span, f.shape[1] - i * span)
+            if n > 0:
+                f[me ^ k, i * span : i * span + n, :] = parts[k][
+                    padded : padded + n, i * TILE : (i + 1) * TILE
+                ].astype(F32)
     half = f2.shape[2]
-    for k in range(nctx):
-        f2[me ^ k] = parts[k][:, :half].astype(F32)
-        f[me ^ k] = parts[k][:, half:].astype(F32)
     for j in range(2):
         gu[:, j * half : (j + 1) * half] = f2[j, 0:rows, :]
         gd[:, j * half : (j + 1) * half] = f2[2 + j, 0:rows, :]
-    q01, k01 = f[0, 0:rows, 0:TILE], f[0, 0:rows, TILE:]
-    v01, o01 = f[1, 0:rows, 0:TILE], f[1, 0:rows, TILE:]
-    qk2, vo2 = f[2, 0:rows, 0:TILE], f[2, 0:rows, TILE:]
+    q01, k01, v01, o01 = (f[j, 0:rows, :] for j in range(4))
+    low, high = slice(padded, padded + padded // 2), slice(padded, padded + rows - padded // 2)
+    qk2 = jnp.concatenate([f[0, low, :], f[1, high, :]], axis=0)
+    vo2 = jnp.concatenate([f[2, low, :], f[3, high, :]], axis=0)
     gq[:, 0:TILE] = q01
     gq[:, TILE:] = qk2[:, 0:HD]
     gk[:, 0:TILE] = k01
@@ -546,10 +564,10 @@
     gv[:, TILE:] = vo2[:, 0:HD]
     go[0:TILE, :] = jnp.transpose(o01)
     go[TILE:, :] = jnp.transpose(vo2)[HD:, :]
-    ex = [f[3, 0:EXTRA, 0:TILE], f[3, 0:EXTRA, TILE:]]
 
     def line(i):
-        return ex[i // EXTRA][i % EXTRA : i % EXTRA + 1, :]
+        at = padded + padded // 2 + i % 8
+        return f[i // 8, at : at + 1, :]
 
     for i in range(6):
         v = jnp.concatenate([line(3 * i), line(3 * i + 1), line(3 * i + 2)], axis=1)
@@ -569,7 +587,6 @@
     me_t = lax.axis_index("tp")
     where = [j * ntp + t for t in (me_t, 1 - me_t) for j in range(nctx)]
     sources = [v.at[j] for v in (own, oth) for j in range(nctx)]
-    span = main + EXTRA
     get_valid = pltpu.make_async_copy(mask, valid, sem.at[0])
     get_valid.start()
 
@@ -582,13 +599,13 @@
     put = one_hot((images * BLOCK, images * BLOCK), hit)
     for i in range(2):
         for b in range(main // BLOCK):
-            lo = i * span + b * BLOCK
+            lo = i * (main + EXTRA) + b * BLOCK
             got = jnp.concatenate([src[lo : lo + BLOCK, :] for src in sources], axis=0)
             outs[i][b * BLOCK * images : (b + 1) * BLOCK * images, :] = nn(put, got)
     get_valid.wait()
     for i in range(2):
         for src, img in zip(sources, where):
-            got = src[i * span + main : (i + 1) * span, :].astype(F32)[0:1, :]
+            got = src[main : main + EXTRA, :].astype(F32)[i : i + 1, :]
             outs[i][pl.ds(main * images + img, 1), :] = jnp.where(
                 valid[img, main] > 0, got, tails[i, pl.ds(img, 1), :]
             )
@@ -645,12 +662,12 @@
         return v, lax.ppermute(v, "dp", xor(ndp, 1))
 
     sources = [w_query, w_key, w_value, w_out, w_up, jnp.transpose(w_down), query_bias, value_bias, up_bias, *vecs]
-    p1, p2q = call(
+    p1, p2q, packed = call(
         "pack_weights",
         functools.partial(pack_weights_kernel, sizes, len(sources)),
-        [sds((padded + EXTRA, p1_cols), BF), sds((padded, ff // 2), BF)],
+        [sds((padded + EXTRA, p1_cols), BF), sds((padded, ff // 2), BF), sds((8, TILE), F32)],
         scratch=held(sources),
-        mib=60,
+        mib=56,
         raw=range(len(sources)),
     )(*sources)
     sources = [tok, cot, valid_mask]
@@ -659,13 +676,12 @@
         one(pack_slots_kernel),
         [sds((2 * main + EXTRA, width), BF)] * nctx + [sds((2, images, width), F32)],
         scratch=held(sources),
-        mib=60,
+        mib=48,
         raw=range(3),
-        after=[p1],
     )(*sources)
     t_in = over("ctx", nctx, sent)
-    w2q = gather_dp("join_quarter", p2q, [sent[0]])
-    w1, w1_got = gather_dp("join_attn", p1, [sent[0]])
+    w2q = gather_dp("join_quarter", p2q, [])
+    w1, w1_got = gather_dp("join_attn", p1, [])
     w2q, w1_early = call(
         "merge_quarter",
         one(merge_quarter_kernel),
@@ -682,12 +698,12 @@
         after=[w1_oth, w2q[0]],
     )(w1_got)
     w1 = [w1, w1_got, w1_oth, *[other(v) for v in late]]
-    x, mid, n1, n2, qkv, ctx, lse, wqkv, wot, vec, ub, cot_in = call(
+    x, mid, n1, n2, qkv, ctx, ctx_full, lse, wqkv, wot, vec, ub, cot_in = call(
         "attention",
         one(attention_kernel),
         [
             sds((total, width), F32), sds((total, width), F32), sds((total, width), BF), sds((total, width), BF),
-            sds((keys, 3 * width), BF), sds((total, width), BF), sds((total, TILE), F32),
+            sds((keys, 3 * width), BF), sds((total, width), BF), sds((total, width), F32), sds((total, TILE), F32),
             sds((width, 3 * width), BF), sds((width, width), BF), sds((EXTRA, width), F32), sds((8, 2 * ff), F32),
             sds((total, width), BF),
         ],
@@ -733,11 +749,11 @@
     ig, g1_own, g1_oth = call(
         "attention_back",
         one(attention_back_kernel),
-        [sds((total, width), BF)] + [sds((4, ndp, padded, 2 * TILE), BF)] * 2,
+        [sds((total, width), BF)] + [sds((4, ndp, padded + padded // 2 + EXTRA, TILE), BF)] * 2,
         scratch=[pltpu.VMEM((total, 3 * width), BF)],
         mib=32,
         after=[s2_send[0]],
-    )(qkv, dctx, lse, ctx, n1, x, dmid, wqkv, vec, g_out, vgrad, ub_own, ub_oth)
+    )(qkv, dctx, lse, ctx_full, n1, x, dmid, wqkv, vec, g_out, vgrad, ub_own, ub_oth)
     half = sds((ndp // 2,) + s2[0].shape[1:], BF)
     keep, send = call(
         "sum_ctx_ff", functools.partial(sum_ctx_halves_kernel, nctx), [half, half], after=[g1_own]
@@ -747,7 +763,7 @@
     back = call(
         "returns",
         one(returns_kernel),
-        sds((nctx, 2 * (main + EXTRA), width), BF),
+        sds((nctx, 2 * main + EXTRA, width), BF),
         after=[s1[1]],
     )(bo, ig)
     returned = lax.all_to_all(back, "ctx", 0, 0)
@@ -766,7 +782,7 @@
         )(keep, lax.ppermute(send, "dp", xor(ndp, stride // 2)))
         stride *= 2
     summed = call(
-        "sum_dp", functools.partial(sum_dp_kernel, ndp), sds((padded, ff // 2 + 2 * TILE), BF)
+        "sum_dp", functools.partial(sum_dp_kernel, ndp), sds((padded + -(-s1[0].shape[1] // (3 * EXTRA)) * EXTRA, ff // 2), BF)
     )(keep, lax.ppermute(send, "dp", xor(ndp, ndp // 2)), *u1)
     shares = over("ctx", nctx, [summed] * nctx)
     back = call("hand_on", hand_on_kernel, sds(returned.shape, BF), after=[summed])(returned)
@@ -788,7 +804,7 @@
         ]
         + [sds((rows,), F32)] * 6,
         scratch=[
-            pltpu.VMEM((nctx, padded, 2 * TILE), F32),
+            pltpu.VMEM((nctx,) + s1[0].shape[1:], F32),
             pltpu.VMEM((nctx, padded, ff // 2), F32),
         ],
         after=[placed],

time: 102 us -> 99.1 us (0.972)
  Pallas kernels: 35 us -> 33.1 us
  starting transfers between devices: 37.1 us -> 35.8 us
  waiting for transfers between devices: 27.8 us -> 28.9 us
    ppermute x18, waiting for transfers between devices: 20 us -> 16.3 us  [over(): lax.ppermute(items[k], axis, xor(n, k))]
    ppermute x2, waiting for transfers between devices: 2.67 us -> 5.68 us  [gather_dp(): lax.ppermute(v, 'dp', xor(ndp, stride))]
    pallas_call x22, Pallas kernels: 35 us -> 33.1 us  [run(): pl.pallas_call(ordered, name=name, out_shape=out_shape, in_specs=specs, o...]
    ppermute x2, waiting for transfers between devices: 3.92 us -> 5.72 us  [gather_dp(): return (v, lax.ppermute(v, 'dp', xor(ndp, 1)))]
  transfers between devices with their start and end apart: 32 -> 32, of which waited for: 17 -> 17; matrix products, arithmetic and copies ran while one was open for 0% -> 0% of each run, Pallas kernels for 28% -> 27%
where the time goes in v5:
time: 99.1 us; the launch traced here: 98.9 us
  starting transfers between devices  35.8 us (36%)
  Pallas kernels  33.1 us (33%)
  waiting for transfers between devices  28.9 us (29%)
  between operations  1.04 us (1%)
    pallas_call x22, Pallas kernels, run(): pl.pallas_call(ordered, name=name, out_shape=out_shape, in_specs=specs, o...  33.1 us
    ppermute x18, starting transfers between devices, over(): lax.ppermute(items[k], axis, xor(n, k))  22.2 us
    ppermute x18, waiting for transfers between devices, over(): lax.ppermute(items[k], axis, xor(n, k))  16.3 us
    ppermute x2, waiting for transfers between devices, gather_dp(): return (v, lax.ppermute(v, 'dp', xor(ndp, 1)))  5.72 us
    ppermute x2, waiting for transfers between devices, gather_dp(): lax.ppermute(v, 'dp', xor(ndp, stride))  5.68 us
    ppermute x2, starting transfers between devices, gather_dp(): lax.ppermute(v, 'dp', xor(ndp, stride))  4.18 us
    all_to_all x1, starting transfers between devices, body(): returned = lax.all_to_all(back, 'ctx', 0, 0)  3.51 us
    ppermute x1, starting transfers between devices, body(): lax.ppermute(send, 'dp', xor(ndp, ndp // 2))  2.22 us
  transfers between devices with their start and end apart: 32, of which 17 were waited for; matrix products, arithmetic and copies ran while one was open for 0% of the time, Pallas kernels for 27%

profile of v5, /device:TPU:0, one launch (start us, length us, event | category | flops | bytes accessed | tf_op | source)
XLA Modules:
  0.0 98.9 jit_solution(7049444967869905659)
XLA Ops:
  0.7 2.2 %pack_weights.1 = (bf16[112,768]{1,0:T(8,128)(2,1)}, bf16[96,384]{1,0:T(8,128)(2,1)}, f32[8,128]{1,0:T(8,128)}) custom-call(bf16[96,192]{1,0:T(8,128)(2,1)} %refs_0_.1, bf16[96,192]{1,0:T(8,128)(2,1)} %refs_1_.1, bf16[96,192]{1,0:T(8,128)(2,1)} %refs_2_.3, bf16[192,96]{1,0:T(8,128)(2,1)} %refs_3_.2, bf16[96,768]{1,0:T(8,128)(2,1)} %refs_4_.1, ...), custom_call_target="tpu_custom_call" | custom-call | flops 2300000000 | bytes 1 | tf_op jit(solution)/shard_map/pack_weights/pallas_call | solution.py:35
  2.9 4.1 %collective-permute-start.5 = (bf16[1,96,384]{2,1,0:T(8,128)(2,1)}, bf16[1,96,384]{2,1,0:T(8,128)(2,1)S(1)}, u32[]{:S(2)}, u32[]{:S(2)}) collective-permute-start(bf16[1,96,384]{2,1,0:T(8,128)(2,1)} %bitcast.20), channel_id=1, source_target_pairs={{0,16},{8,24},{16,0},{24,8},{1,17},{9,25},{17,1},{25,9},{2,18},{10... | collective-permute-start | bytes 221192 | tf_op jit(solution)/shard_map/ppermute | solution.py:660
  8.6 1.8 %collective-permute-start = (bf16[304,384]{1,0:T(8,128)(2,1)S(1)}, bf16[304,384]{1,0:T(8,128)(2,1)S(1)}, u32[]{:S(2)}, u32[]{:S(2)}) collective-permute-start(bf16[304,384]{1,0:T(8,128)(2,1)S(1)} %get-tuple-element.92), channel_id=1, source_target_pairs={{0,2},{2,0},{4,6},{6,4},{1,3},{3,1},{5,7},{7,5},{8,10},{10,8},{12,... | collective-permute-start | bytes 700424 | tf_op jit(solution)/shard_map/ppermute | solution.py:620
  12.2 2.8 %collective-permute-done.5.refs_1_ = bf16[1,96,384]{2,1,0:T(8,128)(2,1)S(1)} collective-permute-done((bf16[1,96,384]{2,1,0:T(8,128)(2,1)}, bf16[1,96,384]{2,1,0:T(8,128)(2,1)S(1)}, u32[]{:S(2)}, u32[]{:S(2)}) %collective-permute-start.5) | collective-permute-done | bytes 73760 | tf_op jit(solution)/shard_map/ppermute | solution.py:660
  15.8 2.8 %collective-permute-done.3.refs_1_ = bf16[1,112,768]{2,1,0:T(8,128)(2,1)S(1)} collective-permute-done((bf16[1,112,768]{2,1,0:T(8,128)(2,1)}, bf16[1,112,768]{2,1,0:T(8,128)(2,1)S(1)}, u32[]{:S(2)}, u32[]{:S(2)}) %collective-permute-start.3) | collective-permute-done | bytes 172064 | tf_op jit(solution)/shard_map/ppermute | solution.py:660
  19.4 2.4 %collective-permute-done.6.refs_5_ = bf16[2,96,384]{2,1,0:T(8,128)(2,1)S(1)} collective-permute-done((bf16[2,96,384]{2,1,0:T(8,128)(2,1)S(1)}, bf16[2,96,384]{2,1,0:T(8,128)(2,1)S(1)}, u32[]{:S(2)}, u32[]{:S(2)}) %collective-permute-start.6) | collective-permute-done | bytes 147488 | tf_op jit(solution)/shard_map/ppermute | solution.py:662
  22.2 2.9 %collective-permute-start.12 = (bf16[384,384]{1,0:T(8,128)(2,1)S(1)}, bf16[384,384]{1,0:T(8,128)(2,1)S(1)}, u32[]{:S(2)}, u32[]{:S(2)}) collective-permute-start(bf16[384,384]{1,0:T(8,128)(2,1)S(1)} %get-tuple-element.98.refs_1_), channel_id=1, source_target_pairs={{0,6},{2,4},{4,2},{6,0},{1,7},{3,5},{5,3},{7,1},{8,14},{10,12},{12... | collective-permute-start | bytes 884744 | tf_op jit(solution)/shard_map/ppermute | solution.py:620
  25.8 3.3 %collective-permute-done.4.refs_2_.refs_5_ = bf16[2,112,768]{2,1,0:T(8,128)(2,1)S(1)} collective-permute-done((bf16[2,112,768]{2,1,0:T(8,128)(2,1)S(1)}, bf16[2,112,768]{2,1,0:T(8,128)(2,1)S(1)}, u32[]{:S(2)}, u32[]{:S(2)}) %collective-permute-start.4) | collective-permute-done | bytes 344096 | tf_op jit(solution)/shard_map/ppermute | solution.py:662
  30.8 5.9 %attention.1 = (f32[592,384]{1,0:T(8,128)S(1)}, f32[592,384]{1,0:T(8,128)S(1)}, bf16[592,384]{1,0:T(8,128)(2,1)S(1)}, bf16[592,384]{1,0:T(8,128)(2,1)S(1)}, bf16...) custom-call(bf16[304,384]{1,0:T(8,128)(2,1)S(1)} %get-tuple-element., ...), custom_call_target="tpu_custom_call" | custom-call | bytes 1 | tf_op jit(solution)/shard_map/attention/pallas_call | solution.py:35
  36.7 2.3 %collective-permute-done.11.refs_3_ = bf16[384,384]{1,0:T(8,128)(2,1)S(1)} collective-permute-done((bf16[384,384]{1,0:T(8,128)(2,1)S(1)}, bf16[384,384]{1,0:T(8,128)(2,1)S(1)}, u32[]{:S(2)}, u32[]{:S(2)}) %collective-permute-start.11) | collective-permute-done | bytes 294944 | tf_op jit(solution)/shard_map/ppermute | solution.py:620
  39.5 2.8 %mlp_own.1 = (bf16[592,768]{1,0:T(8,128)(2,1)S(1)}, bf16[592,768]{1,0:T(8,128)(2,1)S(1)}, f32[8,768]{1,0:T(8,128)S(1)}, bf16[4,4,96,384]{3,2,1,0:T(8,128)(2,1)S(1)}) custom-call(bf16[592,384]{1,0:T(8,128)(2,1)S(1)} %get-tuple-element.106.refs_0_.refs_1_, bf16[592,384]{1,0:T(8,128)(2,1)S(1)} %get-tuple-element.105.refs_1_.refs_2_.refs_4_, ...), custom_call_target="tpu_custom_call" | custom-call | flops 4600000000 | bytes 1 | tf_op jit(solution)/shard_map/mlp_own/pallas_call | solution.py:35
  42.4 2.8 %mlp_oth.1 = (bf16[592,768]{1,0:T(8,128)(2,1)S(1)}, bf16[592,768]{1,0:T(8,128)(2,1)S(1)}, f32[8,768]{1,0:T(8,128)S(1)}, bf16[4,4,96,384]{3,2,1,0:T(8,128)(2,1)S(1)}) custom-call(f32[8,768]{1,0:T(8,128)S(1)} %get-tuple-element.109.refs_0_.refs_12_, bf16[592,384]{1,0:T(8,128)(2,1)S(1)} %get-tuple-element.106.refs_0_.refs_1_, ...), custom_call_target="tpu_custom_call" | custom-call | flops 4600000000 | bytes 1 | tf_op jit(solution)/shard_map/mlp_oth/pallas_call | solution.py:35
  45.7 3.2 %mlp_sums.1 = (bf16[592,384]{1,0:T(8,128)(2,1)S(1)}, f32[592,384]{1,0:T(8,128)S(1)}, bf16[592,384]{1,0:T(8,128)(2,1)S(1)}, f32[384,384]{1,0:T(8,128)S(1)}, f32[16,384]{1,0:T(8,128)S(1)}) custom-call(f32[592,384]{1,0:T(8,128)S(1)} %get-tuple-element.101.refs_0_, bf16[592,384]{1,0:T(8,128)(2,1)S(1)} %get-tuple-element.102.refs_1_, ...), custom_call_target="tpu_custom_call" | custom-call | flops 2300000000 | bytes 1 | tf_op jit(solution)/shard_map/mlp_sums/pallas_call | solution.py:35
  52.8 8.8 %attention_back.1 = (bf16[592,384]{1,0:T(8,128)(2,1)S(1)}, bf16[4,4,160,128]{3,2,1,0:T(8,128)(2,1)S(1)}, bf16[4,4,160,128]{3,2,1,0:T(8,128)(2,1)S(1)}) custom-call(bf16[4,96,384]{2,1,0:T(8,128)(2,1)S(1)} %get-tuple-element.116.refs_0_.refs_1_, bf16[640,1152]{1,0:T(8,128)(2,1)S(1)} %get-tuple-element.117.refs_1_, ...), custom_call_target="tpu_custom_call" | custom-call | flops 12650000384 | bytes 1 | tf_op jit(solution)/shard_map/attention_back/pallas_call | solution.py:35
  61.6 4.1 %collective-permute-done.16.refs_3_ = bf16[4,96,384]{2,1,0:T(8,128)(2,1)S(1)} collective-permute-done((bf16[4,96,384]{2,1,0:T(8,128)(2,1)S(1)}, bf16[4,96,384]{2,1,0:T(8,128)(2,1)S(1)}, u32[]{:S(2)}, u32[]{:S(2)}) %collective-permute-start.16) | collective-permute-done | bytes 294944 | tf_op jit(solution)/shard_map/ppermute | solution.py:620
  70.5 2.4 %collective-permute-done.19.refs_0_.refs_2_ = bf16[4,160,128]{2,1,0:T(8,128)(2,1)S(1)} collective-permute-done((bf16[4,160,128]{2,1,0:T(8,128)(2,1)S(1)}, bf16[4,160,128]{2,1,0:T(8,128)(2,1)S(1)}, u32[]{:S(2)}, u32[]{:S(2)}) %collective-permute-start.19) | collective-permute-done | bytes 163872 | tf_op jit(solution)/shard_map/ppermute | solution.py:620
  74.0 3.5 %all-to-all-start = ((bf16[4,304,384]{2,1,0:T(8,128)(2,1)}), bf16[4,304,384]{2,1,0:T(8,128)(2,1)S(1)}, u32[]{:S(2)}, u32[]{:S(2)}) async-start(bf16[4,304,384]{2,1,0:T(8,128)(2,1)} %returns.1.refs_0_), calls=%async_computation | async-start | bytes 1867776 | tf_op jit(solution)/shard_map/all_to_all | solution.py:769
  77.7 2.2 %collective-permute-start.23 = (bf16[1,96,384]{2,1,0:T(8,128)(2,1)S(1)}, bf16[1,96,384]{2,1,0:T(8,128)(2,1)S(1)}, u32[]{:S(2)}, u32[]{:S(2)}) collective-permute-start(bf16[1,96,384]{2,1,0:T(8,128)(2,1)S(1)} %get-tuple-element.142), channel_id=1, source_target_pairs={{0,16},{8,24},{16,0},{24,8},{1,17},{9,25},{17,1},{25,9},{2,18},{10... | collective-permute-start | bytes 221192 | tf_op jit(solution)/shard_map/ppermute | solution.py:786
  79.9 1.6 %collective-permute-start.24 = (bf16[160,128]{1,0:T(8,128)(2,1)S(1)}, bf16[160,128]{1,0:T(8,128)(2,1)S(1)}, u32[]{:S(2)}, u32[]{:S(2)}) collective-permute-start(bf16[160,128]{1,0:T(8,128)(2,1)S(1)} %get-tuple-element.143), channel_id=1, source_target_pairs={{0,8},{8,0},{16,24},{24,16},{1,9},{9,1},{17,25},{25,17},{2,10},{10... | collective-permute-start | bytes 122888 | tf_op jit(solution)/shard_map/ppermute | solution.py:620
  81.9 2.5 %collective-permute-start.26 = (bf16[160,128]{1,0:T(8,128)(2,1)S(1)}, bf16[160,128]{1,0:T(8,128)(2,1)S(1)}, u32[]{:S(2)}, u32[]{:S(2)}) collective-permute-start(bf16[160,128]{1,0:T(8,128)(2,1)S(1)} %get-tuple-element.145), channel_id=1, source_target_pairs={{0,24},{8,16},{16,8},{24,0},{1,25},{9,17},{17,9},{25,1},{2,26},{10... | collective-permute-start | bytes 122888 | tf_op jit(solution)/shard_map/ppermute | solution.py:620
  84.3 2.4 %collective-permute-done.25.refs_4_ = bf16[160,128]{1,0:T(8,128)(2,1)S(1)} collective-permute-done((bf16[160,128]{1,0:T(8,128)(2,1)S(1)}, bf16[160,128]{1,0:T(8,128)(2,1)S(1)}, u32[]{:S(2)}, u32[]{:S(2)}) %collective-permute-start.25) | collective-permute-done | bytes 40992 | tf_op jit(solution)/shard_map/ppermute | solution.py:620
  87.9 2.9 %collective-permute-start.30 = (bf16[160,384]{1,0:T(8,128)(2,1)S(1)}, bf16[160,384]{1,0:T(8,128)(2,1)S(1)}, u32[]{:S(2)}, u32[]{:S(2)}) collective-permute-start(bf16[160,384]{1,0:T(8,128)(2,1)S(1)} %sum_dp.1.refs_0_.refs_1_), channel_id=1, source_target_pairs={{0,6},{2,4},{4,2},{6,0},{1,7},{3,5},{5,3},{7,1},{8,14},{10,12},{12... | collective-permute-start | bytes 368648 | tf_op jit(solution)/shard_map/ppermute | solution.py:620
  91.5 2.7 %place_slots.1 = (f32[1160,384]{1,0:T(8,128)}, f32[1160,384]{1,0:T(8,128)}, f32[8,128]{1,0:T(8,128)S(1)}) custom-call(bf16[4,304,384]{2,1,0:T(8,128)(2,1)S(1)} %hand_on.1.refs_0_, bf16[4,304,384]{2,1,0:T(8,128)(2,1)S(1)} %collective-permute-done.27.refs_1_, f32[2,8,384]{2,1,0:T(8,128)S(1)} %get-tuple-element.146.refs_2_, s32[8,145]{1,0:T(8,128)S(1)} %copy-done.5), custom_call_target="tpu_custom_call" | custom-call | flops 2644999936 | bytes 1 | tf_op jit(solution)/shard_map/place_slots/pallas_call | solution.py:35
  94.8 2.5 %collective-permute-done.29.refs_3_ = bf16[160,384]{1,0:T(8,128)(2,1)S(1)} collective-permute-done((bf16[160,384]{1,0:T(8,128)(2,1)S(1)}, bf16[160,384]{1,0:T(8,128)(2,1)S(1)}, u32[]{:S(2)}, u32[]{:S(2)}) %collective-permute-start.29) | collective-permute-done | bytes 122912 | tf_op jit(solution)/shard_map/ppermute | solution.py:620
  (74 shorter events, 22.8 us)
Async XLA Ops:
  2.9 12.1 %collective-permute-start.5 = (bf16[1,96,384]{2,1,0:T(8,128)(2,1)}, bf16[1,96,384]{2,1,0:T(8,128)(2,1)S(1)}, u32[]{:S(2)}, u32[]{:S(2)}) collective-permute-start(bf16[1,96,384]{2,1,0:T(8,128)(2,1)} %bitcast.20), channel_id=1, source_target_pairs={{0,16},{8,24},{16,0},{24,8},{1,17},{9,25},{17,1},{25,9},{2,18},{10... | collective-permute-start | bytes 221192 | tf_op jit(solution)/shard_map/ppermute | solution.py:660
  7.0 11.6 %collective-permute-start.3 = (bf16[1,112,768]{2,1,0:T(8,128)(2,1)}, bf16[1,112,768]{2,1,0:T(8,128)(2,1)S(1)}, u32[]{:S(2)}, u32[]{:S(2)}) collective-permute-start(bf16[1,112,768]{2,1,0:T(8,128)(2,1)} %bitcast.18), channel_id=1, source_target_pairs={{0,16},{8,24},{16,0},{24,8},{1,17},{9,25},{17,1},{25,9},{2,18},{10... | collective-permute-start | bytes 516104 | tf_op jit(solution)/shard_map/ppermute | solution.py:660
  8.6 13.2 %collective-permute-start = (bf16[304,384]{1,0:T(8,128)(2,1)S(1)}, bf16[304,384]{1,0:T(8,128)(2,1)S(1)}, u32[]{:S(2)}, u32[]{:S(2)}) collective-permute-start(bf16[304,384]{1,0:T(8,128)(2,1)S(1)} %get-tuple-element.92), channel_id=1, source_target_pairs={{0,2},{2,0},{4,6},{6,4},{1,3},{3,1},{5,7},{7,5},{8,10},{10,8},{12,... | collective-permute-start | bytes 700424 | tf_op jit(solution)/shard_map/ppermute | solution.py:620
  10.4 11.6 %collective-permute-start.1 = (bf16[304,384]{1,0:T(8,128)(2,1)S(1)}, bf16[304,384]{1,0:T(8,128)(2,1)S(1)}, u32[]{:S(2)}, u32[]{:S(2)}) collective-permute-start(bf16[304,384]{1,0:T(8,128)(2,1)S(1)} %get-tuple-element.93), channel_id=1, source_target_pairs={{0,4},{2,6},{4,0},{6,2},{1,5},{3,7},{5,1},{7,3},{8,12},{10,14},{12... | collective-permute-start | bytes 700424 | tf_op jit(solution)/shard_map/ppermute | solution.py:620
  11.9 10.1 %collective-permute-start.2 = (bf16[304,384]{1,0:T(8,128)(2,1)S(1)}, bf16[304,384]{1,0:T(8,128)(2,1)S(1)}, u32[]{:S(2)}, u32[]{:S(2)}) collective-permute-start(bf16[304,384]{1,0:T(8,128)(2,1)S(1)} %get-tuple-element.94), channel_id=1, source_target_pairs={{0,6},{2,4},{4,2},{6,0},{1,7},{3,5},{5,3},{7,1},{8,14},{10,12},{12... | collective-permute-start | bytes 700424 | tf_op jit(solution)/shard_map/ppermute | solution.py:620
  15.1 6.8 %collective-permute-start.6 = (bf16[2,96,384]{2,1,0:T(8,128)(2,1)S(1)}, bf16[2,96,384]{2,1,0:T(8,128)(2,1)S(1)}, u32[]{:S(2)}, u32[]{:S(2)}) collective-permute-start(bf16[2,96,384]{2,1,0:T(8,128)(2,1)S(1)} %join_quarter.1.refs_4_), channel_id=1, source_target_pairs={{0,8},{8,0},{16,24},{24,16},{1,9},{9,1},{17,25},{25,17},{2,10},{10... | collective-permute-start | bytes 442376 | tf_op jit(solution)/shard_map/ppermute | solution.py:662
  18.7 10.4 %collective-permute-start.4 = (bf16[2,112,768]{2,1,0:T(8,128)(2,1)S(1)}, bf16[2,112,768]{2,1,0:T(8,128)(2,1)S(1)}, u32[]{:S(2)}, u32[]{:S(2)}) collective-permute-start(bf16[2,112,768]{2,1,0:T(8,128)(2,1)S(1)} %join_attn.1.refs_3_.refs_4_), channel_id=1, source_target_pairs={{0,8},{8,0},{16,24},{24,16},{1,9},{9,1},{17,25},{25,17},{2,10},{10... | collective-permute-start | bytes 1032200 | tf_op jit(solution)/shard_map/ppermute | solution.py:662
  22.1 6.9 %collective-permute-start.7 = (bf16[2,112,768]{2,1,0:T(8,128)(2,1)S(1)}, bf16[2,112,768]{2,1,0:T(8,128)(2,1)S(1)}, u32[]{:S(2)}, u32[]{:S(2)}) collective-permute-start(bf16[2,112,768]{2,1,0:T(8,128)(2,1)S(1)} %get-tuple-element.97), channel_id=1, source_target_pairs={{0,1},{1,0},{2,3},{3,2},{4,5},{5,4},{6,7},{7,6},{8,9},{9,8},{10,11... | collective-permute-start | bytes 1032200 | tf_op jit(solution)/shard_map/ppermute | solution.py:644
  22.2 14.5 %collective-permute-start.12 = (bf16[384,384]{1,0:T(8,128)(2,1)S(1)}, bf16[384,384]{1,0:T(8,128)(2,1)S(1)}, u32[]{:S(2)}, u32[]{:S(2)}) collective-permute-start(bf16[384,384]{1,0:T(8,128)(2,1)S(1)} %get-tuple-element.98.refs_1_), channel_id=1, source_target_pairs={{0,6},{2,4},{4,2},{6,0},{1,7},{3,5},{5,3},{7,1},{8,14},{10,12},{12... | collective-permute-start | bytes 884744 | tf_op jit(solution)/shard_map/ppermute | solution.py:620
  25.1 13.9 %collective-permute-start.11 = (bf16[384,384]{1,0:T(8,128)(2,1)S(1)}, bf16[384,384]{1,0:T(8,128)(2,1)S(1)}, u32[]{:S(2)}, u32[]{:S(2)}) collective-permute-start(bf16[384,384]{1,0:T(8,128)(2,1)S(1)} %get-tuple-element.98.refs_1_), channel_id=1, source_target_pairs={{0,4},{2,6},{4,0},{6,2},{1,5},{3,7},{5,1},{7,3},{8,12},{10,14},{12... | collective-permute-start | bytes 884744 | tf_op jit(solution)/shard_map/ppermute | solution.py:620
  25.6 13.7 %collective-permute-start.10 = (bf16[384,384]{1,0:T(8,128)(2,1)S(1)}, bf16[384,384]{1,0:T(8,128)(2,1)S(1)}, u32[]{:S(2)}, u32[]{:S(2)}) collective-permute-start(bf16[384,384]{1,0:T(8,128)(2,1)S(1)} %get-tuple-element.98.refs_1_), channel_id=1, source_target_pairs={{0,2},{2,0},{4,6},{6,4},{1,3},{3,1},{5,7},{7,5},{8,10},{10,8},{12,... | collective-permute-start | bytes 884744 | tf_op jit(solution)/shard_map/ppermute | solution.py:620
  49.2 12.4 %collective-permute-start.15 = (bf16[4,96,384]{2,1,0:T(8,128)(2,1)S(1)}, bf16[4,96,384]{2,1,0:T(8,128)(2,1)S(1)}, u32[]{:S(2)}, u32[]{:S(2)}) collective-permute-start(bf16[4,96,384]{2,1,0:T(8,128)(2,1)S(1)} %get-tuple-element.128), channel_id=1, source_target_pairs={{0,2},{2,0},{4,6},{6,4},{1,3},{3,1},{5,7},{7,5},{8,10},{10,8},{12,... | collective-permute-start | bytes 884744 | tf_op jit(solution)/shard_map/ppermute | solution.py:620
  50.7 15.0 %collective-permute-start.16 = (bf16[4,96,384]{2,1,0:T(8,128)(2,1)S(1)}, bf16[4,96,384]{2,1,0:T(8,128)(2,1)S(1)}, u32[]{:S(2)}, u32[]{:S(2)}) collective-permute-start(bf16[4,96,384]{2,1,0:T(8,128)(2,1)S(1)} %get-tuple-element.129), channel_id=1, source_target_pairs={{0,4},{2,6},{4,0},{6,2},{1,5},{3,7},{5,1},{7,3},{8,12},{10,14},{12... | collective-permute-start | bytes 884744 | tf_op jit(solution)/shard_map/ppermute | solution.py:620
  51.3 14.5 %collective-permute-start.17 = (bf16[4,96,384]{2,1,0:T(8,128)(2,1)S(1)}, bf16[4,96,384]{2,1,0:T(8,128)(2,1)S(1)}, u32[]{:S(2)}, u32[]{:S(2)}) collective-permute-start(bf16[4,96,384]{2,1,0:T(8,128)(2,1)S(1)} %get-tuple-element.130), channel_id=1, source_target_pairs={{0,6},{2,4},{4,2},{6,0},{1,7},{3,5},{5,3},{7,1},{8,14},{10,12},{12... | collective-permute-start | bytes 884744 | tf_op jit(solution)/shard_map/ppermute | solution.py:620
  66.1 6.8 %collective-permute-start.19 = (bf16[4,160,128]{2,1,0:T(8,128)(2,1)S(1)}, bf16[4,160,128]{2,1,0:T(8,128)(2,1)S(1)}, u32[]{:S(2)}, u32[]{:S(2)}) collective-permute-start(bf16[4,160,128]{2,1,0:T(8,128)(2,1)S(1)} %get-tuple-element.133), channel_id=1, source_target_pairs={{0,2},{2,0},{4,6},{6,4},{1,3},{3,1},{5,7},{7,5},{8,10},{10,8},{12,... | collective-permute-start | bytes 491528 | tf_op jit(solution)/shard_map/ppermute | solution.py:620
  66.7 10.8 %collective-permute-start.20 = (bf16[4,160,128]{2,1,0:T(8,128)(2,1)S(1)}, bf16[4,160,128]{2,1,0:T(8,128)(2,1)S(1)}, u32[]{:S(2)}, u32[]{:S(2)}) collective-permute-start(bf16[4,160,128]{2,1,0:T(8,128)(2,1)S(1)} %get-tuple-element.137), channel_id=1, source_target_pairs={{0,4},{2,6},{4,0},{6,2},{1,5},{3,7},{5,1},{7,3},{8,12},{10,14},{12... | collective-permute-start | bytes 491528 | tf_op jit(solution)/shard_map/ppermute | solution.py:620
  68.1 9.4 %collective-permute-start.21 = (bf16[4,160,128]{2,1,0:T(8,128)(2,1)S(1)}, bf16[4,160,128]{2,1,0:T(8,128)(2,1)S(1)}, u32[]{:S(2)}, u32[]{:S(2)}) collective-permute-start(bf16[4,160,128]{2,1,0:T(8,128)(2,1)S(1)} %get-tuple-element.138), channel_id=1, source_target_pairs={{0,6},{2,4},{4,2},{6,0},{1,7},{3,5},{5,3},{7,1},{8,14},{10,12},{12... | collective-permute-start | bytes 491528 | tf_op jit(solution)/shard_map/ppermute | solution.py:620
  69.7 7.9 %collective-permute-start.22 = (bf16[2,96,384]{2,1,0:T(8,128)(2,1)S(1)}, bf16[2,96,384]{2,1,0:T(8,128)(2,1)S(1)}, u32[]{:S(2)}, u32[]{:S(2)}) collective-permute-start(bf16[2,96,384]{2,1,0:T(8,128)(2,1)S(1)} %get-tuple-element.140), channel_id=1, source_target_pairs={{0,8},{8,0},{16,24},{24,16},{1,9},{9,1},{17,25},{25,17},{2,10},{10... | collective-permute-start | bytes 442376 | tf_op jit(solution)/shard_map/ppermute | solution.py:782
  74.0 13.7 %all-to-all-start = ((bf16[4,304,384]{2,1,0:T(8,128)(2,1)}), bf16[4,304,384]{2,1,0:T(8,128)(2,1)S(1)}, u32[]{:S(2)}, u32[]{:S(2)}) async-start(bf16[4,304,384]{2,1,0:T(8,128)(2,1)} %returns.1.refs_0_), calls=%async_computation | async-start | bytes 1867776 | tf_op jit(solution)/shard_map/all_to_all | solution.py:769
  77.7 10.0 %collective-permute-start.23 = (bf16[1,96,384]{2,1,0:T(8,128)(2,1)S(1)}, bf16[1,96,384]{2,1,0:T(8,128)(2,1)S(1)}, u32[]{:S(2)}, u32[]{:S(2)}) collective-permute-start(bf16[1,96,384]{2,1,0:T(8,128)(2,1)S(1)} %get-tuple-element.142), channel_id=1, source_target_pairs={{0,16},{8,24},{16,0},{24,8},{1,17},{9,25},{17,1},{25,9},{2,18},{10... | collective-permute-start | bytes 221192 | tf_op jit(solution)/shard_map/ppermute | solution.py:786
  81.9 5.8 %collective-permute-start.26 = (bf16[160,128]{1,0:T(8,128)(2,1)S(1)}, bf16[160,128]{1,0:T(8,128)(2,1)S(1)}, u32[]{:S(2)}, u32[]{:S(2)}) collective-permute-start(bf16[160,128]{1,0:T(8,128)(2,1)S(1)} %get-tuple-element.145), channel_id=1, source_target_pairs={{0,24},{8,16},{16,8},{24,0},{1,25},{9,17},{17,9},{25,1},{2,26},{10... | collective-permute-start | bytes 122888 | tf_op jit(solution)/shard_map/ppermute | solution.py:620
  87.9 6.9 %collective-permute-start.30 = (bf16[160,384]{1,0:T(8,128)(2,1)S(1)}, bf16[160,384]{1,0:T(8,128)(2,1)S(1)}, u32[]{:S(2)}, u32[]{:S(2)}) collective-permute-start(bf16[160,384]{1,0:T(8,128)(2,1)S(1)} %sum_dp.1.refs_0_.refs_1_), channel_id=1, source_target_pairs={{0,6},{2,4},{4,2},{6,0},{1,7},{3,5},{5,3},{7,1},{8,14},{10,12},{12... | collective-permute-start | bytes 368648 | tf_op jit(solution)/shard_map/ppermute | solution.py:620
  90.8 6.5 %collective-permute-start.29 = (bf16[160,384]{1,0:T(8,128)(2,1)S(1)}, bf16[160,384]{1,0:T(8,128)(2,1)S(1)}, u32[]{:S(2)}, u32[]{:S(2)}) collective-permute-start(bf16[160,384]{1,0:T(8,128)(2,1)S(1)} %sum_dp.1.refs_0_.refs_1_), channel_id=1, source_target_pairs={{0,4},{2,6},{4,0},{6,2},{1,5},{3,7},{5,1},{7,3},{8,12},{10,14},{12... | collective-permute-start | bytes 368648 | tf_op jit(solution)/shard_map/ppermute | solution.py:620
  91.4 6.3 %collective-permute-start.28 = (bf16[160,384]{1,0:T(8,128)(2,1)S(1)}, bf16[160,384]{1,0:T(8,128)(2,1)S(1)}, u32[]{:S(2)}, u32[]{:S(2)}) collective-permute-start(bf16[160,384]{1,0:T(8,128)(2,1)S(1)} %sum_dp.1.refs_0_.refs_1_), channel_id=1, source_target_pairs={{0,2},{2,0},{4,6},{6,4},{1,3},{3,1},{5,7},{7,5},{8,10},{10,8},{12,... | collective-permute-start | bytes 368648 | tf_op jit(solution)/shard_map/ppermute | solution.py:620
  (14 other events, 75.2 us)

commit v6 on v5

--- a/solution.py
+++ b/solution.py
@@ -16,7 +16,7 @@
 TILE = 128
 TIMES = {
     "pack_weights": 2.0, "pack_slots": 3.0, "pack_cotangent": 2.0, "attention": 0.0, "mlp_own": 4.0, "mlp_oth": 4.0, "mlp_sums": 2.0, "attention_back": 11.0,
-    "place_grads": 1.0, "place_slots": 2.3, "join_quarter": 20.0, "sum_ctx_attn": 50.0, "sum_ctx_ff": 50.0,
+    "place_grads": 1.0, "place_slots": 2.3, "join_quarter": 20.0, "sum_ctx_attn": 0.5, "sum_dp": 5.0, "sum_ctx_first": 50.0,
 }
 EXTRA = 16
 
@@ -474,27 +474,54 @@
         refs[n + k][...] = v.astype(BF)
 
 
-def halve(axis, stride, item, keep, send):
-    bit = lax.rem(lax.div(lax.axis_index(axis), stride), 2)
+def halve(stride, item, keep, send):
+    bit = lax.rem(lax.div(lax.axis_index("dp"), stride), 2)
     for j in range(keep.shape[0]):
         keep[j] = item(2 * j + bit).astype(BF)
         send[j] = item(2 * j + 1 - bit).astype(BF)
 
 
-def sum_ctx_halves_kernel(n, *refs):
-    terms, (keep, send) = refs[:n], refs[n:]
-
-    def item(i):
-        v = terms[0][i].astype(F32)
-        for t in terms[1:]:
-            v = v + t[i].astype(F32)
-        return v
-
-    halve("dp", 1, item, keep, send)
+def ctx_bits():
+    me = lax.axis_index("ctx")
+    return lax.rem(me, 2), lax.div(me, 2)
+
+
+def sum_core_ff_kernel(own, oth, keep_a, send_a, keep_b, send_b):
+    low, high = ctx_bits()
+    half = own.shape[1] // 2
+
+    def put(to, i, quarter, blocks):
+        to[i] = (own[quarter, blocks].astype(F32) + oth[quarter, blocks].astype(F32)).astype(BF)
+
+    for i in range(2):
+        first, second = slice(0, half), slice(half, 2 * half)
+        put(keep_a, i, 2 * i + low, first)
+        put(send_a, i, 2 * i + 1 - low, first)
+        put(keep_b, i, 2 * high + i, second)
+        put(send_b, i, 2 * (1 - high) + i, second)
+
+
+def sum_ctx_first_kernel(own_a, got_a, own_b, got_b, keep_a, send_a, keep_b, send_b):
+    low, high = ctx_bits()
+    for own, got, keep, send, bit in (
+        (own_a, got_a, keep_a, send_a, high),
+        (own_b, got_b, keep_b, send_b, low),
+    ):
+        keep[...] = (own[bit].astype(F32) + got[bit].astype(F32)).astype(BF)
+        send[...] = (own[1 - bit].astype(F32) + got[1 - bit].astype(F32)).astype(BF)
+
+
+def sum_ctx_second_kernel(own_a, got_a, own_b, got_b, keep, send):
+    bit = lax.rem(lax.axis_index("dp"), 2)
+    half = own_a.shape[0]
+    for j in range(keep.shape[0]):
+        own, got, at = (own_a, got_a, 2 * j) if 2 * j < half else (own_b, got_b, 2 * j - half)
+        for to, i in ((keep, at + bit), (send, at + 1 - bit)):
+            to[j] = (own[i].astype(F32) + got[i].astype(F32)).astype(BF)
 
 
 def add_halves_kernel(stride, own, got, keep, send):
-    halve("dp", stride, lambda i: own[i].astype(F32) + got[i].astype(F32), keep, send)
+    halve(stride, lambda i: own[i].astype(F32) + got[i].astype(F32), keep, send)
 
 
 def sum_dp_kernel(n, own, got, *refs):
@@ -744,27 +771,34 @@
     def by_image(v):
         return jnp.transpose(v.reshape(slots, images, width), (1, 0, 2))
 
-    s2_send = core_sums("sum_core_ff", g2_own, g2_oth, after=[vgrad])
-    s2 = over("ctx", nctx, s2_send)
+    pairs = sds((2, ndp // 2, padded, ff // 2), BF)
+    keep_a, send_a, keep_b, send_b = call("sum_core_ff", sum_core_ff_kernel, [pairs] * 4, after=[vgrad])(
+        g2_own, other(g2_oth)
+    )
+    got_a, got_b = lax.ppermute(send_a, "ctx", xor(nctx, 1)), lax.ppermute(send_b, "ctx", xor(nctx, 2))
     ig, g1_own, g1_oth = call(
         "attention_back",
         one(attention_back_kernel),
         [sds((total, width), BF)] + [sds((4, ndp, padded + padded // 2 + EXTRA, TILE), BF)] * 2,
         scratch=[pltpu.VMEM((total, 3 * width), BF)],
         mib=32,
-        after=[s2_send[0]],
+        after=[keep_a],
     )(qkv, dctx, lse, ctx_full, n1, x, dmid, wqkv, vec, g_out, vgrad, ub_own, ub_oth)
-    half = sds((ndp // 2,) + s2[0].shape[1:], BF)
-    keep, send = call(
-        "sum_ctx_ff", functools.partial(sum_ctx_halves_kernel, nctx), [half, half], after=[g1_own]
-    )(*s2)
-    s1_send = core_sums("sum_core_attn", g1_own, g1_oth, after=[keep])
+    one_quarter = sds(pairs.shape[1:], BF)
+    keep_a, send_a, keep_b, send_b = call(
+        "sum_ctx_first", sum_ctx_first_kernel, [one_quarter] * 4, after=[g1_own]
+    )(keep_a, got_a, keep_b, got_b)
+    got_a, got_b = lax.ppermute(send_a, "ctx", xor(nctx, 2)), lax.ppermute(send_b, "ctx", xor(nctx, 1))
+    s1_send = core_sums("sum_core_attn", g1_own, g1_oth, after=[keep_a])
     s1 = over("ctx", nctx, s1_send)
+    keep, send = call("sum_ctx_second", sum_ctx_second_kernel, [one_quarter] * 2, after=[s1_send[0]])(
+        keep_a, got_a, keep_b, got_b
+    )
     back = call(
         "returns",
         one(returns_kernel),
         sds((nctx, 2 * main + EXTRA, width), BF),
-        after=[s1[1]],
+        after=[keep],
     )(bo, ig)
     returned = lax.all_to_all(back, "ctx", 0, 0)
     u1_send = call(

time: 99.1 us -> 96.1 us (0.970)
  waiting for transfers between devices: 28.9 us -> 25.2 us
    ppermute x18 -> x15, waiting for transfers between devices: 16.3 us -> 9.96 us  [over(): lax.ppermute(items[k], axis, xor(n, k))]
    ppermute x0 -> x4, starting transfers between devices: none -> 4.18 us  [the longest x1 1.58 us: body(): lax.ppermute(send_a, 'ctx', xor(nctx, 2))]
    ppermute x18 -> x15, starting transfers between devices: 22.2 us -> 18.6 us  [over(): lax.ppermute(items[k], axis, xor(n, k))]
    ppermute x0 -> x4, waiting for transfers between devices: none -> 2.44 us  [the longest x1 1.81 us: body(): lax.ppermute(send_b, 'ctx', xor(nctx, 1))]
    pallas_call x22 -> x23, Pallas kernels: 33.1 us -> 33.2 us  [run(): pl.pallas_call(ordered, name=name, out_shape=out_shape, in_specs=specs, o...]
  transfers between devices with their start and end apart: 32 -> 33, of which waited for: 17 -> 19; matrix products, arithmetic and copies ran while one was open for 0% -> 0% of each run, Pallas kernels for 27% -> 28%
where the time goes in v6:
time: 96.1 us; the launch traced here: 95.9 us
  starting transfers between devices  36.5 us (38%)
  Pallas kernels  33.2 us (35%)
  waiting for transfers between devices  25.2 us (26%)
  between operations  1.02 us (1%)
    pallas_call x23, Pallas kernels, run(): pl.pallas_call(ordered, name=name, out_shape=out_shape, in_specs=specs, o...  33.2 us
    ppermute x15, starting transfers between devices, over(): lax.ppermute(items[k], axis, xor(n, k))  18.6 us
    ppermute x15, waiting for transfers between devices, over(): lax.ppermute(items[k], axis, xor(n, k))  9.96 us
    ppermute x2, waiting for transfers between devices, gather_dp(): return (v, lax.ppermute(v, 'dp', xor(ndp, 1)))  5.72 us
    ppermute x2, waiting for transfers between devices, gather_dp(): lax.ppermute(v, 'dp', xor(ndp, stride))  5.68 us
    ppermute x2, starting transfers between devices, gather_dp(): lax.ppermute(v, 'dp', xor(ndp, stride))  4.18 us
    all_to_all x1, starting transfers between devices, body(): returned = lax.all_to_all(back, 'ctx', 0, 0)  3.51 us
    ppermute x1, starting transfers between devices, body(): lax.ppermute(send, 'dp', xor(ndp, ndp // 2))  2.23 us
  transfers between devices with their start and end apart: 33, of which 19 were waited for; matrix products, arithmetic and copies ran while one was open for 0% of the time, Pallas kernels for 28%

profile of v6, /device:TPU:0, one launch (start us, length us, event | category | flops | bytes accessed | tf_op | source)
XLA Modules:
  0.0 95.9 jit_solution(15182981184153302192)
XLA Ops:
  0.7 2.2 %pack_weights.1 = (bf16[112,768]{1,0:T(8,128)(2,1)}, bf16[96,384]{1,0:T(8,128)(2,1)}, f32[8,128]{1,0:T(8,128)}) custom-call(bf16[96,192]{1,0:T(8,128)(2,1)} %refs_0_.1, bf16[96,192]{1,0:T(8,128)(2,1)} %refs_1_.1, bf16[96,192]{1,0:T(8,128)(2,1)} %refs_2_.3, bf16[192,96]{1,0:T(8,128)(2,1)} %refs_3_.2, bf16[96,768]{1,0:T(8,128)(2,1)} %refs_4_.1, ...), custom_call_target="tpu_custom_call" | custom-call | flops 2300000000 | bytes 1 | tf_op jit(solution)/shard_map/pack_weights/pallas_call | solution.py:35
  2.9 4.1 %collective-permute-start.5 = (bf16[1,96,384]{2,1,0:T(8,128)(2,1)}, bf16[1,96,384]{2,1,0:T(8,128)(2,1)S(1)}, u32[]{:S(2)}, u32[]{:S(2)}) collective-permute-start(bf16[1,96,384]{2,1,0:T(8,128)(2,1)} %bitcast.20), channel_id=1, source_target_pairs={{0,16},{8,24},{16,0},{24,8},{1,17},{9,25},{17,1},{25,9},{2,18},{10... | collective-permute-start | bytes 221192 | tf_op jit(solution)/shard_map/ppermute | solution.py:687
  8.6 1.8 %collective-permute-start = (bf16[304,384]{1,0:T(8,128)(2,1)S(1)}, bf16[304,384]{1,0:T(8,128)(2,1)S(1)}, u32[]{:S(2)}, u32[]{:S(2)}) collective-permute-start(bf16[304,384]{1,0:T(8,128)(2,1)S(1)} %get-tuple-element.96), channel_id=1, source_target_pairs={{0,2},{2,0},{4,6},{6,4},{1,3},{3,1},{5,7},{7,5},{8,10},{10,8},{12,... | collective-permute-start | bytes 700424 | tf_op jit(solution)/shard_map/ppermute | solution.py:647
  12.2 2.8 %collective-permute-done.5.refs_1_ = bf16[1,96,384]{2,1,0:T(8,128)(2,1)S(1)} collective-permute-done((bf16[1,96,384]{2,1,0:T(8,128)(2,1)}, bf16[1,96,384]{2,1,0:T(8,128)(2,1)S(1)}, u32[]{:S(2)}, u32[]{:S(2)}) %collective-permute-start.5) | collective-permute-done | bytes 73760 | tf_op jit(solution)/shard_map/ppermute | solution.py:687
  15.8 2.8 %collective-permute-done.3.refs_1_ = bf16[1,112,768]{2,1,0:T(8,128)(2,1)S(1)} collective-permute-done((bf16[1,112,768]{2,1,0:T(8,128)(2,1)}, bf16[1,112,768]{2,1,0:T(8,128)(2,1)S(1)}, u32[]{:S(2)}, u32[]{:S(2)}) %collective-permute-start.3) | collective-permute-done | bytes 172064 | tf_op jit(solution)/shard_map/ppermute | solution.py:687
  19.4 2.4 %collective-permute-done.6.refs_5_ = bf16[2,96,384]{2,1,0:T(8,128)(2,1)S(1)} collective-permute-done((bf16[2,96,384]{2,1,0:T(8,128)(2,1)S(1)}, bf16[2,96,384]{2,1,0:T(8,128)(2,1)S(1)}, u32[]{:S(2)}, u32[]{:S(2)}) %collective-permute-start.6) | collective-permute-done | bytes 147488 | tf_op jit(solution)/shard_map/ppermute | solution.py:689
  22.2 2.9 %collective-permute-start.12 = (bf16[384,384]{1,0:T(8,128)(2,1)S(1)}, bf16[384,384]{1,0:T(8,128)(2,1)S(1)}, u32[]{:S(2)}, u32[]{:S(2)}) collective-permute-start(bf16[384,384]{1,0:T(8,128)(2,1)S(1)} %get-tuple-element.102.refs_1_), channel_id=1, source_target_pairs={{0,6},{2,4},{4,2},{6,0},{1,7},{3,5},{5,3},{7,1},{8,14},{10,12},{12... | collective-permute-start | bytes 884744 | tf_op jit(solution)/shard_map/ppermute | solution.py:647
  25.8 3.3 %collective-permute-done.4.refs_2_.refs_5_ = bf16[2,112,768]{2,1,0:T(8,128)(2,1)S(1)} collective-permute-done((bf16[2,112,768]{2,1,0:T(8,128)(2,1)S(1)}, bf16[2,112,768]{2,1,0:T(8,128)(2,1)S(1)}, u32[]{:S(2)}, u32[]{:S(2)}) %collective-permute-start.4) | collective-permute-done | bytes 344096 | tf_op jit(solution)/shard_map/ppermute | solution.py:689
  30.8 5.9 %attention.1 = (f32[592,384]{1,0:T(8,128)S(1)}, f32[592,384]{1,0:T(8,128)S(1)}, bf16[592,384]{1,0:T(8,128)(2,1)S(1)}, bf16[592,384]{1,0:T(8,128)(2,1)S(1)}, bf16...) custom-call(bf16[304,384]{1,0:T(8,128)(2,1)S(1)} %get-tuple-element., ...), custom_call_target="tpu_custom_call" | custom-call | bytes 1 | tf_op jit(solution)/shard_map/attention/pallas_call | solution.py:35
  36.7 2.3 %collective-permute-done.11.refs_3_ = bf16[384,384]{1,0:T(8,128)(2,1)S(1)} collective-permute-done((bf16[384,384]{1,0:T(8,128)(2,1)S(1)}, bf16[384,384]{1,0:T(8,128)(2,1)S(1)}, u32[]{:S(2)}, u32[]{:S(2)}) %collective-permute-start.11) | collective-permute-done | bytes 294944 | tf_op jit(solution)/shard_map/ppermute | solution.py:647
  39.5 2.8 %mlp_own.1 = (bf16[592,768]{1,0:T(8,128)(2,1)S(1)}, bf16[592,768]{1,0:T(8,128)(2,1)S(1)}, f32[8,768]{1,0:T(8,128)S(1)}, bf16[4,4,96,384]{3,2,1,0:T(8,128)(2,1)S(1)}) custom-call(bf16[592,384]{1,0:T(8,128)(2,1)S(1)} %get-tuple-element.110.refs_0_.refs_1_, bf16[592,384]{1,0:T(8,128)(2,1)S(1)} %get-tuple-element.109.refs_1_.refs_2_.refs_4_, ...), custom_call_target="tpu_custom_call" | custom-call | flops 4600000000 | bytes 1 | tf_op jit(solution)/shard_map/mlp_own/pallas_call | solution.py:35
  42.4 2.8 %mlp_oth.1 = (bf16[592,768]{1,0:T(8,128)(2,1)S(1)}, bf16[592,768]{1,0:T(8,128)(2,1)S(1)}, f32[8,768]{1,0:T(8,128)S(1)}, bf16[4,4,96,384]{3,2,1,0:T(8,128)(2,1)S(1)}) custom-call(f32[8,768]{1,0:T(8,128)S(1)} %get-tuple-element.113.refs_0_.refs_12_, bf16[592,384]{1,0:T(8,128)(2,1)S(1)} %get-tuple-element.110.refs_0_.refs_1_, ...), custom_call_target="tpu_custom_call" | custom-call | flops 4600000000 | bytes 1 | tf_op jit(solution)/shard_map/mlp_oth/pallas_call | solution.py:35
  45.7 3.2 %mlp_sums.1 = (bf16[592,384]{1,0:T(8,128)(2,1)S(1)}, f32[592,384]{1,0:T(8,128)S(1)}, bf16[592,384]{1,0:T(8,128)(2,1)S(1)}, f32[384,384]{1,0:T(8,128)S(1)}, f32[16,384]{1,0:T(8,128)S(1)}) custom-call(f32[592,384]{1,0:T(8,128)S(1)} %get-tuple-element.105.refs_0_, bf16[592,384]{1,0:T(8,128)(2,1)S(1)} %get-tuple-element.106.refs_1_, ...), custom_call_target="tpu_custom_call" | custom-call | flops 2300000000 | bytes 1 | tf_op jit(solution)/shard_map/mlp_sums/pallas_call | solution.py:35
  51.3 8.8 %attention_back.1 = (bf16[592,384]{1,0:T(8,128)(2,1)S(1)}, bf16[4,4,160,128]{3,2,1,0:T(8,128)(2,1)S(1)}, bf16[4,4,160,128]{3,2,1,0:T(8,128)(2,1)S(1)}) custom-call(bf16[2,2,96,384]{3,2,1,0:T(8,128)(2,1)S(1)} %get-tuple-element.120.refs_0_.refs_1_, bf16[640,1152]{1,0:T(8,128)(2,1)S(1)} %get-tuple-element.121.refs_1_, ...), custom_call_target="tpu_custom_call" | custom-call | flops 12650000384 | bytes 1 | tf_op jit(solution)/shard_map/attention_back/pallas_call | solution.py:35
  60.3 1.6 %collective-permute-start.18 = (bf16[2,96,384]{2,1,0:T(8,128)(2,1)S(1)}, bf16[2,96,384]{2,1,0:T(8,128)(2,1)S(1)}, u32[]{:S(2)}, u32[]{:S(2)}) collective-permute-start(bf16[2,96,384]{2,1,0:T(8,128)(2,1)S(1)} %get-tuple-element.138), channel_id=1, source_target_pairs={{0,4},{2,6},{4,0},{6,2},{1,5},{3,7},{5,1},{7,3},{8,12},{10,14},{12... | collective-permute-start | bytes 442376 | tf_op jit(solution)/shard_map/ppermute | solution.py:791
  66.8 1.8 %collective-permute-done.19.refs_4_ = bf16[2,96,384]{2,1,0:T(8,128)(2,1)S(1)} collective-permute-done((bf16[2,96,384]{2,1,0:T(8,128)(2,1)S(1)}, bf16[2,96,384]{2,1,0:T(8,128)(2,1)S(1)}, u32[]{:S(2)}, u32[]{:S(2)}) %collective-permute-start.19) | collective-permute-done | bytes 147488 | tf_op jit(solution)/shard_map/ppermute | solution.py:791
  70.6 3.5 %all-to-all-start = ((bf16[4,304,384]{2,1,0:T(8,128)(2,1)}), bf16[4,304,384]{2,1,0:T(8,128)(2,1)S(1)}, u32[]{:S(2)}, u32[]{:S(2)}) async-start(bf16[4,304,384]{2,1,0:T(8,128)(2,1)} %returns.1.refs_0_), calls=%async_computation | async-start | bytes 1867776 | tf_op jit(solution)/shard_map/all_to_all | solution.py:803
  75.0 2.2 %collective-permute-start.24 = (bf16[1,96,384]{2,1,0:T(8,128)(2,1)S(1)}, bf16[1,96,384]{2,1,0:T(8,128)(2,1)S(1)}, u32[]{:S(2)}, u32[]{:S(2)}) collective-permute-start(bf16[1,96,384]{2,1,0:T(8,128)(2,1)S(1)} %get-tuple-element.150), channel_id=1, source_target_pairs={{0,16},{8,24},{16,0},{24,8},{1,17},{9,25},{17,1},{25,9},{2,18},{10... | collective-permute-start | bytes 221192 | tf_op jit(solution)/shard_map/ppermute | solution.py:820
  77.2 1.9 %collective-permute-start.25 = (bf16[160,128]{1,0:T(8,128)(2,1)S(1)}, bf16[160,128]{1,0:T(8,128)(2,1)S(1)}, u32[]{:S(2)}, u32[]{:S(2)}) collective-permute-start(bf16[160,128]{1,0:T(8,128)(2,1)S(1)} %get-tuple-element.151), channel_id=1, source_target_pairs={{0,8},{8,0},{16,24},{24,16},{1,9},{9,1},{17,25},{25,17},{2,10},{10... | collective-permute-start | bytes 122888 | tf_op jit(solution)/shard_map/ppermute | solution.py:647
  79.2 2.4 %collective-permute-start.27 = (bf16[160,128]{1,0:T(8,128)(2,1)S(1)}, bf16[160,128]{1,0:T(8,128)(2,1)S(1)}, u32[]{:S(2)}, u32[]{:S(2)}) collective-permute-start(bf16[160,128]{1,0:T(8,128)(2,1)S(1)} %get-tuple-element.153), channel_id=1, source_target_pairs={{0,24},{8,16},{16,8},{24,0},{1,25},{9,17},{17,9},{25,1},{2,26},{10... | collective-permute-start | bytes 122888 | tf_op jit(solution)/shard_map/ppermute | solution.py:647
  81.6 2.4 %collective-permute-done.26.refs_4_ = bf16[160,128]{1,0:T(8,128)(2,1)S(1)} collective-permute-done((bf16[160,128]{1,0:T(8,128)(2,1)S(1)}, bf16[160,128]{1,0:T(8,128)(2,1)S(1)}, u32[]{:S(2)}, u32[]{:S(2)}) %collective-permute-start.26) | collective-permute-done | bytes 40992 | tf_op jit(solution)/shard_map/ppermute | solution.py:647
  85.4 2.1 %collective-permute-start.31 = (bf16[160,384]{1,0:T(8,128)(2,1)S(1)}, bf16[160,384]{1,0:T(8,128)(2,1)S(1)}, u32[]{:S(2)}, u32[]{:S(2)}) collective-permute-start(bf16[160,384]{1,0:T(8,128)(2,1)S(1)} %sum_dp.1.refs_0_.refs_1_), channel_id=1, source_target_pairs={{0,6},{2,4},{4,2},{6,0},{1,7},{3,5},{5,3},{7,1},{8,14},{10,12},{12... | collective-permute-start | bytes 368648 | tf_op jit(solution)/shard_map/ppermute | solution.py:647
  89.0 2.7 %place_slots.1 = (f32[1160,384]{1,0:T(8,128)}, f32[1160,384]{1,0:T(8,128)}, f32[8,128]{1,0:T(8,128)S(1)}) custom-call(bf16[4,304,384]{2,1,0:T(8,128)(2,1)S(1)} %hand_on.1.refs_0_, bf16[4,304,384]{2,1,0:T(8,128)(2,1)S(1)} %collective-permute-done.28.refs_1_, f32[2,8,384]{2,1,0:T(8,128)S(1)} %get-tuple-element.154.refs_2_, s32[8,145]{1,0:T(8,128)S(1)} %copy-done.4), custom_call_target="tpu_custom_call" | custom-call | flops 2644999936 | bytes 1 | tf_op jit(solution)/shard_map/place_slots/pallas_call | solution.py:35
  92.5 2.2 %collective-permute-done.30.refs_3_ = bf16[160,384]{1,0:T(8,128)(2,1)S(1)} collective-permute-done((bf16[160,384]{1,0:T(8,128)(2,1)S(1)}, bf16[160,384]{1,0:T(8,128)(2,1)S(1)}, u32[]{:S(2)}, u32[]{:S(2)}) %collective-permute-start.30) | collective-permute-done | bytes 122912 | tf_op jit(solution)/shard_map/ppermute | solution.py:647
  (75 shorter events, 24.0 us)
Async XLA Ops:
  2.9 12.1 %collective-permute-start.5 = (bf16[1,96,384]{2,1,0:T(8,128)(2,1)}, bf16[1,96,384]{2,1,0:T(8,128)(2,1)S(1)}, u32[]{:S(2)}, u32[]{:S(2)}) collective-permute-start(bf16[1,96,384]{2,1,0:T(8,128)(2,1)} %bitcast.20), channel_id=1, source_target_pairs={{0,16},{8,24},{16,0},{24,8},{1,17},{9,25},{17,1},{25,9},{2,18},{10... | collective-permute-start | bytes 221192 | tf_op jit(solution)/shard_map/ppermute | solution.py:687
  7.0 11.6 %collective-permute-start.3 = (bf16[1,112,768]{2,1,0:T(8,128)(2,1)}, bf16[1,112,768]{2,1,0:T(8,128)(2,1)S(1)}, u32[]{:S(2)}, u32[]{:S(2)}) collective-permute-start(bf16[1,112,768]{2,1,0:T(8,128)(2,1)} %bitcast.18), channel_id=1, source_target_pairs={{0,16},{8,24},{16,0},{24,8},{1,17},{9,25},{17,1},{25,9},{2,18},{10... | collective-permute-start | bytes 516104 | tf_op jit(solution)/shard_map/ppermute | solution.py:687
  8.6 13.2 %collective-permute-start = (bf16[304,384]{1,0:T(8,128)(2,1)S(1)}, bf16[304,384]{1,0:T(8,128)(2,1)S(1)}, u32[]{:S(2)}, u32[]{:S(2)}) collective-permute-start(bf16[304,384]{1,0:T(8,128)(2,1)S(1)} %get-tuple-element.96), channel_id=1, source_target_pairs={{0,2},{2,0},{4,6},{6,4},{1,3},{3,1},{5,7},{7,5},{8,10},{10,8},{12,... | collective-permute-start | bytes 700424 | tf_op jit(solution)/shard_map/ppermute | solution.py:647
  10.4 11.6 %collective-permute-start.1 = (bf16[304,384]{1,0:T(8,128)(2,1)S(1)}, bf16[304,384]{1,0:T(8,128)(2,1)S(1)}, u32[]{:S(2)}, u32[]{:S(2)}) collective-permute-start(bf16[304,384]{1,0:T(8,128)(2,1)S(1)} %get-tuple-element.97), channel_id=1, source_target_pairs={{0,4},{2,6},{4,0},{6,2},{1,5},{3,7},{5,1},{7,3},{8,12},{10,14},{12... | collective-permute-start | bytes 700424 | tf_op jit(solution)/shard_map/ppermute | solution.py:647
  11.9 10.1 %collective-permute-start.2 = (bf16[304,384]{1,0:T(8,128)(2,1)S(1)}, bf16[304,384]{1,0:T(8,128)(2,1)S(1)}, u32[]{:S(2)}, u32[]{:S(2)}) collective-permute-start(bf16[304,384]{1,0:T(8,128)(2,1)S(1)} %get-tuple-element.98), channel_id=1, source_target_pairs={{0,6},{2,4},{4,2},{6,0},{1,7},{3,5},{5,3},{7,1},{8,14},{10,12},{12... | collective-permute-start | bytes 700424 | tf_op jit(solution)/shard_map/ppermute | solution.py:647
  15.1 6.8 %collective-permute-start.6 = (bf16[2,96,384]{2,1,0:T(8,128)(2,1)S(1)}, bf16[2,96,384]{2,1,0:T(8,128)(2,1)S(1)}, u32[]{:S(2)}, u32[]{:S(2)}) collective-permute-start(bf16[2,96,384]{2,1,0:T(8,128)(2,1)S(1)} %join_quarter.1.refs_4_), channel_id=1, source_target_pairs={{0,8},{8,0},{16,24},{24,16},{1,9},{9,1},{17,25},{25,17},{2,10},{10... | collective-permute-start | bytes 442376 | tf_op jit(solution)/shard_map/ppermute | solution.py:689
  18.7 10.4 %collective-permute-start.4 = (bf16[2,112,768]{2,1,0:T(8,128)(2,1)S(1)}, bf16[2,112,768]{2,1,0:T(8,128)(2,1)S(1)}, u32[]{:S(2)}, u32[]{:S(2)}) collective-permute-start(bf16[2,112,768]{2,1,0:T(8,128)(2,1)S(1)} %join_attn.1.refs_3_.refs_4_), channel_id=1, source_target_pairs={{0,8},{8,0},{16,24},{24,16},{1,9},{9,1},{17,25},{25,17},{2,10},{10... | collective-permute-start | bytes 1032200 | tf_op jit(solution)/shard_map/ppermute | solution.py:689
  22.1 6.9 %collective-permute-start.7 = (bf16[2,112,768]{2,1,0:T(8,128)(2,1)S(1)}, bf16[2,112,768]{2,1,0:T(8,128)(2,1)S(1)}, u32[]{:S(2)}, u32[]{:S(2)}) collective-permute-start(bf16[2,112,768]{2,1,0:T(8,128)(2,1)S(1)} %get-tuple-element.101), channel_id=1, source_target_pairs={{0,1},{1,0},{2,3},{3,2},{4,5},{5,4},{6,7},{7,6},{8,9},{9,8},{10,11... | collective-permute-start | bytes 1032200 | tf_op jit(solution)/shard_map/ppermute | solution.py:671
  22.2 14.5 %collective-permute-start.12 = (bf16[384,384]{1,0:T(8,128)(2,1)S(1)}, bf16[384,384]{1,0:T(8,128)(2,1)S(1)}, u32[]{:S(2)}, u32[]{:S(2)}) collective-permute-start(bf16[384,384]{1,0:T(8,128)(2,1)S(1)} %get-tuple-element.102.refs_1_), channel_id=1, source_target_pairs={{0,6},{2,4},{4,2},{6,0},{1,7},{3,5},{5,3},{7,1},{8,14},{10,12},{12... | collective-permute-start | bytes 884744 | tf_op jit(solution)/shard_map/ppermute | solution.py:647
  25.1 13.9 %collective-permute-start.11 = (bf16[384,384]{1,0:T(8,128)(2,1)S(1)}, bf16[384,384]{1,0:T(8,128)(2,1)S(1)}, u32[]{:S(2)}, u32[]{:S(2)}) collective-permute-start(bf16[384,384]{1,0:T(8,128)(2,1)S(1)} %get-tuple-element.102.refs_1_), channel_id=1, source_target_pairs={{0,4},{2,6},{4,0},{6,2},{1,5},{3,7},{5,1},{7,3},{8,12},{10,14},{12... | collective-permute-start | bytes 884744 | tf_op jit(solution)/shard_map/ppermute | solution.py:647
  25.6 13.7 %collective-permute-start.10 = (bf16[384,384]{1,0:T(8,128)(2,1)S(1)}, bf16[384,384]{1,0:T(8,128)(2,1)S(1)}, u32[]{:S(2)}, u32[]{:S(2)}) collective-permute-start(bf16[384,384]{1,0:T(8,128)(2,1)S(1)} %get-tuple-element.102.refs_1_), channel_id=1, source_target_pairs={{0,2},{2,0},{4,6},{6,4},{1,3},{3,1},{5,7},{7,5},{8,10},{10,8},{12,... | collective-permute-start | bytes 884744 | tf_op jit(solution)/shard_map/ppermute | solution.py:647
  49.2 10.9 %collective-permute-start.15 = (bf16[2,2,96,384]{3,2,1,0:T(8,128)(2,1)S(1)}, bf16[2,2,96,384]{3,2,1,0:T(8,128)(2,1)S(1)}, u32[]{:S(2)}, u32[]{:S(2)}) collective-permute-start(bf16[2,2,96,384]{3,2,1,0:T(8,128)(2,1)S(1)} %get-tuple-element.132), channel_id=1, source_target_pairs={{0,2},{2,0},{4,6},{6,4},{1,3},{3,1},{5,7},{7,5},{8,10},{10,8},{12,... | collective-permute-start | bytes 884744 | tf_op jit(solution)/shard_map/ppermute | solution.py:778
  50.8 9.4 %collective-permute-start.16 = (bf16[2,2,96,384]{3,2,1,0:T(8,128)(2,1)S(1)}, bf16[2,2,96,384]{3,2,1,0:T(8,128)(2,1)S(1)}, u32[]{:S(2)}, u32[]{:S(2)}) collective-permute-start(bf16[2,2,96,384]{3,2,1,0:T(8,128)(2,1)S(1)} %get-tuple-element.134), channel_id=1, source_target_pairs={{0,4},{2,6},{4,0},{6,2},{1,5},{3,7},{5,1},{7,3},{8,12},{10,14},{12... | collective-permute-start | bytes 884744 | tf_op jit(solution)/shard_map/ppermute | solution.py:778
  60.3 6.5 %collective-permute-start.18 = (bf16[2,96,384]{2,1,0:T(8,128)(2,1)S(1)}, bf16[2,96,384]{2,1,0:T(8,128)(2,1)S(1)}, u32[]{:S(2)}, u32[]{:S(2)}) collective-permute-start(bf16[2,96,384]{2,1,0:T(8,128)(2,1)S(1)} %get-tuple-element.138), channel_id=1, source_target_pairs={{0,4},{2,6},{4,0},{6,2},{1,5},{3,7},{5,1},{7,3},{8,12},{10,14},{12... | collective-permute-start | bytes 442376 | tf_op jit(solution)/shard_map/ppermute | solution.py:791
  61.9 6.7 %collective-permute-start.19 = (bf16[2,96,384]{2,1,0:T(8,128)(2,1)S(1)}, bf16[2,96,384]{2,1,0:T(8,128)(2,1)S(1)}, u32[]{:S(2)}, u32[]{:S(2)}) collective-permute-start(bf16[2,96,384]{2,1,0:T(8,128)(2,1)S(1)} %get-tuple-element.140), channel_id=1, source_target_pairs={{0,2},{2,0},{4,6},{6,4},{1,3},{3,1},{5,7},{7,5},{8,10},{10,8},{12,... | collective-permute-start | bytes 442376 | tf_op jit(solution)/shard_map/ppermute | solution.py:791
  62.6 11.5 %collective-permute-start.20 = (bf16[4,160,128]{2,1,0:T(8,128)(2,1)S(1)}, bf16[4,160,128]{2,1,0:T(8,128)(2,1)S(1)}, u32[]{:S(2)}, u32[]{:S(2)}) collective-permute-start(bf16[4,160,128]{2,1,0:T(8,128)(2,1)S(1)} %get-tuple-element.144), channel_id=1, source_target_pairs={{0,2},{2,0},{4,6},{6,4},{1,3},{3,1},{5,7},{7,5},{8,10},{10,8},{12,... | collective-permute-start | bytes 491528 | tf_op jit(solution)/shard_map/ppermute | solution.py:647
  64.1 10.0 %collective-permute-start.21 = (bf16[4,160,128]{2,1,0:T(8,128)(2,1)S(1)}, bf16[4,160,128]{2,1,0:T(8,128)(2,1)S(1)}, u32[]{:S(2)}, u32[]{:S(2)}) collective-permute-start(bf16[4,160,128]{2,1,0:T(8,128)(2,1)S(1)} %get-tuple-element.145), channel_id=1, source_target_pairs={{0,4},{2,6},{4,0},{6,2},{1,5},{3,7},{5,1},{7,3},{8,12},{10,14},{12... | collective-permute-start | bytes 491528 | tf_op jit(solution)/shard_map/ppermute | solution.py:647
  64.7 10.1 %collective-permute-start.22 = (bf16[4,160,128]{2,1,0:T(8,128)(2,1)S(1)}, bf16[4,160,128]{2,1,0:T(8,128)(2,1)S(1)}, u32[]{:S(2)}, u32[]{:S(2)}) collective-permute-start(bf16[4,160,128]{2,1,0:T(8,128)(2,1)S(1)} %get-tuple-element.146), channel_id=1, source_target_pairs={{0,6},{2,4},{4,2},{6,0},{1,7},{3,5},{5,3},{7,1},{8,14},{10,12},{12... | collective-permute-start | bytes 491528 | tf_op jit(solution)/shard_map/ppermute | solution.py:647
  68.7 6.2 %collective-permute-start.23 = (bf16[2,96,384]{2,1,0:T(8,128)(2,1)S(1)}, bf16[2,96,384]{2,1,0:T(8,128)(2,1)S(1)}, u32[]{:S(2)}, u32[]{:S(2)}) collective-permute-start(bf16[2,96,384]{2,1,0:T(8,128)(2,1)S(1)} %get-tuple-element.148), channel_id=1, source_target_pairs={{0,8},{8,0},{16,24},{24,16},{1,9},{9,1},{17,25},{25,17},{2,10},{10... | collective-permute-start | bytes 442376 | tf_op jit(solution)/shard_map/ppermute | solution.py:816
  70.6 14.6 %all-to-all-start = ((bf16[4,304,384]{2,1,0:T(8,128)(2,1)}), bf16[4,304,384]{2,1,0:T(8,128)(2,1)S(1)}, u32[]{:S(2)}, u32[]{:S(2)}) async-start(bf16[4,304,384]{2,1,0:T(8,128)(2,1)} %returns.1.refs_0_), calls=%async_computation | async-start | bytes 1867776 | tf_op jit(solution)/shard_map/all_to_all | solution.py:803
  75.0 10.0 %collective-permute-start.24 = (bf16[1,96,384]{2,1,0:T(8,128)(2,1)S(1)}, bf16[1,96,384]{2,1,0:T(8,128)(2,1)S(1)}, u32[]{:S(2)}, u32[]{:S(2)}) collective-permute-start(bf16[1,96,384]{2,1,0:T(8,128)(2,1)S(1)} %get-tuple-element.150), channel_id=1, source_target_pairs={{0,16},{8,24},{16,0},{24,8},{1,17},{9,25},{17,1},{25,9},{2,18},{10... | collective-permute-start | bytes 221192 | tf_op jit(solution)/shard_map/ppermute | solution.py:820
  85.4 7.1 %collective-permute-start.31 = (bf16[160,384]{1,0:T(8,128)(2,1)S(1)}, bf16[160,384]{1,0:T(8,128)(2,1)S(1)}, u32[]{:S(2)}, u32[]{:S(2)}) collective-permute-start(bf16[160,384]{1,0:T(8,128)(2,1)S(1)} %sum_dp.1.refs_0_.refs_1_), channel_id=1, source_target_pairs={{0,6},{2,4},{4,2},{6,0},{1,7},{3,5},{5,3},{7,1},{8,14},{10,12},{12... | collective-permute-start | bytes 368648 | tf_op jit(solution)/shard_map/ppermute | solution.py:647
  87.5 7.2 %collective-permute-start.30 = (bf16[160,384]{1,0:T(8,128)(2,1)S(1)}, bf16[160,384]{1,0:T(8,128)(2,1)S(1)}, u32[]{:S(2)}, u32[]{:S(2)}) collective-permute-start(bf16[160,384]{1,0:T(8,128)(2,1)S(1)} %sum_dp.1.refs_0_.refs_1_), channel_id=1, source_target_pairs={{0,4},{2,6},{4,0},{6,2},{1,5},{3,7},{5,1},{7,3},{8,12},{10,14},{12... | collective-permute-start | bytes 368648 | tf_op jit(solution)/shard_map/ppermute | solution.py:647
  88.4 6.4 %collective-permute-start.29 = (bf16[160,384]{1,0:T(8,128)(2,1)S(1)}, bf16[160,384]{1,0:T(8,128)(2,1)S(1)}, u32[]{:S(2)}, u32[]{:S(2)}) collective-permute-start(bf16[160,384]{1,0:T(8,128)(2,1)S(1)} %sum_dp.1.refs_0_.refs_1_), channel_id=1, source_target_pairs={{0,2},{2,0},{4,6},{6,4},{1,3},{3,1},{5,7},{7,5},{8,10},{10,8},{12,... | collective-permute-start | bytes 368648 | tf_op jit(solution)/shard_map/ppermute | solution.py:647
  (14 other events, 64.8 us)

commit v7 on v6

--- a/solution.py
+++ b/solution.py
@@ -333,34 +333,21 @@
     n2_out[...] = (xhat2 * vec_sum[3:4, :] + vec_sum[4:5, :]).astype(BF)
 
 
-def ff_half(n2v, dcot, w, ub, hid, hgr, ubgrad, grads, ndp, rows):
+def mlp_half_kernel(sizes, side, n2, cot, w, ub, hid, hgr, ubgrad, grads):
+    nctx, ntp, ndp, main, width, rows, padded = sizes
     half = w.shape[1] // 2
-    quarter = half // 2
-    for lo in range(0, half, 256):
-        sl = slice(lo, lo + 256)
-        pre = nn(n2v, w[:, sl]) + ub[0:1, sl]
-        hc = nn(dcot, w[:, half + lo : half + lo + 256])
-        act, slope = gelu_pair(pre)
-        h = act.astype(BF)
-        hg = (hc * slope).astype(BF)
-        hid[:, sl] = h
-        hgr[:, sl] = hg
-        ubgrad[:, sl] = jnp.broadcast_to(jnp.sum(hg.astype(F32), axis=0, keepdims=True), (8, 256))
-        for part, g in ((0, tn(n2v, hg).astype(BF)), (1, tn(dcot, h).astype(BF))):
-            for d in range(ndp):
-                for c in range(2):
-                    col = lo + c * TILE
-                    at = slice(col % quarter, col % quarter + TILE)
-                    grads[2 * part + col // quarter, d, 0:rows, at] = (
-                        g[d * rows : (d + 1) * rows, c * TILE : (c + 1) * TILE]
-                    )
-
-
-def mlp_half_kernel(sizes, side, n2, cot, w, ub, hid, hgr, ubgrad, grads):
-    half = w.shape[1] // 2
-    ff_half(
-        n2[...], cot[...], w[...], ub[:, side * half : (side + 1) * half], hid, hgr, ubgrad, grads, sizes[2], sizes[5]
-    )
+    n2v, dcot = n2[...], cot[...]
+    act, slope = gelu_pair(nn(n2v, w[:, :half]) + ub[0:1, side * half : (side + 1) * half])
+    h = act.astype(BF)
+    hg = (nn(dcot, w[:, half:]) * slope).astype(BF)
+    hid[...] = h
+    hgr[...] = hg
+    ubgrad[...] = jnp.broadcast_to(jnp.sum(hg.astype(F32), axis=0, keepdims=True), ubgrad.shape)
+    cols = grads.shape[3]
+    for part, g in ((0, tn(n2v, hg).astype(BF)), (1, tn(dcot, h).astype(BF))):
+        for d in range(ndp):
+            for c in range(half // cols):
+                grads[2 * part + c, d, 0:rows, :] = g[d * rows : (d + 1) * rows, c * cols : (c + 1) * cols]
 
 
 def mlp_sums_kernel(sizes, mid, ctx, wot, vec, cot, w_own, w_oth, hid_own, hid_oth, hgr_own, hgr_oth, bo, dmid, dctx, g_out, vgrad):
@@ -401,18 +388,21 @@
     both = dp.astype(F32) * ctx[:, at]
     qt = jnp.transpose(qp.astype(F32)).astype(BF)
     dt = jnp.transpose(dp.astype(F32)).astype(BF)
-    dq, dk, dv = [], [], []
+    dk, dv = [], []
+    zero = jnp.zeros_like(qp)
+    qs = jnp.concatenate([jnp.where(low, qp, zero), jnp.where(low, zero, qp)], axis=0)
+    ds_ = jnp.concatenate([jnp.where(low, dp, zero), jnp.where(low, zero, dp)], axis=0)
+    bs = jnp.concatenate([jnp.where(low, both, 0.0), jnp.where(low, 0.0, both)], axis=0)
+    inner = jnp.sum(bs, axis=-1, keepdims=True)
+    ls = jnp.concatenate([lse[:, 2 * p : 2 * p + 1], lse[:, 2 * p + 1 : 2 * p + 2]], axis=0)
+    prob = jnp.exp(nt(qs, kp) + off - ls)
+    ds = (prob * (nt(ds_, vp) - inner)).astype(BF)
+    w = prob.astype(BF)
+    dq = nn(ds, kp)
+    dq = jnp.where(low, dq[0:total], dq[total:]) * SCALE
     for a in range(2):
-        sel = low if a == 0 else ~low
-        qa = jnp.where(sel, qp, jnp.zeros_like(qp))
-        da = jnp.where(sel, dp, jnp.zeros_like(dp))
-        inner = jnp.sum(jnp.where(sel, both, 0.0), axis=-1, keepdims=True)
-        prob = jnp.exp(nt(qa, kp) + off - lse[:, 2 * p + a : 2 * p + a + 1])
-        ds = (prob * (nt(da, vp) - inner)).astype(BF)
-        dq.append(nn(ds, kp))
-        dk.append(nn(qt[a * HD : (a + 1) * HD], ds))
-        dv.append(nn(dt[a * HD : (a + 1) * HD], prob.astype(BF)))
-    dq = jnp.where(low, dq[0], dq[1]) * SCALE
+        dk.append(nn(qt[a * HD : (a + 1) * HD], ds[a * total : (a + 1) * total]))
+        dv.append(nn(dt[a * HD : (a + 1) * HD], w[a * total : (a + 1) * total]))
     dk, dv = (jnp.transpose(jnp.concatenate(v, axis=0))[0:total] for v in (dk, dv))
     return dq.astype(BF), dk.astype(BF), dv.astype(BF)
 

time: 96.1 us -> 94.7 us (0.985)
  Pallas kernels: 33.2 us -> 31.5 us
    pallas_call x23, Pallas kernels: 33.2 us -> 31.5 us  [run(): pl.pallas_call(ordered, name=name, out_shape=out_shape, in_specs=specs, o...]
  transfers between devices with their start and end apart: 33 -> 33, of which waited for: 19 -> 20; matrix products, arithmetic and copies ran while one was open for 0% -> 0% of each run, Pallas kernels for 28% -> 27%
where the time goes in v7:
time: 94.7 us; the launch traced here: 94.5 us
  starting transfers between devices  36.1 us (38%)
  Pallas kernels  31.5 us (33%)
  waiting for transfers between devices  25.9 us (27%)
  between operations  1.01 us (1%)
    pallas_call x23, Pallas kernels, run(): pl.pallas_call(ordered, name=name, out_shape=out_shape, in_specs=specs, o...  31.5 us
    ppermute x15, starting transfers between devices, over(): lax.ppermute(items[k], axis, xor(n, k))  18.6 us
    ppermute x15, waiting for transfers between devices, over(): lax.ppermute(items[k], axis, xor(n, k))  9.96 us
    ppermute x2, waiting for transfers between devices, gather_dp(): return (v, lax.ppermute(v, 'dp', xor(ndp, 1)))  5.72 us
    ppermute x2, waiting for transfers between devices, gather_dp(): lax.ppermute(v, 'dp', xor(ndp, stride))  5.68 us
    ppermute x2, starting transfers between devices, gather_dp(): lax.ppermute(v, 'dp', xor(ndp, stride))  4.18 us
    all_to_all x1, starting transfers between devices, body(): returned = lax.all_to_all(back, 'ctx', 0, 0)  3.51 us
    ppermute x1, starting transfers between devices, body(): lax.ppermute(send, 'dp', xor(ndp, ndp // 2))  2.23 us
  transfers between devices with their start and end apart: 33, of which 20 were waited for; matrix products, arithmetic and copies ran while one was open for 0% of the time, Pallas kernels for 27%

profile of v7, /device:TPU:0, one launch (start us, length us, event | category | flops | bytes accessed | tf_op | source)
XLA Modules:
  0.0 94.5 jit_solution(6885563990952559221)
XLA Ops:
  0.7 2.2 %pack_weights.1 = (bf16[112,768]{1,0:T(8,128)(2,1)}, bf16[96,384]{1,0:T(8,128)(2,1)}, f32[8,128]{1,0:T(8,128)}) custom-call(bf16[96,192]{1,0:T(8,128)(2,1)} %refs_0_.1, bf16[96,192]{1,0:T(8,128)(2,1)} %refs_1_.1, bf16[96,192]{1,0:T(8,128)(2,1)} %refs_2_.3, bf16[192,96]{1,0:T(8,128)(2,1)} %refs_3_.2, bf16[96,768]{1,0:T(8,128)(2,1)} %refs_4_.1, ...), custom_call_target="tpu_custom_call" | custom-call | flops 2300000000 | bytes 1 | tf_op jit(solution)/shard_map/pack_weights/pallas_call | solution.py:35
  2.9 4.1 %collective-permute-start.5 = (bf16[1,96,384]{2,1,0:T(8,128)(2,1)}, bf16[1,96,384]{2,1,0:T(8,128)(2,1)S(1)}, u32[]{:S(2)}, u32[]{:S(2)}) collective-permute-start(bf16[1,96,384]{2,1,0:T(8,128)(2,1)} %bitcast.20), channel_id=1, source_target_pairs={{0,16},{8,24},{16,0},{24,8},{1,17},{9,25},{17,1},{25,9},{2,18},{10... | collective-permute-start | bytes 221192 | tf_op jit(solution)/shard_map/ppermute | solution.py:677
  8.6 1.8 %collective-permute-start = (bf16[304,384]{1,0:T(8,128)(2,1)S(1)}, bf16[304,384]{1,0:T(8,128)(2,1)S(1)}, u32[]{:S(2)}, u32[]{:S(2)}) collective-permute-start(bf16[304,384]{1,0:T(8,128)(2,1)S(1)} %get-tuple-element.96), channel_id=1, source_target_pairs={{0,2},{2,0},{4,6},{6,4},{1,3},{3,1},{5,7},{7,5},{8,10},{10,8},{12,... | collective-permute-start | bytes 700424 | tf_op jit(solution)/shard_map/ppermute | solution.py:637
  12.2 2.8 %collective-permute-done.5.refs_1_ = bf16[1,96,384]{2,1,0:T(8,128)(2,1)S(1)} collective-permute-done((bf16[1,96,384]{2,1,0:T(8,128)(2,1)}, bf16[1,96,384]{2,1,0:T(8,128)(2,1)S(1)}, u32[]{:S(2)}, u32[]{:S(2)}) %collective-permute-start.5) | collective-permute-done | bytes 73760 | tf_op jit(solution)/shard_map/ppermute | solution.py:677
  15.8 2.8 %collective-permute-done.3.refs_1_ = bf16[1,112,768]{2,1,0:T(8,128)(2,1)S(1)} collective-permute-done((bf16[1,112,768]{2,1,0:T(8,128)(2,1)}, bf16[1,112,768]{2,1,0:T(8,128)(2,1)S(1)}, u32[]{:S(2)}, u32[]{:S(2)}) %collective-permute-start.3) | collective-permute-done | bytes 172064 | tf_op jit(solution)/shard_map/ppermute | solution.py:677
  19.4 2.4 %collective-permute-done.6.refs_5_ = bf16[2,96,384]{2,1,0:T(8,128)(2,1)S(1)} collective-permute-done((bf16[2,96,384]{2,1,0:T(8,128)(2,1)S(1)}, bf16[2,96,384]{2,1,0:T(8,128)(2,1)S(1)}, u32[]{:S(2)}, u32[]{:S(2)}) %collective-permute-start.6) | collective-permute-done | bytes 147488 | tf_op jit(solution)/shard_map/ppermute | solution.py:679
  22.2 2.9 %collective-permute-start.12 = (bf16[384,384]{1,0:T(8,128)(2,1)S(1)}, bf16[384,384]{1,0:T(8,128)(2,1)S(1)}, u32[]{:S(2)}, u32[]{:S(2)}) collective-permute-start(bf16[384,384]{1,0:T(8,128)(2,1)S(1)} %get-tuple-element.102.refs_1_), channel_id=1, source_target_pairs={{0,6},{2,4},{4,2},{6,0},{1,7},{3,5},{5,3},{7,1},{8,14},{10,12},{12... | collective-permute-start | bytes 884744 | tf_op jit(solution)/shard_map/ppermute | solution.py:637
  25.8 3.3 %collective-permute-done.4.refs_2_.refs_5_ = bf16[2,112,768]{2,1,0:T(8,128)(2,1)S(1)} collective-permute-done((bf16[2,112,768]{2,1,0:T(8,128)(2,1)S(1)}, bf16[2,112,768]{2,1,0:T(8,128)(2,1)S(1)}, u32[]{:S(2)}, u32[]{:S(2)}) %collective-permute-start.4) | collective-permute-done | bytes 344096 | tf_op jit(solution)/shard_map/ppermute | solution.py:679
  30.8 5.9 %attention.1 = (f32[592,384]{1,0:T(8,128)S(1)}, f32[592,384]{1,0:T(8,128)S(1)}, bf16[592,384]{1,0:T(8,128)(2,1)S(1)}, bf16[592,384]{1,0:T(8,128)(2,1)S(1)}, bf16...) custom-call(bf16[304,384]{1,0:T(8,128)(2,1)S(1)} %get-tuple-element., ...), custom_call_target="tpu_custom_call" | custom-call | bytes 1 | tf_op jit(solution)/shard_map/attention/pallas_call | solution.py:35
  36.7 2.3 %collective-permute-done.11.refs_3_ = bf16[384,384]{1,0:T(8,128)(2,1)S(1)} collective-permute-done((bf16[384,384]{1,0:T(8,128)(2,1)S(1)}, bf16[384,384]{1,0:T(8,128)(2,1)S(1)}, u32[]{:S(2)}, u32[]{:S(2)}) %collective-permute-start.11) | collective-permute-done | bytes 294944 | tf_op jit(solution)/shard_map/ppermute | solution.py:637
  39.5 2.2 %mlp_own.1 = (bf16[592,768]{1,0:T(8,128)(2,1)S(1)}, bf16[592,768]{1,0:T(8,128)(2,1)S(1)}, f32[8,768]{1,0:T(8,128)S(1)}, bf16[4,4,96,384]{3,2,1,0:T(8,128)(2,1)S(1)}) custom-call(bf16[592,384]{1,0:T(8,128)(2,1)S(1)} %get-tuple-element.110.refs_0_.refs_1_, bf16[592,384]{1,0:T(8,128)(2,1)S(1)} %get-tuple-element.109.refs_1_.refs_2_.refs_4_, ...), custom_call_target="tpu_custom_call" | custom-call | flops 4600000000 | bytes 1 | tf_op jit(solution)/shard_map/mlp_own/pallas_call | solution.py:35
  42.4 2.2 %mlp_oth.1 = (bf16[592,768]{1,0:T(8,128)(2,1)S(1)}, bf16[592,768]{1,0:T(8,128)(2,1)S(1)}, f32[8,768]{1,0:T(8,128)S(1)}, bf16[4,4,96,384]{3,2,1,0:T(8,128)(2,1)S(1)}) custom-call(f32[8,768]{1,0:T(8,128)S(1)} %get-tuple-element.113.refs_0_.refs_12_, bf16[592,384]{1,0:T(8,128)(2,1)S(1)} %get-tuple-element.110.refs_0_.refs_1_, ...), custom_call_target="tpu_custom_call" | custom-call | flops 4600000000 | bytes 1 | tf_op jit(solution)/shard_map/mlp_oth/pallas_call | solution.py:35
  44.8 3.2 %mlp_sums.1 = (bf16[592,384]{1,0:T(8,128)(2,1)S(1)}, f32[592,384]{1,0:T(8,128)S(1)}, bf16[592,384]{1,0:T(8,128)(2,1)S(1)}, f32[384,384]{1,0:T(8,128)S(1)}, f32[16,384]{1,0:T(8,128)S(1)}) custom-call(f32[592,384]{1,0:T(8,128)S(1)} %get-tuple-element.105.refs_0_, bf16[592,384]{1,0:T(8,128)(2,1)S(1)} %get-tuple-element.106.refs_1_, ...), custom_call_target="tpu_custom_call" | custom-call | flops 2300000000 | bytes 1 | tf_op jit(solution)/shard_map/mlp_sums/pallas_call | solution.py:35
  48.3 1.6 %collective-permute-start.15 = (bf16[2,2,96,384]{3,2,1,0:T(8,128)(2,1)S(1)}, bf16[2,2,96,384]{3,2,1,0:T(8,128)(2,1)S(1)}, u32[]{:S(2)}, u32[]{:S(2)}) collective-permute-start(bf16[2,2,96,384]{3,2,1,0:T(8,128)(2,1)S(1)} %get-tuple-element.132), channel_id=1, source_target_pairs={{0,2},{2,0},{4,6},{6,4},{1,3},{3,1},{5,7},{7,5},{8,10},{10,8},{12,... | collective-permute-start | bytes 884744 | tf_op jit(solution)/shard_map/ppermute | solution.py:768
  50.4 8.2 %attention_back.1 = (bf16[592,384]{1,0:T(8,128)(2,1)S(1)}, bf16[4,4,160,128]{3,2,1,0:T(8,128)(2,1)S(1)}, bf16[4,4,160,128]{3,2,1,0:T(8,128)(2,1)S(1)}) custom-call(bf16[2,2,96,384]{3,2,1,0:T(8,128)(2,1)S(1)} %get-tuple-element.120.refs_0_.refs_1_, bf16[640,1152]{1,0:T(8,128)(2,1)S(1)} %get-tuple-element.121.refs_1_, ...), custom_call_target="tpu_custom_call" | custom-call | flops 12650000384 | bytes 1 | tf_op jit(solution)/shard_map/attention_back/pallas_call | solution.py:35
  65.3 1.8 %collective-permute-done.19.refs_4_ = bf16[2,96,384]{2,1,0:T(8,128)(2,1)S(1)} collective-permute-done((bf16[2,96,384]{2,1,0:T(8,128)(2,1)S(1)}, bf16[2,96,384]{2,1,0:T(8,128)(2,1)S(1)}, u32[]{:S(2)}, u32[]{:S(2)}) %collective-permute-start.19) | collective-permute-done | bytes 147488 | tf_op jit(solution)/shard_map/ppermute | solution.py:781
  69.2 3.5 %all-to-all-start = ((bf16[4,304,384]{2,1,0:T(8,128)(2,1)}), bf16[4,304,384]{2,1,0:T(8,128)(2,1)S(1)}, u32[]{:S(2)}, u32[]{:S(2)}) async-start(bf16[4,304,384]{2,1,0:T(8,128)(2,1)} %returns.1.refs_0_), calls=%async_computation | async-start | bytes 1867776 | tf_op jit(solution)/shard_map/all_to_all | solution.py:793
  73.5 2.2 %collective-permute-start.24 = (bf16[1,96,384]{2,1,0:T(8,128)(2,1)S(1)}, bf16[1,96,384]{2,1,0:T(8,128)(2,1)S(1)}, u32[]{:S(2)}, u32[]{:S(2)}) collective-permute-start(bf16[1,96,384]{2,1,0:T(8,128)(2,1)S(1)} %get-tuple-element.150), channel_id=1, source_target_pairs={{0,16},{8,24},{16,0},{24,8},{1,17},{9,25},{17,1},{25,9},{2,18},{10... | collective-permute-start | bytes 221192 | tf_op jit(solution)/shard_map/ppermute | solution.py:810
  75.8 1.9 %collective-permute-start.25 = (bf16[160,128]{1,0:T(8,128)(2,1)S(1)}, bf16[160,128]{1,0:T(8,128)(2,1)S(1)}, u32[]{:S(2)}, u32[]{:S(2)}) collective-permute-start(bf16[160,128]{1,0:T(8,128)(2,1)S(1)} %get-tuple-element.151), channel_id=1, source_target_pairs={{0,8},{8,0},{16,24},{24,16},{1,9},{9,1},{17,25},{25,17},{2,10},{10... | collective-permute-start | bytes 122888 | tf_op jit(solution)/shard_map/ppermute | solution.py:637
  77.7 2.4 %collective-permute-start.27 = (bf16[160,128]{1,0:T(8,128)(2,1)S(1)}, bf16[160,128]{1,0:T(8,128)(2,1)S(1)}, u32[]{:S(2)}, u32[]{:S(2)}) collective-permute-start(bf16[160,128]{1,0:T(8,128)(2,1)S(1)} %get-tuple-element.153), channel_id=1, source_target_pairs={{0,24},{8,16},{16,8},{24,0},{1,25},{9,17},{17,9},{25,1},{2,26},{10... | collective-permute-start | bytes 122888 | tf_op jit(solution)/shard_map/ppermute | solution.py:637
  80.2 2.4 %collective-permute-done.26.refs_4_ = bf16[160,128]{1,0:T(8,128)(2,1)S(1)} collective-permute-done((bf16[160,128]{1,0:T(8,128)(2,1)S(1)}, bf16[160,128]{1,0:T(8,128)(2,1)S(1)}, u32[]{:S(2)}, u32[]{:S(2)}) %collective-permute-start.26) | collective-permute-done | bytes 40992 | tf_op jit(solution)/shard_map/ppermute | solution.py:637
  84.0 2.1 %collective-permute-start.31 = (bf16[160,384]{1,0:T(8,128)(2,1)S(1)}, bf16[160,384]{1,0:T(8,128)(2,1)S(1)}, u32[]{:S(2)}, u32[]{:S(2)}) collective-permute-start(bf16[160,384]{1,0:T(8,128)(2,1)S(1)} %sum_dp.1.refs_0_.refs_1_), channel_id=1, source_target_pairs={{0,6},{2,4},{4,2},{6,0},{1,7},{3,5},{5,3},{7,1},{8,14},{10,12},{12... | collective-permute-start | bytes 368648 | tf_op jit(solution)/shard_map/ppermute | solution.py:637
  87.5 2.7 %place_slots.1 = (f32[1160,384]{1,0:T(8,128)}, f32[1160,384]{1,0:T(8,128)}, f32[8,128]{1,0:T(8,128)S(1)}) custom-call(bf16[4,304,384]{2,1,0:T(8,128)(2,1)S(1)} %hand_on.1.refs_0_, bf16[4,304,384]{2,1,0:T(8,128)(2,1)S(1)} %collective-permute-done.28.refs_1_, f32[2,8,384]{2,1,0:T(8,128)S(1)} %get-tuple-element.154.refs_2_, s32[8,145]{1,0:T(8,128)S(1)} %copy-done.4), custom_call_target="tpu_custom_call" | custom-call | flops 2644999936 | bytes 1 | tf_op jit(solution)/shard_map/place_slots/pallas_call | solution.py:35
  91.0 2.2 %collective-permute-done.30.refs_3_ = bf16[160,384]{1,0:T(8,128)(2,1)S(1)} collective-permute-done((bf16[160,384]{1,0:T(8,128)(2,1)S(1)}, bf16[160,384]{1,0:T(8,128)(2,1)S(1)}, u32[]{:S(2)}, u32[]{:S(2)}) %collective-permute-start.30) | collective-permute-done | bytes 122912 | tf_op jit(solution)/shard_map/ppermute | solution.py:637
  (75 shorter events, 24.3 us)
Async XLA Ops:
  2.9 12.1 %collective-permute-start.5 = (bf16[1,96,384]{2,1,0:T(8,128)(2,1)}, bf16[1,96,384]{2,1,0:T(8,128)(2,1)S(1)}, u32[]{:S(2)}, u32[]{:S(2)}) collective-permute-start(bf16[1,96,384]{2,1,0:T(8,128)(2,1)} %bitcast.20), channel_id=1, source_target_pairs={{0,16},{8,24},{16,0},{24,8},{1,17},{9,25},{17,1},{25,9},{2,18},{10... | collective-permute-start | bytes 221192 | tf_op jit(solution)/shard_map/ppermute | solution.py:677
  7.0 11.6 %collective-permute-start.3 = (bf16[1,112,768]{2,1,0:T(8,128)(2,1)}, bf16[1,112,768]{2,1,0:T(8,128)(2,1)S(1)}, u32[]{:S(2)}, u32[]{:S(2)}) collective-permute-start(bf16[1,112,768]{2,1,0:T(8,128)(2,1)} %bitcast.18), channel_id=1, source_target_pairs={{0,16},{8,24},{16,0},{24,8},{1,17},{9,25},{17,1},{25,9},{2,18},{10... | collective-permute-start | bytes 516104 | tf_op jit(solution)/shard_map/ppermute | solution.py:677
  8.6 13.2 %collective-permute-start = (bf16[304,384]{1,0:T(8,128)(2,1)S(1)}, bf16[304,384]{1,0:T(8,128)(2,1)S(1)}, u32[]{:S(2)}, u32[]{:S(2)}) collective-permute-start(bf16[304,384]{1,0:T(8,128)(2,1)S(1)} %get-tuple-element.96), channel_id=1, source_target_pairs={{0,2},{2,0},{4,6},{6,4},{1,3},{3,1},{5,7},{7,5},{8,10},{10,8},{12,... | collective-permute-start | bytes 700424 | tf_op jit(solution)/shard_map/ppermute | solution.py:637
  10.4 11.6 %collective-permute-start.1 = (bf16[304,384]{1,0:T(8,128)(2,1)S(1)}, bf16[304,384]{1,0:T(8,128)(2,1)S(1)}, u32[]{:S(2)}, u32[]{:S(2)}) collective-permute-start(bf16[304,384]{1,0:T(8,128)(2,1)S(1)} %get-tuple-element.97), channel_id=1, source_target_pairs={{0,4},{2,6},{4,0},{6,2},{1,5},{3,7},{5,1},{7,3},{8,12},{10,14},{12... | collective-permute-start | bytes 700424 | tf_op jit(solution)/shard_map/ppermute | solution.py:637
  11.9 10.1 %collective-permute-start.2 = (bf16[304,384]{1,0:T(8,128)(2,1)S(1)}, bf16[304,384]{1,0:T(8,128)(2,1)S(1)}, u32[]{:S(2)}, u32[]{:S(2)}) collective-permute-start(bf16[304,384]{1,0:T(8,128)(2,1)S(1)} %get-tuple-element.98), channel_id=1, source_target_pairs={{0,6},{2,4},{4,2},{6,0},{1,7},{3,5},{5,3},{7,1},{8,14},{10,12},{12... | collective-permute-start | bytes 700424 | tf_op jit(solution)/shard_map/ppermute | solution.py:637
  15.1 6.8 %collective-permute-start.6 = (bf16[2,96,384]{2,1,0:T(8,128)(2,1)S(1)}, bf16[2,96,384]{2,1,0:T(8,128)(2,1)S(1)}, u32[]{:S(2)}, u32[]{:S(2)}) collective-permute-start(bf16[2,96,384]{2,1,0:T(8,128)(2,1)S(1)} %join_quarter.1.refs_4_), channel_id=1, source_target_pairs={{0,8},{8,0},{16,24},{24,16},{1,9},{9,1},{17,25},{25,17},{2,10},{10... | collective-permute-start | bytes 442376 | tf_op jit(solution)/shard_map/ppermute | solution.py:679
  18.7 10.4 %collective-permute-start.4 = (bf16[2,112,768]{2,1,0:T(8,128)(2,1)S(1)}, bf16[2,112,768]{2,1,0:T(8,128)(2,1)S(1)}, u32[]{:S(2)}, u32[]{:S(2)}) collective-permute-start(bf16[2,112,768]{2,1,0:T(8,128)(2,1)S(1)} %join_attn.1.refs_3_.refs_4_), channel_id=1, source_target_pairs={{0,8},{8,0},{16,24},{24,16},{1,9},{9,1},{17,25},{25,17},{2,10},{10... | collective-permute-start | bytes 1032200 | tf_op jit(solution)/shard_map/ppermute | solution.py:679
  22.1 6.9 %collective-permute-start.7 = (bf16[2,112,768]{2,1,0:T(8,128)(2,1)S(1)}, bf16[2,112,768]{2,1,0:T(8,128)(2,1)S(1)}, u32[]{:S(2)}, u32[]{:S(2)}) collective-permute-start(bf16[2,112,768]{2,1,0:T(8,128)(2,1)S(1)} %get-tuple-element.101), channel_id=1, source_target_pairs={{0,1},{1,0},{2,3},{3,2},{4,5},{5,4},{6,7},{7,6},{8,9},{9,8},{10,11... | collective-permute-start | bytes 1032200 | tf_op jit(solution)/shard_map/ppermute | solution.py:661
  22.2 14.5 %collective-permute-start.12 = (bf16[384,384]{1,0:T(8,128)(2,1)S(1)}, bf16[384,384]{1,0:T(8,128)(2,1)S(1)}, u32[]{:S(2)}, u32[]{:S(2)}) collective-permute-start(bf16[384,384]{1,0:T(8,128)(2,1)S(1)} %get-tuple-element.102.refs_1_), channel_id=1, source_target_pairs={{0,6},{2,4},{4,2},{6,0},{1,7},{3,5},{5,3},{7,1},{8,14},{10,12},{12... | collective-permute-start | bytes 884744 | tf_op jit(solution)/shard_map/ppermute | solution.py:637
  25.1 13.9 %collective-permute-start.11 = (bf16[384,384]{1,0:T(8,128)(2,1)S(1)}, bf16[384,384]{1,0:T(8,128)(2,1)S(1)}, u32[]{:S(2)}, u32[]{:S(2)}) collective-permute-start(bf16[384,384]{1,0:T(8,128)(2,1)S(1)} %get-tuple-element.102.refs_1_), channel_id=1, source_target_pairs={{0,4},{2,6},{4,0},{6,2},{1,5},{3,7},{5,1},{7,3},{8,12},{10,14},{12... | collective-permute-start | bytes 884744 | tf_op jit(solution)/shard_map/ppermute | solution.py:637
  25.6 13.7 %collective-permute-start.10 = (bf16[384,384]{1,0:T(8,128)(2,1)S(1)}, bf16[384,384]{1,0:T(8,128)(2,1)S(1)}, u32[]{:S(2)}, u32[]{:S(2)}) collective-permute-start(bf16[384,384]{1,0:T(8,128)(2,1)S(1)} %get-tuple-element.102.refs_1_), channel_id=1, source_target_pairs={{0,2},{2,0},{4,6},{6,4},{1,3},{3,1},{5,7},{7,5},{8,10},{10,8},{12,... | collective-permute-start | bytes 884744 | tf_op jit(solution)/shard_map/ppermute | solution.py:637
  48.3 10.4 %collective-permute-start.15 = (bf16[2,2,96,384]{3,2,1,0:T(8,128)(2,1)S(1)}, bf16[2,2,96,384]{3,2,1,0:T(8,128)(2,1)S(1)}, u32[]{:S(2)}, u32[]{:S(2)}) collective-permute-start(bf16[2,2,96,384]{3,2,1,0:T(8,128)(2,1)S(1)} %get-tuple-element.132), channel_id=1, source_target_pairs={{0,2},{2,0},{4,6},{6,4},{1,3},{3,1},{5,7},{7,5},{8,10},{10,8},{12,... | collective-permute-start | bytes 884744 | tf_op jit(solution)/shard_map/ppermute | solution.py:768
  49.9 9.0 %collective-permute-start.16 = (bf16[2,2,96,384]{3,2,1,0:T(8,128)(2,1)S(1)}, bf16[2,2,96,384]{3,2,1,0:T(8,128)(2,1)S(1)}, u32[]{:S(2)}, u32[]{:S(2)}) collective-permute-start(bf16[2,2,96,384]{3,2,1,0:T(8,128)(2,1)S(1)} %get-tuple-element.134), channel_id=1, source_target_pairs={{0,4},{2,6},{4,0},{6,2},{1,5},{3,7},{5,1},{7,3},{8,12},{10,14},{12... | collective-permute-start | bytes 884744 | tf_op jit(solution)/shard_map/ppermute | solution.py:768
  59.0 6.3 %collective-permute-start.18 = (bf16[2,96,384]{2,1,0:T(8,128)(2,1)S(1)}, bf16[2,96,384]{2,1,0:T(8,128)(2,1)S(1)}, u32[]{:S(2)}, u32[]{:S(2)}) collective-permute-start(bf16[2,96,384]{2,1,0:T(8,128)(2,1)S(1)} %get-tuple-element.138), channel_id=1, source_target_pairs={{0,4},{2,6},{4,0},{6,2},{1,5},{3,7},{5,1},{7,3},{8,12},{10,14},{12... | collective-permute-start | bytes 442376 | tf_op jit(solution)/shard_map/ppermute | solution.py:781
  60.4 6.7 %collective-permute-start.19 = (bf16[2,96,384]{2,1,0:T(8,128)(2,1)S(1)}, bf16[2,96,384]{2,1,0:T(8,128)(2,1)S(1)}, u32[]{:S(2)}, u32[]{:S(2)}) collective-permute-start(bf16[2,96,384]{2,1,0:T(8,128)(2,1)S(1)} %get-tuple-element.140), channel_id=1, source_target_pairs={{0,2},{2,0},{4,6},{6,4},{1,3},{3,1},{5,7},{7,5},{8,10},{10,8},{12,... | collective-permute-start | bytes 442376 | tf_op jit(solution)/shard_map/ppermute | solution.py:781
  61.3 11.4 %collective-permute-start.20 = (bf16[4,160,128]{2,1,0:T(8,128)(2,1)S(1)}, bf16[4,160,128]{2,1,0:T(8,128)(2,1)S(1)}, u32[]{:S(2)}, u32[]{:S(2)}) collective-permute-start(bf16[4,160,128]{2,1,0:T(8,128)(2,1)S(1)} %get-tuple-element.144), channel_id=1, source_target_pairs={{0,2},{2,0},{4,6},{6,4},{1,3},{3,1},{5,7},{7,5},{8,10},{10,8},{12,... | collective-permute-start | bytes 491528 | tf_op jit(solution)/shard_map/ppermute | solution.py:637
  62.7 10.0 %collective-permute-start.21 = (bf16[4,160,128]{2,1,0:T(8,128)(2,1)S(1)}, bf16[4,160,128]{2,1,0:T(8,128)(2,1)S(1)}, u32[]{:S(2)}, u32[]{:S(2)}) collective-permute-start(bf16[4,160,128]{2,1,0:T(8,128)(2,1)S(1)} %get-tuple-element.145), channel_id=1, source_target_pairs={{0,4},{2,6},{4,0},{6,2},{1,5},{3,7},{5,1},{7,3},{8,12},{10,14},{12... | collective-permute-start | bytes 491528 | tf_op jit(solution)/shard_map/ppermute | solution.py:637
  63.4 10.0 %collective-permute-start.22 = (bf16[4,160,128]{2,1,0:T(8,128)(2,1)S(1)}, bf16[4,160,128]{2,1,0:T(8,128)(2,1)S(1)}, u32[]{:S(2)}, u32[]{:S(2)}) collective-permute-start(bf16[4,160,128]{2,1,0:T(8,128)(2,1)S(1)} %get-tuple-element.146), channel_id=1, source_target_pairs={{0,6},{2,4},{4,2},{6,0},{1,7},{3,5},{5,3},{7,1},{8,14},{10,12},{12... | collective-permute-start | bytes 491528 | tf_op jit(solution)/shard_map/ppermute | solution.py:637
  67.2 6.2 %collective-permute-start.23 = (bf16[2,96,384]{2,1,0:T(8,128)(2,1)S(1)}, bf16[2,96,384]{2,1,0:T(8,128)(2,1)S(1)}, u32[]{:S(2)}, u32[]{:S(2)}) collective-permute-start(bf16[2,96,384]{2,1,0:T(8,128)(2,1)S(1)} %get-tuple-element.148), channel_id=1, source_target_pairs={{0,8},{8,0},{16,24},{24,16},{1,9},{9,1},{17,25},{25,17},{2,10},{10... | collective-permute-start | bytes 442376 | tf_op jit(solution)/shard_map/ppermute | solution.py:806
  69.2 14.6 %all-to-all-start = ((bf16[4,304,384]{2,1,0:T(8,128)(2,1)}), bf16[4,304,384]{2,1,0:T(8,128)(2,1)S(1)}, u32[]{:S(2)}, u32[]{:S(2)}) async-start(bf16[4,304,384]{2,1,0:T(8,128)(2,1)} %returns.1.refs_0_), calls=%async_computation | async-start | bytes 1867776 | tf_op jit(solution)/shard_map/all_to_all | solution.py:793
  73.5 10.0 %collective-permute-start.24 = (bf16[1,96,384]{2,1,0:T(8,128)(2,1)S(1)}, bf16[1,96,384]{2,1,0:T(8,128)(2,1)S(1)}, u32[]{:S(2)}, u32[]{:S(2)}) collective-permute-start(bf16[1,96,384]{2,1,0:T(8,128)(2,1)S(1)} %get-tuple-element.150), channel_id=1, source_target_pairs={{0,16},{8,24},{16,0},{24,8},{1,17},{9,25},{17,1},{25,9},{2,18},{10... | collective-permute-start | bytes 221192 | tf_op jit(solution)/shard_map/ppermute | solution.py:810
  84.0 7.1 %collective-permute-start.31 = (bf16[160,384]{1,0:T(8,128)(2,1)S(1)}, bf16[160,384]{1,0:T(8,128)(2,1)S(1)}, u32[]{:S(2)}, u32[]{:S(2)}) collective-permute-start(bf16[160,384]{1,0:T(8,128)(2,1)S(1)} %sum_dp.1.refs_0_.refs_1_), channel_id=1, source_target_pairs={{0,6},{2,4},{4,2},{6,0},{1,7},{3,5},{5,3},{7,1},{8,14},{10,12},{12... | collective-permute-start | bytes 368648 | tf_op jit(solution)/shard_map/ppermute | solution.py:637
  86.0 7.2 %collective-permute-start.30 = (bf16[160,384]{1,0:T(8,128)(2,1)S(1)}, bf16[160,384]{1,0:T(8,128)(2,1)S(1)}, u32[]{:S(2)}, u32[]{:S(2)}) collective-permute-start(bf16[160,384]{1,0:T(8,128)(2,1)S(1)} %sum_dp.1.refs_0_.refs_1_), channel_id=1, source_target_pairs={{0,4},{2,6},{4,0},{6,2},{1,5},{3,7},{5,1},{7,3},{8,12},{10,14},{12... | collective-permute-start | bytes 368648 | tf_op jit(solution)/shard_map/ppermute | solution.py:637
  86.9 6.4 %collective-permute-start.29 = (bf16[160,384]{1,0:T(8,128)(2,1)S(1)}, bf16[160,384]{1,0:T(8,128)(2,1)S(1)}, u32[]{:S(2)}, u32[]{:S(2)}) collective-permute-start(bf16[160,384]{1,0:T(8,128)(2,1)S(1)} %sum_dp.1.refs_0_.refs_1_), channel_id=1, source_target_pairs={{0,2},{2,0},{4,6},{6,4},{1,3},{3,1},{5,7},{7,5},{8,10},{10,8},{12,... | collective-permute-start | bytes 368648 | tf_op jit(solution)/shard_map/ppermute | solution.py:637
  (14 other events, 64.6 us)

commit v8 on v7

--- a/solution.py
+++ b/solution.py
@@ -15,8 +15,8 @@
 F32 = jnp.float32
 TILE = 128
 TIMES = {
-    "pack_weights": 2.0, "pack_slots": 3.0, "pack_cotangent": 2.0, "attention": 0.0, "mlp_own": 4.0, "mlp_oth": 4.0, "mlp_sums": 2.0, "attention_back": 11.0,
-    "place_grads": 1.0, "place_slots": 2.3, "join_quarter": 20.0, "sum_ctx_attn": 0.5, "sum_dp": 5.0, "sum_ctx_first": 50.0,
+    "pack_weights": 2.0, "pack_slots": 3.0, "join_quarter": 20.0, "attention": 0.0, "mlp_own": 4.0, "mlp_oth": 4.0, "mlp_sums": 2.0,
+    "attention_back": 11.0, "sum_ctx_first": 50.0, "sum_ctx_attn": 0.5, "sum_dp": 5.0, "place_slots": 2.3, "place_grads": 1.0,
 }
 EXTRA = 16
 
@@ -153,7 +153,7 @@
 
 def pack_weights_kernel(sizes, count, *refs):
     nctx, ntp, ndp, main, width, rows, padded = sizes
-    sources, (p1, p2q, done), refs = refs[:count], refs[count : count + 3], refs[count + 3 :]
+    sources, (p1, p2q), refs = refs[:count], refs[count : count + 2], refs[count + 2 :]
     held, sem = refs[:count], refs[count]
     copies = fetch(sources, held, sem)
     wq, wk, wv, wo, wu, wd, qb, vb, ub = held[:9]
@@ -202,24 +202,21 @@
         block[:, :width],
     )
     p1[padded : padded + EXTRA, 0:width] = mixed.astype(BF)
-    done[...] = jnp.zeros_like(done)
-
-
-def pack_slots_kernel(sizes, *refs):
+
+
+def pack_slots_kernel(sizes, tok, cot, source, *refs):
     nctx, ntp, ndp, main, width, rows, padded = sizes
-    sources, sent, tails, refs = refs[:3], refs[3 : 3 + nctx], refs[3 + nctx], refs[4 + nctx :]
-    held, sem = refs[:3], refs[3]
-    copies = fetch(sources, held, sem)
-    tok, cot, mask = held
+    sent, tails, mask, sem = refs[:nctx], refs[nctx], refs[nctx + 1], refs[nctx + 2]
+    get_mask = pltpu.make_async_copy(source, mask, sem.at[0])
+    get_mask.start()
     images = nctx * ntp
     me_c, me_t = lax.axis_index("ctx"), lax.axis_index("tp")
     wanted = [(me_c ^ k) * ntp + me_t for k in range(nctx)]
     pick = picker(wanted, images)
-    for i in range(2):
-        copies[i].wait()
-        take_images(held[i], sent, i * (main + EXTRA), pick, images, main)
-        tails[i] = held[i][main * images :, :]
-    copies[2].wait()
+    for i, ref in enumerate((tok, cot)):
+        take_images(ref, sent, i * (main + EXTRA), pick, images, main)
+        tails[i] = ref[main * images :, :]
+    get_mask.wait()
     for k in range(nctx):
         gate = mask[wanted[k], main].astype(F32)
         te = tok[pl.ds(main * images + wanted[k], 1), :] * gate
@@ -679,23 +676,22 @@
         return v, lax.ppermute(v, "dp", xor(ndp, 1))
 
     sources = [w_query, w_key, w_value, w_out, w_up, jnp.transpose(w_down), query_bias, value_bias, up_bias, *vecs]
-    p1, p2q, packed = call(
+    p1, p2q = call(
         "pack_weights",
         functools.partial(pack_weights_kernel, sizes, len(sources)),
-        [sds((padded + EXTRA, p1_cols), BF), sds((padded, ff // 2), BF), sds((8, TILE), F32)],
+        [sds((padded + EXTRA, p1_cols), BF), sds((padded, ff // 2), BF)],
         scratch=held(sources),
         mib=56,
         raw=range(len(sources)),
     )(*sources)
-    sources = [tok, cot, valid_mask]
     *sent, tails = call(
         "pack_slots",
         one(pack_slots_kernel),
         [sds((2 * main + EXTRA, width), BF)] * nctx + [sds((2, images, width), F32)],
-        scratch=held(sources),
+        scratch=[pltpu.SMEM(valid_mask.shape, valid_mask.dtype), pltpu.SemaphoreType.DMA((1,))],
         mib=48,
-        raw=range(3),
-    )(*sources)
+        raw=(2,),
+    )(tok, cot, valid_mask)
     t_in = over("ctx", nctx, sent)
     w2q = gather_dp("join_quarter", p2q, [])
     w1, w1_got = gather_dp("join_attn", p1, [])

time: 94.7 us -> 94.3 us (level)
  waiting for transfers between devices: 25.9 us -> 27.2 us
  transfers between devices with their start and end apart: 33 -> 33, of which waited for: 20 -> 18; matrix products, arithmetic and copies ran while one was open for 0% -> 0% of each run, Pallas kernels for 27% -> 26%
where the time goes in v8:
time: 94.3 us; the launch traced here: 94.1 us
  starting transfers between devices  35.3 us (37%)
  Pallas kernels  30.7 us (33%)
  waiting for transfers between devices  27.2 us (29%)
  between operations  1.01 us (1%)
    pallas_call x23, Pallas kernels, run(): pl.pallas_call(ordered, name=name, out_shape=out_shape, in_specs=specs, o...  30.7 us
    ppermute x15, starting transfers between devices, over(): lax.ppermute(items[k], axis, xor(n, k))  18.7 us
    ppermute x15, waiting for transfers between devices, over(): lax.ppermute(items[k], axis, xor(n, k))  10.4 us
    ppermute x2, waiting for transfers between devices, gather_dp(): lax.ppermute(v, 'dp', xor(ndp, stride))  6.44 us
    ppermute x2, waiting for transfers between devices, gather_dp(): return (v, lax.ppermute(v, 'dp', xor(ndp, 1)))  5.76 us
    ppermute x2, starting transfers between devices, gather_dp(): lax.ppermute(v, 'dp', xor(ndp, stride))  4.18 us
    all_to_all x1, starting transfers between devices, body(): returned = lax.all_to_all(back, 'ctx', 0, 0)  3.51 us
    ppermute x1, starting transfers between devices, body(): lax.ppermute(send, 'dp', xor(ndp, ndp // 2))  2 us
  transfers between devices with their start and end apart: 33, of which 18 were waited for; matrix products, arithmetic and copies ran while one was open for 0% of the time, Pallas kernels for 26%

profile of v8, /device:TPU:0, one launch (start us, length us, event | category | flops | bytes accessed | tf_op | source)
XLA Modules:
  0.0 94.1 jit_solution(170280493205871624)
XLA Ops:
  0.7 2.2 %pack_weights.1 = (bf16[112,768]{1,0:T(8,128)(2,1)}, bf16[96,384]{1,0:T(8,128)(2,1)}) custom-call(bf16[96,192]{1,0:T(8,128)(2,1)} %refs_0_.1, bf16[96,192]{1,0:T(8,128)(2,1)} %refs_1_.1, bf16[96,192]{1,0:T(8,128)(2,1)} %refs_2_.3, bf16[192,96]{1,0:T(8,128)(2,1)} %refs_3_.2, bf16[96,768]{1,0:T(8,128)(2,1)} %refs_4_.1, bf16[96,768]{1,0:T(8,128)(2,1)} %bitcast.22, ...), custom_call_target="tpu_custom_call" | custom-call | flops 2300000000 | bytes 1 | tf_op jit(solution)/shard_map/pack_weights/pallas_call | solution.py:35
  2.9 4.1 %collective-permute-start.5 = (bf16[1,96,384]{2,1,0:T(8,128)(2,1)}, bf16[1,96,384]{2,1,0:T(8,128)(2,1)S(1)}, u32[]{:S(2)}, u32[]{:S(2)}) collective-permute-start(bf16[1,96,384]{2,1,0:T(8,128)(2,1)} %bitcast.20), channel_id=1, source_target_pairs={{0,16},{8,24},{16,0},{24,8},{1,17},{9,25},{17,1},{25,9},{2,18},{10... | collective-permute-start | bytes 221192 | tf_op jit(solution)/shard_map/ppermute | solution.py:674
  7.8 1.8 %collective-permute-start = (bf16[304,384]{1,0:T(8,128)(2,1)S(1)}, bf16[304,384]{1,0:T(8,128)(2,1)S(1)}, u32[]{:S(2)}, u32[]{:S(2)}) collective-permute-start(bf16[304,384]{1,0:T(8,128)(2,1)S(1)} %get-tuple-element.96), channel_id=1, source_target_pairs={{0,2},{2,0},{4,6},{6,4},{1,3},{3,1},{5,7},{7,5},{8,10},{10,8},{12,... | collective-permute-start | bytes 700424 | tf_op jit(solution)/shard_map/ppermute | solution.py:634
  11.4 3.6 %collective-permute-done.5.refs_1_ = bf16[1,96,384]{2,1,0:T(8,128)(2,1)S(1)} collective-permute-done((bf16[1,96,384]{2,1,0:T(8,128)(2,1)}, bf16[1,96,384]{2,1,0:T(8,128)(2,1)S(1)}, u32[]{:S(2)}, u32[]{:S(2)}) %collective-permute-start.5) | collective-permute-done | bytes 73760 | tf_op jit(solution)/shard_map/ppermute | solution.py:674
  15.8 2.8 %collective-permute-done.3.refs_1_ = bf16[1,112,768]{2,1,0:T(8,128)(2,1)S(1)} collective-permute-done((bf16[1,112,768]{2,1,0:T(8,128)(2,1)}, bf16[1,112,768]{2,1,0:T(8,128)(2,1)S(1)}, u32[]{:S(2)}, u32[]{:S(2)}) %collective-permute-start.3) | collective-permute-done | bytes 172064 | tf_op jit(solution)/shard_map/ppermute | solution.py:674
  19.4 2.4 %collective-permute-done.6.refs_5_ = bf16[2,96,384]{2,1,0:T(8,128)(2,1)S(1)} collective-permute-done((bf16[2,96,384]{2,1,0:T(8,128)(2,1)S(1)}, bf16[2,96,384]{2,1,0:T(8,128)(2,1)S(1)}, u32[]{:S(2)}, u32[]{:S(2)}) %collective-permute-start.6) | collective-permute-done | bytes 147488 | tf_op jit(solution)/shard_map/ppermute | solution.py:676
  22.0 3.1 %collective-permute-start.12 = (bf16[384,384]{1,0:T(8,128)(2,1)S(1)}, bf16[384,384]{1,0:T(8,128)(2,1)S(1)}, u32[]{:S(2)}, u32[]{:S(2)}) collective-permute-start(bf16[384,384]{1,0:T(8,128)(2,1)S(1)} %get-tuple-element.102.refs_1_), channel_id=1, source_target_pairs={{0,6},{2,4},{4,2},{6,0},{1,7},{3,5},{5,3},{7,1},{8,14},{10,12},{12... | collective-permute-start | bytes 884744 | tf_op jit(solution)/shard_map/ppermute | solution.py:634
  25.7 3.3 %collective-permute-done.4.refs_2_.refs_5_ = bf16[2,112,768]{2,1,0:T(8,128)(2,1)S(1)} collective-permute-done((bf16[2,112,768]{2,1,0:T(8,128)(2,1)S(1)}, bf16[2,112,768]{2,1,0:T(8,128)(2,1)S(1)}, u32[]{:S(2)}, u32[]{:S(2)}) %collective-permute-start.4) | collective-permute-done | bytes 344096 | tf_op jit(solution)/shard_map/ppermute | solution.py:676
  30.8 5.9 %attention.1 = (f32[592,384]{1,0:T(8,128)S(1)}, f32[592,384]{1,0:T(8,128)S(1)}, bf16[592,384]{1,0:T(8,128)(2,1)S(1)}, bf16[592,384]{1,0:T(8,128)(2,1)S(1)}, bf16...) custom-call(bf16[304,384]{1,0:T(8,128)(2,1)S(1)} %get-tuple-element., ...), custom_call_target="tpu_custom_call" | custom-call | bytes 1 | tf_op jit(solution)/shard_map/attention/pallas_call | solution.py:35
  36.7 2.3 %collective-permute-done.11.refs_3_ = bf16[384,384]{1,0:T(8,128)(2,1)S(1)} collective-permute-done((bf16[384,384]{1,0:T(8,128)(2,1)S(1)}, bf16[384,384]{1,0:T(8,128)(2,1)S(1)}, u32[]{:S(2)}, u32[]{:S(2)}) %collective-permute-start.11) | collective-permute-done | bytes 294944 | tf_op jit(solution)/shard_map/ppermute | solution.py:634
  39.5 2.2 %mlp_own.1 = (bf16[592,768]{1,0:T(8,128)(2,1)S(1)}, bf16[592,768]{1,0:T(8,128)(2,1)S(1)}, f32[8,768]{1,0:T(8,128)S(1)}, bf16[4,4,96,384]{3,2,1,0:T(8,128)(2,1)S(1)}) custom-call(bf16[592,384]{1,0:T(8,128)(2,1)S(1)} %get-tuple-element.110.refs_0_.refs_1_, bf16[592,384]{1,0:T(8,128)(2,1)S(1)} %get-tuple-element.109.refs_1_.refs_2_.refs_4_, ...), custom_call_target="tpu_custom_call" | custom-call | flops 4600000000 | bytes 1 | tf_op jit(solution)/shard_map/mlp_own/pallas_call | solution.py:35
  42.4 2.2 %mlp_oth.1 = (bf16[592,768]{1,0:T(8,128)(2,1)S(1)}, bf16[592,768]{1,0:T(8,128)(2,1)S(1)}, f32[8,768]{1,0:T(8,128)S(1)}, bf16[4,4,96,384]{3,2,1,0:T(8,128)(2,1)S(1)}) custom-call(f32[8,768]{1,0:T(8,128)S(1)} %get-tuple-element.113.refs_0_.refs_12_, bf16[592,384]{1,0:T(8,128)(2,1)S(1)} %get-tuple-element.110.refs_0_.refs_1_, ...), custom_call_target="tpu_custom_call" | custom-call | flops 4600000000 | bytes 1 | tf_op jit(solution)/shard_map/mlp_oth/pallas_call | solution.py:35
  44.8 3.3 %mlp_sums.1 = (bf16[592,384]{1,0:T(8,128)(2,1)S(1)}, f32[592,384]{1,0:T(8,128)S(1)}, bf16[592,384]{1,0:T(8,128)(2,1)S(1)}, f32[384,384]{1,0:T(8,128)S(1)}, f32[16,384]{1,0:T(8,128)S(1)}) custom-call(f32[592,384]{1,0:T(8,128)S(1)} %get-tuple-element.105.refs_0_, bf16[592,384]{1,0:T(8,128)(2,1)S(1)} %get-tuple-element.106.refs_1_, ...), custom_call_target="tpu_custom_call" | custom-call | flops 2300000000 | bytes 1 | tf_op jit(solution)/shard_map/mlp_sums/pallas_call | solution.py:35
  48.3 1.6 %collective-permute-start.15 = (bf16[2,2,96,384]{3,2,1,0:T(8,128)(2,1)S(1)}, bf16[2,2,96,384]{3,2,1,0:T(8,128)(2,1)S(1)}, u32[]{:S(2)}, u32[]{:S(2)}) collective-permute-start(bf16[2,2,96,384]{3,2,1,0:T(8,128)(2,1)S(1)} %get-tuple-element.132), channel_id=1, source_target_pairs={{0,2},{2,0},{4,6},{6,4},{1,3},{3,1},{5,7},{7,5},{8,10},{10,8},{12,... | collective-permute-start | bytes 884744 | tf_op jit(solution)/shard_map/ppermute | solution.py:764
  50.4 8.2 %attention_back.1 = (bf16[592,384]{1,0:T(8,128)(2,1)S(1)}, bf16[4,4,160,128]{3,2,1,0:T(8,128)(2,1)S(1)}, bf16[4,4,160,128]{3,2,1,0:T(8,128)(2,1)S(1)}) custom-call(bf16[2,2,96,384]{3,2,1,0:T(8,128)(2,1)S(1)} %get-tuple-element.120.refs_0_.refs_1_, bf16[640,1152]{1,0:T(8,128)(2,1)S(1)} %get-tuple-element.121.refs_1_, ...), custom_call_target="tpu_custom_call" | custom-call | flops 12650000384 | bytes 1 | tf_op jit(solution)/shard_map/attention_back/pallas_call | solution.py:35
  65.3 1.8 %collective-permute-done.19.refs_4_ = bf16[2,96,384]{2,1,0:T(8,128)(2,1)S(1)} collective-permute-done((bf16[2,96,384]{2,1,0:T(8,128)(2,1)S(1)}, bf16[2,96,384]{2,1,0:T(8,128)(2,1)S(1)}, u32[]{:S(2)}, u32[]{:S(2)}) %collective-permute-start.19) | collective-permute-done | bytes 147488 | tf_op jit(solution)/shard_map/ppermute | solution.py:777
  68.4 3.5 %all-to-all-start = ((bf16[4,304,384]{2,1,0:T(8,128)(2,1)}), bf16[4,304,384]{2,1,0:T(8,128)(2,1)S(1)}, u32[]{:S(2)}, u32[]{:S(2)}) async-start(bf16[4,304,384]{2,1,0:T(8,128)(2,1)} %returns.1.refs_0_), calls=%async_computation | async-start | bytes 1867776 | tf_op jit(solution)/shard_map/all_to_all | solution.py:789
  73.6 2.0 %collective-permute-start.24 = (bf16[1,96,384]{2,1,0:T(8,128)(2,1)S(1)}, bf16[1,96,384]{2,1,0:T(8,128)(2,1)S(1)}, u32[]{:S(2)}, u32[]{:S(2)}) collective-permute-start(bf16[1,96,384]{2,1,0:T(8,128)(2,1)S(1)} %get-tuple-element.150), channel_id=1, source_target_pairs={{0,16},{8,24},{16,0},{24,8},{1,17},{9,25},{17,1},{25,9},{2,18},{10... | collective-permute-start | bytes 221192 | tf_op jit(solution)/shard_map/ppermute | solution.py:806
  75.6 1.7 %collective-permute-start.25 = (bf16[160,128]{1,0:T(8,128)(2,1)S(1)}, bf16[160,128]{1,0:T(8,128)(2,1)S(1)}, u32[]{:S(2)}, u32[]{:S(2)}) collective-permute-start(bf16[160,128]{1,0:T(8,128)(2,1)S(1)} %get-tuple-element.151), channel_id=1, source_target_pairs={{0,8},{8,0},{16,24},{24,16},{1,9},{9,1},{17,25},{25,17},{2,10},{10... | collective-permute-start | bytes 122888 | tf_op jit(solution)/shard_map/ppermute | solution.py:634
  77.4 2.6 %collective-permute-start.27 = (bf16[160,128]{1,0:T(8,128)(2,1)S(1)}, bf16[160,128]{1,0:T(8,128)(2,1)S(1)}, u32[]{:S(2)}, u32[]{:S(2)}) collective-permute-start(bf16[160,128]{1,0:T(8,128)(2,1)S(1)} %get-tuple-element.153), channel_id=1, source_target_pairs={{0,24},{8,16},{16,8},{24,0},{1,25},{9,17},{17,9},{25,1},{2,26},{10... | collective-permute-start | bytes 122888 | tf_op jit(solution)/shard_map/ppermute | solution.py:634
  79.9 2.4 %collective-permute-done.26.refs_4_ = bf16[160,128]{1,0:T(8,128)(2,1)S(1)} collective-permute-done((bf16[160,128]{1,0:T(8,128)(2,1)S(1)}, bf16[160,128]{1,0:T(8,128)(2,1)S(1)}, u32[]{:S(2)}, u32[]{:S(2)}) %collective-permute-start.26) | collective-permute-done | bytes 40992 | tf_op jit(solution)/shard_map/ppermute | solution.py:634
  83.7 2.4 %collective-permute-start.31 = (bf16[160,384]{1,0:T(8,128)(2,1)S(1)}, bf16[160,384]{1,0:T(8,128)(2,1)S(1)}, u32[]{:S(2)}, u32[]{:S(2)}) collective-permute-start(bf16[160,384]{1,0:T(8,128)(2,1)S(1)} %sum_dp.1.refs_0_.refs_1_), channel_id=1, source_target_pairs={{0,6},{2,4},{4,2},{6,0},{1,7},{3,5},{5,3},{7,1},{8,14},{10,12},{12... | collective-permute-start | bytes 368648 | tf_op jit(solution)/shard_map/ppermute | solution.py:634
  87.2 2.7 %place_slots.1 = (f32[1160,384]{1,0:T(8,128)}, f32[1160,384]{1,0:T(8,128)}, f32[8,128]{1,0:T(8,128)S(1)}) custom-call(bf16[4,304,384]{2,1,0:T(8,128)(2,1)S(1)} %hand_on.1.refs_0_, bf16[4,304,384]{2,1,0:T(8,128)(2,1)S(1)} %collective-permute-done.28.refs_1_, f32[2,8,384]{2,1,0:T(8,128)S(1)} %get-tuple-element.154.refs_2_, s32[8,145]{1,0:T(8,128)S(1)} %copy-done.4), custom_call_target="tpu_custom_call" | custom-call | flops 2644999936 | bytes 1 | tf_op jit(solution)/shard_map/place_slots/pallas_call | solution.py:35
  90.5 2.4 %collective-permute-done.30.refs_3_ = bf16[160,384]{1,0:T(8,128)(2,1)S(1)} collective-permute-done((bf16[160,384]{1,0:T(8,128)(2,1)S(1)}, bf16[160,384]{1,0:T(8,128)(2,1)S(1)}, u32[]{:S(2)}, u32[]{:S(2)}) %collective-permute-start.30) | collective-permute-done | bytes 122912 | tf_op jit(solution)/shard_map/ppermute | solution.py:634
  (75 shorter events, 22.6 us)
Async XLA Ops:
  2.9 12.1 %collective-permute-start.5 = (bf16[1,96,384]{2,1,0:T(8,128)(2,1)}, bf16[1,96,384]{2,1,0:T(8,128)(2,1)S(1)}, u32[]{:S(2)}, u32[]{:S(2)}) collective-permute-start(bf16[1,96,384]{2,1,0:T(8,128)(2,1)} %bitcast.20), channel_id=1, source_target_pairs={{0,16},{8,24},{16,0},{24,8},{1,17},{9,25},{17,1},{25,9},{2,18},{10... | collective-permute-start | bytes 221192 | tf_op jit(solution)/shard_map/ppermute | solution.py:674
  7.0 11.6 %collective-permute-start.3 = (bf16[1,112,768]{2,1,0:T(8,128)(2,1)}, bf16[1,112,768]{2,1,0:T(8,128)(2,1)S(1)}, u32[]{:S(2)}, u32[]{:S(2)}) collective-permute-start(bf16[1,112,768]{2,1,0:T(8,128)(2,1)} %bitcast.18), channel_id=1, source_target_pairs={{0,16},{8,24},{16,0},{24,8},{1,17},{9,25},{17,1},{25,9},{2,18},{10... | collective-permute-start | bytes 516104 | tf_op jit(solution)/shard_map/ppermute | solution.py:674
  7.8 14.0 %collective-permute-start = (bf16[304,384]{1,0:T(8,128)(2,1)S(1)}, bf16[304,384]{1,0:T(8,128)(2,1)S(1)}, u32[]{:S(2)}, u32[]{:S(2)}) collective-permute-start(bf16[304,384]{1,0:T(8,128)(2,1)S(1)} %get-tuple-element.96), channel_id=1, source_target_pairs={{0,2},{2,0},{4,6},{6,4},{1,3},{3,1},{5,7},{7,5},{8,10},{10,8},{12,... | collective-permute-start | bytes 700424 | tf_op jit(solution)/shard_map/ppermute | solution.py:634
  9.7 12.2 %collective-permute-start.1 = (bf16[304,384]{1,0:T(8,128)(2,1)S(1)}, bf16[304,384]{1,0:T(8,128)(2,1)S(1)}, u32[]{:S(2)}, u32[]{:S(2)}) collective-permute-start(bf16[304,384]{1,0:T(8,128)(2,1)S(1)} %get-tuple-element.97), channel_id=1, source_target_pairs={{0,4},{2,6},{4,0},{6,2},{1,5},{3,7},{5,1},{7,3},{8,12},{10,14},{12... | collective-permute-start | bytes 700424 | tf_op jit(solution)/shard_map/ppermute | solution.py:634
  11.2 10.7 %collective-permute-start.2 = (bf16[304,384]{1,0:T(8,128)(2,1)S(1)}, bf16[304,384]{1,0:T(8,128)(2,1)S(1)}, u32[]{:S(2)}, u32[]{:S(2)}) collective-permute-start(bf16[304,384]{1,0:T(8,128)(2,1)S(1)} %get-tuple-element.98), channel_id=1, source_target_pairs={{0,6},{2,4},{4,2},{6,0},{1,7},{3,5},{5,3},{7,1},{8,14},{10,12},{12... | collective-permute-start | bytes 700424 | tf_op jit(solution)/shard_map/ppermute | solution.py:634
  15.0 6.8 %collective-permute-start.6 = (bf16[2,96,384]{2,1,0:T(8,128)(2,1)S(1)}, bf16[2,96,384]{2,1,0:T(8,128)(2,1)S(1)}, u32[]{:S(2)}, u32[]{:S(2)}) collective-permute-start(bf16[2,96,384]{2,1,0:T(8,128)(2,1)S(1)} %join_quarter.1.refs_4_), channel_id=1, source_target_pairs={{0,8},{8,0},{16,24},{24,16},{1,9},{9,1},{17,25},{25,17},{2,10},{10... | collective-permute-start | bytes 442376 | tf_op jit(solution)/shard_map/ppermute | solution.py:676
  18.7 10.4 %collective-permute-start.4 = (bf16[2,112,768]{2,1,0:T(8,128)(2,1)S(1)}, bf16[2,112,768]{2,1,0:T(8,128)(2,1)S(1)}, u32[]{:S(2)}, u32[]{:S(2)}) collective-permute-start(bf16[2,112,768]{2,1,0:T(8,128)(2,1)S(1)} %join_attn.1.refs_3_.refs_4_), channel_id=1, source_target_pairs={{0,8},{8,0},{16,24},{24,16},{1,9},{9,1},{17,25},{25,17},{2,10},{10... | collective-permute-start | bytes 1032200 | tf_op jit(solution)/shard_map/ppermute | solution.py:676
  22.0 7.1 %collective-permute-start.7 = (bf16[2,112,768]{2,1,0:T(8,128)(2,1)S(1)}, bf16[2,112,768]{2,1,0:T(8,128)(2,1)S(1)}, u32[]{:S(2)}, u32[]{:S(2)}) collective-permute-start(bf16[2,112,768]{2,1,0:T(8,128)(2,1)S(1)} %get-tuple-element.101), channel_id=1, source_target_pairs={{0,1},{1,0},{2,3},{3,2},{4,5},{5,4},{6,7},{7,6},{8,9},{9,8},{10,11... | collective-permute-start | bytes 1032200 | tf_op jit(solution)/shard_map/ppermute | solution.py:658
  22.0 14.7 %collective-permute-start.12 = (bf16[384,384]{1,0:T(8,128)(2,1)S(1)}, bf16[384,384]{1,0:T(8,128)(2,1)S(1)}, u32[]{:S(2)}, u32[]{:S(2)}) collective-permute-start(bf16[384,384]{1,0:T(8,128)(2,1)S(1)} %get-tuple-element.102.refs_1_), channel_id=1, source_target_pairs={{0,6},{2,4},{4,2},{6,0},{1,7},{3,5},{5,3},{7,1},{8,14},{10,12},{12... | collective-permute-start | bytes 884744 | tf_op jit(solution)/shard_map/ppermute | solution.py:634
  25.1 13.9 %collective-permute-start.11 = (bf16[384,384]{1,0:T(8,128)(2,1)S(1)}, bf16[384,384]{1,0:T(8,128)(2,1)S(1)}, u32[]{:S(2)}, u32[]{:S(2)}) collective-permute-start(bf16[384,384]{1,0:T(8,128)(2,1)S(1)} %get-tuple-element.102.refs_1_), channel_id=1, source_target_pairs={{0,4},{2,6},{4,0},{6,2},{1,5},{3,7},{5,1},{7,3},{8,12},{10,14},{12... | collective-permute-start | bytes 884744 | tf_op jit(solution)/shard_map/ppermute | solution.py:634
  25.6 13.7 %collective-permute-start.10 = (bf16[384,384]{1,0:T(8,128)(2,1)S(1)}, bf16[384,384]{1,0:T(8,128)(2,1)S(1)}, u32[]{:S(2)}, u32[]{:S(2)}) collective-permute-start(bf16[384,384]{1,0:T(8,128)(2,1)S(1)} %get-tuple-element.102.refs_1_), channel_id=1, source_target_pairs={{0,2},{2,0},{4,6},{6,4},{1,3},{3,1},{5,7},{7,5},{8,10},{10,8},{12,... | collective-permute-start | bytes 884744 | tf_op jit(solution)/shard_map/ppermute | solution.py:634
  48.3 10.4 %collective-permute-start.15 = (bf16[2,2,96,384]{3,2,1,0:T(8,128)(2,1)S(1)}, bf16[2,2,96,384]{3,2,1,0:T(8,128)(2,1)S(1)}, u32[]{:S(2)}, u32[]{:S(2)}) collective-permute-start(bf16[2,2,96,384]{3,2,1,0:T(8,128)(2,1)S(1)} %get-tuple-element.132), channel_id=1, source_target_pairs={{0,2},{2,0},{4,6},{6,4},{1,3},{3,1},{5,7},{7,5},{8,10},{10,8},{12,... | collective-permute-start | bytes 884744 | tf_op jit(solution)/shard_map/ppermute | solution.py:764
  49.9 9.0 %collective-permute-start.16 = (bf16[2,2,96,384]{3,2,1,0:T(8,128)(2,1)S(1)}, bf16[2,2,96,384]{3,2,1,0:T(8,128)(2,1)S(1)}, u32[]{:S(2)}, u32[]{:S(2)}) collective-permute-start(bf16[2,2,96,384]{3,2,1,0:T(8,128)(2,1)S(1)} %get-tuple-element.134), channel_id=1, source_target_pairs={{0,4},{2,6},{4,0},{6,2},{1,5},{3,7},{5,1},{7,3},{8,12},{10,14},{12... | collective-permute-start | bytes 884744 | tf_op jit(solution)/shard_map/ppermute | solution.py:764
  59.1 6.3 %collective-permute-start.18 = (bf16[2,96,384]{2,1,0:T(8,128)(2,1)S(1)}, bf16[2,96,384]{2,1,0:T(8,128)(2,1)S(1)}, u32[]{:S(2)}, u32[]{:S(2)}) collective-permute-start(bf16[2,96,384]{2,1,0:T(8,128)(2,1)S(1)} %get-tuple-element.138), channel_id=1, source_target_pairs={{0,4},{2,6},{4,0},{6,2},{1,5},{3,7},{5,1},{7,3},{8,12},{10,14},{12... | collective-permute-start | bytes 442376 | tf_op jit(solution)/shard_map/ppermute | solution.py:777
  60.5 6.7 %collective-permute-start.19 = (bf16[2,96,384]{2,1,0:T(8,128)(2,1)S(1)}, bf16[2,96,384]{2,1,0:T(8,128)(2,1)S(1)}, u32[]{:S(2)}, u32[]{:S(2)}) collective-permute-start(bf16[2,96,384]{2,1,0:T(8,128)(2,1)S(1)} %get-tuple-element.140), channel_id=1, source_target_pairs={{0,2},{2,0},{4,6},{6,4},{1,3},{3,1},{5,7},{7,5},{8,10},{10,8},{12,... | collective-permute-start | bytes 442376 | tf_op jit(solution)/shard_map/ppermute | solution.py:777
  61.3 10.7 %collective-permute-start.20 = (bf16[4,160,128]{2,1,0:T(8,128)(2,1)S(1)}, bf16[4,160,128]{2,1,0:T(8,128)(2,1)S(1)}, u32[]{:S(2)}, u32[]{:S(2)}) collective-permute-start(bf16[4,160,128]{2,1,0:T(8,128)(2,1)S(1)} %get-tuple-element.144), channel_id=1, source_target_pairs={{0,2},{2,0},{4,6},{6,4},{1,3},{3,1},{5,7},{7,5},{8,10},{10,8},{12,... | collective-permute-start | bytes 491528 | tf_op jit(solution)/shard_map/ppermute | solution.py:634
  62.7 9.2 %collective-permute-start.21 = (bf16[4,160,128]{2,1,0:T(8,128)(2,1)S(1)}, bf16[4,160,128]{2,1,0:T(8,128)(2,1)S(1)}, u32[]{:S(2)}, u32[]{:S(2)}) collective-permute-start(bf16[4,160,128]{2,1,0:T(8,128)(2,1)S(1)} %get-tuple-element.145), channel_id=1, source_target_pairs={{0,4},{2,6},{4,0},{6,2},{1,5},{3,7},{5,1},{7,3},{8,12},{10,14},{12... | collective-permute-start | bytes 491528 | tf_op jit(solution)/shard_map/ppermute | solution.py:634
  63.4 10.0 %collective-permute-start.22 = (bf16[4,160,128]{2,1,0:T(8,128)(2,1)S(1)}, bf16[4,160,128]{2,1,0:T(8,128)(2,1)S(1)}, u32[]{:S(2)}, u32[]{:S(2)}) collective-permute-start(bf16[4,160,128]{2,1,0:T(8,128)(2,1)S(1)} %get-tuple-element.146), channel_id=1, source_target_pairs={{0,6},{2,4},{4,2},{6,0},{1,7},{3,5},{5,3},{7,1},{8,14},{10,12},{12... | collective-permute-start | bytes 491528 | tf_op jit(solution)/shard_map/ppermute | solution.py:634
  67.2 6.2 %collective-permute-start.23 = (bf16[2,96,384]{2,1,0:T(8,128)(2,1)S(1)}, bf16[2,96,384]{2,1,0:T(8,128)(2,1)S(1)}, u32[]{:S(2)}, u32[]{:S(2)}) collective-permute-start(bf16[2,96,384]{2,1,0:T(8,128)(2,1)S(1)} %get-tuple-element.148), channel_id=1, source_target_pairs={{0,8},{8,0},{16,24},{24,16},{1,9},{9,1},{17,25},{25,17},{2,10},{10... | collective-permute-start | bytes 442376 | tf_op jit(solution)/shard_map/ppermute | solution.py:802
  68.4 15.1 %all-to-all-start = ((bf16[4,304,384]{2,1,0:T(8,128)(2,1)}), bf16[4,304,384]{2,1,0:T(8,128)(2,1)S(1)}, u32[]{:S(2)}, u32[]{:S(2)}) async-start(bf16[4,304,384]{2,1,0:T(8,128)(2,1)} %returns.1.refs_0_), calls=%async_computation | async-start | bytes 1867776 | tf_op jit(solution)/shard_map/all_to_all | solution.py:789
  73.6 9.7 %collective-permute-start.24 = (bf16[1,96,384]{2,1,0:T(8,128)(2,1)S(1)}, bf16[1,96,384]{2,1,0:T(8,128)(2,1)S(1)}, u32[]{:S(2)}, u32[]{:S(2)}) collective-permute-start(bf16[1,96,384]{2,1,0:T(8,128)(2,1)S(1)} %get-tuple-element.150), channel_id=1, source_target_pairs={{0,16},{8,24},{16,0},{24,8},{1,17},{9,25},{17,1},{25,9},{2,18},{10... | collective-permute-start | bytes 221192 | tf_op jit(solution)/shard_map/ppermute | solution.py:806
  83.7 6.9 %collective-permute-start.31 = (bf16[160,384]{1,0:T(8,128)(2,1)S(1)}, bf16[160,384]{1,0:T(8,128)(2,1)S(1)}, u32[]{:S(2)}, u32[]{:S(2)}) collective-permute-start(bf16[160,384]{1,0:T(8,128)(2,1)S(1)} %sum_dp.1.refs_0_.refs_1_), channel_id=1, source_target_pairs={{0,6},{2,4},{4,2},{6,0},{1,7},{3,5},{5,3},{7,1},{8,14},{10,12},{12... | collective-permute-start | bytes 368648 | tf_op jit(solution)/shard_map/ppermute | solution.py:634
  86.0 6.9 %collective-permute-start.30 = (bf16[160,384]{1,0:T(8,128)(2,1)S(1)}, bf16[160,384]{1,0:T(8,128)(2,1)S(1)}, u32[]{:S(2)}, u32[]{:S(2)}) collective-permute-start(bf16[160,384]{1,0:T(8,128)(2,1)S(1)} %sum_dp.1.refs_0_.refs_1_), channel_id=1, source_target_pairs={{0,4},{2,6},{4,0},{6,2},{1,5},{3,7},{5,1},{7,3},{8,12},{10,14},{12... | collective-permute-start | bytes 368648 | tf_op jit(solution)/shard_map/ppermute | solution.py:634
  86.6 6.4 %collective-permute-start.29 = (bf16[160,384]{1,0:T(8,128)(2,1)S(1)}, bf16[160,384]{1,0:T(8,128)(2,1)S(1)}, u32[]{:S(2)}, u32[]{:S(2)}) collective-permute-start(bf16[160,384]{1,0:T(8,128)(2,1)S(1)} %sum_dp.1.refs_0_.refs_1_), channel_id=1, source_target_pairs={{0,2},{2,0},{4,6},{6,4},{1,3},{3,1},{5,7},{7,5},{8,10},{10,8},{12,... | collective-permute-start | bytes 368648 | tf_op jit(solution)/shard_map/ppermute | solution.py:634
  (14 other events, 65.6 us)

commit v9 on v8

--- a/solution.py
+++ b/solution.py
@@ -347,7 +347,7 @@
                 grads[2 * part + c, d, 0:rows, :] = g[d * rows : (d + 1) * rows, c * cols : (c + 1) * cols]
 
 
-def mlp_sums_kernel(sizes, mid, ctx, wot, vec, cot, w_own, w_oth, hid_own, hid_oth, hgr_own, hgr_oth, bo, dmid, dctx, g_out, vgrad):
+def mlp_sums_kernel(sizes, mid, ctx, wot, vec, cot, w_own, w_oth, hgr_own, hgr_oth, dmid, dctx, g_out, vgrad):
     nctx, ntp, ndp, main, width, rows, padded = sizes
     body = nctx * main
     total = body + EXTRA
@@ -363,14 +363,21 @@
     agrad = jnp.where(valid, middle_grad, 0.0).astype(BF)
     dctx[...] = nn(agrad, wot[...]).astype(BF)
     g_out[...] = tn(agrad, ctx[...])
-    mlp_out = nt(hid_own[...], w_own[:, half:]) + nt(hid_oth[...], w_oth[:, half:]) + vec[6:7, :]
-    bo[...] = (middle + jnp.where(valid, mlp_out, 0.0)).astype(BF)
     shape = vgrad.shape
     v = jnp.where(row_is(shape, 2), jnp.sum(n2g * xhat, axis=0, keepdims=True), 0.0)
     v = jnp.where(row_is(shape, 3), jnp.sum(n2g, axis=0, keepdims=True), v)
     v = jnp.where(row_is(shape, 4), jnp.sum(agrad.astype(F32), axis=0, keepdims=True), v)
     v = jnp.where(row_is(shape, 5), jnp.sum(dcot.astype(F32), axis=0, keepdims=True), v)
     vgrad[...] = v
+
+
+def block_out_kernel(sizes, mid, vec, w_own, w_oth, hid_own, hid_oth, bo):
+    nctx, ntp, ndp, main, width, rows, padded = sizes
+    body = nctx * main
+    half = w_own.shape[1] // 2
+    valid = lax.broadcasted_iota(jnp.int32, (body + EXTRA, 1), 0) <= body
+    mlp_out = nt(hid_own[...], w_own[:, half:]) + nt(hid_oth[...], w_oth[:, half:]) + vec[6:7, :]
+    bo[...] = (mid[...] + jnp.where(valid, mlp_out, 0.0)).astype(BF)
 
 
 def pair_back(p, width, total, body, qkv, dctx, lse, ctx):
@@ -740,15 +747,14 @@
 
     hid_own, hgr_own, ub_own, g2_own = mlp_half("mlp_own", 0, w2_own)
     hid_oth, hgr_oth, ub_oth, g2_oth = mlp_half("mlp_oth", 1, w2_oth, [ub_own])
-    bo, dmid, dctx, g_out, vgrad = call(
+    dmid, dctx, g_out, vgrad = call(
         "mlp_sums",
         one(mlp_sums_kernel),
         [
-            sds((total, width), BF), sds((total, width), F32), sds((total, width), BF), sds((width, width), F32),
-            sds((EXTRA, width), F32),
+            sds((total, width), F32), sds((total, width), BF), sds((width, width), F32), sds((EXTRA, width), F32),
         ],
         mib=32,
-    )(mid, ctx, wot, vec, cot_in, w2_own, w2_oth, hid_own, hid_oth, hgr_own, hgr_oth)
+    )(mid, ctx, wot, vec, cot_in, w2_own, w2_oth, hgr_own, hgr_oth)
 
     def core_sums(name, own, oth, after=()):
         outs = [sds(own.shape[1:], BF)] * nctx
@@ -777,7 +783,10 @@
     got_a, got_b = lax.ppermute(send_a, "ctx", xor(nctx, 2)), lax.ppermute(send_b, "ctx", xor(nctx, 1))
     s1_send = core_sums("sum_core_attn", g1_own, g1_oth, after=[keep_a])
     s1 = over("ctx", nctx, s1_send)
-    keep, send = call("sum_ctx_second", sum_ctx_second_kernel, [one_quarter] * 2, after=[s1_send[0]])(
+    bo = call("block_out", one(block_out_kernel), sds((total, width), BF), mib=16, after=[s1_send[0]])(
+        mid, vec, w2_own, w2_oth, hid_own, hid_oth
+    )
+    keep, send = call("sum_ctx_second", sum_ctx_second_kernel, [one_quarter] * 2, after=[bo])(
         keep_a, got_a, keep_b, got_b
     )
     back = call(

time: 94.3 us -> 93.7 us (level)
    pallas_call x23 -> x24, Pallas kernels: 30.7 us -> 30.9 us  [run(): pl.pallas_call(ordered, name=name, out_shape=out_shape, in_specs=specs, o...]
  transfers between devices with their start and end apart: 33 -> 33, of which waited for: 18 -> 18; matrix products, arithmetic and copies ran while one was open for 0% -> 0% of each run, Pallas kernels for 26% -> 27%
where the time goes in v9:
time: 93.7 us; the launch traced here: 93.5 us
  starting transfers between devices  35.3 us (38%)
  Pallas kernels  30.9 us (33%)
  waiting for transfers between devices  26.3 us (28%)
  between operations  1.01 us (1%)
    pallas_call x24, Pallas kernels, run(): pl.pallas_call(ordered, name=name, out_shape=out_shape, in_specs=specs, o...  30.9 us
    ppermute x15, starting transfers between devices, over(): lax.ppermute(items[k], axis, xor(n, k))  18.7 us
    ppermute x15, waiting for transfers between devices, over(): lax.ppermute(items[k], axis, xor(n, k))  10.4 us
    ppermute x2, waiting for transfers between devices, gather_dp(): lax.ppermute(v, 'dp', xor(ndp, stride))  6.44 us
    ppermute x2, waiting for transfers between devices, gather_dp(): return (v, lax.ppermute(v, 'dp', xor(ndp, 1)))  5.76 us
    ppermute x2, starting transfers between devices, gather_dp(): lax.ppermute(v, 'dp', xor(ndp, stride))  4.18 us
    all_to_all x1, starting transfers between devices, body(): returned = lax.all_to_all(back, 'ctx', 0, 0)  3.51 us
    ppermute x7, waiting for transfers between devices, other(): return lax.ppermute(v, 'tp', flip)  2.17 us
  transfers between devices with their start and end apart: 33, of which 18 were waited for; matrix products, arithmetic and copies ran while one was open for 0% of the time, Pallas kernels for 27%

profile of v9, /device:TPU:0, one launch (start us, length us, event | category | flops | bytes accessed | tf_op | source)
XLA Modules:
  0.0 93.5 jit_solution(8231069300521999105)
XLA Ops:
  0.7 2.2 %pack_weights.1 = (bf16[112,768]{1,0:T(8,128)(2,1)}, bf16[96,384]{1,0:T(8,128)(2,1)}) custom-call(bf16[96,192]{1,0:T(8,128)(2,1)} %refs_0_.1, bf16[96,192]{1,0:T(8,128)(2,1)} %refs_1_.1, bf16[96,192]{1,0:T(8,128)(2,1)} %refs_2_.3, bf16[192,96]{1,0:T(8,128)(2,1)} %refs_3_.2, bf16[96,768]{1,0:T(8,128)(2,1)} %refs_4_.1, bf16[96,768]{1,0:T(8,128)(2,1)} %bitcast.22, ...), custom_call_target="tpu_custom_call" | custom-call | flops 2300000000 | bytes 1 | tf_op jit(solution)/shard_map/pack_weights/pallas_call | solution.py:35
  2.9 4.1 %collective-permute-start.5 = (bf16[1,96,384]{2,1,0:T(8,128)(2,1)}, bf16[1,96,384]{2,1,0:T(8,128)(2,1)S(1)}, u32[]{:S(2)}, u32[]{:S(2)}) collective-permute-start(bf16[1,96,384]{2,1,0:T(8,128)(2,1)} %bitcast.20), channel_id=1, source_target_pairs={{0,16},{8,24},{16,0},{24,8},{1,17},{9,25},{17,1},{25,9},{2,18},{10... | collective-permute-start | bytes 221192 | tf_op jit(solution)/shard_map/ppermute | solution.py:681
  7.8 1.8 %collective-permute-start = (bf16[304,384]{1,0:T(8,128)(2,1)S(1)}, bf16[304,384]{1,0:T(8,128)(2,1)S(1)}, u32[]{:S(2)}, u32[]{:S(2)}) collective-permute-start(bf16[304,384]{1,0:T(8,128)(2,1)S(1)} %get-tuple-element.95), channel_id=1, source_target_pairs={{0,2},{2,0},{4,6},{6,4},{1,3},{3,1},{5,7},{7,5},{8,10},{10,8},{12,... | collective-permute-start | bytes 700424 | tf_op jit(solution)/shard_map/ppermute | solution.py:641
  11.4 3.6 %collective-permute-done.5.refs_1_ = bf16[1,96,384]{2,1,0:T(8,128)(2,1)S(1)} collective-permute-done((bf16[1,96,384]{2,1,0:T(8,128)(2,1)}, bf16[1,96,384]{2,1,0:T(8,128)(2,1)S(1)}, u32[]{:S(2)}, u32[]{:S(2)}) %collective-permute-start.5) | collective-permute-done | bytes 73760 | tf_op jit(solution)/shard_map/ppermute | solution.py:681
  15.8 2.8 %collective-permute-done.3.refs_1_ = bf16[1,112,768]{2,1,0:T(8,128)(2,1)S(1)} collective-permute-done((bf16[1,112,768]{2,1,0:T(8,128)(2,1)}, bf16[1,112,768]{2,1,0:T(8,128)(2,1)S(1)}, u32[]{:S(2)}, u32[]{:S(2)}) %collective-permute-start.3) | collective-permute-done | bytes 172064 | tf_op jit(solution)/shard_map/ppermute | solution.py:681
  19.4 2.4 %collective-permute-done.6.refs_5_ = bf16[2,96,384]{2,1,0:T(8,128)(2,1)S(1)} collective-permute-done((bf16[2,96,384]{2,1,0:T(8,128)(2,1)S(1)}, bf16[2,96,384]{2,1,0:T(8,128)(2,1)S(1)}, u32[]{:S(2)}, u32[]{:S(2)}) %collective-permute-start.6) | collective-permute-done | bytes 147488 | tf_op jit(solution)/shard_map/ppermute | solution.py:683
  22.0 3.1 %collective-permute-start.12 = (bf16[384,384]{1,0:T(8,128)(2,1)S(1)}, bf16[384,384]{1,0:T(8,128)(2,1)S(1)}, u32[]{:S(2)}, u32[]{:S(2)}) collective-permute-start(bf16[384,384]{1,0:T(8,128)(2,1)S(1)} %get-tuple-element.101.refs_1_), channel_id=1, source_target_pairs={{0,6},{2,4},{4,2},{6,0},{1,7},{3,5},{5,3},{7,1},{8,14},{10,12},{12... | collective-permute-start | bytes 884744 | tf_op jit(solution)/shard_map/ppermute | solution.py:641
  25.7 3.3 %collective-permute-done.4.refs_2_.refs_5_ = bf16[2,112,768]{2,1,0:T(8,128)(2,1)S(1)} collective-permute-done((bf16[2,112,768]{2,1,0:T(8,128)(2,1)S(1)}, bf16[2,112,768]{2,1,0:T(8,128)(2,1)S(1)}, u32[]{:S(2)}, u32[]{:S(2)}) %collective-permute-start.4) | collective-permute-done | bytes 344096 | tf_op jit(solution)/shard_map/ppermute | solution.py:683
  30.8 5.9 %attention.1 = (f32[592,384]{1,0:T(8,128)S(1)}, f32[592,384]{1,0:T(8,128)S(1)}, bf16[592,384]{1,0:T(8,128)(2,1)S(1)}, bf16[592,384]{1,0:T(8,128)(2,1)S(1)}, bf16...) custom-call(bf16[304,384]{1,0:T(8,128)(2,1)S(1)} %get-tuple-element., ...), custom_call_target="tpu_custom_call" | custom-call | bytes 1 | tf_op jit(solution)/shard_map/attention/pallas_call | solution.py:35
  36.7 2.3 %collective-permute-done.11.refs_3_ = bf16[384,384]{1,0:T(8,128)(2,1)S(1)} collective-permute-done((bf16[384,384]{1,0:T(8,128)(2,1)S(1)}, bf16[384,384]{1,0:T(8,128)(2,1)S(1)}, u32[]{:S(2)}, u32[]{:S(2)}) %collective-permute-start.11) | collective-permute-done | bytes 294944 | tf_op jit(solution)/shard_map/ppermute | solution.py:641
  39.5 2.2 %mlp_own.1 = (bf16[592,768]{1,0:T(8,128)(2,1)S(1)}, bf16[592,768]{1,0:T(8,128)(2,1)S(1)}, f32[8,768]{1,0:T(8,128)S(1)}, bf16[4,4,96,384]{3,2,1,0:T(8,128)(2,1)S(1)}) custom-call(bf16[592,384]{1,0:T(8,128)(2,1)S(1)} %get-tuple-element.109.refs_0_.refs_1_, bf16[592,384]{1,0:T(8,128)(2,1)S(1)} %get-tuple-element.108.refs_1_.refs_2_.refs_4_, ...), custom_call_target="tpu_custom_call" | custom-call | flops 4600000000 | bytes 1 | tf_op jit(solution)/shard_map/mlp_own/pallas_call | solution.py:35
  42.4 2.3 %mlp_oth.1 = (bf16[592,768]{1,0:T(8,128)(2,1)S(1)}, bf16[592,768]{1,0:T(8,128)(2,1)S(1)}, f32[8,768]{1,0:T(8,128)S(1)}, bf16[4,4,96,384]{3,2,1,0:T(8,128)(2,1)S(1)}) custom-call(f32[8,768]{1,0:T(8,128)S(1)} %get-tuple-element.112.refs_0_.refs_12_, bf16[592,384]{1,0:T(8,128)(2,1)S(1)} %get-tuple-element.109.refs_0_.refs_1_, ...), custom_call_target="tpu_custom_call" | custom-call | flops 4600000000 | bytes 1 | tf_op jit(solution)/shard_map/mlp_oth/pallas_call | solution.py:35
  44.8 2.3 %mlp_sums.1 = (f32[592,384]{1,0:T(8,128)S(1)}, bf16[592,384]{1,0:T(8,128)(2,1)S(1)}, f32[384,384]{1,0:T(8,128)S(1)}, f32[16,384]{1,0:T(8,128)S(1)}) custom-call(f32[592,384]{1,0:T(8,128)S(1)} %get-tuple-element.104.refs_0_.refs_1_, bf16[592,384]{1,0:T(8,128)(2,1)S(1)} %get-tuple-element.105.refs_1_, bf16[384,384]{1,0:T(8,128)(2,1)S(1)} %get-tuple-element.106.refs_2_, ...), custom_call_target="tpu_custom_call" | custom-call | flops 2300000000 | bytes 1 | tf_op jit(solution)/shard_map/mlp_sums/pallas_call | solution.py:35
  47.8 1.5 %collective-permute-start.15 = (bf16[2,2,96,384]{3,2,1,0:T(8,128)(2,1)S(1)}, bf16[2,2,96,384]{3,2,1,0:T(8,128)(2,1)S(1)}, u32[]{:S(2)}, u32[]{:S(2)}) collective-permute-start(bf16[2,2,96,384]{3,2,1,0:T(8,128)(2,1)S(1)} %get-tuple-element.129), channel_id=1, source_target_pairs={{0,2},{2,0},{4,6},{6,4},{1,3},{3,1},{5,7},{7,5},{8,10},{10,8},{12,... | collective-permute-start | bytes 884744 | tf_op jit(solution)/shard_map/ppermute | solution.py:770
  49.9 8.1 %attention_back.1 = (bf16[592,384]{1,0:T(8,128)(2,1)S(1)}, bf16[4,4,160,128]{3,2,1,0:T(8,128)(2,1)S(1)}, bf16[4,4,160,128]{3,2,1,0:T(8,128)(2,1)S(1)}) custom-call(bf16[2,2,96,384]{3,2,1,0:T(8,128)(2,1)S(1)} %get-tuple-element.117.refs_0_.refs_1_, bf16[640,1152]{1,0:T(8,128)(2,1)S(1)} %get-tuple-element.118.refs_1_, ...), custom_call_target="tpu_custom_call" | custom-call | flops 12650000384 | bytes 1 | tf_op jit(solution)/shard_map/attention_back/pallas_call | solution.py:35
  60.6 1.6 %collective-permute-start.20 = (bf16[4,160,128]{2,1,0:T(8,128)(2,1)S(1)}, bf16[4,160,128]{2,1,0:T(8,128)(2,1)S(1)}, u32[]{:S(2)}, u32[]{:S(2)}) collective-permute-start(bf16[4,160,128]{2,1,0:T(8,128)(2,1)S(1)} %get-tuple-element.142), channel_id=1, source_target_pairs={{0,2},{2,0},{4,6},{6,4},{1,3},{3,1},{5,7},{7,5},{8,10},{10,8},{12,... | collective-permute-start | bytes 491528 | tf_op jit(solution)/shard_map/ppermute | solution.py:641
  67.8 3.5 %all-to-all-start = ((bf16[4,304,384]{2,1,0:T(8,128)(2,1)}), bf16[4,304,384]{2,1,0:T(8,128)(2,1)S(1)}, u32[]{:S(2)}, u32[]{:S(2)}) async-start(bf16[4,304,384]{2,1,0:T(8,128)(2,1)} %returns.1.refs_0_), calls=%async_computation | async-start | bytes 1867776 | tf_op jit(solution)/shard_map/all_to_all | solution.py:798
  73.0 2.0 %collective-permute-start.24 = (bf16[1,96,384]{2,1,0:T(8,128)(2,1)S(1)}, bf16[1,96,384]{2,1,0:T(8,128)(2,1)S(1)}, u32[]{:S(2)}, u32[]{:S(2)}) collective-permute-start(bf16[1,96,384]{2,1,0:T(8,128)(2,1)S(1)} %get-tuple-element.148), channel_id=1, source_target_pairs={{0,16},{8,24},{16,0},{24,8},{1,17},{9,25},{17,1},{25,9},{2,18},{10... | collective-permute-start | bytes 221192 | tf_op jit(solution)/shard_map/ppermute | solution.py:815
  74.9 1.7 %collective-permute-start.25 = (bf16[160,128]{1,0:T(8,128)(2,1)S(1)}, bf16[160,128]{1,0:T(8,128)(2,1)S(1)}, u32[]{:S(2)}, u32[]{:S(2)}) collective-permute-start(bf16[160,128]{1,0:T(8,128)(2,1)S(1)} %get-tuple-element.149), channel_id=1, source_target_pairs={{0,8},{8,0},{16,24},{24,16},{1,9},{9,1},{17,25},{25,17},{2,10},{10... | collective-permute-start | bytes 122888 | tf_op jit(solution)/shard_map/ppermute | solution.py:641
  76.8 2.6 %collective-permute-start.27 = (bf16[160,128]{1,0:T(8,128)(2,1)S(1)}, bf16[160,128]{1,0:T(8,128)(2,1)S(1)}, u32[]{:S(2)}, u32[]{:S(2)}) collective-permute-start(bf16[160,128]{1,0:T(8,128)(2,1)S(1)} %get-tuple-element.151), channel_id=1, source_target_pairs={{0,24},{8,16},{16,8},{24,0},{1,25},{9,17},{17,9},{25,1},{2,26},{10... | collective-permute-start | bytes 122888 | tf_op jit(solution)/shard_map/ppermute | solution.py:641
  79.3 2.4 %collective-permute-done.26.refs_4_ = bf16[160,128]{1,0:T(8,128)(2,1)S(1)} collective-permute-done((bf16[160,128]{1,0:T(8,128)(2,1)S(1)}, bf16[160,128]{1,0:T(8,128)(2,1)S(1)}, u32[]{:S(2)}, u32[]{:S(2)}) %collective-permute-start.26) | collective-permute-done | bytes 40992 | tf_op jit(solution)/shard_map/ppermute | solution.py:641
  83.0 2.4 %collective-permute-start.31 = (bf16[160,384]{1,0:T(8,128)(2,1)S(1)}, bf16[160,384]{1,0:T(8,128)(2,1)S(1)}, u32[]{:S(2)}, u32[]{:S(2)}) collective-permute-start(bf16[160,384]{1,0:T(8,128)(2,1)S(1)} %sum_dp.1.refs_0_.refs_1_), channel_id=1, source_target_pairs={{0,6},{2,4},{4,2},{6,0},{1,7},{3,5},{5,3},{7,1},{8,14},{10,12},{12... | collective-permute-start | bytes 368648 | tf_op jit(solution)/shard_map/ppermute | solution.py:641
  86.6 2.7 %place_slots.1 = (f32[1160,384]{1,0:T(8,128)}, f32[1160,384]{1,0:T(8,128)}, f32[8,128]{1,0:T(8,128)S(1)}) custom-call(bf16[4,304,384]{2,1,0:T(8,128)(2,1)S(1)} %hand_on.1.refs_0_, bf16[4,304,384]{2,1,0:T(8,128)(2,1)S(1)} %collective-permute-done.28.refs_1_, f32[2,8,384]{2,1,0:T(8,128)S(1)} %get-tuple-element.152.refs_2_, s32[8,145]{1,0:T(8,128)S(1)} %copy-done.4), custom_call_target="tpu_custom_call" | custom-call | flops 2644999936 | bytes 1 | tf_op jit(solution)/shard_map/place_slots/pallas_call | solution.py:35
  89.9 2.4 %collective-permute-done.30.refs_3_ = bf16[160,384]{1,0:T(8,128)(2,1)S(1)} collective-permute-done((bf16[160,384]{1,0:T(8,128)(2,1)S(1)}, bf16[160,384]{1,0:T(8,128)(2,1)S(1)}, u32[]{:S(2)}, u32[]{:S(2)}) %collective-permute-start.30) | collective-permute-done | bytes 122912 | tf_op jit(solution)/shard_map/ppermute | solution.py:641
  (76 shorter events, 23.2 us)
Async XLA Ops:
  2.9 12.1 %collective-permute-start.5 = (bf16[1,96,384]{2,1,0:T(8,128)(2,1)}, bf16[1,96,384]{2,1,0:T(8,128)(2,1)S(1)}, u32[]{:S(2)}, u32[]{:S(2)}) collective-permute-start(bf16[1,96,384]{2,1,0:T(8,128)(2,1)} %bitcast.20), channel_id=1, source_target_pairs={{0,16},{8,24},{16,0},{24,8},{1,17},{9,25},{17,1},{25,9},{2,18},{10... | collective-permute-start | bytes 221192 | tf_op jit(solution)/shard_map/ppermute | solution.py:681
  7.0 11.6 %collective-permute-start.3 = (bf16[1,112,768]{2,1,0:T(8,128)(2,1)}, bf16[1,112,768]{2,1,0:T(8,128)(2,1)S(1)}, u32[]{:S(2)}, u32[]{:S(2)}) collective-permute-start(bf16[1,112,768]{2,1,0:T(8,128)(2,1)} %bitcast.18), channel_id=1, source_target_pairs={{0,16},{8,24},{16,0},{24,8},{1,17},{9,25},{17,1},{25,9},{2,18},{10... | collective-permute-start | bytes 516104 | tf_op jit(solution)/shard_map/ppermute | solution.py:681
  7.8 14.0 %collective-permute-start = (bf16[304,384]{1,0:T(8,128)(2,1)S(1)}, bf16[304,384]{1,0:T(8,128)(2,1)S(1)}, u32[]{:S(2)}, u32[]{:S(2)}) collective-permute-start(bf16[304,384]{1,0:T(8,128)(2,1)S(1)} %get-tuple-element.95), channel_id=1, source_target_pairs={{0,2},{2,0},{4,6},{6,4},{1,3},{3,1},{5,7},{7,5},{8,10},{10,8},{12,... | collective-permute-start | bytes 700424 | tf_op jit(solution)/shard_map/ppermute | solution.py:641
  9.7 12.2 %collective-permute-start.1 = (bf16[304,384]{1,0:T(8,128)(2,1)S(1)}, bf16[304,384]{1,0:T(8,128)(2,1)S(1)}, u32[]{:S(2)}, u32[]{:S(2)}) collective-permute-start(bf16[304,384]{1,0:T(8,128)(2,1)S(1)} %get-tuple-element.96), channel_id=1, source_target_pairs={{0,4},{2,6},{4,0},{6,2},{1,5},{3,7},{5,1},{7,3},{8,12},{10,14},{12... | collective-permute-start | bytes 700424 | tf_op jit(solution)/shard_map/ppermute | solution.py:641
  11.2 10.7 %collective-permute-start.2 = (bf16[304,384]{1,0:T(8,128)(2,1)S(1)}, bf16[304,384]{1,0:T(8,128)(2,1)S(1)}, u32[]{:S(2)}, u32[]{:S(2)}) collective-permute-start(bf16[304,384]{1,0:T(8,128)(2,1)S(1)} %get-tuple-element.97), channel_id=1, source_target_pairs={{0,6},{2,4},{4,2},{6,0},{1,7},{3,5},{5,3},{7,1},{8,14},{10,12},{12... | collective-permute-start | bytes 700424 | tf_op jit(solution)/shard_map/ppermute | solution.py:641
  15.0 6.8 %collective-permute-start.6 = (bf16[2,96,384]{2,1,0:T(8,128)(2,1)S(1)}, bf16[2,96,384]{2,1,0:T(8,128)(2,1)S(1)}, u32[]{:S(2)}, u32[]{:S(2)}) collective-permute-start(bf16[2,96,384]{2,1,0:T(8,128)(2,1)S(1)} %join_quarter.1.refs_4_), channel_id=1, source_target_pairs={{0,8},{8,0},{16,24},{24,16},{1,9},{9,1},{17,25},{25,17},{2,10},{10... | collective-permute-start | bytes 442376 | tf_op jit(solution)/shard_map/ppermute | solution.py:683
  18.7 10.4 %collective-permute-start.4 = (bf16[2,112,768]{2,1,0:T(8,128)(2,1)S(1)}, bf16[2,112,768]{2,1,0:T(8,128)(2,1)S(1)}, u32[]{:S(2)}, u32[]{:S(2)}) collective-permute-start(bf16[2,112,768]{2,1,0:T(8,128)(2,1)S(1)} %join_attn.1.refs_3_.refs_4_), channel_id=1, source_target_pairs={{0,8},{8,0},{16,24},{24,16},{1,9},{9,1},{17,25},{25,17},{2,10},{10... | collective-permute-start | bytes 1032200 | tf_op jit(solution)/shard_map/ppermute | solution.py:683
  22.0 7.1 %collective-permute-start.7 = (bf16[2,112,768]{2,1,0:T(8,128)(2,1)S(1)}, bf16[2,112,768]{2,1,0:T(8,128)(2,1)S(1)}, u32[]{:S(2)}, u32[]{:S(2)}) collective-permute-start(bf16[2,112,768]{2,1,0:T(8,128)(2,1)S(1)} %get-tuple-element.100), channel_id=1, source_target_pairs={{0,1},{1,0},{2,3},{3,2},{4,5},{5,4},{6,7},{7,6},{8,9},{9,8},{10,11... | collective-permute-start | bytes 1032200 | tf_op jit(solution)/shard_map/ppermute | solution.py:665
  22.0 14.7 %collective-permute-start.12 = (bf16[384,384]{1,0:T(8,128)(2,1)S(1)}, bf16[384,384]{1,0:T(8,128)(2,1)S(1)}, u32[]{:S(2)}, u32[]{:S(2)}) collective-permute-start(bf16[384,384]{1,0:T(8,128)(2,1)S(1)} %get-tuple-element.101.refs_1_), channel_id=1, source_target_pairs={{0,6},{2,4},{4,2},{6,0},{1,7},{3,5},{5,3},{7,1},{8,14},{10,12},{12... | collective-permute-start | bytes 884744 | tf_op jit(solution)/shard_map/ppermute | solution.py:641
  25.1 13.9 %collective-permute-start.11 = (bf16[384,384]{1,0:T(8,128)(2,1)S(1)}, bf16[384,384]{1,0:T(8,128)(2,1)S(1)}, u32[]{:S(2)}, u32[]{:S(2)}) collective-permute-start(bf16[384,384]{1,0:T(8,128)(2,1)S(1)} %get-tuple-element.101.refs_1_), channel_id=1, source_target_pairs={{0,4},{2,6},{4,0},{6,2},{1,5},{3,7},{5,1},{7,3},{8,12},{10,14},{12... | collective-permute-start | bytes 884744 | tf_op jit(solution)/shard_map/ppermute | solution.py:641
  25.6 13.7 %collective-permute-start.10 = (bf16[384,384]{1,0:T(8,128)(2,1)S(1)}, bf16[384,384]{1,0:T(8,128)(2,1)S(1)}, u32[]{:S(2)}, u32[]{:S(2)}) collective-permute-start(bf16[384,384]{1,0:T(8,128)(2,1)S(1)} %get-tuple-element.101.refs_1_), channel_id=1, source_target_pairs={{0,2},{2,0},{4,6},{6,4},{1,3},{3,1},{5,7},{7,5},{8,10},{10,8},{12,... | collective-permute-start | bytes 884744 | tf_op jit(solution)/shard_map/ppermute | solution.py:641
  47.8 10.3 %collective-permute-start.15 = (bf16[2,2,96,384]{3,2,1,0:T(8,128)(2,1)S(1)}, bf16[2,2,96,384]{3,2,1,0:T(8,128)(2,1)S(1)}, u32[]{:S(2)}, u32[]{:S(2)}) collective-permute-start(bf16[2,2,96,384]{3,2,1,0:T(8,128)(2,1)S(1)} %get-tuple-element.129), channel_id=1, source_target_pairs={{0,2},{2,0},{4,6},{6,4},{1,3},{3,1},{5,7},{7,5},{8,10},{10,8},{12,... | collective-permute-start | bytes 884744 | tf_op jit(solution)/shard_map/ppermute | solution.py:770
  49.4 8.8 %collective-permute-start.16 = (bf16[2,2,96,384]{3,2,1,0:T(8,128)(2,1)S(1)}, bf16[2,2,96,384]{3,2,1,0:T(8,128)(2,1)S(1)}, u32[]{:S(2)}, u32[]{:S(2)}) collective-permute-start(bf16[2,2,96,384]{3,2,1,0:T(8,128)(2,1)S(1)} %get-tuple-element.131), channel_id=1, source_target_pairs={{0,4},{2,6},{4,0},{6,2},{1,5},{3,7},{5,1},{7,3},{8,12},{10,14},{12... | collective-permute-start | bytes 884744 | tf_op jit(solution)/shard_map/ppermute | solution.py:770
  58.3 6.9 %collective-permute-start.18 = (bf16[2,96,384]{2,1,0:T(8,128)(2,1)S(1)}, bf16[2,96,384]{2,1,0:T(8,128)(2,1)S(1)}, u32[]{:S(2)}, u32[]{:S(2)}) collective-permute-start(bf16[2,96,384]{2,1,0:T(8,128)(2,1)S(1)} %get-tuple-element.137), channel_id=1, source_target_pairs={{0,4},{2,6},{4,0},{6,2},{1,5},{3,7},{5,1},{7,3},{8,12},{10,14},{12... | collective-permute-start | bytes 442376 | tf_op jit(solution)/shard_map/ppermute | solution.py:783
  59.9 6.7 %collective-permute-start.19 = (bf16[2,96,384]{2,1,0:T(8,128)(2,1)S(1)}, bf16[2,96,384]{2,1,0:T(8,128)(2,1)S(1)}, u32[]{:S(2)}, u32[]{:S(2)}) collective-permute-start(bf16[2,96,384]{2,1,0:T(8,128)(2,1)S(1)} %get-tuple-element.139), channel_id=1, source_target_pairs={{0,2},{2,0},{4,6},{6,4},{1,3},{3,1},{5,7},{7,5},{8,10},{10,8},{12,... | collective-permute-start | bytes 442376 | tf_op jit(solution)/shard_map/ppermute | solution.py:783
  60.6 10.8 %collective-permute-start.20 = (bf16[4,160,128]{2,1,0:T(8,128)(2,1)S(1)}, bf16[4,160,128]{2,1,0:T(8,128)(2,1)S(1)}, u32[]{:S(2)}, u32[]{:S(2)}) collective-permute-start(bf16[4,160,128]{2,1,0:T(8,128)(2,1)S(1)} %get-tuple-element.142), channel_id=1, source_target_pairs={{0,2},{2,0},{4,6},{6,4},{1,3},{3,1},{5,7},{7,5},{8,10},{10,8},{12,... | collective-permute-start | bytes 491528 | tf_op jit(solution)/shard_map/ppermute | solution.py:641
  62.1 9.2 %collective-permute-start.21 = (bf16[4,160,128]{2,1,0:T(8,128)(2,1)S(1)}, bf16[4,160,128]{2,1,0:T(8,128)(2,1)S(1)}, u32[]{:S(2)}, u32[]{:S(2)}) collective-permute-start(bf16[4,160,128]{2,1,0:T(8,128)(2,1)S(1)} %get-tuple-element.143), channel_id=1, source_target_pairs={{0,4},{2,6},{4,0},{6,2},{1,5},{3,7},{5,1},{7,3},{8,12},{10,14},{12... | collective-permute-start | bytes 491528 | tf_op jit(solution)/shard_map/ppermute | solution.py:641
  62.7 10.1 %collective-permute-start.22 = (bf16[4,160,128]{2,1,0:T(8,128)(2,1)S(1)}, bf16[4,160,128]{2,1,0:T(8,128)(2,1)S(1)}, u32[]{:S(2)}, u32[]{:S(2)}) collective-permute-start(bf16[4,160,128]{2,1,0:T(8,128)(2,1)S(1)} %get-tuple-element.144), channel_id=1, source_target_pairs={{0,6},{2,4},{4,2},{6,0},{1,7},{3,5},{5,3},{7,1},{8,14},{10,12},{12... | collective-permute-start | bytes 491528 | tf_op jit(solution)/shard_map/ppermute | solution.py:641
  66.6 6.3 %collective-permute-start.23 = (bf16[2,96,384]{2,1,0:T(8,128)(2,1)S(1)}, bf16[2,96,384]{2,1,0:T(8,128)(2,1)S(1)}, u32[]{:S(2)}, u32[]{:S(2)}) collective-permute-start(bf16[2,96,384]{2,1,0:T(8,128)(2,1)S(1)} %get-tuple-element.146), channel_id=1, source_target_pairs={{0,8},{8,0},{16,24},{24,16},{1,9},{9,1},{17,25},{25,17},{2,10},{10... | collective-permute-start | bytes 442376 | tf_op jit(solution)/shard_map/ppermute | solution.py:811
  67.8 15.1 %all-to-all-start = ((bf16[4,304,384]{2,1,0:T(8,128)(2,1)}), bf16[4,304,384]{2,1,0:T(8,128)(2,1)S(1)}, u32[]{:S(2)}, u32[]{:S(2)}) async-start(bf16[4,304,384]{2,1,0:T(8,128)(2,1)} %returns.1.refs_0_), calls=%async_computation | async-start | bytes 1867776 | tf_op jit(solution)/shard_map/all_to_all | solution.py:798
  73.0 9.7 %collective-permute-start.24 = (bf16[1,96,384]{2,1,0:T(8,128)(2,1)S(1)}, bf16[1,96,384]{2,1,0:T(8,128)(2,1)S(1)}, u32[]{:S(2)}, u32[]{:S(2)}) collective-permute-start(bf16[1,96,384]{2,1,0:T(8,128)(2,1)S(1)} %get-tuple-element.148), channel_id=1, source_target_pairs={{0,16},{8,24},{16,0},{24,8},{1,17},{9,25},{17,1},{25,9},{2,18},{10... | collective-permute-start | bytes 221192 | tf_op jit(solution)/shard_map/ppermute | solution.py:815
  83.0 6.9 %collective-permute-start.31 = (bf16[160,384]{1,0:T(8,128)(2,1)S(1)}, bf16[160,384]{1,0:T(8,128)(2,1)S(1)}, u32[]{:S(2)}, u32[]{:S(2)}) collective-permute-start(bf16[160,384]{1,0:T(8,128)(2,1)S(1)} %sum_dp.1.refs_0_.refs_1_), channel_id=1, source_target_pairs={{0,6},{2,4},{4,2},{6,0},{1,7},{3,5},{5,3},{7,1},{8,14},{10,12},{12... | collective-permute-start | bytes 368648 | tf_op jit(solution)/shard_map/ppermute | solution.py:641
  85.4 6.9 %collective-permute-start.30 = (bf16[160,384]{1,0:T(8,128)(2,1)S(1)}, bf16[160,384]{1,0:T(8,128)(2,1)S(1)}, u32[]{:S(2)}, u32[]{:S(2)}) collective-permute-start(bf16[160,384]{1,0:T(8,128)(2,1)S(1)} %sum_dp.1.refs_0_.refs_1_), channel_id=1, source_target_pairs={{0,4},{2,6},{4,0},{6,2},{1,5},{3,7},{5,1},{7,3},{8,12},{10,14},{12... | collective-permute-start | bytes 368648 | tf_op jit(solution)/shard_map/ppermute | solution.py:641
  86.0 6.4 %collective-permute-start.29 = (bf16[160,384]{1,0:T(8,128)(2,1)S(1)}, bf16[160,384]{1,0:T(8,128)(2,1)S(1)}, u32[]{:S(2)}, u32[]{:S(2)}) collective-permute-start(bf16[160,384]{1,0:T(8,128)(2,1)S(1)} %sum_dp.1.refs_0_.refs_1_), channel_id=1, source_target_pairs={{0,2},{2,0},{4,6},{6,4},{1,3},{3,1},{5,7},{7,5},{8,10},{10,8},{12,... | collective-permute-start | bytes 368648 | tf_op jit(solution)/shard_map/ppermute | solution.py:641
  (14 other events, 65.0 us)

commit v10 on v9

--- a/solution.py
+++ b/solution.py
@@ -371,13 +371,15 @@
     vgrad[...] = v
 
 
-def block_out_kernel(sizes, mid, vec, w_own, w_oth, hid_own, hid_oth, bo):
+def results_kernel(sizes, mid, vec, w_own, w_oth, hid_own, hid_oth, x, dmid, n1_grad, bo, ig):
     nctx, ntp, ndp, main, width, rows, padded = sizes
     body = nctx * main
     half = w_own.shape[1] // 2
     valid = lax.broadcasted_iota(jnp.int32, (body + EXTRA, 1), 0) <= body
     mlp_out = nt(hid_own[...], w_own[:, half:]) + nt(hid_oth[...], w_oth[:, half:]) + vec[6:7, :]
     bo[...] = (mid[...] + jnp.where(valid, mlp_out, 0.0)).astype(BF)
+    xhat, r = norm_stats(x[...])
+    ig[...] = (dmid[...] + norm_back(n1_grad[...] * vec[1:2, :], xhat, r)).astype(BF)
 
 
 def pair_back(p, width, total, body, qkv, dctx, lse, ctx):
@@ -413,8 +415,8 @@
 
 def attention_back_kernel(sizes, *refs):
     nctx, ntp, ndp, main, width, rows, padded = sizes
-    qkv, dctx, lse, ctx, n1, x_in, dmid, wqkv, vec, g_out, vgrad, ub_own, ub_oth = refs[:13]
-    ig, g_own, g_oth, dqkv = refs[13:]
+    qkv, dctx, lse, ctx, n1, x_in, wqkv, g_out, vgrad, ub_own, ub_oth = refs[:11]
+    n1_grad, g_own, g_oth, dqkv = refs[11:]
     body = nctx * main
     total = body + EXTRA
     for p in range(3):
@@ -434,9 +436,8 @@
                 shared = tiles[4 + j // 2][e * rows + lo : e * rows + min(rows, lo + half)]
                 to[j, e, padded : padded + shared.shape[0], :] = shared.astype(BF)
     dn1 = nt(d, wqkv[...])
-    xhat, r = norm_stats(x_in[...])
-    grad = dmid[...] + norm_back(dn1 * vec[1:2, :], xhat, r)
-    ig[...] = grad.astype(BF)
+    n1_grad[...] = dn1
+    xhat, _ = norm_stats(x_in[...])
     gains = jnp.sum(dn1 * xhat, axis=0, keepdims=True)
     shifts = jnp.sum(dn1, axis=0, keepdims=True)
     vecs = [gains, shifts] + [vgrad[i : i + 1, :] for i in range(2, 6)]
@@ -768,14 +769,14 @@
         g2_own, other(g2_oth)
     )
     got_a, got_b = lax.ppermute(send_a, "ctx", xor(nctx, 1)), lax.ppermute(send_b, "ctx", xor(nctx, 2))
-    ig, g1_own, g1_oth = call(
+    n1_grad, g1_own, g1_oth = call(
         "attention_back",
         one(attention_back_kernel),
-        [sds((total, width), BF)] + [sds((4, ndp, padded + padded // 2 + EXTRA, TILE), BF)] * 2,
+        [sds((total, width), F32)] + [sds((4, ndp, padded + padded // 2 + EXTRA, TILE), BF)] * 2,
         scratch=[pltpu.VMEM((total, 3 * width), BF)],
         mib=32,
         after=[keep_a],
-    )(qkv, dctx, lse, ctx_full, n1, x, dmid, wqkv, vec, g_out, vgrad, ub_own, ub_oth)
+    )(qkv, dctx, lse, ctx_full, n1, x, wqkv, g_out, vgrad, ub_own, ub_oth)
     one_quarter = sds(pairs.shape[1:], BF)
     keep_a, send_a, keep_b, send_b = call(
         "sum_ctx_first", sum_ctx_first_kernel, [one_quarter] * 4, after=[g1_own]
@@ -783,9 +784,9 @@
     got_a, got_b = lax.ppermute(send_a, "ctx", xor(nctx, 2)), lax.ppermute(send_b, "ctx", xor(nctx, 1))
     s1_send = core_sums("sum_core_attn", g1_own, g1_oth, after=[keep_a])
     s1 = over("ctx", nctx, s1_send)
-    bo = call("block_out", one(block_out_kernel), sds((total, width), BF), mib=16, after=[s1_send[0]])(
-        mid, vec, w2_own, w2_oth, hid_own, hid_oth
-    )
+    bo, ig = call(
+        "results", one(results_kernel), [sds((total, width), BF)] * 2, mib=16, after=[s1_send[0]]
+    )(mid, vec, w2_own, w2_oth, hid_own, hid_oth, x, dmid, n1_grad)
     keep, send = call("sum_ctx_second", sum_ctx_second_kernel, [one_quarter] * 2, after=[bo])(
         keep_a, got_a, keep_b, got_b
     )

time: 93.7 us -> 93.2 us (level)
  transfers between devices with their start and end apart: 33 -> 33, of which waited for: 18 -> 18; matrix products, arithmetic and copies ran while one was open for 0% -> 0% of each run, Pallas kernels for 27% -> 26%
where the time goes in v10:
time: 93.2 us; the launch traced here: 93 us
  starting transfers between devices  35.3 us (38%)
  Pallas kernels  30.4 us (33%)
  waiting for transfers between devices  26.3 us (28%)
  between operations  1.01 us (1%)
    pallas_call x24, Pallas kernels, run(): pl.pallas_call(ordered, name=name, out_shape=out_shape, in_specs=specs, o...  30.4 us
    ppermute x15, starting transfers between devices, over(): lax.ppermute(items[k], axis, xor(n, k))  18.7 us
    ppermute x15, waiting for transfers between devices, over(): lax.ppermute(items[k], axis, xor(n, k))  10.5 us
    ppermute x2, waiting for transfers between devices, gather_dp(): lax.ppermute(v, 'dp', xor(ndp, stride))  6.44 us
    ppermute x2, waiting for transfers between devices, gather_dp(): return (v, lax.ppermute(v, 'dp', xor(ndp, 1)))  5.76 us
    ppermute x2, starting transfers between devices, gather_dp(): lax.ppermute(v, 'dp', xor(ndp, stride))  4.18 us
    all_to_all x1, starting transfers between devices, body(): returned = lax.all_to_all(back, 'ctx', 0, 0)  3.51 us
    ppermute x7, waiting for transfers between devices, other(): return lax.ppermute(v, 'tp', flip)  2.19 us
  transfers between devices with their start and end apart: 33, of which 18 were waited for; matrix products, arithmetic and copies ran while one was open for 0% of the time, Pallas kernels for 26%

profile of v10, /device:TPU:0, one launch (start us, length us, event | category | flops | bytes accessed | tf_op | source)
XLA Modules:
  0.0 93.0 jit_solution(7227818433458036661)
XLA Ops:
  0.7 2.2 %pack_weights.1 = (bf16[112,768]{1,0:T(8,128)(2,1)}, bf16[96,384]{1,0:T(8,128)(2,1)}) custom-call(bf16[96,192]{1,0:T(8,128)(2,1)} %refs_0_.1, bf16[96,192]{1,0:T(8,128)(2,1)} %refs_1_.1, bf16[96,192]{1,0:T(8,128)(2,1)} %refs_2_.3, bf16[192,96]{1,0:T(8,128)(2,1)} %refs_3_.2, bf16[96,768]{1,0:T(8,128)(2,1)} %refs_4_.1, bf16[96,768]{1,0:T(8,128)(2,1)} %bitcast.22, ...), custom_call_target="tpu_custom_call" | custom-call | flops 2300000000 | bytes 1 | tf_op jit(solution)/shard_map/pack_weights/pallas_call | solution.py:35
  2.9 4.1 %collective-permute-start.5 = (bf16[1,96,384]{2,1,0:T(8,128)(2,1)}, bf16[1,96,384]{2,1,0:T(8,128)(2,1)S(1)}, u32[]{:S(2)}, u32[]{:S(2)}) collective-permute-start(bf16[1,96,384]{2,1,0:T(8,128)(2,1)} %bitcast.20), channel_id=1, source_target_pairs={{0,16},{8,24},{16,0},{24,8},{1,17},{9,25},{17,1},{25,9},{2,18},{10... | collective-permute-start | bytes 221192 | tf_op jit(solution)/shard_map/ppermute | solution.py:682
  7.8 1.8 %collective-permute-start = (bf16[304,384]{1,0:T(8,128)(2,1)S(1)}, bf16[304,384]{1,0:T(8,128)(2,1)S(1)}, u32[]{:S(2)}, u32[]{:S(2)}) collective-permute-start(bf16[304,384]{1,0:T(8,128)(2,1)S(1)} %get-tuple-element.97), channel_id=1, source_target_pairs={{0,2},{2,0},{4,6},{6,4},{1,3},{3,1},{5,7},{7,5},{8,10},{10,8},{12,... | collective-permute-start | bytes 700424 | tf_op jit(solution)/shard_map/ppermute | solution.py:642
  9.7 1.5 %collective-permute-start.1 = (bf16[304,384]{1,0:T(8,128)(2,1)S(1)}, bf16[304,384]{1,0:T(8,128)(2,1)S(1)}, u32[]{:S(2)}, u32[]{:S(2)}) collective-permute-start(bf16[304,384]{1,0:T(8,128)(2,1)S(1)} %get-tuple-element.98), channel_id=1, source_target_pairs={{0,4},{2,6},{4,0},{6,2},{1,5},{3,7},{5,1},{7,3},{8,12},{10,14},{12... | collective-permute-start | bytes 700424 | tf_op jit(solution)/shard_map/ppermute | solution.py:642
  11.4 3.6 %collective-permute-done.5.refs_1_ = bf16[1,96,384]{2,1,0:T(8,128)(2,1)S(1)} collective-permute-done((bf16[1,96,384]{2,1,0:T(8,128)(2,1)}, bf16[1,96,384]{2,1,0:T(8,128)(2,1)S(1)}, u32[]{:S(2)}, u32[]{:S(2)}) %collective-permute-start.5) | collective-permute-done | bytes 73760 | tf_op jit(solution)/shard_map/ppermute | solution.py:682
  15.8 2.8 %collective-permute-done.3.refs_1_ = bf16[1,112,768]{2,1,0:T(8,128)(2,1)S(1)} collective-permute-done((bf16[1,112,768]{2,1,0:T(8,128)(2,1)}, bf16[1,112,768]{2,1,0:T(8,128)(2,1)S(1)}, u32[]{:S(2)}, u32[]{:S(2)}) %collective-permute-start.3) | collective-permute-done | bytes 172064 | tf_op jit(solution)/shard_map/ppermute | solution.py:682
  19.4 2.4 %collective-permute-done.6.refs_5_ = bf16[2,96,384]{2,1,0:T(8,128)(2,1)S(1)} collective-permute-done((bf16[2,96,384]{2,1,0:T(8,128)(2,1)S(1)}, bf16[2,96,384]{2,1,0:T(8,128)(2,1)S(1)}, u32[]{:S(2)}, u32[]{:S(2)}) %collective-permute-start.6) | collective-permute-done | bytes 147488 | tf_op jit(solution)/shard_map/ppermute | solution.py:684
  22.0 3.1 %collective-permute-start.12 = (bf16[384,384]{1,0:T(8,128)(2,1)S(1)}, bf16[384,384]{1,0:T(8,128)(2,1)S(1)}, u32[]{:S(2)}, u32[]{:S(2)}) collective-permute-start(bf16[384,384]{1,0:T(8,128)(2,1)S(1)} %get-tuple-element.103.refs_1_), channel_id=1, source_target_pairs={{0,6},{2,4},{4,2},{6,0},{1,7},{3,5},{5,3},{7,1},{8,14},{10,12},{12... | collective-permute-start | bytes 884744 | tf_op jit(solution)/shard_map/ppermute | solution.py:642
  25.7 3.3 %collective-permute-done.4.refs_2_.refs_5_ = bf16[2,112,768]{2,1,0:T(8,128)(2,1)S(1)} collective-permute-done((bf16[2,112,768]{2,1,0:T(8,128)(2,1)S(1)}, bf16[2,112,768]{2,1,0:T(8,128)(2,1)S(1)}, u32[]{:S(2)}, u32[]{:S(2)}) %collective-permute-start.4) | collective-permute-done | bytes 344096 | tf_op jit(solution)/shard_map/ppermute | solution.py:684
  30.8 5.8 %attention.1 = (f32[592,384]{1,0:T(8,128)S(1)}, f32[592,384]{1,0:T(8,128)S(1)}, bf16[592,384]{1,0:T(8,128)(2,1)S(1)}, bf16[592,384]{1,0:T(8,128)(2,1)S(1)}, bf16...) custom-call(bf16[304,384]{1,0:T(8,128)(2,1)S(1)} %get-tuple-element., ...), custom_call_target="tpu_custom_call" | custom-call | bytes 1 | tf_op jit(solution)/shard_map/attention/pallas_call | solution.py:35
  36.6 2.4 %collective-permute-done.11.refs_3_ = bf16[384,384]{1,0:T(8,128)(2,1)S(1)} collective-permute-done((bf16[384,384]{1,0:T(8,128)(2,1)S(1)}, bf16[384,384]{1,0:T(8,128)(2,1)S(1)}, u32[]{:S(2)}, u32[]{:S(2)}) %collective-permute-start.11) | collective-permute-done | bytes 294944 | tf_op jit(solution)/shard_map/ppermute | solution.py:642
  39.5 2.2 %mlp_own.1 = (bf16[592,768]{1,0:T(8,128)(2,1)S(1)}, bf16[592,768]{1,0:T(8,128)(2,1)S(1)}, f32[8,768]{1,0:T(8,128)S(1)}, bf16[4,4,96,384]{3,2,1,0:T(8,128)(2,1)S(1)}) custom-call(bf16[592,384]{1,0:T(8,128)(2,1)S(1)} %get-tuple-element.111.refs_0_.refs_1_, bf16[592,384]{1,0:T(8,128)(2,1)S(1)} %get-tuple-element.110.refs_1_.refs_2_.refs_4_, ...), custom_call_target="tpu_custom_call" | custom-call | flops 4600000000 | bytes 1 | tf_op jit(solution)/shard_map/mlp_own/pallas_call | solution.py:35
  42.4 2.2 %mlp_oth.1 = (bf16[592,768]{1,0:T(8,128)(2,1)S(1)}, bf16[592,768]{1,0:T(8,128)(2,1)S(1)}, f32[8,768]{1,0:T(8,128)S(1)}, bf16[4,4,96,384]{3,2,1,0:T(8,128)(2,1)S(1)}) custom-call(f32[8,768]{1,0:T(8,128)S(1)} %get-tuple-element.114.refs_0_.refs_10_, bf16[592,384]{1,0:T(8,128)(2,1)S(1)} %get-tuple-element.111.refs_0_.refs_1_, ...), custom_call_target="tpu_custom_call" | custom-call | flops 4600000000 | bytes 1 | tf_op jit(solution)/shard_map/mlp_oth/pallas_call | solution.py:35
  44.8 2.3 %mlp_sums.1 = (f32[592,384]{1,0:T(8,128)S(1)}, bf16[592,384]{1,0:T(8,128)(2,1)S(1)}, f32[384,384]{1,0:T(8,128)S(1)}, f32[16,384]{1,0:T(8,128)S(1)}) custom-call(f32[592,384]{1,0:T(8,128)S(1)} %get-tuple-element.106.refs_0_.refs_1_, bf16[592,384]{1,0:T(8,128)(2,1)S(1)} %get-tuple-element.107.refs_1_, bf16[384,384]{1,0:T(8,128)(2,1)S(1)} %get-tuple-element.108.refs_2_, ...), custom_call_target="tpu_custom_call" | custom-call | flops 2300000000 | bytes 1 | tf_op jit(solution)/shard_map/mlp_sums/pallas_call | solution.py:35
  47.8 1.6 %collective-permute-start.15 = (bf16[2,2,96,384]{3,2,1,0:T(8,128)(2,1)S(1)}, bf16[2,2,96,384]{3,2,1,0:T(8,128)(2,1)S(1)}, u32[]{:S(2)}, u32[]{:S(2)}) collective-permute-start(bf16[2,2,96,384]{3,2,1,0:T(8,128)(2,1)S(1)} %get-tuple-element.130), channel_id=1, source_target_pairs={{0,2},{2,0},{4,6},{6,4},{1,3},{3,1},{5,7},{7,5},{8,10},{10,8},{12,... | collective-permute-start | bytes 884744 | tf_op jit(solution)/shard_map/ppermute | solution.py:771
  49.9 7.7 %attention_back.1 = (f32[592,384]{1,0:T(8,128)S(1)}, bf16[4,4,160,128]{3,2,1,0:T(8,128)(2,1)S(1)}, bf16[4,4,160,128]{3,2,1,0:T(8,128)(2,1)S(1)}) custom-call(bf16[2,2,96,384]{3,2,1,0:T(8,128)(2,1)S(1)} %get-tuple-element.119.refs_0_.refs_1_, bf16[640,1152]{1,0:T(8,128)(2,1)S(1)} %get-tuple-element.120.refs_1_, ...), custom_call_target="tpu_custom_call" | custom-call | flops 12650000384 | bytes 1 | tf_op jit(solution)/shard_map/attention_back/pallas_call | solution.py:35
  67.3 3.5 %all-to-all-start = ((bf16[4,304,384]{2,1,0:T(8,128)(2,1)}), bf16[4,304,384]{2,1,0:T(8,128)(2,1)S(1)}, u32[]{:S(2)}, u32[]{:S(2)}) async-start(bf16[4,304,384]{2,1,0:T(8,128)(2,1)} %returns.1.refs_0_), calls=%async_computation | async-start | bytes 1867776 | tf_op jit(solution)/shard_map/all_to_all | solution.py:799
  72.5 2.0 %collective-permute-start.24 = (bf16[1,96,384]{2,1,0:T(8,128)(2,1)S(1)}, bf16[1,96,384]{2,1,0:T(8,128)(2,1)S(1)}, u32[]{:S(2)}, u32[]{:S(2)}) collective-permute-start(bf16[1,96,384]{2,1,0:T(8,128)(2,1)S(1)} %get-tuple-element.152), channel_id=1, source_target_pairs={{0,16},{8,24},{16,0},{24,8},{1,17},{9,25},{17,1},{25,9},{2,18},{10... | collective-permute-start | bytes 221192 | tf_op jit(solution)/shard_map/ppermute | solution.py:816
  74.5 1.7 %collective-permute-start.25 = (bf16[160,128]{1,0:T(8,128)(2,1)S(1)}, bf16[160,128]{1,0:T(8,128)(2,1)S(1)}, u32[]{:S(2)}, u32[]{:S(2)}) collective-permute-start(bf16[160,128]{1,0:T(8,128)(2,1)S(1)} %get-tuple-element.153), channel_id=1, source_target_pairs={{0,8},{8,0},{16,24},{24,16},{1,9},{9,1},{17,25},{25,17},{2,10},{10... | collective-permute-start | bytes 122888 | tf_op jit(solution)/shard_map/ppermute | solution.py:642
  76.3 2.6 %collective-permute-start.27 = (bf16[160,128]{1,0:T(8,128)(2,1)S(1)}, bf16[160,128]{1,0:T(8,128)(2,1)S(1)}, u32[]{:S(2)}, u32[]{:S(2)}) collective-permute-start(bf16[160,128]{1,0:T(8,128)(2,1)S(1)} %get-tuple-element.155), channel_id=1, source_target_pairs={{0,24},{8,16},{16,8},{24,0},{1,25},{9,17},{17,9},{25,1},{2,26},{10... | collective-permute-start | bytes 122888 | tf_op jit(solution)/shard_map/ppermute | solution.py:642
  78.9 2.4 %collective-permute-done.26.refs_4_ = bf16[160,128]{1,0:T(8,128)(2,1)S(1)} collective-permute-done((bf16[160,128]{1,0:T(8,128)(2,1)S(1)}, bf16[160,128]{1,0:T(8,128)(2,1)S(1)}, u32[]{:S(2)}, u32[]{:S(2)}) %collective-permute-start.26) | collective-permute-done | bytes 40992 | tf_op jit(solution)/shard_map/ppermute | solution.py:642
  82.6 2.4 %collective-permute-start.31 = (bf16[160,384]{1,0:T(8,128)(2,1)S(1)}, bf16[160,384]{1,0:T(8,128)(2,1)S(1)}, u32[]{:S(2)}, u32[]{:S(2)}) collective-permute-start(bf16[160,384]{1,0:T(8,128)(2,1)S(1)} %sum_dp.1.refs_0_.refs_1_), channel_id=1, source_target_pairs={{0,6},{2,4},{4,2},{6,0},{1,7},{3,5},{5,3},{7,1},{8,14},{10,12},{12... | collective-permute-start | bytes 368648 | tf_op jit(solution)/shard_map/ppermute | solution.py:642
  86.1 2.7 %place_slots.1 = (f32[1160,384]{1,0:T(8,128)}, f32[1160,384]{1,0:T(8,128)}, f32[8,128]{1,0:T(8,128)S(1)}) custom-call(bf16[4,304,384]{2,1,0:T(8,128)(2,1)S(1)} %hand_on.1.refs_0_, bf16[4,304,384]{2,1,0:T(8,128)(2,1)S(1)} %collective-permute-done.28.refs_1_, f32[2,8,384]{2,1,0:T(8,128)S(1)} %get-tuple-element.156.refs_2_, s32[8,145]{1,0:T(8,128)S(1)} %copy-done.4), custom_call_target="tpu_custom_call" | custom-call | flops 2644999936 | bytes 1 | tf_op jit(solution)/shard_map/place_slots/pallas_call | solution.py:35
  89.4 2.4 %collective-permute-done.30.refs_3_ = bf16[160,384]{1,0:T(8,128)(2,1)S(1)} collective-permute-done((bf16[160,384]{1,0:T(8,128)(2,1)S(1)}, bf16[160,384]{1,0:T(8,128)(2,1)S(1)}, u32[]{:S(2)}, u32[]{:S(2)}) %collective-permute-start.30) | collective-permute-done | bytes 122912 | tf_op jit(solution)/shard_map/ppermute | solution.py:642
  (76 shorter events, 23.2 us)
Async XLA Ops:
  2.9 12.1 %collective-permute-start.5 = (bf16[1,96,384]{2,1,0:T(8,128)(2,1)}, bf16[1,96,384]{2,1,0:T(8,128)(2,1)S(1)}, u32[]{:S(2)}, u32[]{:S(2)}) collective-permute-start(bf16[1,96,384]{2,1,0:T(8,128)(2,1)} %bitcast.20), channel_id=1, source_target_pairs={{0,16},{8,24},{16,0},{24,8},{1,17},{9,25},{17,1},{25,9},{2,18},{10... | collective-permute-start | bytes 221192 | tf_op jit(solution)/shard_map/ppermute | solution.py:682
  7.0 11.6 %collective-permute-start.3 = (bf16[1,112,768]{2,1,0:T(8,128)(2,1)}, bf16[1,112,768]{2,1,0:T(8,128)(2,1)S(1)}, u32[]{:S(2)}, u32[]{:S(2)}) collective-permute-start(bf16[1,112,768]{2,1,0:T(8,128)(2,1)} %bitcast.18), channel_id=1, source_target_pairs={{0,16},{8,24},{16,0},{24,8},{1,17},{9,25},{17,1},{25,9},{2,18},{10... | collective-permute-start | bytes 516104 | tf_op jit(solution)/shard_map/ppermute | solution.py:682
  7.8 14.0 %collective-permute-start = (bf16[304,384]{1,0:T(8,128)(2,1)S(1)}, bf16[304,384]{1,0:T(8,128)(2,1)S(1)}, u32[]{:S(2)}, u32[]{:S(2)}) collective-permute-start(bf16[304,384]{1,0:T(8,128)(2,1)S(1)} %get-tuple-element.97), channel_id=1, source_target_pairs={{0,2},{2,0},{4,6},{6,4},{1,3},{3,1},{5,7},{7,5},{8,10},{10,8},{12,... | collective-permute-start | bytes 700424 | tf_op jit(solution)/shard_map/ppermute | solution.py:642
  9.7 12.2 %collective-permute-start.1 = (bf16[304,384]{1,0:T(8,128)(2,1)S(1)}, bf16[304,384]{1,0:T(8,128)(2,1)S(1)}, u32[]{:S(2)}, u32[]{:S(2)}) collective-permute-start(bf16[304,384]{1,0:T(8,128)(2,1)S(1)} %get-tuple-element.98), channel_id=1, source_target_pairs={{0,4},{2,6},{4,0},{6,2},{1,5},{3,7},{5,1},{7,3},{8,12},{10,14},{12... | collective-permute-start | bytes 700424 | tf_op jit(solution)/shard_map/ppermute | solution.py:642
  11.2 10.7 %collective-permute-start.2 = (bf16[304,384]{1,0:T(8,128)(2,1)S(1)}, bf16[304,384]{1,0:T(8,128)(2,1)S(1)}, u32[]{:S(2)}, u32[]{:S(2)}) collective-permute-start(bf16[304,384]{1,0:T(8,128)(2,1)S(1)} %get-tuple-element.99), channel_id=1, source_target_pairs={{0,6},{2,4},{4,2},{6,0},{1,7},{3,5},{5,3},{7,1},{8,14},{10,12},{12... | collective-permute-start | bytes 700424 | tf_op jit(solution)/shard_map/ppermute | solution.py:642
  15.0 6.8 %collective-permute-start.6 = (bf16[2,96,384]{2,1,0:T(8,128)(2,1)S(1)}, bf16[2,96,384]{2,1,0:T(8,128)(2,1)S(1)}, u32[]{:S(2)}, u32[]{:S(2)}) collective-permute-start(bf16[2,96,384]{2,1,0:T(8,128)(2,1)S(1)} %join_quarter.1.refs_4_), channel_id=1, source_target_pairs={{0,8},{8,0},{16,24},{24,16},{1,9},{9,1},{17,25},{25,17},{2,10},{10... | collective-permute-start | bytes 442376 | tf_op jit(solution)/shard_map/ppermute | solution.py:684
  18.7 10.4 %collective-permute-start.4 = (bf16[2,112,768]{2,1,0:T(8,128)(2,1)S(1)}, bf16[2,112,768]{2,1,0:T(8,128)(2,1)S(1)}, u32[]{:S(2)}, u32[]{:S(2)}) collective-permute-start(bf16[2,112,768]{2,1,0:T(8,128)(2,1)S(1)} %join_attn.1.refs_3_.refs_4_), channel_id=1, source_target_pairs={{0,8},{8,0},{16,24},{24,16},{1,9},{9,1},{17,25},{25,17},{2,10},{10... | collective-permute-start | bytes 1032200 | tf_op jit(solution)/shard_map/ppermute | solution.py:684
  22.0 7.1 %collective-permute-start.7 = (bf16[2,112,768]{2,1,0:T(8,128)(2,1)S(1)}, bf16[2,112,768]{2,1,0:T(8,128)(2,1)S(1)}, u32[]{:S(2)}, u32[]{:S(2)}) collective-permute-start(bf16[2,112,768]{2,1,0:T(8,128)(2,1)S(1)} %get-tuple-element.102), channel_id=1, source_target_pairs={{0,1},{1,0},{2,3},{3,2},{4,5},{5,4},{6,7},{7,6},{8,9},{9,8},{10,11... | collective-permute-start | bytes 1032200 | tf_op jit(solution)/shard_map/ppermute | solution.py:666
  22.0 14.6 %collective-permute-start.12 = (bf16[384,384]{1,0:T(8,128)(2,1)S(1)}, bf16[384,384]{1,0:T(8,128)(2,1)S(1)}, u32[]{:S(2)}, u32[]{:S(2)}) collective-permute-start(bf16[384,384]{1,0:T(8,128)(2,1)S(1)} %get-tuple-element.103.refs_1_), channel_id=1, source_target_pairs={{0,6},{2,4},{4,2},{6,0},{1,7},{3,5},{5,3},{7,1},{8,14},{10,12},{12... | collective-permute-start | bytes 884744 | tf_op jit(solution)/shard_map/ppermute | solution.py:642
  25.1 13.9 %collective-permute-start.11 = (bf16[384,384]{1,0:T(8,128)(2,1)S(1)}, bf16[384,384]{1,0:T(8,128)(2,1)S(1)}, u32[]{:S(2)}, u32[]{:S(2)}) collective-permute-start(bf16[384,384]{1,0:T(8,128)(2,1)S(1)} %get-tuple-element.103.refs_1_), channel_id=1, source_target_pairs={{0,4},{2,6},{4,0},{6,2},{1,5},{3,7},{5,1},{7,3},{8,12},{10,14},{12... | collective-permute-start | bytes 884744 | tf_op jit(solution)/shard_map/ppermute | solution.py:642
  25.6 13.7 %collective-permute-start.10 = (bf16[384,384]{1,0:T(8,128)(2,1)S(1)}, bf16[384,384]{1,0:T(8,128)(2,1)S(1)}, u32[]{:S(2)}, u32[]{:S(2)}) collective-permute-start(bf16[384,384]{1,0:T(8,128)(2,1)S(1)} %get-tuple-element.103.refs_1_), channel_id=1, source_target_pairs={{0,2},{2,0},{4,6},{6,4},{1,3},{3,1},{5,7},{7,5},{8,10},{10,8},{12,... | collective-permute-start | bytes 884744 | tf_op jit(solution)/shard_map/ppermute | solution.py:642
  47.8 9.8 %collective-permute-start.15 = (bf16[2,2,96,384]{3,2,1,0:T(8,128)(2,1)S(1)}, bf16[2,2,96,384]{3,2,1,0:T(8,128)(2,1)S(1)}, u32[]{:S(2)}, u32[]{:S(2)}) collective-permute-start(bf16[2,2,96,384]{3,2,1,0:T(8,128)(2,1)S(1)} %get-tuple-element.130), channel_id=1, source_target_pairs={{0,2},{2,0},{4,6},{6,4},{1,3},{3,1},{5,7},{7,5},{8,10},{10,8},{12,... | collective-permute-start | bytes 884744 | tf_op jit(solution)/shard_map/ppermute | solution.py:771
  49.4 8.8 %collective-permute-start.16 = (bf16[2,2,96,384]{3,2,1,0:T(8,128)(2,1)S(1)}, bf16[2,2,96,384]{3,2,1,0:T(8,128)(2,1)S(1)}, u32[]{:S(2)}, u32[]{:S(2)}) collective-permute-start(bf16[2,2,96,384]{3,2,1,0:T(8,128)(2,1)S(1)} %get-tuple-element.132), channel_id=1, source_target_pairs={{0,4},{2,6},{4,0},{6,2},{1,5},{3,7},{5,1},{7,3},{8,12},{10,14},{12... | collective-permute-start | bytes 884744 | tf_op jit(solution)/shard_map/ppermute | solution.py:771
  58.3 7.0 %collective-permute-start.18 = (bf16[2,96,384]{2,1,0:T(8,128)(2,1)S(1)}, bf16[2,96,384]{2,1,0:T(8,128)(2,1)S(1)}, u32[]{:S(2)}, u32[]{:S(2)}) collective-permute-start(bf16[2,96,384]{2,1,0:T(8,128)(2,1)S(1)} %get-tuple-element.141), channel_id=1, source_target_pairs={{0,4},{2,6},{4,0},{6,2},{1,5},{3,7},{5,1},{7,3},{8,12},{10,14},{12... | collective-permute-start | bytes 442376 | tf_op jit(solution)/shard_map/ppermute | solution.py:784
  59.4 6.7 %collective-permute-start.19 = (bf16[2,96,384]{2,1,0:T(8,128)(2,1)S(1)}, bf16[2,96,384]{2,1,0:T(8,128)(2,1)S(1)}, u32[]{:S(2)}, u32[]{:S(2)}) collective-permute-start(bf16[2,96,384]{2,1,0:T(8,128)(2,1)S(1)} %get-tuple-element.143), channel_id=1, source_target_pairs={{0,2},{2,0},{4,6},{6,4},{1,3},{3,1},{5,7},{7,5},{8,10},{10,8},{12,... | collective-permute-start | bytes 442376 | tf_op jit(solution)/shard_map/ppermute | solution.py:784
  60.5 10.4 %collective-permute-start.20 = (bf16[4,160,128]{2,1,0:T(8,128)(2,1)S(1)}, bf16[4,160,128]{2,1,0:T(8,128)(2,1)S(1)}, u32[]{:S(2)}, u32[]{:S(2)}) collective-permute-start(bf16[4,160,128]{2,1,0:T(8,128)(2,1)S(1)} %get-tuple-element.146), channel_id=1, source_target_pairs={{0,2},{2,0},{4,6},{6,4},{1,3},{3,1},{5,7},{7,5},{8,10},{10,8},{12,... | collective-permute-start | bytes 491528 | tf_op jit(solution)/shard_map/ppermute | solution.py:642
  61.6 9.2 %collective-permute-start.21 = (bf16[4,160,128]{2,1,0:T(8,128)(2,1)S(1)}, bf16[4,160,128]{2,1,0:T(8,128)(2,1)S(1)}, u32[]{:S(2)}, u32[]{:S(2)}) collective-permute-start(bf16[4,160,128]{2,1,0:T(8,128)(2,1)S(1)} %get-tuple-element.147), channel_id=1, source_target_pairs={{0,4},{2,6},{4,0},{6,2},{1,5},{3,7},{5,1},{7,3},{8,12},{10,14},{12... | collective-permute-start | bytes 491528 | tf_op jit(solution)/shard_map/ppermute | solution.py:642
  62.6 9.7 %collective-permute-start.22 = (bf16[4,160,128]{2,1,0:T(8,128)(2,1)S(1)}, bf16[4,160,128]{2,1,0:T(8,128)(2,1)S(1)}, u32[]{:S(2)}, u32[]{:S(2)}) collective-permute-start(bf16[4,160,128]{2,1,0:T(8,128)(2,1)S(1)} %get-tuple-element.148), channel_id=1, source_target_pairs={{0,6},{2,4},{4,2},{6,0},{1,7},{3,5},{5,3},{7,1},{8,14},{10,12},{12... | collective-permute-start | bytes 491528 | tf_op jit(solution)/shard_map/ppermute | solution.py:642
  66.1 6.2 %collective-permute-start.23 = (bf16[2,96,384]{2,1,0:T(8,128)(2,1)S(1)}, bf16[2,96,384]{2,1,0:T(8,128)(2,1)S(1)}, u32[]{:S(2)}, u32[]{:S(2)}) collective-permute-start(bf16[2,96,384]{2,1,0:T(8,128)(2,1)S(1)} %get-tuple-element.150), channel_id=1, source_target_pairs={{0,8},{8,0},{16,24},{24,16},{1,9},{9,1},{17,25},{25,17},{2,10},{10... | collective-permute-start | bytes 442376 | tf_op jit(solution)/shard_map/ppermute | solution.py:812
  67.3 15.1 %all-to-all-start = ((bf16[4,304,384]{2,1,0:T(8,128)(2,1)}), bf16[4,304,384]{2,1,0:T(8,128)(2,1)S(1)}, u32[]{:S(2)}, u32[]{:S(2)}) async-start(bf16[4,304,384]{2,1,0:T(8,128)(2,1)} %returns.1.refs_0_), calls=%async_computation | async-start | bytes 1867776 | tf_op jit(solution)/shard_map/all_to_all | solution.py:799
  72.5 9.7 %collective-permute-start.24 = (bf16[1,96,384]{2,1,0:T(8,128)(2,1)S(1)}, bf16[1,96,384]{2,1,0:T(8,128)(2,1)S(1)}, u32[]{:S(2)}, u32[]{:S(2)}) collective-permute-start(bf16[1,96,384]{2,1,0:T(8,128)(2,1)S(1)} %get-tuple-element.152), channel_id=1, source_target_pairs={{0,16},{8,24},{16,0},{24,8},{1,17},{9,25},{17,1},{25,9},{2,18},{10... | collective-permute-start | bytes 221192 | tf_op jit(solution)/shard_map/ppermute | solution.py:816
  82.6 6.9 %collective-permute-start.31 = (bf16[160,384]{1,0:T(8,128)(2,1)S(1)}, bf16[160,384]{1,0:T(8,128)(2,1)S(1)}, u32[]{:S(2)}, u32[]{:S(2)}) collective-permute-start(bf16[160,384]{1,0:T(8,128)(2,1)S(1)} %sum_dp.1.refs_0_.refs_1_), channel_id=1, source_target_pairs={{0,6},{2,4},{4,2},{6,0},{1,7},{3,5},{5,3},{7,1},{8,14},{10,12},{12... | collective-permute-start | bytes 368648 | tf_op jit(solution)/shard_map/ppermute | solution.py:642
  84.9 6.9 %collective-permute-start.30 = (bf16[160,384]{1,0:T(8,128)(2,1)S(1)}, bf16[160,384]{1,0:T(8,128)(2,1)S(1)}, u32[]{:S(2)}, u32[]{:S(2)}) collective-permute-start(bf16[160,384]{1,0:T(8,128)(2,1)S(1)} %sum_dp.1.refs_0_.refs_1_), channel_id=1, source_target_pairs={{0,4},{2,6},{4,0},{6,2},{1,5},{3,7},{5,1},{7,3},{8,12},{10,14},{12... | collective-permute-start | bytes 368648 | tf_op jit(solution)/shard_map/ppermute | solution.py:642
  85.5 6.4 %collective-permute-start.29 = (bf16[160,384]{1,0:T(8,128)(2,1)S(1)}, bf16[160,384]{1,0:T(8,128)(2,1)S(1)}, u32[]{:S(2)}, u32[]{:S(2)}) collective-permute-start(bf16[160,384]{1,0:T(8,128)(2,1)S(1)} %sum_dp.1.refs_0_.refs_1_), channel_id=1, source_target_pairs={{0,2},{2,0},{4,6},{6,4},{1,3},{3,1},{5,7},{7,5},{8,10},{10,8},{12,... | collective-permute-start | bytes 368648 | tf_op jit(solution)/shard_map/ppermute | solution.py:642
  (14 other events, 65.4 us)

commit v11 on v10

--- a/solution.py
+++ b/solution.py
@@ -457,7 +457,7 @@
 def sum_core_kernel(n, own, oth, *outs):
     me = lax.axis_index("ctx")
     for k in range(n):
-        outs[k][...] = (own[me ^ k].astype(F32) + oth[me ^ k].astype(F32)).astype(BF)
+        outs[k][...] = own[me ^ k] + oth[me ^ k]
 
 
 def sum_ctx_kernel(n, ndp, *refs):
@@ -486,7 +486,7 @@
     half = own.shape[1] // 2
 
     def put(to, i, quarter, blocks):
-        to[i] = (own[quarter, blocks].astype(F32) + oth[quarter, blocks].astype(F32)).astype(BF)
+        to[i] = own[quarter, blocks] + oth[quarter, blocks]
 
     for i in range(2):
         first, second = slice(0, half), slice(half, 2 * half)
@@ -502,8 +502,8 @@
         (own_a, got_a, keep_a, send_a, high),
         (own_b, got_b, keep_b, send_b, low),
     ):
-        keep[...] = (own[bit].astype(F32) + got[bit].astype(F32)).astype(BF)
-        send[...] = (own[1 - bit].astype(F32) + got[1 - bit].astype(F32)).astype(BF)
+        keep[...] = own[bit] + got[bit]
+        send[...] = own[1 - bit] + got[1 - bit]
 
 
 def sum_ctx_second_kernel(own_a, got_a, own_b, got_b, keep, send):
@@ -512,7 +512,7 @@
     for j in range(keep.shape[0]):
         own, got, at = (own_a, got_a, 2 * j) if 2 * j < half else (own_b, got_b, 2 * j - half)
         for to, i in ((keep, at + bit), (send, at + 1 - bit)):
-            to[j] = (own[i].astype(F32) + got[i].astype(F32)).astype(BF)
+            to[j] = own[i] + got[i]
 
 
 def add_halves_kernel(stride, own, got, keep, send):

time: 93.2 us -> 93 us (level)
  no operation moved by 1% of the time
where the time goes in v11:
time: 93 us; the launch traced here: 92.9 us
  starting transfers between devices  35.2 us (38%)
  Pallas kernels  30.3 us (33%)
  waiting for transfers between devices  26.4 us (28%)
  between operations  1.01 us (1%)
    pallas_call x24, Pallas kernels, run(): pl.pallas_call(ordered, name=name, out_shape=out_shape, in_specs=specs, o...  30.3 us
    ppermute x15, starting transfers between devices, over(): lax.ppermute(items[k], axis, xor(n, k))  18.7 us
    ppermute x15, waiting for transfers between devices, over(): lax.ppermute(items[k], axis, xor(n, k))  10.5 us
    ppermute x2, waiting for transfers between devices, gather_dp(): lax.ppermute(v, 'dp', xor(ndp, stride))  6.44 us
    ppermute x2, waiting for transfers between devices, gather_dp(): return (v, lax.ppermute(v, 'dp', xor(ndp, 1)))  5.76 us
    ppermute x2, starting transfers between devices, gather_dp(): lax.ppermute(v, 'dp', xor(ndp, stride))  4.18 us
    all_to_all x1, starting transfers between devices, body(): returned = lax.all_to_all(back, 'ctx', 0, 0)  3.51 us
    ppermute x7, waiting for transfers between devices, other(): return lax.ppermute(v, 'tp', flip)  2.19 us
  transfers between devices with their start and end apart: 33, of which 18 were waited for; matrix products, arithmetic and copies ran while one was open for 0% of the time, Pallas kernels for 26%

profile of v11, /device:TPU:0, one launch (start us, length us, event | category | flops | bytes accessed | tf_op | source)
XLA Modules:
  0.0 92.9 jit_solution(14630829000464865710)
XLA Ops:
  0.7 2.2 %pack_weights.1 = (bf16[112,768]{1,0:T(8,128)(2,1)}, bf16[96,384]{1,0:T(8,128)(2,1)}) custom-call(bf16[96,192]{1,0:T(8,128)(2,1)} %refs_0_.1, bf16[96,192]{1,0:T(8,128)(2,1)} %refs_1_.1, bf16[96,192]{1,0:T(8,128)(2,1)} %refs_2_.3, bf16[192,96]{1,0:T(8,128)(2,1)} %refs_3_.2, bf16[96,768]{1,0:T(8,128)(2,1)} %refs_4_.1, bf16[96,768]{1,0:T(8,128)(2,1)} %bitcast.22, ...), custom_call_target="tpu_custom_call" | custom-call | flops 2300000000 | bytes 1 | tf_op jit(solution)/shard_map/pack_weights/pallas_call | solution.py:35
  2.9 4.1 %collective-permute-start.5 = (bf16[1,96,384]{2,1,0:T(8,128)(2,1)}, bf16[1,96,384]{2,1,0:T(8,128)(2,1)S(1)}, u32[]{:S(2)}, u32[]{:S(2)}) collective-permute-start(bf16[1,96,384]{2,1,0:T(8,128)(2,1)} %bitcast.20), channel_id=1, source_target_pairs={{0,16},{8,24},{16,0},{24,8},{1,17},{9,25},{17,1},{25,9},{2,18},{10... | collective-permute-start | bytes 221192 | tf_op jit(solution)/shard_map/ppermute | solution.py:682
  7.8 1.8 %collective-permute-start = (bf16[304,384]{1,0:T(8,128)(2,1)S(1)}, bf16[304,384]{1,0:T(8,128)(2,1)S(1)}, u32[]{:S(2)}, u32[]{:S(2)}) collective-permute-start(bf16[304,384]{1,0:T(8,128)(2,1)S(1)} %get-tuple-element.97), channel_id=1, source_target_pairs={{0,2},{2,0},{4,6},{6,4},{1,3},{3,1},{5,7},{7,5},{8,10},{10,8},{12,... | collective-permute-start | bytes 700424 | tf_op jit(solution)/shard_map/ppermute | solution.py:642
  9.7 1.5 %collective-permute-start.1 = (bf16[304,384]{1,0:T(8,128)(2,1)S(1)}, bf16[304,384]{1,0:T(8,128)(2,1)S(1)}, u32[]{:S(2)}, u32[]{:S(2)}) collective-permute-start(bf16[304,384]{1,0:T(8,128)(2,1)S(1)} %get-tuple-element.98), channel_id=1, source_target_pairs={{0,4},{2,6},{4,0},{6,2},{1,5},{3,7},{5,1},{7,3},{8,12},{10,14},{12... | collective-permute-start | bytes 700424 | tf_op jit(solution)/shard_map/ppermute | solution.py:642
  11.4 3.6 %collective-permute-done.5.refs_1_ = bf16[1,96,384]{2,1,0:T(8,128)(2,1)S(1)} collective-permute-done((bf16[1,96,384]{2,1,0:T(8,128)(2,1)}, bf16[1,96,384]{2,1,0:T(8,128)(2,1)S(1)}, u32[]{:S(2)}, u32[]{:S(2)}) %collective-permute-start.5) | collective-permute-done | bytes 73760 | tf_op jit(solution)/shard_map/ppermute | solution.py:682
  15.8 2.8 %collective-permute-done.3.refs_1_ = bf16[1,112,768]{2,1,0:T(8,128)(2,1)S(1)} collective-permute-done((bf16[1,112,768]{2,1,0:T(8,128)(2,1)}, bf16[1,112,768]{2,1,0:T(8,128)(2,1)S(1)}, u32[]{:S(2)}, u32[]{:S(2)}) %collective-permute-start.3) | collective-permute-done | bytes 172064 | tf_op jit(solution)/shard_map/ppermute | solution.py:682
  19.4 2.4 %collective-permute-done.6.refs_5_ = bf16[2,96,384]{2,1,0:T(8,128)(2,1)S(1)} collective-permute-done((bf16[2,96,384]{2,1,0:T(8,128)(2,1)S(1)}, bf16[2,96,384]{2,1,0:T(8,128)(2,1)S(1)}, u32[]{:S(2)}, u32[]{:S(2)}) %collective-permute-start.6) | collective-permute-done | bytes 147488 | tf_op jit(solution)/shard_map/ppermute | solution.py:684
  22.0 3.1 %collective-permute-start.12 = (bf16[384,384]{1,0:T(8,128)(2,1)S(1)}, bf16[384,384]{1,0:T(8,128)(2,1)S(1)}, u32[]{:S(2)}, u32[]{:S(2)}) collective-permute-start(bf16[384,384]{1,0:T(8,128)(2,1)S(1)} %get-tuple-element.103.refs_1_), channel_id=1, source_target_pairs={{0,6},{2,4},{4,2},{6,0},{1,7},{3,5},{5,3},{7,1},{8,14},{10,12},{12... | collective-permute-start | bytes 884744 | tf_op jit(solution)/shard_map/ppermute | solution.py:642
  25.7 3.3 %collective-permute-done.4.refs_2_.refs_5_ = bf16[2,112,768]{2,1,0:T(8,128)(2,1)S(1)} collective-permute-done((bf16[2,112,768]{2,1,0:T(8,128)(2,1)S(1)}, bf16[2,112,768]{2,1,0:T(8,128)(2,1)S(1)}, u32[]{:S(2)}, u32[]{:S(2)}) %collective-permute-start.4) | collective-permute-done | bytes 344096 | tf_op jit(solution)/shard_map/ppermute | solution.py:684
  30.8 5.8 %attention.1 = (f32[592,384]{1,0:T(8,128)S(1)}, f32[592,384]{1,0:T(8,128)S(1)}, bf16[592,384]{1,0:T(8,128)(2,1)S(1)}, bf16[592,384]{1,0:T(8,128)(2,1)S(1)}, bf16...) custom-call(bf16[304,384]{1,0:T(8,128)(2,1)S(1)} %get-tuple-element., ...), custom_call_target="tpu_custom_call" | custom-call | bytes 1 | tf_op jit(solution)/shard_map/attention/pallas_call | solution.py:35
  36.6 2.4 %collective-permute-done.11.refs_3_ = bf16[384,384]{1,0:T(8,128)(2,1)S(1)} collective-permute-done((bf16[384,384]{1,0:T(8,128)(2,1)S(1)}, bf16[384,384]{1,0:T(8,128)(2,1)S(1)}, u32[]{:S(2)}, u32[]{:S(2)}) %collective-permute-start.11) | collective-permute-done | bytes 294944 | tf_op jit(solution)/shard_map/ppermute | solution.py:642
  39.5 2.2 %mlp_own.1 = (bf16[592,768]{1,0:T(8,128)(2,1)S(1)}, bf16[592,768]{1,0:T(8,128)(2,1)S(1)}, f32[8,768]{1,0:T(8,128)S(1)}, bf16[4,4,96,384]{3,2,1,0:T(8,128)(2,1)S(1)}) custom-call(bf16[592,384]{1,0:T(8,128)(2,1)S(1)} %get-tuple-element.111.refs_0_.refs_1_, bf16[592,384]{1,0:T(8,128)(2,1)S(1)} %get-tuple-element.110.refs_1_.refs_2_.refs_4_, ...), custom_call_target="tpu_custom_call" | custom-call | flops 4600000000 | bytes 1 | tf_op jit(solution)/shard_map/mlp_own/pallas_call | solution.py:35
  42.4 2.2 %mlp_oth.1 = (bf16[592,768]{1,0:T(8,128)(2,1)S(1)}, bf16[592,768]{1,0:T(8,128)(2,1)S(1)}, f32[8,768]{1,0:T(8,128)S(1)}, bf16[4,4,96,384]{3,2,1,0:T(8,128)(2,1)S(1)}) custom-call(f32[8,768]{1,0:T(8,128)S(1)} %get-tuple-element.114.refs_0_.refs_10_, bf16[592,384]{1,0:T(8,128)(2,1)S(1)} %get-tuple-element.111.refs_0_.refs_1_, ...), custom_call_target="tpu_custom_call" | custom-call | flops 4600000000 | bytes 1 | tf_op jit(solution)/shard_map/mlp_oth/pallas_call | solution.py:35
  44.8 2.3 %mlp_sums.1 = (f32[592,384]{1,0:T(8,128)S(1)}, bf16[592,384]{1,0:T(8,128)(2,1)S(1)}, f32[384,384]{1,0:T(8,128)S(1)}, f32[16,384]{1,0:T(8,128)S(1)}) custom-call(f32[592,384]{1,0:T(8,128)S(1)} %get-tuple-element.106.refs_0_.refs_1_, bf16[592,384]{1,0:T(8,128)(2,1)S(1)} %get-tuple-element.107.refs_1_, bf16[384,384]{1,0:T(8,128)(2,1)S(1)} %get-tuple-element.108.refs_2_, ...), custom_call_target="tpu_custom_call" | custom-call | flops 2300000000 | bytes 1 | tf_op jit(solution)/shard_map/mlp_sums/pallas_call | solution.py:35
  47.7 1.6 %collective-permute-start.15 = (bf16[2,2,96,384]{3,2,1,0:T(8,128)(2,1)S(1)}, bf16[2,2,96,384]{3,2,1,0:T(8,128)(2,1)S(1)}, u32[]{:S(2)}, u32[]{:S(2)}) collective-permute-start(bf16[2,2,96,384]{3,2,1,0:T(8,128)(2,1)S(1)} %get-tuple-element.130), channel_id=1, source_target_pairs={{0,2},{2,0},{4,6},{6,4},{1,3},{3,1},{5,7},{7,5},{8,10},{10,8},{12,... | collective-permute-start | bytes 884744 | tf_op jit(solution)/shard_map/ppermute | solution.py:771
  49.8 7.7 %attention_back.1 = (f32[592,384]{1,0:T(8,128)S(1)}, bf16[4,4,160,128]{3,2,1,0:T(8,128)(2,1)S(1)}, bf16[4,4,160,128]{3,2,1,0:T(8,128)(2,1)S(1)}) custom-call(bf16[2,2,96,384]{3,2,1,0:T(8,128)(2,1)S(1)} %get-tuple-element.119.refs_0_.refs_1_, bf16[640,1152]{1,0:T(8,128)(2,1)S(1)} %get-tuple-element.120.refs_1_, ...), custom_call_target="tpu_custom_call" | custom-call | flops 12650000384 | bytes 1 | tf_op jit(solution)/shard_map/attention_back/pallas_call | solution.py:35
  67.2 3.5 %all-to-all-start = ((bf16[4,304,384]{2,1,0:T(8,128)(2,1)}), bf16[4,304,384]{2,1,0:T(8,128)(2,1)S(1)}, u32[]{:S(2)}, u32[]{:S(2)}) async-start(bf16[4,304,384]{2,1,0:T(8,128)(2,1)} %returns.1.refs_0_), calls=%async_computation | async-start | bytes 1867776 | tf_op jit(solution)/shard_map/all_to_all | solution.py:799
  72.3 2.0 %collective-permute-start.24 = (bf16[1,96,384]{2,1,0:T(8,128)(2,1)S(1)}, bf16[1,96,384]{2,1,0:T(8,128)(2,1)S(1)}, u32[]{:S(2)}, u32[]{:S(2)}) collective-permute-start(bf16[1,96,384]{2,1,0:T(8,128)(2,1)S(1)} %get-tuple-element.152), channel_id=1, source_target_pairs={{0,16},{8,24},{16,0},{24,8},{1,17},{9,25},{17,1},{25,9},{2,18},{10... | collective-permute-start | bytes 221192 | tf_op jit(solution)/shard_map/ppermute | solution.py:816
  74.3 1.8 %collective-permute-start.25 = (bf16[160,128]{1,0:T(8,128)(2,1)S(1)}, bf16[160,128]{1,0:T(8,128)(2,1)S(1)}, u32[]{:S(2)}, u32[]{:S(2)}) collective-permute-start(bf16[160,128]{1,0:T(8,128)(2,1)S(1)} %get-tuple-element.153), channel_id=1, source_target_pairs={{0,8},{8,0},{16,24},{24,16},{1,9},{9,1},{17,25},{25,17},{2,10},{10... | collective-permute-start | bytes 122888 | tf_op jit(solution)/shard_map/ppermute | solution.py:642
  76.2 2.5 %collective-permute-start.27 = (bf16[160,128]{1,0:T(8,128)(2,1)S(1)}, bf16[160,128]{1,0:T(8,128)(2,1)S(1)}, u32[]{:S(2)}, u32[]{:S(2)}) collective-permute-start(bf16[160,128]{1,0:T(8,128)(2,1)S(1)} %get-tuple-element.155), channel_id=1, source_target_pairs={{0,24},{8,16},{16,8},{24,0},{1,25},{9,17},{17,9},{25,1},{2,26},{10... | collective-permute-start | bytes 122888 | tf_op jit(solution)/shard_map/ppermute | solution.py:642
  78.7 2.4 %collective-permute-done.26.refs_4_ = bf16[160,128]{1,0:T(8,128)(2,1)S(1)} collective-permute-done((bf16[160,128]{1,0:T(8,128)(2,1)S(1)}, bf16[160,128]{1,0:T(8,128)(2,1)S(1)}, u32[]{:S(2)}, u32[]{:S(2)}) %collective-permute-start.26) | collective-permute-done | bytes 40992 | tf_op jit(solution)/shard_map/ppermute | solution.py:642
  82.4 2.4 %collective-permute-start.31 = (bf16[160,384]{1,0:T(8,128)(2,1)S(1)}, bf16[160,384]{1,0:T(8,128)(2,1)S(1)}, u32[]{:S(2)}, u32[]{:S(2)}) collective-permute-start(bf16[160,384]{1,0:T(8,128)(2,1)S(1)} %sum_dp.1.refs_0_.refs_1_), channel_id=1, source_target_pairs={{0,6},{2,4},{4,2},{6,0},{1,7},{3,5},{5,3},{7,1},{8,14},{10,12},{12... | collective-permute-start | bytes 368648 | tf_op jit(solution)/shard_map/ppermute | solution.py:642
  86.0 2.7 %place_slots.1 = (f32[1160,384]{1,0:T(8,128)}, f32[1160,384]{1,0:T(8,128)}, f32[8,128]{1,0:T(8,128)S(1)}) custom-call(bf16[4,304,384]{2,1,0:T(8,128)(2,1)S(1)} %hand_on.1.refs_0_, bf16[4,304,384]{2,1,0:T(8,128)(2,1)S(1)} %collective-permute-done.28.refs_1_, f32[2,8,384]{2,1,0:T(8,128)S(1)} %get-tuple-element.156.refs_2_, s32[8,145]{1,0:T(8,128)S(1)} %copy-done.4), custom_call_target="tpu_custom_call" | custom-call | flops 2644999936 | bytes 1 | tf_op jit(solution)/shard_map/place_slots/pallas_call | solution.py:35
  89.3 2.4 %collective-permute-done.30.refs_3_ = bf16[160,384]{1,0:T(8,128)(2,1)S(1)} collective-permute-done((bf16[160,384]{1,0:T(8,128)(2,1)S(1)}, bf16[160,384]{1,0:T(8,128)(2,1)S(1)}, u32[]{:S(2)}, u32[]{:S(2)}) %collective-permute-start.30) | collective-permute-done | bytes 122912 | tf_op jit(solution)/shard_map/ppermute | solution.py:642
  (76 shorter events, 23.2 us)
Async XLA Ops:
  2.9 12.1 %collective-permute-start.5 = (bf16[1,96,384]{2,1,0:T(8,128)(2,1)}, bf16[1,96,384]{2,1,0:T(8,128)(2,1)S(1)}, u32[]{:S(2)}, u32[]{:S(2)}) collective-permute-start(bf16[1,96,384]{2,1,0:T(8,128)(2,1)} %bitcast.20), channel_id=1, source_target_pairs={{0,16},{8,24},{16,0},{24,8},{1,17},{9,25},{17,1},{25,9},{2,18},{10... | collective-permute-start | bytes 221192 | tf_op jit(solution)/shard_map/ppermute | solution.py:682
  7.0 11.6 %collective-permute-start.3 = (bf16[1,112,768]{2,1,0:T(8,128)(2,1)}, bf16[1,112,768]{2,1,0:T(8,128)(2,1)S(1)}, u32[]{:S(2)}, u32[]{:S(2)}) collective-permute-start(bf16[1,112,768]{2,1,0:T(8,128)(2,1)} %bitcast.18), channel_id=1, source_target_pairs={{0,16},{8,24},{16,0},{24,8},{1,17},{9,25},{17,1},{25,9},{2,18},{10... | collective-permute-start | bytes 516104 | tf_op jit(solution)/shard_map/ppermute | solution.py:682
  7.8 14.0 %collective-permute-start = (bf16[304,384]{1,0:T(8,128)(2,1)S(1)}, bf16[304,384]{1,0:T(8,128)(2,1)S(1)}, u32[]{:S(2)}, u32[]{:S(2)}) collective-permute-start(bf16[304,384]{1,0:T(8,128)(2,1)S(1)} %get-tuple-element.97), channel_id=1, source_target_pairs={{0,2},{2,0},{4,6},{6,4},{1,3},{3,1},{5,7},{7,5},{8,10},{10,8},{12,... | collective-permute-start | bytes 700424 | tf_op jit(solution)/shard_map/ppermute | solution.py:642
  9.7 12.2 %collective-permute-start.1 = (bf16[304,384]{1,0:T(8,128)(2,1)S(1)}, bf16[304,384]{1,0:T(8,128)(2,1)S(1)}, u32[]{:S(2)}, u32[]{:S(2)}) collective-permute-start(bf16[304,384]{1,0:T(8,128)(2,1)S(1)} %get-tuple-element.98), channel_id=1, source_target_pairs={{0,4},{2,6},{4,0},{6,2},{1,5},{3,7},{5,1},{7,3},{8,12},{10,14},{12... | collective-permute-start | bytes 700424 | tf_op jit(solution)/shard_map/ppermute | solution.py:642
  11.2 10.7 %collective-permute-start.2 = (bf16[304,384]{1,0:T(8,128)(2,1)S(1)}, bf16[304,384]{1,0:T(8,128)(2,1)S(1)}, u32[]{:S(2)}, u32[]{:S(2)}) collective-permute-start(bf16[304,384]{1,0:T(8,128)(2,1)S(1)} %get-tuple-element.99), channel_id=1, source_target_pairs={{0,6},{2,4},{4,2},{6,0},{1,7},{3,5},{5,3},{7,1},{8,14},{10,12},{12... | collective-permute-start | bytes 700424 | tf_op jit(solution)/shard_map/ppermute | solution.py:642
  15.0 6.8 %collective-permute-start.6 = (bf16[2,96,384]{2,1,0:T(8,128)(2,1)S(1)}, bf16[2,96,384]{2,1,0:T(8,128)(2,1)S(1)}, u32[]{:S(2)}, u32[]{:S(2)}) collective-permute-start(bf16[2,96,384]{2,1,0:T(8,128)(2,1)S(1)} %join_quarter.1.refs_4_), channel_id=1, source_target_pairs={{0,8},{8,0},{16,24},{24,16},{1,9},{9,1},{17,25},{25,17},{2,10},{10... | collective-permute-start | bytes 442376 | tf_op jit(solution)/shard_map/ppermute | solution.py:684
  18.7 10.4 %collective-permute-start.4 = (bf16[2,112,768]{2,1,0:T(8,128)(2,1)S(1)}, bf16[2,112,768]{2,1,0:T(8,128)(2,1)S(1)}, u32[]{:S(2)}, u32[]{:S(2)}) collective-permute-start(bf16[2,112,768]{2,1,0:T(8,128)(2,1)S(1)} %join_attn.1.refs_3_.refs_4_), channel_id=1, source_target_pairs={{0,8},{8,0},{16,24},{24,16},{1,9},{9,1},{17,25},{25,17},{2,10},{10... | collective-permute-start | bytes 1032200 | tf_op jit(solution)/shard_map/ppermute | solution.py:684
  22.0 7.1 %collective-permute-start.7 = (bf16[2,112,768]{2,1,0:T(8,128)(2,1)S(1)}, bf16[2,112,768]{2,1,0:T(8,128)(2,1)S(1)}, u32[]{:S(2)}, u32[]{:S(2)}) collective-permute-start(bf16[2,112,768]{2,1,0:T(8,128)(2,1)S(1)} %get-tuple-element.102), channel_id=1, source_target_pairs={{0,1},{1,0},{2,3},{3,2},{4,5},{5,4},{6,7},{7,6},{8,9},{9,8},{10,11... | collective-permute-start | bytes 1032200 | tf_op jit(solution)/shard_map/ppermute | solution.py:666
  22.0 14.6 %collective-permute-start.12 = (bf16[384,384]{1,0:T(8,128)(2,1)S(1)}, bf16[384,384]{1,0:T(8,128)(2,1)S(1)}, u32[]{:S(2)}, u32[]{:S(2)}) collective-permute-start(bf16[384,384]{1,0:T(8,128)(2,1)S(1)} %get-tuple-element.103.refs_1_), channel_id=1, source_target_pairs={{0,6},{2,4},{4,2},{6,0},{1,7},{3,5},{5,3},{7,1},{8,14},{10,12},{12... | collective-permute-start | bytes 884744 | tf_op jit(solution)/shard_map/ppermute | solution.py:642
  25.1 13.9 %collective-permute-start.11 = (bf16[384,384]{1,0:T(8,128)(2,1)S(1)}, bf16[384,384]{1,0:T(8,128)(2,1)S(1)}, u32[]{:S(2)}, u32[]{:S(2)}) collective-permute-start(bf16[384,384]{1,0:T(8,128)(2,1)S(1)} %get-tuple-element.103.refs_1_), channel_id=1, source_target_pairs={{0,4},{2,6},{4,0},{6,2},{1,5},{3,7},{5,1},{7,3},{8,12},{10,14},{12... | collective-permute-start | bytes 884744 | tf_op jit(solution)/shard_map/ppermute | solution.py:642
  25.6 13.7 %collective-permute-start.10 = (bf16[384,384]{1,0:T(8,128)(2,1)S(1)}, bf16[384,384]{1,0:T(8,128)(2,1)S(1)}, u32[]{:S(2)}, u32[]{:S(2)}) collective-permute-start(bf16[384,384]{1,0:T(8,128)(2,1)S(1)} %get-tuple-element.103.refs_1_), channel_id=1, source_target_pairs={{0,2},{2,0},{4,6},{6,4},{1,3},{3,1},{5,7},{7,5},{8,10},{10,8},{12,... | collective-permute-start | bytes 884744 | tf_op jit(solution)/shard_map/ppermute | solution.py:642
  47.7 9.8 %collective-permute-start.15 = (bf16[2,2,96,384]{3,2,1,0:T(8,128)(2,1)S(1)}, bf16[2,2,96,384]{3,2,1,0:T(8,128)(2,1)S(1)}, u32[]{:S(2)}, u32[]{:S(2)}) collective-permute-start(bf16[2,2,96,384]{3,2,1,0:T(8,128)(2,1)S(1)} %get-tuple-element.130), channel_id=1, source_target_pairs={{0,2},{2,0},{4,6},{6,4},{1,3},{3,1},{5,7},{7,5},{8,10},{10,8},{12,... | collective-permute-start | bytes 884744 | tf_op jit(solution)/shard_map/ppermute | solution.py:771
  49.3 8.8 %collective-permute-start.16 = (bf16[2,2,96,384]{3,2,1,0:T(8,128)(2,1)S(1)}, bf16[2,2,96,384]{3,2,1,0:T(8,128)(2,1)S(1)}, u32[]{:S(2)}, u32[]{:S(2)}) collective-permute-start(bf16[2,2,96,384]{3,2,1,0:T(8,128)(2,1)S(1)} %get-tuple-element.132), channel_id=1, source_target_pairs={{0,4},{2,6},{4,0},{6,2},{1,5},{3,7},{5,1},{7,3},{8,12},{10,14},{12... | collective-permute-start | bytes 884744 | tf_op jit(solution)/shard_map/ppermute | solution.py:771
  58.1 7.0 %collective-permute-start.18 = (bf16[2,96,384]{2,1,0:T(8,128)(2,1)S(1)}, bf16[2,96,384]{2,1,0:T(8,128)(2,1)S(1)}, u32[]{:S(2)}, u32[]{:S(2)}) collective-permute-start(bf16[2,96,384]{2,1,0:T(8,128)(2,1)S(1)} %get-tuple-element.141), channel_id=1, source_target_pairs={{0,4},{2,6},{4,0},{6,2},{1,5},{3,7},{5,1},{7,3},{8,12},{10,14},{12... | collective-permute-start | bytes 442376 | tf_op jit(solution)/shard_map/ppermute | solution.py:784
  59.2 6.7 %collective-permute-start.19 = (bf16[2,96,384]{2,1,0:T(8,128)(2,1)S(1)}, bf16[2,96,384]{2,1,0:T(8,128)(2,1)S(1)}, u32[]{:S(2)}, u32[]{:S(2)}) collective-permute-start(bf16[2,96,384]{2,1,0:T(8,128)(2,1)S(1)} %get-tuple-element.143), channel_id=1, source_target_pairs={{0,2},{2,0},{4,6},{6,4},{1,3},{3,1},{5,7},{7,5},{8,10},{10,8},{12,... | collective-permute-start | bytes 442376 | tf_op jit(solution)/shard_map/ppermute | solution.py:784
  60.3 10.4 %collective-permute-start.20 = (bf16[4,160,128]{2,1,0:T(8,128)(2,1)S(1)}, bf16[4,160,128]{2,1,0:T(8,128)(2,1)S(1)}, u32[]{:S(2)}, u32[]{:S(2)}) collective-permute-start(bf16[4,160,128]{2,1,0:T(8,128)(2,1)S(1)} %get-tuple-element.146), channel_id=1, source_target_pairs={{0,2},{2,0},{4,6},{6,4},{1,3},{3,1},{5,7},{7,5},{8,10},{10,8},{12,... | collective-permute-start | bytes 491528 | tf_op jit(solution)/shard_map/ppermute | solution.py:642
  61.5 9.2 %collective-permute-start.21 = (bf16[4,160,128]{2,1,0:T(8,128)(2,1)S(1)}, bf16[4,160,128]{2,1,0:T(8,128)(2,1)S(1)}, u32[]{:S(2)}, u32[]{:S(2)}) collective-permute-start(bf16[4,160,128]{2,1,0:T(8,128)(2,1)S(1)} %get-tuple-element.147), channel_id=1, source_target_pairs={{0,4},{2,6},{4,0},{6,2},{1,5},{3,7},{5,1},{7,3},{8,12},{10,14},{12... | collective-permute-start | bytes 491528 | tf_op jit(solution)/shard_map/ppermute | solution.py:642
  62.5 9.7 %collective-permute-start.22 = (bf16[4,160,128]{2,1,0:T(8,128)(2,1)S(1)}, bf16[4,160,128]{2,1,0:T(8,128)(2,1)S(1)}, u32[]{:S(2)}, u32[]{:S(2)}) collective-permute-start(bf16[4,160,128]{2,1,0:T(8,128)(2,1)S(1)} %get-tuple-element.148), channel_id=1, source_target_pairs={{0,6},{2,4},{4,2},{6,0},{1,7},{3,5},{5,3},{7,1},{8,14},{10,12},{12... | collective-permute-start | bytes 491528 | tf_op jit(solution)/shard_map/ppermute | solution.py:642
  66.0 6.3 %collective-permute-start.23 = (bf16[2,96,384]{2,1,0:T(8,128)(2,1)S(1)}, bf16[2,96,384]{2,1,0:T(8,128)(2,1)S(1)}, u32[]{:S(2)}, u32[]{:S(2)}) collective-permute-start(bf16[2,96,384]{2,1,0:T(8,128)(2,1)S(1)} %get-tuple-element.150), channel_id=1, source_target_pairs={{0,8},{8,0},{16,24},{24,16},{1,9},{9,1},{17,25},{25,17},{2,10},{10... | collective-permute-start | bytes 442376 | tf_op jit(solution)/shard_map/ppermute | solution.py:812
  67.2 15.1 %all-to-all-start = ((bf16[4,304,384]{2,1,0:T(8,128)(2,1)}), bf16[4,304,384]{2,1,0:T(8,128)(2,1)S(1)}, u32[]{:S(2)}, u32[]{:S(2)}) async-start(bf16[4,304,384]{2,1,0:T(8,128)(2,1)} %returns.1.refs_0_), calls=%async_computation | async-start | bytes 1867776 | tf_op jit(solution)/shard_map/all_to_all | solution.py:799
  72.3 9.7 %collective-permute-start.24 = (bf16[1,96,384]{2,1,0:T(8,128)(2,1)S(1)}, bf16[1,96,384]{2,1,0:T(8,128)(2,1)S(1)}, u32[]{:S(2)}, u32[]{:S(2)}) collective-permute-start(bf16[1,96,384]{2,1,0:T(8,128)(2,1)S(1)} %get-tuple-element.152), channel_id=1, source_target_pairs={{0,16},{8,24},{16,0},{24,8},{1,17},{9,25},{17,1},{25,9},{2,18},{10... | collective-permute-start | bytes 221192 | tf_op jit(solution)/shard_map/ppermute | solution.py:816
  82.4 6.9 %collective-permute-start.31 = (bf16[160,384]{1,0:T(8,128)(2,1)S(1)}, bf16[160,384]{1,0:T(8,128)(2,1)S(1)}, u32[]{:S(2)}, u32[]{:S(2)}) collective-permute-start(bf16[160,384]{1,0:T(8,128)(2,1)S(1)} %sum_dp.1.refs_0_.refs_1_), channel_id=1, source_target_pairs={{0,6},{2,4},{4,2},{6,0},{1,7},{3,5},{5,3},{7,1},{8,14},{10,12},{12... | collective-permute-start | bytes 368648 | tf_op jit(solution)/shard_map/ppermute | solution.py:642
  84.8 6.9 %collective-permute-start.30 = (bf16[160,384]{1,0:T(8,128)(2,1)S(1)}, bf16[160,384]{1,0:T(8,128)(2,1)S(1)}, u32[]{:S(2)}, u32[]{:S(2)}) collective-permute-start(bf16[160,384]{1,0:T(8,128)(2,1)S(1)} %sum_dp.1.refs_0_.refs_1_), channel_id=1, source_target_pairs={{0,4},{2,6},{4,0},{6,2},{1,5},{3,7},{5,1},{7,3},{8,12},{10,14},{12... | collective-permute-start | bytes 368648 | tf_op jit(solution)/shard_map/ppermute | solution.py:642
  85.3 6.4 %collective-permute-start.29 = (bf16[160,384]{1,0:T(8,128)(2,1)S(1)}, bf16[160,384]{1,0:T(8,128)(2,1)S(1)}, u32[]{:S(2)}, u32[]{:S(2)}) collective-permute-start(bf16[160,384]{1,0:T(8,128)(2,1)S(1)} %sum_dp.1.refs_0_.refs_1_), channel_id=1, source_target_pairs={{0,2},{2,0},{4,6},{6,4},{1,3},{3,1},{5,7},{7,5},{8,10},{10,8},{12,... | collective-permute-start | bytes 368648 | tf_op jit(solution)/shard_map/ppermute | solution.py:642
  (14 other events, 65.2 us)
